TPU v7x, 256 devices: a whole 4x4x8 slice. The times are simulated.
256 devices in a mesh: replica: 4 (over x), fsdp: 64 (over z, y, core).
Axes of the slice: x: 4, y: 4, z: 8, core: 2. Of those that a mesh axis runs over, the one named last changes fastest.
Arguments:
- grad_parts: bfloat16 [4, 4096, 12, 1024], P('replica', 'fsdp'), may hold values from -13 to 13
- col_widths: int32 [12], replicated, may hold values from 512 to 1024, as said below
- assignment: int32 [48], replicated, may hold values from 0 to 63, as said below
- left_stat: float32 [128, 1024, 1024], P('fsdp', 'replica'), may hold values from -1 to 40
- right_stat: float32 [128, 1024, 1024], P('fsdp', 'replica'), may hold values from -1 to 40
- left_root: bfloat16 [128, 1024, 1024], P('fsdp', None, 'replica'), may hold values from -0.25 to 5
- right_root: bfloat16 [128, 1024, 1024], P('fsdp', None, 'replica'), may hold values from -0.25 to 5
Outputs:
- update: bfloat16 [4096, 12, 1024], P('fsdp', None, 'replica')
- left_new: float32 [128, 1024, 1024], P('fsdp', 'replica')
- right_new: float32 [128, 1024, 1024], P('fsdp', 'replica')
Inputs may be any that keep to these rules, and one draw needn't show every extreme that they name: `assignment`: each worker index is named by at most 2 blocks, and some worker by exactly 2. `col_widths`: exactly one column block is 512 wide, every other one 1024.
All inputs are finite; a program needn't handle non-finite values.
Results may differ from a plain program's by a relative error of at most 0.012.
Values may be sent and summed in bfloat16 or wider, within the bound.
No kernel may reach another device: no remote copies, remote signals or barrier semaphores. Data moves between devices by JAX's collectives and lax.ppermute only.
A program may use at most 128 MiB of HBM per device.

v0:
```python
import jax
import jax.numpy as jnp
from jax import lax
from jax.sharding import PartitionSpec as P

DECAY = 0.99
SHRINKAGE = 0.1
EPSILON = 1e-06


def slot_tables(assignment, workers, slots):
    blocks = jnp.arange(assignment.shape[0], dtype=jnp.int32)
    same_worker = assignment[:, None] == assignment[None, :]
    earlier = blocks[None, :] < blocks[:, None]
    slot_rank = jnp.sum((same_worker & earlier).astype(jnp.int32), axis=1)
    slot_ids = assignment * slots + slot_rank
    wanted = jnp.arange(workers * slots, dtype=jnp.int32)
    slot_hits = (slot_ids[None, :] == wanted[:, None]).astype(jnp.int32)
    filled = jnp.sum(slot_hits, axis=1) > 0
    block_ids = jnp.sum(slot_hits * blocks[None, :], axis=1)
    return (slot_rank, filled, block_ids)


def on_device(grad_parts, col_widths, assignment, left_stat, right_stat, left_root, right_root):
    workers = lax.axis_size("fsdp")
    me_rep = lax.axis_index("replica")
    me_work = lax.axis_index("fsdp")
    slots = left_stat.shape[0]
    quarter = left_stat.shape[1]
    block_size = left_stat.shape[2]
    rows_dev = grad_parts.shape[1]
    ncols = grad_parts.shape[2]
    per_row = block_size // rows_dev
    slot_rank, filled, block_ids = slot_tables(assignment, workers, slots)
    row_block = block_ids // ncols
    col_block = block_ids % ncols
    col_index = jnp.arange(block_size, dtype=jnp.int32)
    col_mask = (col_index[None, :] < col_widths[:, None]).astype(jnp.float32)
    terms = grad_parts[0].astype(jnp.float32) * col_mask[None]
    summed = lax.psum_scatter(
        terms.astype(jnp.bfloat16), "replica", scatter_dimension=2, tiled=True
    ).astype(jnp.float32)
    by_block = jnp.transpose(summed, (1, 0, 2))
    pick_col = col_block.reshape(workers, slots).T
    send_live = (filled & (row_block == me_work // per_row)).reshape(workers, slots).T
    outgoing = (
        jnp.take(by_block, pick_col, axis=0) * send_live.astype(jnp.float32)[:, :, None, None]
    )
    incoming = lax.all_to_all(
        outgoing.astype(jnp.bfloat16), "fsdp", split_axis=1, concat_axis=1, tiled=True
    ).astype(outgoing.dtype)
    my_blocks = lax.dynamic_slice_in_dim(block_ids, me_work * slots, slots)
    my_filled = lax.dynamic_slice_in_dim(filled, me_work * slots, slots)
    my_row = my_blocks // ncols
    my_col = my_blocks % ncols
    looked_up = jnp.sum(
        jnp.where(
            my_col[:, None] == jnp.arange(ncols, dtype=jnp.int32)[None, :], col_widths[None, :], 0
        ),
        axis=1,
    )
    my_width = jnp.where(my_filled, looked_up, block_size)

    def take_rows(received, first_row):
        return lax.dynamic_slice_in_dim(received, first_row, per_row, 0)

    pieces = jax.vmap(take_rows)(incoming, my_row * per_row)
    g_cols = pieces.reshape(slots, block_size, quarter)
    g_full = lax.all_gather(g_cols.astype(jnp.bfloat16), "replica", axis=2, tiled=True).astype(
        g_cols.dtype
    )
    left_wide = lax.all_gather(left_root, "replica", axis=2, tiled=True)
    own_rows = lax.dynamic_slice_in_dim(g_full, me_rep * quarter, quarter, 1)
    left_total = DECAY * left_stat + (1.0 - DECAY) * jnp.einsum(
        "sqk,spk->sqp", own_rows, g_full, precision=lax.Precision.HIGHEST
    )
    right_total = DECAY * right_stat + (1.0 - DECAY) * jnp.einsum(
        "skq,skp->sqp", g_cols, g_full, precision=lax.Precision.HIGHEST
    )
    global_rows = me_rep * quarter + jnp.arange(quarter, dtype=jnp.int32)
    unit_rows = (col_index[None, :] == global_rows[:, None]).astype(jnp.float32)
    within_width = (global_rows[None, :] < my_width[:, None]).astype(jnp.float32)
    left_part = jnp.sum(left_total * unit_rows[None], axis=(1, 2))
    right_part = jnp.sum(jnp.sum(right_total * unit_rows[None], axis=2) * within_width, axis=1)
    g_half = g_full.astype(jnp.bfloat16)
    left_prod = jnp.einsum(
        "sik,skp->sip", left_wide, g_half, preferred_element_type=jnp.float32
    ).astype(jnp.bfloat16)
    precond = jnp.einsum("sik,skq->siq", left_prod, right_root, preferred_element_type=jnp.float32)
    precond = precond * within_width[:, None, :]
    grad_square = jnp.sum(g_full * g_full, axis=(1, 2))
    precond_part = jnp.sum(precond * precond, axis=(1, 2))
    left_trace, right_trace, precond_square = lax.psum(
        (left_part, right_part, precond_part), "replica"
    )
    left_new = (1.0 - SHRINKAGE) * left_total + (SHRINKAGE * left_trace / block_size)[
        :, None, None
    ] * unit_rows[None]
    right_scale = SHRINKAGE * right_trace / my_width.astype(jnp.float32)
    right_new = (1.0 - SHRINKAGE) * right_total + right_scale[:, None, None] * (
        unit_rows[None] * within_width[:, :, None]
    )
    graft_scale = jnp.sqrt(grad_square / (precond_square + EPSILON))
    graft_update = (precond * graft_scale[:, None, None]).astype(jnp.bfloat16)
    update_rows = graft_update.reshape(slots, per_row, rows_dev, quarter)
    spread_rows = jnp.broadcast_to(
        update_rows[:, None], (slots, workers // per_row, per_row, rows_dev, quarter)
    )
    spread_rows = spread_rows.reshape(slots, workers, rows_dev, quarter)
    dest_group = jnp.arange(workers, dtype=jnp.int32) // per_row
    return_live = my_filled[:, None] & (my_row[:, None] == dest_group[None, :])
    returning = jnp.where(return_live[:, :, None, None], spread_rows, jnp.zeros((), jnp.bfloat16))
    arrived = lax.all_to_all(returning, "fsdp", split_axis=1, concat_axis=1, tiled=True)
    owner_first = me_work // per_row * ncols
    owner_worker = lax.dynamic_slice_in_dim(assignment, owner_first, ncols)
    owner_slot = lax.dynamic_slice_in_dim(slot_rank, owner_first, ncols)
    flattened = arrived.reshape(slots * workers, rows_dev, quarter)
    picked = jnp.take(flattened, owner_slot * workers + owner_worker, axis=0)
    update = jnp.transpose(picked, (1, 0, 2))
    return (update, left_new, right_new)


def solution(mesh):
    in_specs = (
        P("replica", "fsdp", None, None),
        P(),
        P(),
        P("fsdp", "replica", None),
        P("fsdp", "replica", None),
        P("fsdp", None, "replica"),
        P("fsdp", None, "replica"),
    )
    out_specs = (P("fsdp", None, "replica"), P("fsdp", "replica", None), P("fsdp", "replica", None))
    return jax.shard_map(
        on_device, mesh=mesh, in_specs=in_specs, out_specs=out_specs, check_vma=False
    )
```

profile of v0, /device:TPU:1, one launch (start us, length us, event | category | flops | bytes accessed | tf_op | source)
XLA Modules:
  0.0 414.8 jit_solution(532072931385713774)
XLA Ops:
  7.2 0.8 fusion.9
  8.0 3.0 fusion.4
  11.1 0.2 convert_reduce_fusion.1
  12.3 30.0 %reduce-scatter.2.cloned.1.call-done = bf16[64,12,256]{2,0,1:T(8,128)(2,1)} async-done(((bf16[64,12,1024]{2,0,1:T(8,128)(2,1)}), bf16[64,12,256]{2,0,1:T(8,128)(2,1)}) %reduce-scatter.2.cloned.1.call-update) | async-done | bytes 393232 | tf_op jit(solution)/shard_map/reduce_scatter | solution.py:40
  42.3 1.1 convert_bitcast_fusion
  43.4 4.3 %gather_fusion = f32[128,64,256]{2,1,0:T(8,128)} fusion(f32[12,64,256]{2,1,0:T(8,128)S(1)} %convert_bitcast_fusion, s32[1024]{0:T(1024)S(1)} %pad_clamp_fusion.1), kind=kCustom, calls=%fused_computation | custom fusion | bytes 16777728 | tf_op jit(solution)/shard_map/jit(_take)/gather | solution.py:47
  47.7 5.2 %fusion.1 = bf16[2,64,64,256]{3,2,0,1:T(8,128)(2,1)} fusion(f32[2,64,64,256]{3,2,1,0:T(8,128)} %bitcast.36, f32[2,64]{0,1:T(8,128)S(1)} %convert_bitcast_fusion.1, pred[2,64]{0,1:T(8,128)(4,1)S(1)} %compare_and_fusion), kind=kLoop, calls=%fused_computation.6 | loop fusion | flops 6291456 | bytes 12583552 | tf_op jit(solution)/shard_map/convert_element_type | solution.py:50
  52.9 11.8 %all-to-all-start = ((bf16[2,64,64,256]{3,2,0,1:T(8,128)(2,1)}), bf16[2,64,64,256]{3,2,0,1:T(8,128)(2,1)}, u32[]{:S(2)}, u32[]{:S(2)}) async-start(bf16[2,64,64,256]{3,2,0,1:T(8,128)(2,1)} %fusion.1), calls=%async_computation.1 | async-start | bytes 8388608 | tf_op jit(solution)/shard_map/all_to_all | solution.py:49
  64.9 94.3 %all-to-all-done = bf16[2,64,64,256]{3,2,0,1:T(8,128)(2,1)} async-done(((bf16[2,64,64,256]{3,2,0,1:T(8,128)(2,1)}), bf16[2,64,64,256]{3,2,0,1:T(8,128)(2,1)}, u32[]{:S(2)}, u32[]{:S(2)}) %all-to-all-start) | async-done | bytes 4194336 | tf_op jit(solution)/shard_map/all_to_all | solution.py:49
  159.1 2.8 gather_fusion.2
  161.9 1.3 copy.47
  163.3 0.7 all-gather.5.cloned.1.call-update
  164.1 0.2 fusion.15
  164.7 1.2 fusion.8
  165.8 3.8 gather_fusion.3
  169.6 40.8 %all-gather.3.cloned.1.call-done = bf16[2,1024,1024]{1,2,0:T(8,128)(2,1)} async-done(((bf16[2,1024,256]{1,2,0:T(8,128)(2,1)}), bf16[2,1024,1024]{1,2,0:T(8,128)(2,1)}) %all-gather.3.cloned.1.call-update) | async-done | bytes 4194320 | tf_op jit(solution)/shard_map/all_gather | solution.py:69
  210.4 4.8 %multiply_add_fusion.3 = f32[2,256,1024]{2,1,0:T(8,128)S(1)} fusion(f32[2,256,1024]{2,1,0:T(8,128)} %param.10, bf16[2,1024,1024]{1,2,0:T(8,128)(2,1)} %all-gather.3.cloned.1.call-done, s32[]{:T(128)S(6)} %select_n.104), kind=kOutput, calls=%fused_computation.18 | convolution fusion | flops 1075314688 | bytes 9437188 | tf_op jit(solution)/shard_map/sqk,spk->sqp/dot_general | solution.py:74
  215.4 0.7 copy-done.5
  216.1 3.5 multiply_reduce_fusion.1
  219.5 0.2 fusion.14
  219.7 46.6 %all-gather.5.cloned.1.call-done = bf16[2,1024,1024]{2,1,0:T(8,128)(2,1)} async-done(((bf16[2,1024,256]{2,1,0:T(8,128)(2,1)}), bf16[2,1024,1024]{2,1,0:T(8,128)(2,1)}) %all-gather.5.cloned.1.call-update) | async-done | bytes 4194320 | tf_op jit(solution)/shard_map/all_gather | solution.py:72
  266.3 10.8 %multiply_reduce_fusion.3 = (f32[2]{0:T(128)S(1)}, f32[2,1024,256]{2,1,0:T(8,128)}) fusion(f32[2,256]{1,0:T(2,128)S(1)} %compare_convert_fusion, bf16[2,1024,256]{2,1,0:T(8,128)(2,1)S(1)} %copy-done, bf16[2,1024,1024]{1,2,0:T(8,128)(2,1)} %all-gather.3.cloned.1.call-done, bf16[2,1024,1024]{2,1,0:T(8,128)(2,1)} %all-gather.5.cloned.1.call-done), kind=kOutput, calls=%fused_computation.20 | convolution fusion | flops 5372379136 | bytes 11536392 | tf_op jit(solution)/shard_map/sik,skq->siq/dot_general | solution.py:89
  277.1 7.8 %all-reduce.1 = (f32[2]{0:T(128)S(1)}, f32[2]{0:T(128)S(1)}, f32[2]{0:T(128)S(1)}) all-reduce(f32[2]{0:T(128)S(1)} %get-tuple-element.20, f32[2]{0:T(128)S(1)} %get-tuple-element.4, f32[2]{0:T(128)S(1)} %fusion.14), channel_id=1, replica_groups=mesh['replica'=4,'fsdp'=64] {'replica'}, use_global_device_ids=true, to_apply=%region_7.8 | all-reduce | flops 6 | bytes 48 | tf_op jit(solution)/shard_map/psum | solution.py:93
  284.9 3.5 multiply_reduce_fusion
  288.5 0.5 multiply_convert_fusion
  289.0 2.7 bitcast_select_fusion
  291.7 13.8 %all-to-all-start.1 = ((bf16[2,64,64,256]{3,2,0,1:T(8,128)(2,1)}), bf16[2,64,64,256]{3,2,0,1:T(8,128)(2,1)}, u32[]{:S(2)}, u32[]{:S(2)}) async-start(bf16[2,64,64,256]{3,2,0,1:T(8,128)(2,1)} %bitcast_select_fusion), calls=%async_computation.2 | async-start | bytes 8388608 | tf_op jit(solution)/shard_map/all_to_all | solution.py:113
  305.7 4.4 %multiply_add_fusion = (f32[2,256,1024]{2,1,0:T(8,128)}, f32[2,256,1024]{2,1,0:T(8,128)}) fusion(f32[2,256,1024]{2,1,0:T(8,128)} %get-tuple-element.22, f32[2,256]{1,0:T(2,128)S(1)} %compare_convert_fusion, f32[2]{0:T(128)S(1)} %convert_divide_fusion, f32[256,1024]{1,0:T(8,128)} %fusion.8, f32[2]{0:T(128)S(1)} %broadcast_multiply_fusion, ...), kind=kLoop, calls=%fused_computation.13 | loop fusion | flops 3670016 | bytes 9439248 | tf_op jit(solution)/shard_map/add | solution.py:100
  310.1 89.9 %all-to-all-done.1 = bf16[2,64,64,256]{3,2,0,1:T(8,128)(2,1)} async-done(((bf16[2,64,64,256]{3,2,0,1:T(8,128)(2,1)}), bf16[2,64,64,256]{3,2,0,1:T(8,128)(2,1)}, u32[]{:S(2)}, u32[]{:S(2)}) %all-to-all-start.1) | async-done | bytes 4194336 | tf_op jit(solution)/shard_map/all_to_all | solution.py:113
  399.9 4.7 %copy.50 = bf16[2,64,64,256]{3,2,1,0:T(8,128)(2,1)} copy(bf16[2,64,64,256]{3,2,0,1:T(8,128)(2,1)} %all-to-all-done.1) | data formatting | bytes 8388608 | tf_op jit(solution)/shard_map/all_to_all | solution.py:113
  404.7 2.8 gather_fusion.1
  407.5 0.9 select_bitcast_fusion
  (47 shorter events, 1.9 us)
Async XLA Ops:
  7.2 259.2 %copy-start = (bf16[2,1024,256]{2,1,0:T(8,128)(2,1)S(1)}, bf16[2,1024,256]{2,1,0:T(8,128)(2,1)}, u32[]{:S(2)}) copy-start(bf16[2,1024,256]{2,1,0:T(8,128)(2,1)} %param.13) | copy-start | bytes 3145732
  7.2 35.1 %reduce-scatter.2.cloned.1.call-start = ((), (), s32[]{:S(2)}) async-start(), calls=%async_computation.3 | async-start | bytes 1966080 | tf_op jit(solution)/shard_map/reduce_scatter | solution.py:40
  8.0 3.0 copy-start.7
  52.9 106.2 %all-to-all-start = ((bf16[2,64,64,256]{3,2,0,1:T(8,128)(2,1)}), bf16[2,64,64,256]{3,2,0,1:T(8,128)(2,1)}, u32[]{:S(2)}, u32[]{:S(2)}) async-start(bf16[2,64,64,256]{3,2,0,1:T(8,128)(2,1)} %fusion.1), calls=%async_computation.1 | async-start | bytes 8388608 | tf_op jit(solution)/shard_map/all_to_all | solution.py:49
  64.7 145.7 %all-gather.3.cloned.1.call-start = ((), (), s32[]{:S(2)}) async-start(), calls=%async_computation.4 | async-start | bytes 5242880 | tf_op jit(solution)/shard_map/all_gather | solution.py:69
  161.9 2.2 copy-start.6
  163.3 103.0 %all-gather.5.cloned.1.call-start = ((), (), s32[]{:S(2)}) async-start(), calls=%async_computation.5 | async-start | bytes 5242880 | tf_op jit(solution)/shard_map/all_gather | solution.py:72
  210.4 4.8 %copy-start.1 = (bf16[2,1024,1024]{1,2,0:T(8,128)(2,1)S(1)}, bf16[2,1024,1024]{1,2,0:T(8,128)(2,1)}, u32[]{:S(2)}) copy-start(bf16[2,1024,1024]{1,2,0:T(8,128)(2,1)} %all-gather.3.cloned.1.call-done) | copy-start | bytes 12582916
  210.4 4.8 %copy-start.2 = (f32[256,1024]{1,0:T(8,128)S(1)}, f32[256,1024]{1,0:T(8,128)}, u32[]{:S(2)}) copy-start(f32[256,1024]{1,0:T(8,128)} %fusion.8) | copy-start | bytes 3145732
  210.4 5.0 %copy-start.3 = (bf16[2,16,64,256]{3,2,1,0:T(8,128)(2,1)S(1)}, bf16[2,16,64,256]{3,2,1,0:T(8,128)(2,1)}, u32[]{:S(2)}) copy-start(bf16[2,16,64,256]{3,2,1,0:T(8,128)(2,1)} %gather_fusion.3) | copy-start | bytes 3145732
  210.4 5.7 %copy-start.5 = (f32[2,256,1024]{2,1,0:T(8,128)S(1)}, f32[2,256,1024]{2,1,0:T(8,128)}, u32[]{:S(2)}) copy-start(f32[2,256,1024]{2,1,0:T(8,128)} %param.11) | copy-start | bytes 6291460
  284.9 3.6 copy-start.4
  291.7 108.3 %all-to-all-start.1 = ((bf16[2,64,64,256]{3,2,0,1:T(8,128)(2,1)}), bf16[2,64,64,256]{3,2,0,1:T(8,128)(2,1)}, u32[]{:S(2)}, u32[]{:S(2)}) async-start(bf16[2,64,64,256]{3,2,0,1:T(8,128)(2,1)} %bitcast_select_fusion), calls=%async_computation.2 | async-start | bytes 8388608 | tf_op jit(solution)/shard_map/all_to_all | solution.py:113
Sparse Core Ops, SparseCore 0:
  11.2 31.0 reduce-scatter.1
  163.4 46.9 all-gather.2
  212.2 54.0 all-gather.4
where the time goes:
time: 416 us; the launch traced here: 415 us
  waiting for transfers between devices  302 us (73%)
  starting transfers between devices  25.8 us (6%)
  other arithmetic  24.5 us (6%)
  local copies, waits for them, and re-layouts  21.5 us (5%)
  matrix products  19 us (5%)
  between operations  14 us (3%)
  blocking collectives  7.84 us (2%)
    all_to_all x1, waiting for transfers between devices, on_device(): lax.all_to_all(outgoing.astype(jnp.bfloat16), 'fsdp', split_axis=1, conca...  94.3 us
    all_to_all x1, waiting for transfers between devices, on_device(): lax.all_to_all(returning, 'fsdp', split_axis=1, concat_axis=1, tiled=True)  89.9 us
    all_gather x1, waiting for transfers between devices, on_device(): left_wide = lax.all_gather(left_root, 'replica', axis=2, tiled=True)  46.6 us
    all_gather x1, waiting for transfers between devices, on_device(): lax.all_gather(g_cols.astype(jnp.bfloat16), 'replica', axis=2, tiled=True)  40.8 us
    reduce_scatter x1, waiting for transfers between devices, on_device(): lax.psum_scatter(terms.astype(jnp.bfloat16), 'replica', scatter_dimension...  30 us
    all_to_all x1, starting transfers between devices, on_device(): lax.all_to_all(returning, 'fsdp', split_axis=1, concat_axis=1, tiled=True)  13.8 us
    all_to_all x1, starting transfers between devices, on_device(): lax.all_to_all(outgoing.astype(jnp.bfloat16), 'fsdp', split_axis=1, conca...  11.8 us
    dot_general x1, matrix products, on_device(): jnp.einsum('sik,skq->siq', left_prod, right_root, preferred_element_type=...  10.8 us
  transfers between devices with their start and end apart: 5, of which 5 were waited for; matrix products, arithmetic and copies ran while one was open for 5% of the time, Pallas kernels for 0%

commit v1 on v0

v1 whole, which is shorter than its diff:
```python
import jax
import jax.numpy as jnp
from jax import lax
from jax.sharding import PartitionSpec as P

DECAY = 0.99
SHRINKAGE = 0.1
EPSILON = 1e-06
F32 = jnp.float32
BF16 = jnp.bfloat16


def slot_tables(assignment, workers, slots):
    blocks = jnp.arange(assignment.shape[0], dtype=jnp.int32)
    same_worker = assignment[:, None] == assignment[None, :]
    earlier = blocks[None, :] < blocks[:, None]
    slot_rank = jnp.sum((same_worker & earlier).astype(jnp.int32), axis=1)
    slot_ids = assignment * slots + slot_rank
    wanted = jnp.arange(workers * slots, dtype=jnp.int32)
    slot_hits = (slot_ids[None, :] == wanted[:, None]).astype(jnp.int32)
    filled = jnp.sum(slot_hits, axis=1) > 0
    block_ids = jnp.sum(slot_hits * blocks[None, :], axis=1)
    return (slot_ids, filled, block_ids)


def on_device(grad_parts, col_widths, assignment, left_stat, right_stat, left_root, right_root):
    workers = lax.axis_size("fsdp")
    reps = lax.axis_size("replica")
    me_rep = lax.axis_index("replica")
    me_work = lax.axis_index("fsdp")
    slots, quarter, block_size = left_stat.shape
    rows_dev = grad_parts.shape[1]
    ncols = grad_parts.shape[2]
    per_row = block_size // rows_dev
    groups = workers // per_row
    piece = rows_dev // groups
    nblocks = assignment.shape[0]
    me_group = me_work // per_row

    def turn_x(value, shift):
        pairs = [(a, (a + shift) % reps) for a in range(reps)]
        return lax.ppermute(value, "replica", pairs)

    def turn_group(value, shift):
        pairs = [(a, (a + shift * per_row) % workers) for a in range(workers)]
        return lax.ppermute(value, "fsdp", pairs)

    def sum_x(value):
        total = value
        for shift in range(1, reps):
            total = total + turn_x(value, shift)
        return total

    slot_ids, filled, block_ids = slot_tables(assignment, workers, slots)
    col_index = jnp.arange(block_size, dtype=jnp.int32)
    col_mask = (col_index[None, :] < col_widths[:, None]).astype(F32)

    terms = (grad_parts[0].astype(F32) * col_mask[None]).astype(BF16)

    def columns_of(rep):
        cut = lax.dynamic_slice_in_dim(terms, rep * quarter, quarter, 2)
        return jnp.transpose(cut, (1, 0, 2))

    summed = columns_of(me_rep).astype(F32)
    for shift in (1, 3, 2):
        summed = summed + turn_x(columns_of((me_rep + shift) % reps), shift).astype(F32)
    summed = summed.astype(BF16)

    my_blocks = lax.dynamic_slice_in_dim(block_ids, me_work * slots, slots)
    my_filled = lax.dynamic_slice_in_dim(filled, me_work * slots, slots)
    my_col = my_blocks % ncols
    looked_up = jnp.sum(
        jnp.where(
            my_col[:, None] == jnp.arange(ncols, dtype=jnp.int32)[None, :], col_widths[None, :], 0
        ),
        axis=1,
    )
    my_width = jnp.where(my_filled, looked_up, block_size)
    global_rows = me_rep * quarter + jnp.arange(quarter, dtype=jnp.int32)
    unit_rows = (col_index[None, :] == global_rows[:, None]).astype(F32)
    within_width = (global_rows[None, :] < my_width[:, None]).astype(F32)
    left_diag = jnp.sum(left_stat * unit_rows[None], axis=(1, 2))
    right_diag = jnp.sum(jnp.sum(right_stat * unit_rows[None], axis=2) * within_width, axis=1)
    diag_sums = sum_x(jnp.stack([left_diag, right_diag]))

    left_wide = lax.all_gather(left_root, "replica", axis=0, tiled=False)

    summed = summed.reshape(ncols, groups, piece, quarter)

    def rows_of(group):
        return lax.dynamic_index_in_dim(summed, group, 1, keepdims=False)

    held = [rows_of(me_group)]
    for shift in range(1, groups):
        held.append(turn_group(rows_of((me_group + shift) % groups), shift))
    held = jnp.concatenate(held, axis=0)
    place = ((me_group - block_ids // ncols) % groups) * ncols + block_ids % ncols
    outgoing = jnp.take(held, place, axis=0).reshape(workers, slots, piece, quarter)
    incoming = lax.all_to_all(outgoing, "fsdp", split_axis=0, concat_axis=0, tiled=True)
    g_mine = jnp.transpose(
        incoming.reshape(groups, per_row, slots, piece, quarter), (2, 1, 0, 3, 4)
    ).reshape(slots, block_size, quarter)
    g_mine = jnp.where(my_filled[:, None, None], g_mine, jnp.zeros((), BF16))

    half = block_size // 2
    g_prev = turn_x(g_mine, 1)
    g_next = turn_x(g_mine, reps - 1)
    g_far = jnp.concatenate(
        [turn_x(g_prev[:, :half], 1), turn_x(g_next[:, half:], reps - 1)], axis=1
    )
    g_all = jnp.stack([g_mine, g_prev, g_far, g_next])
    order = (me_rep - jnp.arange(reps, dtype=jnp.int32)) % reps
    g_all = jnp.take(g_all, order, axis=0)

    right_quarters = right_root.reshape(slots, reps, quarter, quarter)
    right_prod = jnp.einsum(
        "xsik,sxkq->siq", g_all, right_quarters, preferred_element_type=F32
    ).astype(BF16)
    right_prod = right_prod.reshape(slots, reps, quarter, quarter)
    precond = jnp.einsum("xsik,sxkq->siq", left_wide, right_prod, preferred_element_type=F32)
    precond = precond * within_width[:, None, :]
    wide = g_all.astype(F32)
    grad_square = jnp.sum(wide * wide, axis=(0, 2, 3))
    precond_square = sum_x(jnp.sum(precond * precond, axis=(1, 2)))
    graft_scale = jnp.sqrt(grad_square / (precond_square + EPSILON))
    graft_update = (precond * graft_scale[:, None, None]).astype(BF16)

    returning = jnp.transpose(
        graft_update.reshape(slots, per_row, groups, piece, quarter), (2, 1, 0, 3, 4)
    ).reshape(workers, slots, piece, quarter)
    arrived = lax.all_to_all(returning, "fsdp", split_axis=0, concat_axis=0, tiled=True)
    arrived = arrived.reshape(workers * slots, piece, quarter)

    own_rows = lax.dynamic_slice_in_dim(g_all, me_rep * quarter, quarter, 2)
    left_gram = jnp.einsum("xsqk,xspk->sqp", own_rows, g_all, preferred_element_type=F32)
    right_gram = jnp.einsum("skq,xskp->sqxp", g_mine, g_all, preferred_element_type=F32)
    right_gram = right_gram.reshape(slots, quarter, block_size)
    left_total = DECAY * left_stat + (1.0 - DECAY) * left_gram
    right_total = DECAY * right_stat + (1.0 - DECAY) * right_gram
    traces = DECAY * diag_sums + (1.0 - DECAY) * grad_square[None, :]
    left_new = (1.0 - SHRINKAGE) * left_total + (SHRINKAGE * traces[0] / block_size)[
        :, None, None
    ] * unit_rows[None]
    right_scale = SHRINKAGE * traces[1] / my_width.astype(F32)
    right_new = (1.0 - SHRINKAGE) * right_total + right_scale[:, None, None] * (
        unit_rows[None] * within_width[:, :, None]
    )

    def blocks_of(group):
        ids = lax.dynamic_slice_in_dim(slot_ids, group * ncols, ncols)
        return jnp.take(arrived, ids, axis=0)

    back = [blocks_of(me_group)]
    for shift in range(1, groups):
        back.append(turn_group(blocks_of((me_group + shift) % groups), shift))
    back = jnp.stack(back)
    order = (me_group - jnp.arange(groups, dtype=jnp.int32)) % groups
    back = jnp.take(back, order, axis=0)
    update = jnp.transpose(back, (0, 2, 1, 3)).reshape(rows_dev, ncols, quarter)
    return (update, left_new, right_new)


def solution(mesh):
    in_specs = (
        P("replica", "fsdp", None, None),
        P(),
        P(),
        P("fsdp", "replica", None),
        P("fsdp", "replica", None),
        P("fsdp", None, "replica"),
        P("fsdp", None, "replica"),
    )
    out_specs = (P("fsdp", None, "replica"), P("fsdp", "replica", None), P("fsdp", "replica", None))
    return jax.shard_map(
        on_device, mesh=mesh, in_specs=in_specs, out_specs=out_specs, check_vma=False
    )
```

time: 416 us -> 233 us (0.56)
  waiting for transfers between devices: 302 us -> 107 us
  starting transfers between devices: 25.8 us -> 60.1 us
  other arithmetic: 24.5 us -> 16.5 us
  blocking collectives: 7.84 us -> 0 us
    all_to_all x2, waiting for transfers between devices: 184 us -> 49.3 us  [the longest x1 27.6 us: on_device(): lax.all_to_all(outgoing, 'fsdp', split_axis=0, concat_axis=0, tiled=True)]
    all_gather x2 -> x1, waiting for transfers between devices: 87.4 us -> 0.02 us  [on_device(): left_wide = lax.all_gather(left_root, 'replica', axis=0, tiled=False)]
    ppermute x0 -> x19, waiting for transfers between devices: none -> 57.6 us  [the longest x13 43.9 us: turn_x(): return lax.ppermute(value, 'replica', pairs)]
    ppermute x0 -> x19, starting transfers between devices: none -> 34.7 us  [the longest x13 18.4 us: turn_x(): return lax.ppermute(value, 'replica', pairs)]
    reduce_scatter x1 -> x0, waiting for transfers between devices: 30 us -> none  [on_device(): lax.psum_scatter(terms.astype(jnp.bfloat16), 'replica', scatter_dimension...]
    psum x1 -> x0, blocking collectives: 7.84 us -> none  [on_device(): lax.psum((left_part, right_part, precond_part), 'replica')]
    convert_element_type x7 -> x5, other arithmetic: 10.8 us -> 4.42 us  [the longest x1 1.84 us: on_device(): terms = (grad_parts[0].astype(F32) * col_mask[None]).astype(BF16)]
    gather x4 -> x7, local copies, waits for them, and re-layouts: 13.6 us -> 8.4 us  [the longest x1 4.97 us: on_device(): g_all = jnp.take(g_all, order, axis=0)]
  transfers between devices with their start and end apart: 5 -> 22, of which waited for: 5 -> 13; matrix products, arithmetic and copies ran while one was open for 5% -> 17% of each run, Pallas kernels for 0% -> 0%
where the time goes in v1:
time: 233 us; the launch traced here: 232 us
  waiting for transfers between devices  107 us (46%)
  starting transfers between devices  60.1 us (26%)
  local copies, waits for them, and re-layouts  17.7 us (8%)
  other arithmetic  16.5 us (7%)
  matrix products  16.5 us (7%)
  between operations  14.7 us (6%)
    ppermute x13, waiting for transfers between devices, turn_x(): return lax.ppermute(value, 'replica', pairs)  43.9 us
    all_to_all x1, waiting for transfers between devices, on_device(): lax.all_to_all(outgoing, 'fsdp', split_axis=0, concat_axis=0, tiled=True)  27.6 us
    all_to_all x1, waiting for transfers between devices, on_device(): lax.all_to_all(returning, 'fsdp', split_axis=0, concat_axis=0, tiled=True)  21.7 us
    ppermute x13, starting transfers between devices, turn_x(): return lax.ppermute(value, 'replica', pairs)  18.4 us
    ppermute x6, starting transfers between devices, turn_group(): return lax.ppermute(value, 'fsdp', pairs)  16.3 us
    ppermute x6, waiting for transfers between devices, turn_group(): return lax.ppermute(value, 'fsdp', pairs)  13.8 us
    all_to_all x1, starting transfers between devices, on_device(): lax.all_to_all(outgoing, 'fsdp', split_axis=0, concat_axis=0, tiled=True)  13.2 us
    all_to_all x1, starting transfers between devices, on_device(): lax.all_to_all(returning, 'fsdp', split_axis=0, concat_axis=0, tiled=True)  12.2 us
  transfers between devices with their start and end apart: 22, of which 13 were waited for; matrix products, arithmetic and copies ran while one was open for 17% of the time, Pallas kernels for 0%

profile of v1, /device:TPU:1, one launch (start us, length us, event | category | flops | bytes accessed | tf_op | source)
XLA Modules:
  0.0 232.5 jit_solution(1947869310118029488)
XLA Ops:
  8.1 1.8 fusion.2
  10.8 2.0 collective-permute-start
  14.2 1.7 collective-permute-start.2
  17.2 3.8 %collective-permute-done = bf16[12,64,256]{2,1,0:T(8,128)(2,1)} collective-permute-done((bf16[12,64,256]{2,1,0:T(8,128)(2,1)}, bf16[12,64,256]{2,1,0:T(8,128)(2,1)}, u32[]{:S(2)}, u32[]{:S(2)}) %collective-permute-start) | collective-permute-done | bytes 393248 | tf_op jit(solution)/shard_map/ppermute | solution.py:42
  22.4 10.2 %collective-permute-done.2 = bf16[12,64,256]{2,1,0:T(8,128)(2,1)} collective-permute-done((bf16[12,64,256]{2,1,0:T(8,128)(2,1)S(1)}, bf16[12,64,256]{2,1,0:T(8,128)(2,1)}, u32[]{:S(2)}, u32[]{:S(2)}) %collective-permute-start.2) | collective-permute-done | bytes 393248 | tf_op jit(solution)/shard_map/ppermute | solution.py:42
  34.2 3.0 %collective-permute-start.3 = (bf16[12,16,256]{2,1,0:T(8,128)(2,1)S(1)}, bf16[12,16,256]{2,1,0:T(8,128)(2,1)S(1)}, u32[]{:S(2)}, u32[]{:S(2)}) collective-permute-start(bf16[12,16,256]{2,1,0:T(8,128)(2,1)S(1)} %get-tuple-element.28), channel_id=1, source_target_pairs={{0,16},{1,17},{2,18},{3,19},{4,20},{5,21},{6,22},{7,23},{8,24},{9,... | collective-permute-start | bytes 294920 | tf_op jit(solution)/shard_map/ppermute | solution.py:46
  37.3 5.0 %collective-permute-start.4 = (bf16[12,16,256]{2,1,0:T(8,128)(2,1)S(1)}, bf16[12,16,256]{2,1,0:T(8,128)(2,1)S(1)}, u32[]{:S(2)}, u32[]{:S(2)}) collective-permute-start(bf16[12,16,256]{2,1,0:T(8,128)(2,1)S(1)} %get-tuple-element.27), channel_id=1, source_target_pairs={{0,32},{1,33},{2,34},{3,35},{4,36},{5,37},{6,38},{7,39},{8,40},{9,... | collective-permute-start | bytes 294920 | tf_op jit(solution)/shard_map/ppermute | solution.py:46
  42.3 2.4 %collective-permute-start.5 = (bf16[12,16,256]{2,1,0:T(8,128)(2,1)S(1)}, bf16[12,16,256]{2,1,0:T(8,128)(2,1)S(1)}, u32[]{:S(2)}, u32[]{:S(2)}) collective-permute-start(bf16[12,16,256]{2,1,0:T(8,128)(2,1)S(1)} %get-tuple-element.26), channel_id=1, source_target_pairs={{0,48},{1,49},{2,50},{3,51},{4,52},{5,53},{6,54},{7,55},{8,56},{9,... | collective-permute-start | bytes 294920 | tf_op jit(solution)/shard_map/ppermute | solution.py:46
  44.7 1.9 collective-permute-done.4
  46.6 1.8 collective-permute-done.5
  50.3 13.2 %all-to-all-start = ((bf16[64,2,16,256]{3,2,1,0:T(8,128)(2,1)}), bf16[64,2,16,256]{3,2,1,0:T(8,128)(2,1)S(1)}, u32[]{:S(2)}, u32[]{:S(2)}) async-start(bf16[64,2,16,256]{3,2,1,0:T(8,128)(2,1)} %broadcast_select_fusion.1), calls=%async_computation | async-start | bytes 2097152 | tf_op jit(solution)/shard_map/all_to_all | solution.py:99
  63.9 27.6 %all-to-all-done = bf16[64,2,16,256]{3,2,1,0:T(8,128)(2,1)S(1)} async-done(((bf16[64,2,16,256]{3,2,1,0:T(8,128)(2,1)}), bf16[64,2,16,256]{3,2,1,0:T(8,128)(2,1)S(1)}, u32[]{:S(2)}, u32[]{:S(2)}) %all-to-all-start) | async-done | bytes 1048608 | tf_op jit(solution)/shard_map/all_to_all | solution.py:99
  92.3 2.2 collective-permute-start.8
  98.4 18.0 %collective-permute-done.6 = bf16[2,1024,256]{2,1,0:T(8,128)(2,1)S(1)} collective-permute-done((bf16[2,1024,256]{2,1,0:T(8,128)(2,1)S(1)}, bf16[2,1024,256]{2,1,0:T(8,128)(2,1)S(1)}, u32[]{:S(2)}, u32[]{:S(2)}) %collective-permute-start.6) | collective-permute-done | bytes 1048608 | tf_op jit(solution)/shard_map/ppermute | solution.py:42
  116.7 2.7 %collective-permute-start.9 = (bf16[2,512,256]{2,1,0:T(8,128)(2,1)S(1)}, bf16[2,512,256]{2,1,0:T(8,128)(2,1)S(1)}, u32[]{:S(2)}, u32[]{:S(2)}) collective-permute-start(bf16[2,512,256]{2,1,0:T(8,128)(2,1)S(1)} %slice.31), channel_id=1, source_target_pairs={{0,192},{64,0},{128,64},{192,128},{1,193},{65,1},{129,65},{193,129... | collective-permute-start | bytes 1572872 | tf_op jit(solution)/shard_map/ppermute | solution.py:42
  119.7 9.3 %collective-permute-done.7 = bf16[2,512,256]{2,1,0:T(8,128)(2,1)S(1)} collective-permute-done((bf16[2,512,256]{2,1,0:T(8,128)(2,1)S(1)}, bf16[2,512,256]{2,1,0:T(8,128)(2,1)S(1)}, u32[]{:S(2)}, u32[]{:S(2)}) %collective-permute-start.7) | collective-permute-done | bytes 524320 | tf_op jit(solution)/shard_map/ppermute | solution.py:42
  129.1 2.2 pad_maximum_fusion
  131.3 5.0 %gather_fusion.1 = bf16[4,2,1024,256]{3,2,1,0:T(8,128)(2,1)} fusion(bf16[4,2,1024,256]{3,2,1,0:T(8,128)(2,1)} %pad_maximum_fusion, s32[1024]{0:T(1024)S(1)} %pad_clamp_fusion.5), kind=kCustom, calls=%fused_computation.5 | custom fusion | bytes 8388624 | tf_op jit(solution)/shard_map/jit(_take)/gather | solution.py:113
  136.3 4.0 %multiply_reduce_fusion = (f32[2]{0:T(128)S(1)}, bf16[4,2,1024,256]{3,2,0,1:T(8,128)(2,1)S(1)}) fusion(bf16[4,2,1024,256]{3,2,1,0:T(8,128)(2,1)} %gather_fusion.1, pred[4]{0:T(512)(128)(4,1)S(1)} %get-tuple-element.41), kind=kLoop, calls=%fused_computation.7 | loop fusion | flops 8388606 | bytes 8388620 | tf_op jit(solution)/shard_map/reduce_sum | solution.py:123
  140.2 3.1 %convolution_multiply_fusion = f32[2,256,4,256]{1,3,2,0:T(8,128)} fusion(bf16[4,2,1024,256]{3,2,0,1:T(8,128)(2,1)S(1)} %get-tuple-element.19, bf16[2,1024,256]{2,1,0:T(8,128)(2,1)S(1)} %bitcast_select_fusion), kind=kOutput, calls=%fused_computation.25 | convolution fusion | flops 1074266112 | bytes 7340032 | tf_op jit(solution)/shard_map/skq,xskp->sqxp/dot_general | solution.py:136
  143.3 2.9 %copy.76 = f32[2,256,1024]{2,1,0:T(8,128)} copy(f32[2,256,1024]{1,2,0:T(8,128)} %bitcast.118) | data formatting | bytes 4194304 | tf_op jit(solution)/shard_map/mul | solution.py:139
  146.2 3.4 %bitcast_convert_fusion = bf16[2,1024,256]{2,1,0:T(8,128)(2,1)S(1)} fusion(bf16[4,2,1024,256]{3,2,0,1:T(8,128)(2,1)} %copy-done.1, bf16[2,4,256,256]{3,2,1,0:T(8,128)(2,1)S(1)} %bitcast.116), kind=kOutput, calls=%fused_computation.19 | convolution fusion | flops 1074266112 | bytes 6291456 | tf_op jit(solution)/shard_map/xsik,sxkq->siq/dot_general | solution.py:116
  149.7 4.0 %multiply_reduce_fusion.3 = (f32[2]{0:T(128)S(1)}, f32[2,256,1024,1]{2,1,3,0:T(8,128)S(1)}) fusion(f32[2,256]{1,0:T(2,128)S(1)} %compare_convert_fusion, bf16[2,4,256,256]{3,2,1,0:T(8,128)(2,1)S(1)} %bitcast.138, bf16[4,2,1024,256]{3,2,1,0:T(8,128)(2,1)} %bitcast.137), kind=kOutput, calls=%fused_computation.24 | convolution fusion | flops 1075314688 | bytes 7342088 | tf_op jit(solution)/shard_map/xsik,sxkq->siq/dot_general | solution.py:120
  153.7 3.7 %collective-permute-start.11 = (f32[2]{0:T(128)S(1)}, f32[2]{0:T(128)S(1)}, u32[]{:S(2)}, u32[]{:S(2)}) collective-permute-start(f32[2]{0:T(128)S(1)} %get-tuple-element.39), channel_id=1, source_target_pairs={{0,128},{64,192},{128,0},{192,64},{1,129},{65,193},{129,1},{193,65... | collective-permute-start | bytes 32 | tf_op jit(solution)/shard_map/ppermute | solution.py:42
  159.8 2.0 multiply_add_fusion
  163.1 2.4 %copy.66 = bf16[4,16,2,16,256]{4,3,2,1,0:T(8,128)(2,1)} copy(bf16[4,16,2,16,256]{4,3,0,1,2:T(8,128)(2,1)} %bitcast.121) | data formatting | bytes 2097152 | tf_op jit(solution)/shard_map/transpose | solution.py:128
  165.5 12.2 %all-to-all-start.1 = ((bf16[64,2,16,256]{3,2,1,0:T(8,128)(2,1)}), bf16[64,2,16,256]{3,2,1,0:T(8,128)(2,1)S(1)}, u32[]{:S(2)}, u32[]{:S(2)}) async-start(bf16[64,2,16,256]{3,2,1,0:T(8,128)(2,1)} %bitcast.34), calls=%async_computation.1 | async-start | bytes 2097152 | tf_op jit(solution)/shard_map/all_to_all | solution.py:131
  177.9 6.1 %fusion.5 = f32[2,256,1024]{2,1,0:T(8,128)} fusion(f32[2,256,1024]{2,1,0:T(8,128)} %param.12, bf16[4,2,1024,256]{3,2,0,1:T(8,128)(2,1)} %copy-done.1, f32[2]{0:T(128)S(1)} %multiply_bitcast_fusion, f32[256,1024]{1,0:T(8,128)S(1)} %fusion.9, s32[]{:T(128)S(6)} %select_n.270), kind=kOutput, calls=%fused_computation.17 | convolution fusion | flops 1076887552 | bytes 10485772 | tf_op jit(solution)/shard_map/xsqk,xspk->sqp/dot_general | solution.py:135
  184.0 21.7 %all-to-all-done.1 = bf16[64,2,16,256]{3,2,1,0:T(8,128)(2,1)S(1)} async-done(((bf16[64,2,16,256]{3,2,1,0:T(8,128)(2,1)}), bf16[64,2,16,256]{3,2,1,0:T(8,128)(2,1)S(1)}, u32[]{:S(2)}, u32[]{:S(2)}) %all-to-all-start.1) | async-done | bytes 1048608 | tf_op jit(solution)/shard_map/all_to_all | solution.py:131
  208.6 4.2 %collective-permute-start.14 = (bf16[12,16,256]{2,1,0:T(8,128)(2,1)S(1)}, bf16[12,16,256]{2,1,0:T(8,128)(2,1)S(1)}, u32[]{:S(2)}, u32[]{:S(2)}) collective-permute-start(bf16[12,16,256]{2,1,0:T(8,128)(2,1)S(1)} %broadcast_select_fusion.3), channel_id=1, source_target_pairs={{0,32},{1,33},{2,34},{3,35},{4,36},{5,37},{6,38},{7,39},{8,40},{9,... | collective-permute-start | bytes 294920 | tf_op jit(solution)/shard_map/ppermute | solution.py:46
  214.4 6.8 %collective-permute-done.14 = bf16[12,16,256]{2,1,0:T(8,128)(2,1)S(1)} collective-permute-done((bf16[12,16,256]{2,1,0:T(8,128)(2,1)S(1)}, bf16[12,16,256]{2,1,0:T(8,128)(2,1)S(1)}, u32[]{:S(2)}, u32[]{:S(2)}) %collective-permute-start.14) | collective-permute-done | bytes 98336 | tf_op jit(solution)/shard_map/ppermute | solution.py:46
  221.2 2.9 %collective-permute-done.15 = bf16[12,16,256]{2,1,0:T(8,128)(2,1)S(1)} collective-permute-done((bf16[12,16,256]{2,1,0:T(8,128)(2,1)S(1)}, bf16[12,16,256]{2,1,0:T(8,128)(2,1)S(1)}, u32[]{:S(2)}, u32[]{:S(2)}) %collective-permute-start.15) | collective-permute-done | bytes 98336 | tf_op jit(solution)/shard_map/ppermute | solution.py:46
  (104 shorter events, 24.6 us)
Async XLA Ops:
  7.2 139.0 %copy-start = (bf16[2,1024,256]{2,1,0:T(8,128)(2,1)S(1)}, bf16[2,1024,256]{2,1,0:T(8,128)(2,1)}, u32[]{:S(2)}) copy-start(bf16[2,1024,256]{2,1,0:T(8,128)(2,1)} %param.15) | copy-start | bytes 3145732
  7.2 142.5 %all-gather.3.cloned.1.call-start = ((), (), s32[]{:S(2)}) async-start(), calls=%async_computation.2 | async-start | bytes 5242880 | tf_op jit(solution)/shard_map/all_gather | solution.py:86
  9.9 6.1 %copy-start.7 = (s32[48]{0:T(128)S(1)}, s32[48]{0:T(128)}, u32[]{:S(2)}) copy-start(s32[48]{0:T(128)} %param.11) | copy-start | bytes 580
  10.8 10.2 %collective-permute-start = (bf16[12,64,256]{2,1,0:T(8,128)(2,1)}, bf16[12,64,256]{2,1,0:T(8,128)(2,1)}, u32[]{:S(2)}, u32[]{:S(2)}) collective-permute-start(bf16[12,64,256]{2,1,0:T(8,128)(2,1)} %get-tuple-element.22), channel_id=1, source_target_pairs={{0,64},{64,128},{128,192},{192,0},{1,65},{65,129},{129,193},{193,1... | collective-permute-start | bytes 1179656 | tf_op jit(solution)/shard_map/ppermute | solution.py:42
  12.9 9.5 %collective-permute-start.1 = (bf16[12,64,256]{2,1,0:T(8,128)(2,1)S(1)}, bf16[12,64,256]{2,1,0:T(8,128)(2,1)}, u32[]{:S(2)}, u32[]{:S(2)}) collective-permute-start(bf16[12,64,256]{2,1,0:T(8,128)(2,1)S(1)} %get-tuple-element.24), channel_id=1, source_target_pairs={{0,192},{64,0},{128,64},{192,128},{1,193},{65,1},{129,65},{193,129... | collective-permute-start | bytes 1179656 | tf_op jit(solution)/shard_map/ppermute | solution.py:42
  14.2 18.4 %collective-permute-start.2 = (bf16[12,64,256]{2,1,0:T(8,128)(2,1)S(1)}, bf16[12,64,256]{2,1,0:T(8,128)(2,1)}, u32[]{:S(2)}, u32[]{:S(2)}) collective-permute-start(bf16[12,64,256]{2,1,0:T(8,128)(2,1)S(1)} %get-tuple-element.23), channel_id=1, source_target_pairs={{0,128},{64,192},{128,0},{192,64},{1,129},{65,193},{129,1},{193,65... | collective-permute-start | bytes 1179656 | tf_op jit(solution)/shard_map/ppermute | solution.py:42
  34.2 10.5 %collective-permute-start.3 = (bf16[12,16,256]{2,1,0:T(8,128)(2,1)S(1)}, bf16[12,16,256]{2,1,0:T(8,128)(2,1)S(1)}, u32[]{:S(2)}, u32[]{:S(2)}) collective-permute-start(bf16[12,16,256]{2,1,0:T(8,128)(2,1)S(1)} %get-tuple-element.28), channel_id=1, source_target_pairs={{0,16},{1,17},{2,18},{3,19},{4,20},{5,21},{6,22},{7,23},{8,24},{9,... | collective-permute-start | bytes 294920 | tf_op jit(solution)/shard_map/ppermute | solution.py:46
  37.3 9.3 %collective-permute-start.4 = (bf16[12,16,256]{2,1,0:T(8,128)(2,1)S(1)}, bf16[12,16,256]{2,1,0:T(8,128)(2,1)S(1)}, u32[]{:S(2)}, u32[]{:S(2)}) collective-permute-start(bf16[12,16,256]{2,1,0:T(8,128)(2,1)S(1)} %get-tuple-element.27), channel_id=1, source_target_pairs={{0,32},{1,33},{2,34},{3,35},{4,36},{5,37},{6,38},{7,39},{8,40},{9,... | collective-permute-start | bytes 294920 | tf_op jit(solution)/shard_map/ppermute | solution.py:46
  42.3 6.2 %collective-permute-start.5 = (bf16[12,16,256]{2,1,0:T(8,128)(2,1)S(1)}, bf16[12,16,256]{2,1,0:T(8,128)(2,1)S(1)}, u32[]{:S(2)}, u32[]{:S(2)}) collective-permute-start(bf16[12,16,256]{2,1,0:T(8,128)(2,1)S(1)} %get-tuple-element.26), channel_id=1, source_target_pairs={{0,48},{1,49},{2,50},{3,51},{4,52},{5,53},{6,54},{7,55},{8,56},{9,... | collective-permute-start | bytes 294920 | tf_op jit(solution)/shard_map/ppermute | solution.py:46
  49.1 14.4 %copy-start.6 = (s32[12]{0:T(128)S(1)}, s32[12]{0:T(128)}, u32[]{:S(2)}) copy-start(s32[12]{0:T(128)} %param.10) | copy-start | bytes 148
  50.3 41.2 %all-to-all-start = ((bf16[64,2,16,256]{3,2,1,0:T(8,128)(2,1)}), bf16[64,2,16,256]{3,2,1,0:T(8,128)(2,1)S(1)}, u32[]{:S(2)}, u32[]{:S(2)}) async-start(bf16[64,2,16,256]{3,2,1,0:T(8,128)(2,1)} %broadcast_select_fusion.1), calls=%async_computation | async-start | bytes 2097152 | tf_op jit(solution)/shard_map/all_to_all | solution.py:99
  91.5 3.2 %copy-start.4 = (f32[2,256,1024]{2,1,0:T(8,128)S(1)}, f32[2,256,1024]{2,1,0:T(8,128)}, u32[]{:S(2)}) copy-start(f32[2,256,1024]{2,1,0:T(8,128)} %param.12) | copy-start | bytes 6291460
  91.6 3.1 %copy-start.2 = (f32[2,256,1024]{2,1,0:T(8,128)S(1)}, f32[2,256,1024]{2,1,0:T(8,128)}, u32[]{:S(2)}) copy-start(f32[2,256,1024]{2,1,0:T(8,128)} %param.13) | copy-start | bytes 6291460
  91.8 24.6 %collective-permute-start.6 = (bf16[2,1024,256]{2,1,0:T(8,128)(2,1)S(1)}, bf16[2,1024,256]{2,1,0:T(8,128)(2,1)S(1)}, u32[]{:S(2)}, u32[]{:S(2)}) collective-permute-start(bf16[2,1024,256]{2,1,0:T(8,128)(2,1)S(1)} %bitcast_select_fusion), channel_id=1, source_target_pairs={{0,64},{64,128},{128,192},{192,0},{1,65},{65,129},{129,193},{193,1... | collective-permute-start | bytes 3145736 | tf_op jit(solution)/shard_map/ppermute | solution.py:42
  92.3 24.4 %collective-permute-start.8 = (bf16[2,1024,256]{2,1,0:T(8,128)(2,1)S(1)}, bf16[2,1024,256]{2,1,0:T(8,128)(2,1)S(1)}, u32[]{:S(2)}, u32[]{:S(2)}) collective-permute-start(bf16[2,1024,256]{2,1,0:T(8,128)(2,1)S(1)} %bitcast_select_fusion), channel_id=1, source_target_pairs={{0,192},{64,0},{128,64},{192,128},{1,193},{65,1},{129,65},{193,129... | collective-permute-start | bytes 3145736 | tf_op jit(solution)/shard_map/ppermute | solution.py:42
  95.6 64.2 %collective-permute-start.16 = (f32[2,2]{1,0:T(2,128)S(1)}, f32[2,2]{1,0:T(2,128)S(1)}, u32[]{:S(2)}, u32[]{:S(2)}) collective-permute-start(f32[2,2]{1,0:T(2,128)S(1)} %pad_maximum_fusion.3), channel_id=1, source_target_pairs={{0,64},{64,128},{128,192},{192,0},{1,65},{65,129},{129,193},{193,1... | collective-permute-start | bytes 56 | tf_op jit(solution)/shard_map/ppermute | solution.py:42
  95.7 64.1 %collective-permute-start.17 = (f32[2,2]{1,0:T(2,128)S(1)}, f32[2,2]{1,0:T(2,128)S(1)}, u32[]{:S(2)}, u32[]{:S(2)}) collective-permute-start(f32[2,2]{1,0:T(2,128)S(1)} %pad_maximum_fusion.3), channel_id=1, source_target_pairs={{0,128},{64,192},{128,0},{192,64},{1,129},{65,193},{129,1},{193,65... | collective-permute-start | bytes 56 | tf_op jit(solution)/shard_map/ppermute | solution.py:42
  97.0 62.8 %collective-permute-start.18 = (f32[2,2]{1,0:T(2,128)S(1)}, f32[2,2]{1,0:T(2,128)S(1)}, u32[]{:S(2)}, u32[]{:S(2)}) collective-permute-start(f32[2,2]{1,0:T(2,128)S(1)} %pad_maximum_fusion.3), channel_id=1, source_target_pairs={{0,192},{64,0},{128,64},{192,128},{1,193},{65,1},{129,65},{193,129... | collective-permute-start | bytes 56 | tf_op jit(solution)/shard_map/ppermute | solution.py:42
  116.4 12.6 %collective-permute-start.7 = (bf16[2,512,256]{2,1,0:T(8,128)(2,1)S(1)}, bf16[2,512,256]{2,1,0:T(8,128)(2,1)S(1)}, u32[]{:S(2)}, u32[]{:S(2)}) collective-permute-start(bf16[2,512,256]{2,1,0:T(8,128)(2,1)S(1)} %slice.30), channel_id=1, source_target_pairs={{0,64},{64,128},{128,192},{192,0},{1,65},{65,129},{129,193},{193,1... | collective-permute-start | bytes 1572872 | tf_op jit(solution)/shard_map/ppermute | solution.py:42
  116.7 12.3 %collective-permute-start.9 = (bf16[2,512,256]{2,1,0:T(8,128)(2,1)S(1)}, bf16[2,512,256]{2,1,0:T(8,128)(2,1)S(1)}, u32[]{:S(2)}, u32[]{:S(2)}) collective-permute-start(bf16[2,512,256]{2,1,0:T(8,128)(2,1)S(1)} %slice.31), channel_id=1, source_target_pairs={{0,192},{64,0},{128,64},{192,128},{1,193},{65,1},{129,65},{193,129... | collective-permute-start | bytes 1572872 | tf_op jit(solution)/shard_map/ppermute | solution.py:42
  140.2 3.1 %copy-start.1 = (bf16[4,2,1024,256]{3,2,0,1:T(8,128)(2,1)}, bf16[4,2,1024,256]{3,2,0,1:T(8,128)(2,1)S(1)}, u32[]{:S(2)}) copy-start(bf16[4,2,1024,256]{3,2,0,1:T(8,128)(2,1)S(1)} %get-tuple-element.19) | copy-start | bytes 12582916
  149.7 10.2 %copy-start.3 = (f32[2,256,1024]{2,1,0:T(8,128)S(1)}, f32[2,256,1024]{2,1,0:T(8,128)}, u32[]{:S(2)}) copy-start(f32[2,256,1024]{2,1,0:T(8,128)} %param.13) | copy-start | bytes 6291460
  149.7 10.2 %copy-start.5 = (f32[2,256,1024]{2,1,0:T(8,128)S(1)}, f32[2,256,1024]{2,1,0:T(8,128)}, u32[]{:S(2)}) copy-start(f32[2,256,1024]{2,1,0:T(8,128)} %copy.76) | copy-start | bytes 6291460
  153.7 3.7 %collective-permute-start.10 = (f32[2]{0:T(128)S(1)}, f32[2]{0:T(128)S(1)}, u32[]{:S(2)}, u32[]{:S(2)}) collective-permute-start(f32[2]{0:T(128)S(1)} %get-tuple-element.39), channel_id=1, source_target_pairs={{0,64},{64,128},{128,192},{192,0},{1,65},{65,129},{129,193},{193,1... | collective-permute-start | bytes 32 | tf_op jit(solution)/shard_map/ppermute | solution.py:42
  153.7 4.9 %collective-permute-start.11 = (f32[2]{0:T(128)S(1)}, f32[2]{0:T(128)S(1)}, u32[]{:S(2)}, u32[]{:S(2)}) collective-permute-start(f32[2]{0:T(128)S(1)} %get-tuple-element.39), channel_id=1, source_target_pairs={{0,128},{64,192},{128,0},{192,64},{1,129},{65,193},{129,1},{193,65... | collective-permute-start | bytes 32 | tf_op jit(solution)/shard_map/ppermute | solution.py:42
  157.4 2.4 %collective-permute-start.12 = (f32[2]{0:T(128)S(1)}, f32[2]{0:T(128)S(1)}, u32[]{:S(2)}, u32[]{:S(2)}) collective-permute-start(f32[2]{0:T(128)S(1)} %get-tuple-element.39), channel_id=1, source_target_pairs={{0,192},{64,0},{128,64},{192,128},{1,193},{65,1},{129,65},{193,129... | collective-permute-start | bytes 32 | tf_op jit(solution)/shard_map/ppermute | solution.py:42
  165.5 40.1 %all-to-all-start.1 = ((bf16[64,2,16,256]{3,2,1,0:T(8,128)(2,1)}), bf16[64,2,16,256]{3,2,1,0:T(8,128)(2,1)S(1)}, u32[]{:S(2)}, u32[]{:S(2)}) async-start(bf16[64,2,16,256]{3,2,1,0:T(8,128)(2,1)} %bitcast.34), calls=%async_computation.1 | async-start | bytes 2097152 | tf_op jit(solution)/shard_map/all_to_all | solution.py:131
  206.9 7.6 %collective-permute-start.13 = (bf16[12,16,256]{2,1,0:T(8,128)(2,1)S(1)}, bf16[12,16,256]{2,1,0:T(8,128)(2,1)S(1)}, u32[]{:S(2)}, u32[]{:S(2)}) collective-permute-start(bf16[12,16,256]{2,1,0:T(8,128)(2,1)S(1)} %broadcast_select_fusion.4), channel_id=1, source_target_pairs={{0,16},{1,17},{2,18},{3,19},{4,20},{5,21},{6,22},{7,23},{8,24},{9,... | collective-permute-start | bytes 294920 | tf_op jit(solution)/shard_map/ppermute | solution.py:46
  208.6 12.6 %collective-permute-start.14 = (bf16[12,16,256]{2,1,0:T(8,128)(2,1)S(1)}, bf16[12,16,256]{2,1,0:T(8,128)(2,1)S(1)}, u32[]{:S(2)}, u32[]{:S(2)}) collective-permute-start(bf16[12,16,256]{2,1,0:T(8,128)(2,1)S(1)} %broadcast_select_fusion.3), channel_id=1, source_target_pairs={{0,32},{1,33},{2,34},{3,35},{4,36},{5,37},{6,38},{7,39},{8,40},{9,... | collective-permute-start | bytes 294920 | tf_op jit(solution)/shard_map/ppermute | solution.py:46
  213.5 10.6 %collective-permute-start.15 = (bf16[12,16,256]{2,1,0:T(8,128)(2,1)S(1)}, bf16[12,16,256]{2,1,0:T(8,128)(2,1)S(1)}, u32[]{:S(2)}, u32[]{:S(2)}) collective-permute-start(bf16[12,16,256]{2,1,0:T(8,128)(2,1)S(1)} %broadcast_select_fusion.2), channel_id=1, source_target_pairs={{0,48},{1,49},{2,50},{3,51},{4,52},{5,53},{6,54},{7,55},{8,56},{9,... | collective-permute-start | bytes 294920 | tf_op jit(solution)/shard_map/ppermute | solution.py:46
Sparse Core Ops, SparseCore 0:
  16.0 53.3 all-gather.2

commit v2 on v1

v2 whole, which is shorter than its diff:
```python
import jax
import jax.numpy as jnp
from jax import lax
from jax.experimental import pallas as pl
from jax.experimental.pallas import tpu as pltpu
from jax.sharding import PartitionSpec as P

DECAY = 0.99
SHRINKAGE = 0.1
EPSILON = 1e-06
F32 = jnp.float32
BF16 = jnp.bfloat16
VMEM_LIMIT = 48 * 1024 * 1024
SMEM_SPEC = pl.BlockSpec(memory_space=pltpu.SMEM)


def slot_tables(assignment, workers, slots):
    blocks = jnp.arange(assignment.shape[0], dtype=jnp.int32)
    same_worker = assignment[:, None] == assignment[None, :]
    earlier = blocks[None, :] < blocks[:, None]
    slot_rank = jnp.sum((same_worker & earlier).astype(jnp.int32), axis=1)
    slot_ids = assignment * slots + slot_rank
    wanted = jnp.arange(workers * slots, dtype=jnp.int32)
    slot_hits = (slot_ids[None, :] == wanted[:, None]).astype(jnp.int32)
    filled = jnp.sum(slot_hits, axis=1) > 0
    block_ids = jnp.sum(slot_hits * blocks[None, :], axis=1)
    return (slot_ids, filled, block_ids)


def dot(a, b, contract=(1, 0)):
    dims = (((contract[0],), (contract[1],)), ((), ()))
    return lax.dot_general(a, b, dims, preferred_element_type=F32)


def fold(values):
    rows = values.shape[0]
    part = values[:, :128]
    for first in range(128, values.shape[1], 128):
        part = part + values[:, first : first + 128]
    return jnp.sum(part.reshape(rows // 8, 8, 128), axis=0)


def root_kernel(meta, g0, g1, g3, far0, far1, right, l0, l1, l2, l3, out, sums, far, rights, prods):
    slot = pl.program_id(0)
    me = meta[0]
    width = meta[1 + slot]
    reps = 4
    size = g0.shape[1]
    quarter = g0.shape[2]

    @pl.when(slot == 0)
    def _():
        far[...] = far0[0]

    @pl.when(slot == 1)
    def _():
        far[...] = far1[0]

    def place(turn):
        q = lax.rem(me + reps - turn, reps)
        return pl.ds(pl.multiple_of(q * quarter, quarter), quarter)

    for t in range(reps):
        rights[t * quarter : (t + 1) * quarter, :] = right[0, place(t), :]
    for t in range(reps):
        rows = place(t)
        wide = jnp.concatenate([g0[0, rows, :], g1[0, rows, :], far[rows, :], g3[0, rows, :]], 1)
        prods[t * quarter : (t + 1) * quarter, :] = dot(wide, rights[...]).astype(BF16)
    column = me * quarter + lax.broadcasted_iota(jnp.int32, (quarter, quarter), 1)
    keep = (column < width).astype(F32)
    p_sum = jnp.zeros((8, 128), F32)
    g_sum = jnp.zeros((8, 128), F32)
    for n in range(size // quarter):
        rows = slice(n * quarter, (n + 1) * quarter)
        wide = jnp.concatenate([l0[0, rows, :], l1[0, rows, :], l2[0, rows, :], l3[0, rows, :]], 1)
        value = dot(wide, prods[...]) * keep
        out[0, rows, :] = value
        p_sum = p_sum + fold(value * value)
        own = g0[0, rows, :].astype(F32)
        g_sum = g_sum + fold(own * own)
    sums[0, 0] = p_sum
    sums[0, 1] = g_sum


def scale_kernel(groups, per_row, value, s0, s1, s2, s3, out):
    slots, _, quarter = value.shape
    piece = out.shape[2]
    total = s0[...] + s1[...] + s2[...] + s3[...]
    for s in range(slots):
        p_square = jnp.sum(total[s, 0], keepdims=True)
        g_square = jnp.sum(total[s, 1], keepdims=True)
        scale = jnp.sqrt(g_square / (p_square + EPSILON))
        for p in range(per_row):
            for i in range(groups):
                first = (p * groups + i) * piece
                out[i * per_row + p, s] = (value[s, first : first + piece, :] * scale).astype(BF16)


def stat_kernel(meta, adds, g0, g1, g3, far0, far1, left, right, after, left_new, right_new, far):
    del after
    slot = pl.program_id(0)
    me = meta[0]
    width = meta[1 + slot]
    left_add = adds[0, slot]
    right_add = adds[1, slot]
    reps = 4
    quarter = g0.shape[2]
    keep = 1.0 - SHRINKAGE

    @pl.when(slot == 0)
    def _():
        far[...] = far0[0]

    @pl.when(slot == 1)
    def _():
        far[...] = far1[0]

    def wide(rows):
        return jnp.concatenate([g0[0, rows, :], g1[0, rows, :], far[rows, :], g3[0, rows, :]], 1)

    row = lax.broadcasted_iota(jnp.int32, (quarter, quarter), 0)
    col = lax.broadcasted_iota(jnp.int32, (quarter, quarter), 1)
    first = pl.multiple_of(me * quarter, quarter)
    mine = wide(pl.ds(first, quarter))
    for n in range(reps):
        cols = slice(n * quarter, (n + 1) * quarter)
        gram = dot(mine, wide(cols), (1, 1))
        total = DECAY * left[0, :, cols] + (1.0 - DECAY) * gram
        on = col + n * quarter == row + first
        left_new[0, :, cols] = keep * total + jnp.where(on, left_add, 0.0)
    for t, block in enumerate((g0, g1, None, g3)):
        q = lax.rem(me + reps - t, reps)
        cols = pl.ds(pl.multiple_of(q * quarter, quarter), quarter)
        gram = dot(g0[0], far[...] if block is None else block[0], (0, 0))
        total = keep * (DECAY * right[0, :, cols] + (1.0 - DECAY) * gram)
        if t == 0:
            on = (col == row) & (row + first < width)
            total = total + jnp.where(on, right_add, 0.0)
        right_new[0, :, cols] = total


def on_device(grad_parts, col_widths, assignment, left_stat, right_stat, left_root, right_root):
    workers = lax.axis_size("fsdp")
    reps = lax.axis_size("replica")
    me_rep = lax.axis_index("replica")
    me_work = lax.axis_index("fsdp")
    slots, quarter, block_size = left_stat.shape
    rows_dev = grad_parts.shape[1]
    ncols = grad_parts.shape[2]
    per_row = block_size // rows_dev
    groups = workers // per_row
    piece = rows_dev // groups
    me_group = me_work // per_row

    def turn_x(value, shift):
        pairs = [(a, (a + shift) % reps) for a in range(reps)]
        return lax.ppermute(value, "replica", pairs)

    def turn_group(value, shift):
        pairs = [(a, (a + shift * per_row) % workers) for a in range(workers)]
        return lax.ppermute(value, "fsdp", pairs)

    slot_ids, filled, block_ids = slot_tables(assignment, workers, slots)
    col_index = jnp.arange(block_size, dtype=jnp.int32)
    col_mask = (col_index[None, :] < col_widths[:, None]).astype(F32)
    terms = (grad_parts[0].astype(F32) * col_mask[None]).astype(BF16)

    def columns_of(rep):
        cut = lax.dynamic_slice_in_dim(terms, rep * quarter, quarter, 2)
        return jnp.transpose(cut, (1, 0, 2))

    summed = columns_of(me_rep).astype(F32)
    for shift in (1, 3, 2):
        summed = summed + turn_x(columns_of((me_rep + shift) % reps), shift).astype(F32)
    summed = summed.astype(BF16)
    summed, left_root = lax.optimization_barrier((summed, left_root))

    my_blocks = lax.dynamic_slice_in_dim(block_ids, me_work * slots, slots)
    my_filled = lax.dynamic_slice_in_dim(filled, me_work * slots, slots)
    my_col = my_blocks % ncols
    looked_up = jnp.sum(
        jnp.where(
            my_col[:, None] == jnp.arange(ncols, dtype=jnp.int32)[None, :], col_widths[None, :], 0
        ),
        axis=1,
    )
    my_width = jnp.where(my_filled, looked_up, block_size)
    meta = jnp.concatenate([me_rep[None], my_width]).astype(jnp.int32)
    global_rows = me_rep * quarter + jnp.arange(quarter, dtype=jnp.int32)
    unit_rows = (col_index[None, :] == global_rows[:, None]).astype(F32)
    within_width = (global_rows[None, :] < my_width[:, None]).astype(F32)
    left_diag = jnp.sum(left_stat * unit_rows[None], axis=(1, 2))
    right_diag = jnp.sum(jnp.sum(right_stat * unit_rows[None], axis=2) * within_width, axis=1)
    diag_own = jnp.stack([left_diag, right_diag])

    left_roots = [left_root] + [turn_x(left_root, shift) for shift in (1, 2, 3)]

    summed = summed.reshape(ncols, groups, piece, quarter)

    def rows_of(group):
        return lax.dynamic_index_in_dim(summed, group, 1, keepdims=False)

    held = [rows_of(me_group)]
    for shift in range(1, groups):
        held.append(turn_group(rows_of((me_group + shift) % groups), shift))
    held = jnp.concatenate(held, axis=0)
    place = ((me_group - block_ids // ncols) % groups) * ncols + block_ids % ncols
    outgoing = jnp.take(held, place, axis=0, mode="clip")
    outgoing = outgoing.reshape(workers, slots, piece, quarter)
    incoming = lax.all_to_all(outgoing, "fsdp", split_axis=0, concat_axis=0, tiled=True)
    g_mine = jnp.transpose(
        incoming.reshape(groups, per_row, slots, piece, quarter), (2, 1, 0, 3, 4)
    ).reshape(slots, block_size, quarter)
    g_mine = jnp.where(my_filled[:, None, None], g_mine, jnp.zeros((), BF16))

    g_prev = turn_x(g_mine, 1)
    g_next = turn_x(g_mine, reps - 1)
    g_far0 = turn_x(g_prev[:1], 1)
    g_far1 = turn_x(g_next[1:], reps - 1)
    diag_sums = diag_own
    for shift in (1, 2, 3):
        diag_sums = diag_sums + turn_x(diag_own, shift)

    by_slot = lambda *dims: pl.BlockSpec((1,) + dims, lambda s: (s,) + (0,) * len(dims))
    whole = lambda *dims: pl.BlockSpec(dims, lambda s: (0,) * len(dims))
    col_spec = by_slot(block_size, quarter)
    far_spec = whole(1, block_size, quarter)
    row_spec = by_slot(quarter, block_size)
    col_shape = (slots, block_size, quarter)
    params = pltpu.CompilerParams(vmem_limit_bytes=VMEM_LIMIT)
    precond, sums = pl.pallas_call(
        root_kernel,
        grid=(slots,),
        in_specs=[SMEM_SPEC] + [col_spec] * 3 + [far_spec] * 2 + [col_spec] * 5,
        out_specs=[col_spec, by_slot(2, 8, 128)],
        out_shape=[
            jax.ShapeDtypeStruct(col_shape, F32),
            jax.ShapeDtypeStruct((slots, 2, 8, 128), F32),
        ],
        scratch_shapes=[pltpu.VMEM((block_size, quarter), BF16)] * 3,
        compiler_params=params,
        cost_estimate=pl.CostEstimate(
            flops=8 * block_size * block_size * quarter,
            bytes_accessed=22 * block_size * quarter * 2,
            transcendentals=0,
        ),
        name="root_products",
    )(meta, g_mine, g_prev, g_next, g_far0, g_far1, right_root, *left_roots)
    all_sums = [sums] + [turn_x(sums, shift) for shift in (1, 2, 3)]
    returning = pl.pallas_call(
        lambda *refs: scale_kernel(groups, per_row, *refs),
        out_shape=jax.ShapeDtypeStruct((workers, slots, piece, quarter), BF16),
        compiler_params=params,
        name="graft_scale",
    )(precond, *all_sums)
    arrived = lax.all_to_all(returning, "fsdp", split_axis=0, concat_axis=0, tiled=True)
    arrived = arrived.reshape(workers * slots, piece, quarter)

    grad_square = jnp.sum(sum(s[:, 1] for s in all_sums), axis=(1, 2))
    traces = DECAY * diag_sums + (1.0 - DECAY) * grad_square[None, :]
    divisors = jnp.stack([jnp.full((slots,), block_size, F32), my_width.astype(F32)])
    adds = SHRINKAGE * traces / divisors
    left_new, right_new = pl.pallas_call(
        stat_kernel,
        grid=(slots,),
        in_specs=[SMEM_SPEC] * 2
        + [col_spec] * 3
        + [far_spec] * 2
        + [row_spec] * 2
        + [pl.BlockSpec(memory_space=pl.ANY)],
        out_specs=[row_spec] * 2,
        out_shape=[jax.ShapeDtypeStruct(left_stat.shape, F32)] * 2,
        scratch_shapes=[pltpu.VMEM((block_size, quarter), BF16)],
        compiler_params=params,
        cost_estimate=pl.CostEstimate(
            flops=8 * block_size * block_size * quarter,
            bytes_accessed=40 * block_size * quarter * 2,
            transcendentals=0,
        ),
        name="stat_update",
    )(meta, adds, g_mine, g_prev, g_next, g_far0, g_far1, left_stat, right_stat, returning)

    def blocks_of(group):
        ids = lax.dynamic_slice_in_dim(slot_ids, group * ncols, ncols)
        return jnp.take(arrived, ids, axis=0, mode="clip")

    back = [blocks_of(me_group)]
    for shift in range(1, groups):
        back.append(turn_group(blocks_of((me_group + shift) % groups), shift))
    back = jnp.stack(back)
    order = (me_group - jnp.arange(groups, dtype=jnp.int32)) % groups
    back = jnp.take(back, order, axis=0, mode="clip")
    update = jnp.transpose(back, (0, 2, 1, 3)).reshape(rows_dev, ncols, quarter)
    return (update, left_new, right_new)


def solution(mesh):
    in_specs = (
        P("replica", "fsdp", None, None),
        P(),
        P(),
        P("fsdp", "replica", None),
        P("fsdp", "replica", None),
        P("fsdp", None, "replica"),
        P("fsdp", None, "replica"),
    )
    out_specs = (P("fsdp", None, "replica"), P("fsdp", "replica", None), P("fsdp", "replica", None))
    return jax.shard_map(
        on_device, mesh=mesh, in_specs=in_specs, out_specs=out_specs, check_vma=False
    )
```

time: 233 us -> 241 us (1.034)
  waiting for transfers between devices: 107 us -> 146 us
  matrix products: 16.5 us -> 0 us
  between operations: 14.7 us -> 1.06 us
  Pallas kernels: 0 us -> 12.6 us
  other arithmetic: 16.5 us -> 8.13 us
  starting transfers between devices: 60.1 us -> 57.3 us
    ppermute x13 -> x16, waiting for transfers between devices: 43.9 us -> 92 us  [turn_x(): return lax.ppermute(value, 'replica', pairs)]
    dot_general x4 -> x0, matrix products: 16.5 us -> none  [the longest x1 6.06 us: on_device(): jnp.einsum('xsqk,xspk->sqp', own_rows, g_all, preferred_element_type=F32)]
    pallas_call x0 -> x3, Pallas kernels: none -> 12.6 us  [the longest x1 5.92 us: on_device(): pl.pallas_call(stat_kernel, grid=(slots,), in_specs=[SMEM_SPEC] * 2 + [co...]
    ppermute x6, waiting for transfers between devices: 13.8 us -> 6.54 us  [turn_group(): return lax.ppermute(value, 'fsdp', pairs)]
    reduce_sum x2, other arithmetic: 4.06 us -> 0.2 us  [the longest x1 0.1 us: on_device(): grad_square = jnp.sum(sum((s[:, 1] for s in all_sums)), axis=(1, 2))]
    unnamed x16 -> x24, local copies, waits for them, and re-layouts: 0.05 us -> 3.71 us
    mul x1 -> x0, local copies, waits for them, and re-layouts: 2.88 us -> none  [on_device(): right_total = DECAY * right_stat + (1.0 - DECAY) * right_gram]
    all_to_all x1, starting transfers between devices: 13.2 us -> 10.4 us  [on_device(): lax.all_to_all(outgoing, 'fsdp', split_axis=0, concat_axis=0, tiled=True)]
  transfers between devices with their start and end apart: 22 -> 24, of which waited for: 13 -> 17; matrix products, arithmetic and copies ran while one was open for 17% -> 4% of each run, Pallas kernels for 0% -> 2%
where the time goes in v2:
time: 241 us; the launch traced here: 240 us
  waiting for transfers between devices  146 us (61%)
  starting transfers between devices  57.3 us (24%)
  local copies, waits for them, and re-layouts  15.5 us (6%)
  Pallas kernels  12.6 us (5%)
  other arithmetic  8.13 us (3%)
    ppermute x16, waiting for transfers between devices, turn_x(): return lax.ppermute(value, 'replica', pairs)  92 us
    all_to_all x1, waiting for transfers between devices, on_device(): lax.all_to_all(outgoing, 'fsdp', split_axis=0, concat_axis=0, tiled=True)  27.6 us
    ppermute x16, starting transfers between devices, turn_x(): return lax.ppermute(value, 'replica', pairs)  20.9 us
    all_to_all x1, waiting for transfers between devices, on_device(): lax.all_to_all(returning, 'fsdp', split_axis=0, concat_axis=0, tiled=True)  19.7 us
    ppermute x6, starting transfers between devices, turn_group(): return lax.ppermute(value, 'fsdp', pairs)  16.2 us
    all_to_all x1, starting transfers between devices, on_device(): lax.all_to_all(outgoing, 'fsdp', split_axis=0, concat_axis=0, tiled=True)  10.4 us
    all_to_all x1, starting transfers between devices, on_device(): lax.all_to_all(returning, 'fsdp', split_axis=0, concat_axis=0, tiled=True)  9.76 us
    gather x4, local copies, waits for them, and re-layouts, blocks_of(): return jnp.take(arrived, ids, axis=0, mode='clip')  8.37 us
  transfers between devices with their start and end apart: 24, of which 17 were waited for; matrix products, arithmetic and copies ran while one was open for 4% of the time, Pallas kernels for 2%

profile of v2, /device:TPU:1, one launch (start us, length us, event | category | flops | bytes accessed | tf_op | source)
XLA Modules:
  0.0 240.5 jit_solution(8873795518124057393)
XLA Ops:
  1.4 1.9 fusion
  3.4 2.1 collective-permute-start
  6.9 1.6 collective-permute-start.2
  9.0 4.4 %collective-permute-done = bf16[12,64,256]{2,1,0:T(8,128)(2,1)S(1)} collective-permute-done((bf16[12,64,256]{2,1,0:T(8,128)(2,1)S(1)}, bf16[12,64,256]{2,1,0:T(8,128)(2,1)S(1)}, u32[]{:S(2)}, u32[]{:S(2)}) %collective-permute-start) | collective-permute-done | bytes 393248 | tf_op jit(solution)/shard_map/ppermute | solution.py:157
  14.9 10.2 %collective-permute-done.2 = bf16[12,64,256]{2,1,0:T(8,128)(2,1)} collective-permute-done((bf16[12,64,256]{2,1,0:T(8,128)(2,1)S(1)}, bf16[12,64,256]{2,1,0:T(8,128)(2,1)}, u32[]{:S(2)}, u32[]{:S(2)}) %collective-permute-start.2) | collective-permute-done | bytes 393248 | tf_op jit(solution)/shard_map/ppermute | solution.py:157
  26.3 3.1 %collective-permute-start.3 = (bf16[12,16,256]{2,1,0:T(8,128)(2,1)S(1)}, bf16[12,16,256]{2,1,0:T(8,128)(2,1)S(1)}, u32[]{:S(2)}, u32[]{:S(2)}) collective-permute-start(bf16[12,16,256]{2,1,0:T(8,128)(2,1)S(1)} %get-tuple-element.28), channel_id=1, source_target_pairs={{0,16},{1,17},{2,18},{3,19},{4,20},{5,21},{6,22},{7,23},{8,24},{9,... | collective-permute-start | bytes 294920 | tf_op jit(solution)/shard_map/ppermute | solution.py:161
  29.4 5.1 %collective-permute-start.4 = (bf16[12,16,256]{2,1,0:T(8,128)(2,1)S(1)}, bf16[12,16,256]{2,1,0:T(8,128)(2,1)S(1)}, u32[]{:S(2)}, u32[]{:S(2)}) collective-permute-start(bf16[12,16,256]{2,1,0:T(8,128)(2,1)S(1)} %get-tuple-element.27), channel_id=1, source_target_pairs={{0,32},{1,33},{2,34},{3,35},{4,36},{5,37},{6,38},{7,39},{8,40},{9,... | collective-permute-start | bytes 294920 | tf_op jit(solution)/shard_map/ppermute | solution.py:161
  34.5 2.4 collective-permute-start.5
  36.9 2.0 collective-permute-done.4
  38.9 4.5 %collective-permute-done.5 = bf16[12,16,256]{2,1,0:T(8,128)(2,1)S(1)} collective-permute-done((bf16[12,16,256]{2,1,0:T(8,128)(2,1)S(1)}, bf16[12,16,256]{2,1,0:T(8,128)(2,1)S(1)}, u32[]{:S(2)}, u32[]{:S(2)}) %collective-permute-start.5) | collective-permute-done | bytes 98336 | tf_op jit(solution)/shard_map/ppermute | solution.py:161
  43.5 1.6 gather_fusion
  45.1 10.4 %all-to-all-start = ((bf16[64,2,16,256]{3,2,1,0:T(8,128)(2,1)}), bf16[64,2,16,256]{3,2,1,0:T(8,128)(2,1)S(1)}, u32[]{:S(2)}, u32[]{:S(2)}) async-start(bf16[64,2,16,256]{3,2,1,0:T(8,128)(2,1)} %bitcast.15), calls=%async_computation | async-start | bytes 2097152 | tf_op jit(solution)/shard_map/all_to_all | solution.py:210
  55.9 27.6 %all-to-all-done = bf16[64,2,16,256]{3,2,1,0:T(8,128)(2,1)S(1)} async-done(((bf16[64,2,16,256]{3,2,1,0:T(8,128)(2,1)}), bf16[64,2,16,256]{3,2,1,0:T(8,128)(2,1)S(1)}, u32[]{:S(2)}, u32[]{:S(2)}) %all-to-all-start) | async-done | bytes 1048608 | tf_op jit(solution)/shard_map/all_to_all | solution.py:210
  84.4 2.1 collective-permute-start.7
  89.2 19.1 %collective-permute-done.6.g1 = bf16[2,1024,256]{2,1,0:T(8,128)(2,1)S(1)} collective-permute-done((bf16[2,1024,256]{2,1,0:T(8,128)(2,1)S(1)}, bf16[2,1024,256]{2,1,0:T(8,128)(2,1)S(1)}, u32[]{:S(2)}, u32[]{:S(2)}) %collective-permute-start.6) | collective-permute-done | bytes 1048608 | tf_op jit(solution)/shard_map/ppermute | solution.py:157
  108.6 3.4 %collective-permute-start.9 = (bf16[1,1024,256]{2,1,0:T(8,128)(2,1)S(1)}, bf16[1,1024,256]{2,1,0:T(8,128)(2,1)S(1)}, u32[]{:S(2)}, u32[]{:S(2)}) collective-permute-start(bf16[1,1024,256]{2,1,0:T(8,128)(2,1)S(1)} %slice.37), channel_id=1, source_target_pairs={{0,192},{64,0},{128,64},{192,128},{1,193},{65,1},{129,65},{193,129... | collective-permute-start | bytes 1572872 | tf_op jit(solution)/shard_map/ppermute | solution.py:157
  112.1 19.1 %collective-permute-done.10.l1 = bf16[2,1024,256]{2,1,0:T(8,128)(2,1)S(1)} collective-permute-done((bf16[2,1024,256]{2,1,0:T(8,128)(2,1)S(1)}, bf16[2,1024,256]{2,1,0:T(8,128)(2,1)S(1)}, u32[]{:S(2)}, u32[]{:S(2)}) %collective-permute-start.10) | collective-permute-done | bytes 1048608 | tf_op jit(solution)/shard_map/ppermute | solution.py:157
  131.2 21.9 %collective-permute-done.11.l2 = bf16[2,1024,256]{2,1,0:T(8,128)(2,1)S(1)} collective-permute-done((bf16[2,1024,256]{2,1,0:T(8,128)(2,1)S(1)}, bf16[2,1024,256]{2,1,0:T(8,128)(2,1)S(1)}, u32[]{:S(2)}, u32[]{:S(2)}) %collective-permute-start.11) | collective-permute-done | bytes 1048608 | tf_op jit(solution)/shard_map/ppermute | solution.py:157
  153.1 11.5 %collective-permute-done.8.far0 = bf16[1,1024,256]{2,1,0:T(8,128)(2,1)S(1)} collective-permute-done((bf16[1,1024,256]{2,1,0:T(8,128)(2,1)S(1)}, bf16[1,1024,256]{2,1,0:T(8,128)(2,1)S(1)}, u32[]{:S(2)}, u32[]{:S(2)}) %collective-permute-start.8) | collective-permute-done | bytes 524320 | tf_op jit(solution)/shard_map/ppermute | solution.py:157
  164.6 5.5 %root_products.1 = (f32[2,1024,256]{2,1,0:T(8,128)}, f32[2,2,8,128]{3,2,1,0:T(8,128)S(1)}) custom-call(s32[3]{0:T(128)S(1)} %pad_add_fusion.meta, bf16[2,1024,256]{2,1,0:T(8,128)(2,1)S(1)} %bitcast_select_fusion.g0, bf16[2,1024,256]{2,1,0:T(8,128)(2,1)S(1)} %collective-permute-done.6.g1, bf16[2,1024,256]{2,1,0:T(8,128)(2,1)S(1)} %collective-permute-done.7.g3, ...), custom_call_target="tpu_custom_call" | custom-call | flops 2147483648 | bytes 11534336 | tf_op jit(solution)/shard_map/root_products/pallas_call | solution.py:231
  170.2 3.4 %collective-permute-start.14 = (f32[2,2,8,128]{3,2,1,0:T(8,128)S(1)}, f32[2,2,8,128]{3,2,1,0:T(8,128)S(1)}, u32[]{:S(2)}, u32[]{:S(2)}) collective-permute-start(f32[2,2,8,128]{3,2,1,0:T(8,128)S(1)} %get-tuple-element.12.refs_1_), channel_id=1, source_target_pairs={{0,128},{64,192},{128,0},{192,64},{1,129},{65,193},{129,1},{193,65... | collective-permute-start | bytes 49160 | tf_op jit(solution)/shard_map/ppermute | solution.py:157
  176.5 1.6 copy-done.4
  179.3 9.8 %all-to-all-start.1 = ((bf16[64,2,16,256]{3,2,1,0:T(8,128)(2,1)}), bf16[64,2,16,256]{3,2,1,0:T(8,128)(2,1)}, u32[]{:S(2)}, u32[]{:S(2)}) async-start(bf16[64,2,16,256]{3,2,1,0:T(8,128)(2,1)} %graft_scale.1.after), calls=%async_computation.1 | async-start | bytes 2097152 | tf_op jit(solution)/shard_map/all_to_all | solution.py:256
  189.2 2.8 %multiply_reduce_fusion.1 = (f32[2]{0:T(128)S(1)}, f32[2,256]{1,0:T(2,128)S(1)}) fusion(f32[2,256,1024]{2,1,0:T(8,128)} %left.1, f32[256,1024]{1,0:T(8,128)S(1)} %fusion.1, f32[2,256,1024]{2,1,0:T(8,128)} %right.3), kind=kLoop, calls=%fused_computation.9 | loop fusion | flops 2096638 | bytes 5244936 | tf_op jit(solution)/shard_map/reduce_sum | solution.py:192
  192.3 2.1 collective-permute-start.20
  197.3 19.7 %all-to-all-done.1 = bf16[64,2,16,256]{3,2,1,0:T(8,128)(2,1)} async-done(((bf16[64,2,16,256]{3,2,1,0:T(8,128)(2,1)}), bf16[64,2,16,256]{3,2,1,0:T(8,128)(2,1)}, u32[]{:S(2)}, u32[]{:S(2)}) %all-to-all-start.1) | async-done | bytes 1048608 | tf_op jit(solution)/shard_map/all_to_all | solution.py:256
  217.0 2.4 %gather_fusion.2 = bf16[12,16,256]{2,1,0:T(8,128)(2,1)} fusion(bf16[128,16,256]{2,1,0:T(8,128)(2,1)} %bitcast.19, s32[1024]{0:T(1024)S(1)} %pad_clamp_fusion.3), kind=kCustom, calls=%fused_computation.2 | custom fusion | bytes 196656 | tf_op jit(solution)/shard_map/jit(_take)/gather | solution.py:285
  220.4 2.4 %gather_fusion.3 = bf16[12,16,256]{2,1,0:T(8,128)(2,1)} fusion(bf16[128,16,256]{2,1,0:T(8,128)(2,1)} %bitcast.19, s32[1024]{0:T(1024)S(1)} %pad_clamp_fusion.2), kind=kCustom, calls=%fused_computation.3 | custom fusion | bytes 196656 | tf_op jit(solution)/shard_map/jit(_take)/gather | solution.py:285
  222.8 4.1 %collective-permute-start.17 = (bf16[12,16,256]{2,1,0:T(8,128)(2,1)}, bf16[12,16,256]{2,1,0:T(8,128)(2,1)S(1)}, u32[]{:S(2)}, u32[]{:S(2)}) collective-permute-start(bf16[12,16,256]{2,1,0:T(8,128)(2,1)} %gather_fusion.3), channel_id=1, source_target_pairs={{0,32},{1,33},{2,34},{3,35},{4,36},{5,37},{6,38},{7,39},{8,40},{9,... | collective-permute-start | bytes 294920 | tf_op jit(solution)/shard_map/ppermute | solution.py:161
  226.9 1.8 gather_fusion.4
  231.3 5.9 %stat_update.1 = (f32[2,256,1024]{2,1,0:T(8,128)}, f32[2,256,1024]{2,1,0:T(8,128)}) custom-call(s32[3]{0:T(128)S(1)} %pad_add_fusion.meta, f32[2,2]{1,0:T(2,128)S(1)} %pad_divide_fusion.adds, bf16[2,1024,256]{2,1,0:T(8,128)(2,1)S(1)} %bitcast_select_fusion.g0, bf16[2,1024,256]{2,1,0:T(8,128)(2,1)S(1)} %collective-permute-done.6.g1, ...), custom_call_target="tpu_custom_call" | custom-call | flops 2147483648 | bytes 20971520 | tf_op jit(solution)/shard_map/stat_update/pallas_call | solution.py:263
  237.2 1.8 gather_fusion.1
  (86 shorter events, 22.0 us)
Async XLA Ops:
  1.4 7.2 %copy-start.11 = (s32[48]{0:T(128)S(1)}, s32[48]{0:T(128)}, u32[]{:S(2)}) copy-start(s32[48]{0:T(128)} %param.9) | copy-start | bytes 580
  3.4 9.9 %collective-permute-start = (bf16[12,64,256]{2,1,0:T(8,128)(2,1)S(1)}, bf16[12,64,256]{2,1,0:T(8,128)(2,1)S(1)}, u32[]{:S(2)}, u32[]{:S(2)}) collective-permute-start(bf16[12,64,256]{2,1,0:T(8,128)(2,1)S(1)} %get-tuple-element.22), channel_id=1, source_target_pairs={{0,64},{64,128},{128,192},{192,0},{1,65},{65,129},{129,193},{193,1... | collective-permute-start | bytes 1179656 | tf_op jit(solution)/shard_map/ppermute | solution.py:157
  5.6 9.3 %collective-permute-start.1 = (bf16[12,64,256]{2,1,0:T(8,128)(2,1)S(1)}, bf16[12,64,256]{2,1,0:T(8,128)(2,1)S(1)}, u32[]{:S(2)}, u32[]{:S(2)}) collective-permute-start(bf16[12,64,256]{2,1,0:T(8,128)(2,1)S(1)} %get-tuple-element.24), channel_id=1, source_target_pairs={{0,192},{64,0},{128,64},{192,128},{1,193},{65,1},{129,65},{193,129... | collective-permute-start | bytes 1179656 | tf_op jit(solution)/shard_map/ppermute | solution.py:157
  6.9 18.1 %collective-permute-start.2 = (bf16[12,64,256]{2,1,0:T(8,128)(2,1)S(1)}, bf16[12,64,256]{2,1,0:T(8,128)(2,1)}, u32[]{:S(2)}, u32[]{:S(2)}) collective-permute-start(bf16[12,64,256]{2,1,0:T(8,128)(2,1)S(1)} %get-tuple-element.23), channel_id=1, source_target_pairs={{0,128},{64,192},{128,0},{192,64},{1,129},{65,193},{129,1},{193,65... | collective-permute-start | bytes 1179656 | tf_op jit(solution)/shard_map/ppermute | solution.py:157
  26.3 10.6 %collective-permute-start.3 = (bf16[12,16,256]{2,1,0:T(8,128)(2,1)S(1)}, bf16[12,16,256]{2,1,0:T(8,128)(2,1)S(1)}, u32[]{:S(2)}, u32[]{:S(2)}) collective-permute-start(bf16[12,16,256]{2,1,0:T(8,128)(2,1)S(1)} %get-tuple-element.28), channel_id=1, source_target_pairs={{0,16},{1,17},{2,18},{3,19},{4,20},{5,21},{6,22},{7,23},{8,24},{9,... | collective-permute-start | bytes 294920 | tf_op jit(solution)/shard_map/ppermute | solution.py:161
  29.4 9.5 %collective-permute-start.4 = (bf16[12,16,256]{2,1,0:T(8,128)(2,1)S(1)}, bf16[12,16,256]{2,1,0:T(8,128)(2,1)S(1)}, u32[]{:S(2)}, u32[]{:S(2)}) collective-permute-start(bf16[12,16,256]{2,1,0:T(8,128)(2,1)S(1)} %get-tuple-element.27), channel_id=1, source_target_pairs={{0,32},{1,33},{2,34},{3,35},{4,36},{5,37},{6,38},{7,39},{8,40},{9,... | collective-permute-start | bytes 294920 | tf_op jit(solution)/shard_map/ppermute | solution.py:161
  34.5 8.9 %collective-permute-start.5 = (bf16[12,16,256]{2,1,0:T(8,128)(2,1)S(1)}, bf16[12,16,256]{2,1,0:T(8,128)(2,1)S(1)}, u32[]{:S(2)}, u32[]{:S(2)}) collective-permute-start(bf16[12,16,256]{2,1,0:T(8,128)(2,1)S(1)} %get-tuple-element.26), channel_id=1, source_target_pairs={{0,48},{1,49},{2,50},{3,51},{4,52},{5,53},{6,54},{7,55},{8,56},{9,... | collective-permute-start | bytes 294920 | tf_op jit(solution)/shard_map/ppermute | solution.py:161
  43.5 12.1 %copy-start.10 = (s32[12]{0:T(128)S(1)}, s32[12]{0:T(128)}, u32[]{:S(2)}) copy-start(s32[12]{0:T(128)} %param.8) | copy-start | bytes 148
  45.1 38.4 %all-to-all-start = ((bf16[64,2,16,256]{3,2,1,0:T(8,128)(2,1)}), bf16[64,2,16,256]{3,2,1,0:T(8,128)(2,1)S(1)}, u32[]{:S(2)}, u32[]{:S(2)}) async-start(bf16[64,2,16,256]{3,2,1,0:T(8,128)(2,1)} %bitcast.15), calls=%async_computation | async-start | bytes 2097152 | tf_op jit(solution)/shard_map/all_to_all | solution.py:210
  83.6 81.0 %copy-start.5 = (bf16[2,1024,256]{2,1,0:T(8,128)(2,1)S(1)}, bf16[2,1024,256]{2,1,0:T(8,128)(2,1)}, u32[]{:S(2)}) copy-start(bf16[2,1024,256]{2,1,0:T(8,128)(2,1)} %right.2) | copy-start | bytes 3145732
  83.8 24.6 %collective-permute-start.6 = (bf16[2,1024,256]{2,1,0:T(8,128)(2,1)S(1)}, bf16[2,1024,256]{2,1,0:T(8,128)(2,1)S(1)}, u32[]{:S(2)}, u32[]{:S(2)}) collective-permute-start(bf16[2,1024,256]{2,1,0:T(8,128)(2,1)S(1)} %bitcast_select_fusion.g0), channel_id=1, source_target_pairs={{0,64},{64,128},{128,192},{192,0},{1,65},{65,129},{129,193},{193,1... | collective-permute-start | bytes 3145736 | tf_op jit(solution)/shard_map/ppermute | solution.py:157
  84.4 24.1 %collective-permute-start.7 = (bf16[2,1024,256]{2,1,0:T(8,128)(2,1)S(1)}, bf16[2,1024,256]{2,1,0:T(8,128)(2,1)S(1)}, u32[]{:S(2)}, u32[]{:S(2)}) collective-permute-start(bf16[2,1024,256]{2,1,0:T(8,128)(2,1)S(1)} %bitcast_select_fusion.g0), channel_id=1, source_target_pairs={{0,192},{64,0},{128,64},{192,128},{1,193},{65,1},{129,65},{193,129... | collective-permute-start | bytes 3145736 | tf_op jit(solution)/shard_map/ppermute | solution.py:157
  86.6 44.6 %collective-permute-start.10 = (bf16[2,1024,256]{2,1,0:T(8,128)(2,1)S(1)}, bf16[2,1024,256]{2,1,0:T(8,128)(2,1)S(1)}, u32[]{:S(2)}, u32[]{:S(2)}) collective-permute-start(bf16[2,1024,256]{2,1,0:T(8,128)(2,1)S(1)} %copy-done.6), channel_id=1, source_target_pairs={{0,64},{64,128},{128,192},{192,0},{1,65},{65,129},{129,193},{193,1... | collective-permute-start | bytes 3145736 | tf_op jit(solution)/shard_map/ppermute | solution.py:157
  86.6 66.5 %collective-permute-start.11 = (bf16[2,1024,256]{2,1,0:T(8,128)(2,1)S(1)}, bf16[2,1024,256]{2,1,0:T(8,128)(2,1)S(1)}, u32[]{:S(2)}, u32[]{:S(2)}) collective-permute-start(bf16[2,1024,256]{2,1,0:T(8,128)(2,1)S(1)} %copy-done.6), channel_id=1, source_target_pairs={{0,128},{64,192},{128,0},{192,64},{1,129},{65,193},{129,1},{193,65... | collective-permute-start | bytes 3145736 | tf_op jit(solution)/shard_map/ppermute | solution.py:157
  87.7 65.3 %collective-permute-start.12 = (bf16[2,1024,256]{2,1,0:T(8,128)(2,1)S(1)}, bf16[2,1024,256]{2,1,0:T(8,128)(2,1)S(1)}, u32[]{:S(2)}, u32[]{:S(2)}) collective-permute-start(bf16[2,1024,256]{2,1,0:T(8,128)(2,1)S(1)} %copy-done.6), channel_id=1, source_target_pairs={{0,192},{64,0},{128,64},{192,128},{1,193},{65,1},{129,65},{193,129... | collective-permute-start | bytes 3145736 | tf_op jit(solution)/shard_map/ppermute | solution.py:157
  108.4 56.1 %collective-permute-start.8 = (bf16[1,1024,256]{2,1,0:T(8,128)(2,1)S(1)}, bf16[1,1024,256]{2,1,0:T(8,128)(2,1)S(1)}, u32[]{:S(2)}, u32[]{:S(2)}) collective-permute-start(bf16[1,1024,256]{2,1,0:T(8,128)(2,1)S(1)} %slice.36), channel_id=1, source_target_pairs={{0,64},{64,128},{128,192},{192,0},{1,65},{65,129},{129,193},{193,1... | collective-permute-start | bytes 1572872 | tf_op jit(solution)/shard_map/ppermute | solution.py:157
  108.6 56.0 %collective-permute-start.9 = (bf16[1,1024,256]{2,1,0:T(8,128)(2,1)S(1)}, bf16[1,1024,256]{2,1,0:T(8,128)(2,1)S(1)}, u32[]{:S(2)}, u32[]{:S(2)}) collective-permute-start(bf16[1,1024,256]{2,1,0:T(8,128)(2,1)S(1)} %slice.37), channel_id=1, source_target_pairs={{0,192},{64,0},{128,64},{192,128},{1,193},{65,1},{129,65},{193,129... | collective-permute-start | bytes 1572872 | tf_op jit(solution)/shard_map/ppermute | solution.py:157
  131.2 33.4 %copy-start.7 = (bf16[2,1024,256]{2,1,0:T(8,128)(2,1)}, bf16[2,1024,256]{2,1,0:T(8,128)(2,1)S(1)}, u32[]{:S(2)}) copy-start(bf16[2,1024,256]{2,1,0:T(8,128)(2,1)S(1)} %collective-permute-done.10.l1) | copy-start | bytes 3145732
  153.1 11.5 %copy-start.8 = (bf16[2,1024,256]{2,1,0:T(8,128)(2,1)}, bf16[2,1024,256]{2,1,0:T(8,128)(2,1)S(1)}, u32[]{:S(2)}) copy-start(bf16[2,1024,256]{2,1,0:T(8,128)(2,1)S(1)} %collective-permute-done.11.l2) | copy-start | bytes 3145732
  153.1 11.5 %copy-start.9 = (bf16[2,1024,256]{2,1,0:T(8,128)(2,1)}, bf16[2,1024,256]{2,1,0:T(8,128)(2,1)S(1)}, u32[]{:S(2)}) copy-start(bf16[2,1024,256]{2,1,0:T(8,128)(2,1)S(1)} %collective-permute-done.12.l3) | copy-start | bytes 3145732
  164.6 5.5 %copy-start = (bf16[1,1024,256]{2,1,0:T(8,128)(2,1)}, bf16[1,1024,256]{2,1,0:T(8,128)(2,1)S(1)}, u32[]{:S(2)}) copy-start(bf16[1,1024,256]{2,1,0:T(8,128)(2,1)S(1)} %collective-permute-done.8.far0) | copy-start | bytes 1572868
  164.6 5.5 %copy-start.2 = (bf16[1,1024,256]{2,1,0:T(8,128)(2,1)}, bf16[1,1024,256]{2,1,0:T(8,128)(2,1)S(1)}, u32[]{:S(2)}) copy-start(bf16[1,1024,256]{2,1,0:T(8,128)(2,1)S(1)} %collective-permute-done.9.far1) | copy-start | bytes 1572868
  170.1 3.9 %collective-permute-start.13 = (f32[2,2,8,128]{3,2,1,0:T(8,128)S(1)}, f32[2,2,8,128]{3,2,1,0:T(8,128)S(1)}, u32[]{:S(2)}, u32[]{:S(2)}) collective-permute-start(f32[2,2,8,128]{3,2,1,0:T(8,128)S(1)} %get-tuple-element.12.refs_1_), channel_id=1, source_target_pairs={{0,64},{64,128},{128,192},{192,0},{1,65},{65,129},{129,193},{193,1... | collective-permute-start | bytes 49160 | tf_op jit(solution)/shard_map/ppermute | solution.py:157
  170.2 4.7 %collective-permute-start.14 = (f32[2,2,8,128]{3,2,1,0:T(8,128)S(1)}, f32[2,2,8,128]{3,2,1,0:T(8,128)S(1)}, u32[]{:S(2)}, u32[]{:S(2)}) collective-permute-start(f32[2,2,8,128]{3,2,1,0:T(8,128)S(1)} %get-tuple-element.12.refs_1_), channel_id=1, source_target_pairs={{0,128},{64,192},{128,0},{192,64},{1,129},{65,193},{129,1},{193,65... | collective-permute-start | bytes 49160 | tf_op jit(solution)/shard_map/ppermute | solution.py:157
  173.6 2.9 %collective-permute-start.15 = (f32[2,2,8,128]{3,2,1,0:T(8,128)S(1)}, f32[2,2,8,128]{3,2,1,0:T(8,128)S(1)}, u32[]{:S(2)}, u32[]{:S(2)}) collective-permute-start(f32[2,2,8,128]{3,2,1,0:T(8,128)S(1)} %get-tuple-element.12.refs_1_), channel_id=1, source_target_pairs={{0,192},{64,0},{128,64},{192,128},{1,193},{65,1},{129,65},{193,129... | collective-permute-start | bytes 49160 | tf_op jit(solution)/shard_map/ppermute | solution.py:157
  179.3 37.7 %all-to-all-start.1 = ((bf16[64,2,16,256]{3,2,1,0:T(8,128)(2,1)}), bf16[64,2,16,256]{3,2,1,0:T(8,128)(2,1)}, u32[]{:S(2)}, u32[]{:S(2)}) async-start(bf16[64,2,16,256]{3,2,1,0:T(8,128)(2,1)} %graft_scale.1.after), calls=%async_computation.1 | async-start | bytes 2097152 | tf_op jit(solution)/shard_map/all_to_all | solution.py:256
  192.2 4.1 %collective-permute-start.19 = (f32[2,2]{1,0:T(2,128)S(1)}, f32[2,2]{1,0:T(2,128)S(1)}, u32[]{:S(2)}, u32[]{:S(2)}) collective-permute-start(f32[2,2]{1,0:T(2,128)S(1)} %pad_maximum_fusion.2), channel_id=1, source_target_pairs={{0,64},{64,128},{128,192},{192,0},{1,65},{65,129},{129,193},{193,1... | collective-permute-start | bytes 56 | tf_op jit(solution)/shard_map/ppermute | solution.py:157
  192.3 4.4 %collective-permute-start.20 = (f32[2,2]{1,0:T(2,128)S(1)}, f32[2,2]{1,0:T(2,128)S(1)}, u32[]{:S(2)}, u32[]{:S(2)}) collective-permute-start(f32[2,2]{1,0:T(2,128)S(1)} %pad_maximum_fusion.2), channel_id=1, source_target_pairs={{0,128},{64,192},{128,0},{192,64},{1,129},{65,193},{129,1},{193,65... | collective-permute-start | bytes 56 | tf_op jit(solution)/shard_map/ppermute | solution.py:157
  194.4 2.8 %collective-permute-start.21 = (f32[2,2]{1,0:T(2,128)S(1)}, f32[2,2]{1,0:T(2,128)S(1)}, u32[]{:S(2)}, u32[]{:S(2)}) collective-permute-start(f32[2,2]{1,0:T(2,128)S(1)} %pad_maximum_fusion.2), channel_id=1, source_target_pairs={{0,192},{64,0},{128,64},{192,128},{1,193},{65,1},{129,65},{193,129... | collective-permute-start | bytes 56 | tf_op jit(solution)/shard_map/ppermute | solution.py:157
  219.4 19.7 %collective-permute-start.16 = (bf16[12,16,256]{2,1,0:T(8,128)(2,1)}, bf16[12,16,256]{2,1,0:T(8,128)(2,1)S(1)}, u32[]{:S(2)}, u32[]{:S(2)}) collective-permute-start(bf16[12,16,256]{2,1,0:T(8,128)(2,1)} %gather_fusion.2), channel_id=1, source_target_pairs={{0,16},{1,17},{2,18},{3,19},{4,20},{5,21},{6,22},{7,23},{8,24},{9,... | collective-permute-start | bytes 294920 | tf_op jit(solution)/shard_map/ppermute | solution.py:161
  222.8 16.2 %collective-permute-start.17 = (bf16[12,16,256]{2,1,0:T(8,128)(2,1)}, bf16[12,16,256]{2,1,0:T(8,128)(2,1)S(1)}, u32[]{:S(2)}, u32[]{:S(2)}) collective-permute-start(bf16[12,16,256]{2,1,0:T(8,128)(2,1)} %gather_fusion.3), channel_id=1, source_target_pairs={{0,32},{1,33},{2,34},{3,35},{4,36},{5,37},{6,38},{7,39},{8,40},{9,... | collective-permute-start | bytes 294920 | tf_op jit(solution)/shard_map/ppermute | solution.py:161
  228.7 10.3 %collective-permute-start.18 = (bf16[12,16,256]{2,1,0:T(8,128)(2,1)S(1)}, bf16[12,16,256]{2,1,0:T(8,128)(2,1)S(1)}, u32[]{:S(2)}, u32[]{:S(2)}) collective-permute-start(bf16[12,16,256]{2,1,0:T(8,128)(2,1)S(1)} %gather_fusion.4), channel_id=1, source_target_pairs={{0,48},{1,49},{2,50},{3,51},{4,52},{5,53},{6,54},{7,55},{8,56},{9,... | collective-permute-start | bytes 294920 | tf_op jit(solution)/shard_map/ppermute | solution.py:161
  (4 other events, 6.7 us)

commit v3 on v2

--- a/solution.py
+++ b/solution.py
@@ -40,7 +40,9 @@
     return jnp.sum(part.reshape(rows // 8, 8, 128), axis=0)
 
 
-def root_kernel(meta, g0, g1, g3, far0, far1, right, l0, l1, l2, l3, out, sums, far, rights, prods):
+def root_kernel(meta, *refs):
+    g0, g1, g3, far0, far1, l0, l1, l3, lfar0, lfar1, right = refs[:11]
+    out, sums, far, lfar, rights, prods = refs[11:]
     slot = pl.program_id(0)
     me = meta[0]
     width = meta[1 + slot]
@@ -51,10 +53,12 @@
     @pl.when(slot == 0)
     def _():
         far[...] = far0[0]
+        lfar[...] = lfar0[0]
 
     @pl.when(slot == 1)
     def _():
         far[...] = far1[0]
+        lfar[...] = lfar1[0]
 
     def place(turn):
         q = lax.rem(me + reps - turn, reps)
@@ -72,7 +76,7 @@
     g_sum = jnp.zeros((8, 128), F32)
     for n in range(size // quarter):
         rows = slice(n * quarter, (n + 1) * quarter)
-        wide = jnp.concatenate([l0[0, rows, :], l1[0, rows, :], l2[0, rows, :], l3[0, rows, :]], 1)
+        wide = jnp.concatenate([l0[0, rows, :], l1[0, rows, :], lfar[rows, :], l3[0, rows, :]], 1)
         value = dot(wide, prods[...]) * keep
         out[0, rows, :] = value
         p_sum = p_sum + fold(value * value)
@@ -80,6 +84,21 @@
         g_sum = g_sum + fold(own * own)
     sums[0, 0] = p_sum
     sums[0, 1] = g_sum
+
+
+def spread_kernel(place, h0, h1, h2, h3, out, held):
+    workers, slots = out.shape[:2]
+    for n, ref in enumerate((h0, h1, h2, h3)):
+        held[n * ref.shape[0] : (n + 1) * ref.shape[0]] = ref[...]
+    for w in range(workers):
+        for s in range(slots):
+            out[w, s] = held[place[w * slots + s]]
+
+
+def collect_kernel(wanted, arrived, *outs):
+    for n, out in enumerate(outs):
+        for j in range(out.shape[0]):
+            out[j] = arrived[wanted[n * out.shape[0] + j]]
 
 
 def scale_kernel(groups, per_row, value, s0, s1, s2, s3, out):
@@ -169,10 +188,25 @@
         cut = lax.dynamic_slice_in_dim(terms, rep * quarter, quarter, 2)
         return jnp.transpose(cut, (1, 0, 2))
 
-    summed = columns_of(me_rep).astype(F32)
-    for shift in (1, 3, 2):
-        summed = summed + turn_x(columns_of((me_rep + shift) % reps), shift).astype(F32)
-    summed = summed.astype(BF16)
+    def add(a, b):
+        return (a.astype(F32) + b.astype(F32)).astype(BF16)
+
+    half = ncols // 2
+    up, down = columns_of((me_rep + 1) % reps), columns_of((me_rep + 3) % reps)
+    far = columns_of((me_rep + 2) % reps)
+    relay_up = turn_x(far[:half], 1)
+    relay_down = turn_x(far[half:], 3)
+    direct_up = turn_x(up[half:], 1)
+    direct_down = turn_x(down[:half], 3)
+    joint_up = turn_x(add(up[:half], relay_up), 1)
+    joint_down = turn_x(add(down[half:], relay_down), 3)
+    own = columns_of(me_rep).astype(F32)
+    summed = jnp.concatenate(
+        [
+            own[:half] + joint_up.astype(F32) + direct_down.astype(F32),
+            own[half:] + direct_up.astype(F32) + joint_down.astype(F32),
+        ]
+    ).astype(BF16)
     summed, left_root = lax.optimization_barrier((summed, left_root))
 
     my_blocks = lax.dynamic_slice_in_dim(block_ids, me_work * slots, slots)
@@ -193,7 +227,10 @@
     right_diag = jnp.sum(jnp.sum(right_stat * unit_rows[None], axis=2) * within_width, axis=1)
     diag_own = jnp.stack([left_diag, right_diag])
 
-    left_roots = [left_root] + [turn_x(left_root, shift) for shift in (1, 2, 3)]
+    l_prev = turn_x(left_root, 1)
+    l_next = turn_x(left_root, 3)
+    l_far0 = turn_x(left_root[:1], 2)
+    l_far1 = turn_x(l_next[1:], 3)
 
     summed = summed.reshape(ncols, groups, piece, quarter)
 
@@ -203,16 +240,25 @@
     held = [rows_of(me_group)]
     for shift in range(1, groups):
         held.append(turn_group(rows_of((me_group + shift) % groups), shift))
-    held = jnp.concatenate(held, axis=0)
     place = ((me_group - block_ids // ncols) % groups) * ncols + block_ids % ncols
-    outgoing = jnp.take(held, place, axis=0, mode="clip")
-    outgoing = outgoing.reshape(workers, slots, piece, quarter)
+    params = pltpu.CompilerParams(vmem_limit_bytes=VMEM_LIMIT)
+    outgoing = pl.pallas_call(
+        spread_kernel,
+        in_specs=[SMEM_SPEC] + [pl.BlockSpec(memory_space=pltpu.VMEM)] * groups,
+        out_shape=jax.ShapeDtypeStruct((workers, slots, piece, quarter), BF16),
+        scratch_shapes=[pltpu.VMEM((groups * ncols, piece, quarter), BF16)],
+        compiler_params=params,
+        name="spread",
+    )(place.astype(jnp.int32), *held)
     incoming = lax.all_to_all(outgoing, "fsdp", split_axis=0, concat_axis=0, tiled=True)
     g_mine = jnp.transpose(
         incoming.reshape(groups, per_row, slots, piece, quarter), (2, 1, 0, 3, 4)
     ).reshape(slots, block_size, quarter)
     g_mine = jnp.where(my_filled[:, None, None], g_mine, jnp.zeros((), BF16))
 
+    g_mine, l_prev, l_next, l_far0, l_far1 = lax.optimization_barrier(
+        (g_mine, l_prev, l_next, l_far0, l_far1)
+    )
     g_prev = turn_x(g_mine, 1)
     g_next = turn_x(g_mine, reps - 1)
     g_far0 = turn_x(g_prev[:1], 1)
@@ -227,17 +273,16 @@
     far_spec = whole(1, block_size, quarter)
     row_spec = by_slot(quarter, block_size)
     col_shape = (slots, block_size, quarter)
-    params = pltpu.CompilerParams(vmem_limit_bytes=VMEM_LIMIT)
     precond, sums = pl.pallas_call(
         root_kernel,
         grid=(slots,),
-        in_specs=[SMEM_SPEC] + [col_spec] * 3 + [far_spec] * 2 + [col_spec] * 5,
+        in_specs=[SMEM_SPEC] + ([col_spec] * 3 + [far_spec] * 2) * 2 + [col_spec],
         out_specs=[col_spec, by_slot(2, 8, 128)],
         out_shape=[
             jax.ShapeDtypeStruct(col_shape, F32),
             jax.ShapeDtypeStruct((slots, 2, 8, 128), F32),
         ],
-        scratch_shapes=[pltpu.VMEM((block_size, quarter), BF16)] * 3,
+        scratch_shapes=[pltpu.VMEM((block_size, quarter), BF16)] * 4,
         compiler_params=params,
         cost_estimate=pl.CostEstimate(
             flops=8 * block_size * block_size * quarter,
@@ -245,7 +290,12 @@
             transcendentals=0,
         ),
         name="root_products",
-    )(meta, g_mine, g_prev, g_next, g_far0, g_far1, right_root, *left_roots)
+    )(
+        meta,
+        *(g_mine, g_prev, g_next, g_far0, g_far1),
+        *(left_root, l_prev, l_next, l_far0, l_far1),
+        right_root,
+    )
     all_sums = [sums] + [turn_x(sums, shift) for shift in (1, 2, 3)]
     returning = pl.pallas_call(
         lambda *refs: scale_kernel(groups, per_row, *refs),
@@ -280,13 +330,17 @@
         name="stat_update",
     )(meta, adds, g_mine, g_prev, g_next, g_far0, g_far1, left_stat, right_stat, returning)
 
-    def blocks_of(group):
-        ids = lax.dynamic_slice_in_dim(slot_ids, group * ncols, ncols)
-        return jnp.take(arrived, ids, axis=0, mode="clip")
-
-    back = [blocks_of(me_group)]
-    for shift in range(1, groups):
-        back.append(turn_group(blocks_of((me_group + shift) % groups), shift))
+    arrived, left_new, right_new = lax.optimization_barrier((arrived, left_new, right_new))
+    block = jnp.arange(groups * ncols, dtype=jnp.int32)
+    wanted = jnp.take(slot_ids, (block + me_group * ncols) % (groups * ncols), mode="clip")
+    back = pl.pallas_call(
+        collect_kernel,
+        in_specs=[SMEM_SPEC, pl.BlockSpec(memory_space=pltpu.VMEM)],
+        out_shape=[jax.ShapeDtypeStruct((ncols, piece, quarter), BF16)] * groups,
+        compiler_params=params,
+        name="collect",
+    )(wanted, arrived)
+    back = [back[0]] + [turn_group(back[shift], shift) for shift in range(1, groups)]
     back = jnp.stack(back)
     order = (me_group - jnp.arange(groups, dtype=jnp.int32)) % groups
     back = jnp.take(back, order, axis=0, mode="clip")

time: 241 us -> 214 us (0.89)
  waiting for transfers between devices: 146 us -> 107 us
  starting transfers between devices: 57.3 us -> 71 us
  local copies, waits for them, and re-layouts: 15.5 us -> 11.4 us
  Pallas kernels: 12.6 us -> 15.6 us
    all_to_all x1, waiting for transfers between devices: 27.6 us -> 0.01 us  [on_device(): lax.all_to_all(outgoing, 'fsdp', split_axis=0, concat_axis=0, tiled=True)]
    ppermute x16 -> x20, waiting for transfers between devices: 92 us -> 81.4 us  [turn_x(): return lax.ppermute(value, 'replica', pairs)]
    gather x5 -> x1, local copies, waits for them, and re-layouts: 9.99 us -> 0.78 us  [on_device(): jnp.take(slot_ids, (block + me_group * ncols) % (groups * ncols), mode='c...]
    all_to_all x1, waiting for transfers between devices: 19.7 us -> 11.4 us  [on_device(): lax.all_to_all(returning, 'fsdp', split_axis=0, concat_axis=0, tiled=True)]
    ppermute x6, waiting for transfers between devices: 6.54 us -> 14.3 us  [turn_group(): return lax.ppermute(value, 'fsdp', pairs)]
    ppermute x16 -> x20, starting transfers between devices: 20.9 us -> 26.6 us  [turn_x(): return lax.ppermute(value, 'replica', pairs)]
    all_to_all x1, starting transfers between devices: 9.76 us -> 14.7 us  [on_device(): lax.all_to_all(returning, 'fsdp', split_axis=0, concat_axis=0, tiled=True)]
    all_to_all x1, starting transfers between devices: 10.4 us -> 13.5 us  [on_device(): lax.all_to_all(outgoing, 'fsdp', split_axis=0, concat_axis=0, tiled=True)]
  transfers between devices with their start and end apart: 24 -> 28, of which waited for: 17 -> 20; matrix products, arithmetic and copies ran while one was open for 4% -> 4% of each run, Pallas kernels for 2% -> 3%
where the time goes in v3:
time: 214 us; the launch traced here: 213 us
  waiting for transfers between devices  107 us (50%)
  starting transfers between devices  71 us (33%)
  Pallas kernels  15.6 us (7%)
  local copies, waits for them, and re-layouts  11.4 us (5%)
  other arithmetic  7.37 us (3%)
    ppermute x20, waiting for transfers between devices, turn_x(): return lax.ppermute(value, 'replica', pairs)  81.4 us
    ppermute x20, starting transfers between devices, turn_x(): return lax.ppermute(value, 'replica', pairs)  26.6 us
    ppermute x6, starting transfers between devices, turn_group(): return lax.ppermute(value, 'fsdp', pairs)  16.2 us
    all_to_all x1, starting transfers between devices, on_device(): lax.all_to_all(returning, 'fsdp', split_axis=0, concat_axis=0, tiled=True)  14.7 us
    ppermute x6, waiting for transfers between devices, turn_group(): return lax.ppermute(value, 'fsdp', pairs)  14.3 us
    all_to_all x1, starting transfers between devices, on_device(): lax.all_to_all(outgoing, 'fsdp', split_axis=0, concat_axis=0, tiled=True)  13.5 us
    all_to_all x1, waiting for transfers between devices, on_device(): lax.all_to_all(returning, 'fsdp', split_axis=0, concat_axis=0, tiled=True)  11.4 us
    unnamed x24, local copies, waits for them, and re-layouts  6.24 us
  transfers between devices with their start and end apart: 28, of which 20 were waited for; matrix products, arithmetic and copies ran while one was open for 4% of the time, Pallas kernels for 3%

profile of v3, /device:TPU:1, one launch (start us, length us, event | category | flops | bytes accessed | tf_op | source)
XLA Modules:
  0.0 213.5 jit_solution(14349914466283693069)
XLA Ops:
  1.4 1.8 fusion
  3.5 3.4 %collective-permute-start.4 = (bf16[6,64,256]{2,1,0:T(8,128)(2,1)S(1)}, bf16[6,64,256]{2,1,0:T(8,128)(2,1)S(1)}, u32[]{:S(2)}, u32[]{:S(2)}) collective-permute-start(bf16[6,64,256]{2,1,0:T(8,128)(2,1)S(1)} %get-tuple-element.57), channel_id=1, source_target_pairs={{0,192},{64,0},{128,64},{192,128},{1,193},{65,1},{129,65},{193,129... | collective-permute-start | bytes 589832 | tf_op jit(solution)/shard_map/ppermute | solution.py:176
  7.0 2.8 %collective-permute-start.2 = (bf16[6,64,256]{2,1,0:T(8,128)(2,1)S(1)}, bf16[6,64,256]{2,1,0:T(8,128)(2,1)S(1)}, u32[]{:S(2)}, u32[]{:S(2)}) collective-permute-start(bf16[6,64,256]{2,1,0:T(8,128)(2,1)S(1)} %slice.71), channel_id=1, source_target_pairs={{0,192},{64,0},{128,64},{192,128},{1,193},{65,1},{129,65},{193,129... | collective-permute-start | bytes 589832 | tf_op jit(solution)/shard_map/ppermute | solution.py:176
  10.6 3.5 %collective-permute-start.5 = (bf16[6,64,256]{2,1,0:T(8,128)(2,1)S(1)}, bf16[6,64,256]{2,1,0:T(8,128)(2,1)S(1)}, u32[]{:S(2)}, u32[]{:S(2)}) collective-permute-start(bf16[6,64,256]{2,1,0:T(8,128)(2,1)S(1)} %add_convert_fusion), channel_id=1, source_target_pairs={{0,192},{64,0},{128,64},{192,128},{1,193},{65,1},{129,65},{193,129... | collective-permute-start | bytes 589832 | tf_op jit(solution)/shard_map/ppermute | solution.py:176
  14.7 3.3 %collective-permute-done.3 = bf16[6,64,256]{2,1,0:T(8,128)(2,1)S(1)} collective-permute-done((bf16[6,64,256]{2,1,0:T(8,128)(2,1)S(1)}, bf16[6,64,256]{2,1,0:T(8,128)(2,1)S(1)}, u32[]{:S(2)}, u32[]{:S(2)}) %collective-permute-start.3) | collective-permute-done | bytes 196640 | tf_op jit(solution)/shard_map/ppermute | solution.py:176
  18.0 3.1 %collective-permute-done.1 = bf16[6,64,256]{2,1,0:T(8,128)(2,1)S(1)} collective-permute-done((bf16[6,64,256]{2,1,0:T(8,128)(2,1)S(1)}, bf16[6,64,256]{2,1,0:T(8,128)(2,1)S(1)}, u32[]{:S(2)}, u32[]{:S(2)}) %collective-permute-start.1) | collective-permute-done | bytes 196640 | tf_op jit(solution)/shard_map/ppermute | solution.py:176
  21.3 3.1 %collective-permute-start.6 = (bf16[12,16,256]{2,1,0:T(8,128)(2,1)S(1)}, bf16[12,16,256]{2,1,0:T(8,128)(2,1)S(1)}, u32[]{:S(2)}, u32[]{:S(2)}) collective-permute-start(bf16[12,16,256]{2,1,0:T(8,128)(2,1)S(1)} %get-tuple-element.54), channel_id=1, source_target_pairs={{0,16},{1,17},{2,18},{3,19},{4,20},{5,21},{6,22},{7,23},{8,24},{9,... | collective-permute-start | bytes 294920 | tf_op jit(solution)/shard_map/ppermute | solution.py:180
  24.4 5.1 %collective-permute-start.7 = (bf16[12,16,256]{2,1,0:T(8,128)(2,1)S(1)}, bf16[12,16,256]{2,1,0:T(8,128)(2,1)S(1)}, u32[]{:S(2)}, u32[]{:S(2)}) collective-permute-start(bf16[12,16,256]{2,1,0:T(8,128)(2,1)S(1)} %get-tuple-element.53), channel_id=1, source_target_pairs={{0,32},{1,33},{2,34},{3,35},{4,36},{5,37},{6,38},{7,39},{8,40},{9,... | collective-permute-start | bytes 294920 | tf_op jit(solution)/shard_map/ppermute | solution.py:180
  29.5 2.4 %collective-permute-start.8 = (bf16[12,16,256]{2,1,0:T(8,128)(2,1)S(1)}, bf16[12,16,256]{2,1,0:T(8,128)(2,1)S(1)}, u32[]{:S(2)}, u32[]{:S(2)}) collective-permute-start(bf16[12,16,256]{2,1,0:T(8,128)(2,1)S(1)} %get-tuple-element.52), channel_id=1, source_target_pairs={{0,48},{1,49},{2,50},{3,51},{4,52},{5,53},{6,54},{7,55},{8,56},{9,... | collective-permute-start | bytes 294920 | tf_op jit(solution)/shard_map/ppermute | solution.py:180
  33.3 2.2 %collective-permute-done.8.h3 = bf16[12,16,256]{2,1,0:T(8,128)(2,1)S(1)} collective-permute-done((bf16[12,16,256]{2,1,0:T(8,128)(2,1)S(1)}, bf16[12,16,256]{2,1,0:T(8,128)(2,1)S(1)}, u32[]{:S(2)}, u32[]{:S(2)}) %collective-permute-start.8) | collective-permute-done | bytes 98336 | tf_op jit(solution)/shard_map/ppermute | solution.py:180
  35.5 1.6 spread.1
  37.1 13.5 %all-to-all-start = ((bf16[64,2,16,256]{3,2,1,0:T(8,128)(2,1)}), bf16[64,2,16,256]{3,2,1,0:T(8,128)(2,1)S(1)}, u32[]{:S(2)}, u32[]{:S(2)}) async-start(bf16[64,2,16,256]{3,2,1,0:T(8,128)(2,1)} %spread.1), calls=%async_computation | async-start | bytes 2097152 | tf_op jit(solution)/shard_map/all_to_all | solution.py:253
  52.2 1.9 slice.56
  54.4 20.9 %collective-permute-done.10.refs_7_ = bf16[2,1024,256]{2,1,0:T(8,128)(2,1)S(1)} collective-permute-done((bf16[2,1024,256]{2,1,0:T(8,128)(2,1)}, bf16[2,1024,256]{2,1,0:T(8,128)(2,1)S(1)}, u32[]{:S(2)}, u32[]{:S(2)}) %collective-permute-start.10) | collective-permute-done | bytes 1048608 | tf_op jit(solution)/shard_map/ppermute | solution.py:176
  77.1 1.6 collective-permute-start.12
  79.2 7.2 %collective-permute-done.11.refs_8_ = bf16[1,1024,256]{2,1,0:T(8,128)(2,1)S(1)} collective-permute-done((bf16[1,1024,256]{2,1,0:T(8,128)(2,1)}, bf16[1,1024,256]{2,1,0:T(8,128)(2,1)S(1)}, u32[]{:S(2)}, u32[]{:S(2)}) %collective-permute-start.11) | collective-permute-done | bytes 524320 | tf_op jit(solution)/shard_map/ppermute | solution.py:176
  87.9 9.8 %collective-permute-done.12.refs_9_ = bf16[1,1024,256]{2,1,0:T(8,128)(2,1)S(1)} collective-permute-done((bf16[1,1024,256]{2,1,0:T(8,128)(2,1)}, bf16[1,1024,256]{2,1,0:T(8,128)(2,1)S(1)}, u32[]{:S(2)}, u32[]{:S(2)}) %collective-permute-start.12) | collective-permute-done | bytes 524320 | tf_op jit(solution)/shard_map/ppermute | solution.py:176
  98.9 2.7 %collective-permute-start.14 = (bf16[2,1024,256]{2,1,0:T(8,128)(2,1)S(1)}, bf16[2,1024,256]{2,1,0:T(8,128)(2,1)S(1)}, u32[]{:S(2)}, u32[]{:S(2)}) collective-permute-start(bf16[2,1024,256]{2,1,0:T(8,128)(2,1)S(1)} %bitcast_select_fusion.refs_0_.g0), channel_id=1, source_target_pairs={{0,192},{64,0},{128,64},{192,128},{1,193},{65,1},{129,65},{193,129... | collective-permute-start | bytes 3145736 | tf_op jit(solution)/shard_map/ppermute | solution.py:176
  101.6 22.4 %collective-permute-done.13.refs_1_.g1 = bf16[2,1024,256]{2,1,0:T(8,128)(2,1)S(1)} collective-permute-done((bf16[2,1024,256]{2,1,0:T(8,128)(2,1)S(1)}, bf16[2,1024,256]{2,1,0:T(8,128)(2,1)S(1)}, u32[]{:S(2)}, u32[]{:S(2)}) %collective-permute-start.13) | collective-permute-done | bytes 1048608 | tf_op jit(solution)/shard_map/ppermute | solution.py:176
  124.2 2.7 %collective-permute-start.16 = (bf16[1,1024,256]{2,1,0:T(8,128)(2,1)S(1)}, bf16[1,1024,256]{2,1,0:T(8,128)(2,1)S(1)}, u32[]{:S(2)}, u32[]{:S(2)}) collective-permute-start(bf16[1,1024,256]{2,1,0:T(8,128)(2,1)S(1)} %slice.78), channel_id=1, source_target_pairs={{0,192},{64,0},{128,64},{192,128},{1,193},{65,1},{129,65},{193,129... | collective-permute-start | bytes 1572872 | tf_op jit(solution)/shard_map/ppermute | solution.py:176
  127.0 10.0 %collective-permute-done.15.refs_3_.far0 = bf16[1,1024,256]{2,1,0:T(8,128)(2,1)S(1)} collective-permute-done((bf16[1,1024,256]{2,1,0:T(8,128)(2,1)S(1)}, bf16[1,1024,256]{2,1,0:T(8,128)(2,1)S(1)}, u32[]{:S(2)}, u32[]{:S(2)}) %collective-permute-start.15) | collective-permute-done | bytes 524320 | tf_op jit(solution)/shard_map/ppermute | solution.py:176
  137.1 5.6 %root_products.1 = (f32[2,1024,256]{2,1,0:T(8,128)}, f32[2,2,8,128]{3,2,1,0:T(8,128)S(1)}) custom-call(s32[3]{0:T(128)S(1)} %pad_add_fusion.meta, bf16[2,1024,256]{2,1,0:T(8,128)(2,1)S(1)} %bitcast_select_fusion.refs_0_.g0, bf16[2,1024,256]{2,1,0:T(8,128)(2,1)S(1)} %collective-permute-done.13.refs_1_.g1, ...), custom_call_target="tpu_custom_call" | custom-call | flops 2147483648 | bytes 11534336 | tf_op jit(solution)/shard_map/root_products/pallas_call | solution.py:276
  143.1 3.2 %collective-permute-start.18 = (f32[2,2,8,128]{3,2,1,0:T(8,128)S(1)}, f32[2,2,8,128]{3,2,1,0:T(8,128)S(1)}, u32[]{:S(2)}, u32[]{:S(2)}) collective-permute-start(f32[2,2,8,128]{3,2,1,0:T(8,128)S(1)} %get-tuple-element.29.refs_1_), channel_id=1, source_target_pairs={{0,128},{64,192},{128,0},{192,64},{1,129},{65,193},{129,1},{193,65... | collective-permute-start | bytes 49160 | tf_op jit(solution)/shard_map/ppermute | solution.py:176
  151.7 14.7 %all-to-all-start.1 = ((bf16[64,2,16,256]{3,2,1,0:T(8,128)(2,1)}), bf16[64,2,16,256]{3,2,1,0:T(8,128)(2,1)}, u32[]{:S(2)}, u32[]{:S(2)}) async-start(bf16[64,2,16,256]{3,2,1,0:T(8,128)(2,1)} %graft_scale.1.after), calls=%async_computation.1 | async-start | bytes 2097152 | tf_op jit(solution)/shard_map/all_to_all | solution.py:306
  166.6 2.8 %multiply_reduce_fusion.1 = (f32[2]{0:T(128)S(1)}, f32[2,256]{1,0:T(2,128)S(1)}) fusion(f32[2,256,1024]{2,1,0:T(8,128)} %left.1, f32[256,1024]{1,0:T(8,128)S(1)} %fusion.1, f32[2,256,1024]{2,1,0:T(8,128)} %right.1), kind=kLoop, calls=%fused_computation.5 | loop fusion | flops 2096638 | bytes 5244936 | tf_op jit(solution)/shard_map/reduce_sum | solution.py:226
  169.7 2.4 %collective-permute-start.21 = (f32[2,2]{1,0:T(2,128)S(1)}, f32[2,2]{1,0:T(2,128)S(1)}, u32[]{:S(2)}, u32[]{:S(2)}) collective-permute-start(f32[2,2]{1,0:T(2,128)S(1)} %pad_maximum_fusion.2), channel_id=1, source_target_pairs={{0,128},{64,192},{128,0},{192,64},{1,129},{65,193},{129,1},{193,65... | collective-permute-start | bytes 56 | tf_op jit(solution)/shard_map/ppermute | solution.py:176
  177.0 5.9 %stat_update.1 = (f32[2,256,1024]{2,1,0:T(8,128)}, f32[2,256,1024]{2,1,0:T(8,128)}) custom-call(s32[3]{0:T(128)S(1)} %pad_add_fusion.meta, f32[2,2]{1,0:T(2,128)S(1)} %pad_divide_fusion.adds, bf16[2,1024,256]{2,1,0:T(8,128)(2,1)S(1)} %bitcast_select_fusion.refs_0_.g0, bf16[2,1024,256]{2,1,0:T(8,128)(2,1)S(1)} %collective-permute-done.13.refs_1_.g1, ...), custom_call_target="tpu_custom_call" | custom-call | flops 2147483648 | bytes 20971520 | tf_op jit(solution)/shard_map/stat_update/pallas_call | solution.py:313
  182.9 11.4 %all-to-all-done.1 = bf16[64,2,16,256]{3,2,1,0:T(8,128)(2,1)} async-done(((bf16[64,2,16,256]{3,2,1,0:T(8,128)(2,1)}), bf16[64,2,16,256]{3,2,1,0:T(8,128)(2,1)}, u32[]{:S(2)}, u32[]{:S(2)}) %all-to-all-start.1) | async-done | bytes 1048608 | tf_op jit(solution)/shard_map/all_to_all | solution.py:306
  196.7 4.1 %collective-permute-start.24 = (bf16[12,16,256]{2,1,0:T(8,128)(2,1)S(1)}, bf16[12,16,256]{2,1,0:T(8,128)(2,1)S(1)}, u32[]{:S(2)}, u32[]{:S(2)}) collective-permute-start(bf16[12,16,256]{2,1,0:T(8,128)(2,1)S(1)} %get-tuple-element.35), channel_id=1, source_target_pairs={{0,32},{1,33},{2,34},{3,35},{4,36},{5,37},{6,38},{7,39},{8,40},{9,... | collective-permute-start | bytes 294920 | tf_op jit(solution)/shard_map/ppermute | solution.py:180
  201.3 1.9 collective-permute-done.23
  203.2 7.0 %collective-permute-done.24 = bf16[12,16,256]{2,1,0:T(8,128)(2,1)S(1)} collective-permute-done((bf16[12,16,256]{2,1,0:T(8,128)(2,1)S(1)}, bf16[12,16,256]{2,1,0:T(8,128)(2,1)S(1)}, u32[]{:S(2)}, u32[]{:S(2)}) %collective-permute-start.24) | collective-permute-done | bytes 98336 | tf_op jit(solution)/shard_map/ppermute | solution.py:180
  210.2 1.9 collective-permute-done.25
  (95 shorter events, 26.7 us)
Async XLA Ops:
  3.2 6.6 %copy-start.11 = (s32[48]{0:T(128)S(1)}, s32[48]{0:T(128)}, u32[]{:S(2)}) copy-start(s32[48]{0:T(128)} %param.9) | copy-start | bytes 580
  3.5 7.0 %collective-permute-start.4 = (bf16[6,64,256]{2,1,0:T(8,128)(2,1)S(1)}, bf16[6,64,256]{2,1,0:T(8,128)(2,1)S(1)}, u32[]{:S(2)}, u32[]{:S(2)}) collective-permute-start(bf16[6,64,256]{2,1,0:T(8,128)(2,1)S(1)} %get-tuple-element.57), channel_id=1, source_target_pairs={{0,192},{64,0},{128,64},{192,128},{1,193},{65,1},{129,65},{193,129... | collective-permute-start | bytes 589832 | tf_op jit(solution)/shard_map/ppermute | solution.py:176
  6.9 7.1 %collective-permute-start = (bf16[6,64,256]{2,1,0:T(8,128)(2,1)S(1)}, bf16[6,64,256]{2,1,0:T(8,128)(2,1)S(1)}, u32[]{:S(2)}, u32[]{:S(2)}) collective-permute-start(bf16[6,64,256]{2,1,0:T(8,128)(2,1)S(1)} %get-tuple-element.56), channel_id=1, source_target_pairs={{0,64},{64,128},{128,192},{192,0},{1,65},{65,129},{129,193},{193,1... | collective-permute-start | bytes 589832 | tf_op jit(solution)/shard_map/ppermute | solution.py:176
  7.0 7.8 %collective-permute-start.2 = (bf16[6,64,256]{2,1,0:T(8,128)(2,1)S(1)}, bf16[6,64,256]{2,1,0:T(8,128)(2,1)S(1)}, u32[]{:S(2)}, u32[]{:S(2)}) collective-permute-start(bf16[6,64,256]{2,1,0:T(8,128)(2,1)S(1)} %slice.71), channel_id=1, source_target_pairs={{0,192},{64,0},{128,64},{192,128},{1,193},{65,1},{129,65},{193,129... | collective-permute-start | bytes 589832 | tf_op jit(solution)/shard_map/ppermute | solution.py:176
  9.7 8.3 %collective-permute-start.3 = (bf16[6,64,256]{2,1,0:T(8,128)(2,1)S(1)}, bf16[6,64,256]{2,1,0:T(8,128)(2,1)S(1)}, u32[]{:S(2)}, u32[]{:S(2)}) collective-permute-start(bf16[6,64,256]{2,1,0:T(8,128)(2,1)S(1)} %slice.73), channel_id=1, source_target_pairs={{0,64},{64,128},{128,192},{192,0},{1,65},{65,129},{129,193},{193,1... | collective-permute-start | bytes 589832 | tf_op jit(solution)/shard_map/ppermute | solution.py:176
  10.6 7.4 %collective-permute-start.5 = (bf16[6,64,256]{2,1,0:T(8,128)(2,1)S(1)}, bf16[6,64,256]{2,1,0:T(8,128)(2,1)S(1)}, u32[]{:S(2)}, u32[]{:S(2)}) collective-permute-start(bf16[6,64,256]{2,1,0:T(8,128)(2,1)S(1)} %add_convert_fusion), channel_id=1, source_target_pairs={{0,192},{64,0},{128,64},{192,128},{1,193},{65,1},{129,65},{193,129... | collective-permute-start | bytes 589832 | tf_op jit(solution)/shard_map/ppermute | solution.py:176
  14.1 7.0 %collective-permute-start.1 = (bf16[6,64,256]{2,1,0:T(8,128)(2,1)S(1)}, bf16[6,64,256]{2,1,0:T(8,128)(2,1)S(1)}, u32[]{:S(2)}, u32[]{:S(2)}) collective-permute-start(bf16[6,64,256]{2,1,0:T(8,128)(2,1)S(1)} %add_convert_fusion.1), channel_id=1, source_target_pairs={{0,64},{64,128},{128,192},{192,0},{1,65},{65,129},{129,193},{193,1... | collective-permute-start | bytes 589832 | tf_op jit(solution)/shard_map/ppermute | solution.py:176
  21.3 10.6 %collective-permute-start.6 = (bf16[12,16,256]{2,1,0:T(8,128)(2,1)S(1)}, bf16[12,16,256]{2,1,0:T(8,128)(2,1)S(1)}, u32[]{:S(2)}, u32[]{:S(2)}) collective-permute-start(bf16[12,16,256]{2,1,0:T(8,128)(2,1)S(1)} %get-tuple-element.54), channel_id=1, source_target_pairs={{0,16},{1,17},{2,18},{3,19},{4,20},{5,21},{6,22},{7,23},{8,24},{9,... | collective-permute-start | bytes 294920 | tf_op jit(solution)/shard_map/ppermute | solution.py:180
  24.4 8.9 %collective-permute-start.7 = (bf16[12,16,256]{2,1,0:T(8,128)(2,1)S(1)}, bf16[12,16,256]{2,1,0:T(8,128)(2,1)S(1)}, u32[]{:S(2)}, u32[]{:S(2)}) collective-permute-start(bf16[12,16,256]{2,1,0:T(8,128)(2,1)S(1)} %get-tuple-element.53), channel_id=1, source_target_pairs={{0,32},{1,33},{2,34},{3,35},{4,36},{5,37},{6,38},{7,39},{8,40},{9,... | collective-permute-start | bytes 294920 | tf_op jit(solution)/shard_map/ppermute | solution.py:180
  29.5 6.0 %collective-permute-start.8 = (bf16[12,16,256]{2,1,0:T(8,128)(2,1)S(1)}, bf16[12,16,256]{2,1,0:T(8,128)(2,1)S(1)}, u32[]{:S(2)}, u32[]{:S(2)}) collective-permute-start(bf16[12,16,256]{2,1,0:T(8,128)(2,1)S(1)} %get-tuple-element.52), channel_id=1, source_target_pairs={{0,48},{1,49},{2,50},{3,51},{4,52},{5,53},{6,54},{7,55},{8,56},{9,... | collective-permute-start | bytes 294920 | tf_op jit(solution)/shard_map/ppermute | solution.py:180
  37.1 41.5 %copy-start.10 = (s32[12]{0:T(128)S(1)}, s32[12]{0:T(128)}, u32[]{:S(2)}) copy-start(s32[12]{0:T(128)} %param.8) | copy-start | bytes 148
  37.1 41.8 %all-to-all-start = ((bf16[64,2,16,256]{3,2,1,0:T(8,128)(2,1)}), bf16[64,2,16,256]{3,2,1,0:T(8,128)(2,1)S(1)}, u32[]{:S(2)}, u32[]{:S(2)}) async-start(bf16[64,2,16,256]{3,2,1,0:T(8,128)(2,1)} %spread.1), calls=%async_computation | async-start | bytes 2097152 | tf_op jit(solution)/shard_map/all_to_all | solution.py:253
  50.6 24.7 %collective-permute-start.10 = (bf16[2,1024,256]{2,1,0:T(8,128)(2,1)}, bf16[2,1024,256]{2,1,0:T(8,128)(2,1)S(1)}, u32[]{:S(2)}, u32[]{:S(2)}) collective-permute-start(bf16[2,1024,256]{2,1,0:T(8,128)(2,1)} %refs_5_), channel_id=1, source_target_pairs={{0,192},{64,0},{128,64},{192,128},{1,193},{65,1},{129,65},{193,129... | collective-permute-start | bytes 3145736 | tf_op jit(solution)/shard_map/ppermute | solution.py:176
  51.2 36.7 %collective-permute-start.9 = (bf16[2,1024,256]{2,1,0:T(8,128)(2,1)}, bf16[2,1024,256]{2,1,0:T(8,128)(2,1)}, u32[]{:S(2)}, u32[]{:S(2)}) collective-permute-start(bf16[2,1024,256]{2,1,0:T(8,128)(2,1)} %refs_5_), channel_id=1, source_target_pairs={{0,64},{64,128},{128,192},{192,0},{1,65},{65,129},{129,193},{193,1... | collective-permute-start | bytes 3145736 | tf_op jit(solution)/shard_map/ppermute | solution.py:176
  54.1 32.3 %collective-permute-start.11 = (bf16[1,1024,256]{2,1,0:T(8,128)(2,1)}, bf16[1,1024,256]{2,1,0:T(8,128)(2,1)S(1)}, u32[]{:S(2)}, u32[]{:S(2)}) collective-permute-start(bf16[1,1024,256]{2,1,0:T(8,128)(2,1)} %slice.56), channel_id=1, source_target_pairs={{0,128},{64,192},{128,0},{192,64},{1,129},{65,193},{129,1},{193,65... | collective-permute-start | bytes 1572872 | tf_op jit(solution)/shard_map/ppermute | solution.py:176
  77.1 20.6 %collective-permute-start.12 = (bf16[1,1024,256]{2,1,0:T(8,128)(2,1)}, bf16[1,1024,256]{2,1,0:T(8,128)(2,1)S(1)}, u32[]{:S(2)}, u32[]{:S(2)}) collective-permute-start(bf16[1,1024,256]{2,1,0:T(8,128)(2,1)} %slice.76), channel_id=1, source_target_pairs={{0,192},{64,0},{128,64},{192,128},{1,193},{65,1},{129,65},{193,129... | collective-permute-start | bytes 1572872 | tf_op jit(solution)/shard_map/ppermute | solution.py:176
  87.9 49.2 %copy-start.6 = (bf16[1,1024,256]{2,1,0:T(8,128)(2,1)S(1)}, bf16[1,1024,256]{2,1,0:T(8,128)(2,1)}, u32[]{:S(2)}) copy-start(bf16[1,1024,256]{2,1,0:T(8,128)(2,1)} %copy-done.5) | copy-start | bytes 1572868
  98.5 25.6 %collective-permute-start.13 = (bf16[2,1024,256]{2,1,0:T(8,128)(2,1)S(1)}, bf16[2,1024,256]{2,1,0:T(8,128)(2,1)S(1)}, u32[]{:S(2)}, u32[]{:S(2)}) collective-permute-start(bf16[2,1024,256]{2,1,0:T(8,128)(2,1)S(1)} %bitcast_select_fusion.refs_0_.g0), channel_id=1, source_target_pairs={{0,64},{64,128},{128,192},{192,0},{1,65},{65,129},{129,193},{193,1... | collective-permute-start | bytes 3145736 | tf_op jit(solution)/shard_map/ppermute | solution.py:176
  98.9 38.1 %copy-start.8 = (bf16[1,1024,256]{2,1,0:T(8,128)(2,1)S(1)}, bf16[1,1024,256]{2,1,0:T(8,128)(2,1)}, u32[]{:S(2)}) copy-start(bf16[1,1024,256]{2,1,0:T(8,128)(2,1)} %copy-done.7) | copy-start | bytes 1572868
  98.9 25.2 %collective-permute-start.14 = (bf16[2,1024,256]{2,1,0:T(8,128)(2,1)S(1)}, bf16[2,1024,256]{2,1,0:T(8,128)(2,1)S(1)}, u32[]{:S(2)}, u32[]{:S(2)}) collective-permute-start(bf16[2,1024,256]{2,1,0:T(8,128)(2,1)S(1)} %bitcast_select_fusion.refs_0_.g0), channel_id=1, source_target_pairs={{0,192},{64,0},{128,64},{192,128},{1,193},{65,1},{129,65},{193,129... | collective-permute-start | bytes 3145736 | tf_op jit(solution)/shard_map/ppermute | solution.py:176
  124.1 13.0 %collective-permute-start.15 = (bf16[1,1024,256]{2,1,0:T(8,128)(2,1)S(1)}, bf16[1,1024,256]{2,1,0:T(8,128)(2,1)S(1)}, u32[]{:S(2)}, u32[]{:S(2)}) collective-permute-start(bf16[1,1024,256]{2,1,0:T(8,128)(2,1)S(1)} %slice.77), channel_id=1, source_target_pairs={{0,64},{64,128},{128,192},{192,0},{1,65},{65,129},{129,193},{193,1... | collective-permute-start | bytes 1572872 | tf_op jit(solution)/shard_map/ppermute | solution.py:176
  124.2 12.9 %collective-permute-start.16 = (bf16[1,1024,256]{2,1,0:T(8,128)(2,1)S(1)}, bf16[1,1024,256]{2,1,0:T(8,128)(2,1)S(1)}, u32[]{:S(2)}, u32[]{:S(2)}) collective-permute-start(bf16[1,1024,256]{2,1,0:T(8,128)(2,1)S(1)} %slice.78), channel_id=1, source_target_pairs={{0,192},{64,0},{128,64},{192,128},{1,193},{65,1},{129,65},{193,129... | collective-permute-start | bytes 1572872 | tf_op jit(solution)/shard_map/ppermute | solution.py:176
  142.7 4.0 %collective-permute-start.17 = (f32[2,2,8,128]{3,2,1,0:T(8,128)S(1)}, f32[2,2,8,128]{3,2,1,0:T(8,128)S(1)}, u32[]{:S(2)}, u32[]{:S(2)}) collective-permute-start(f32[2,2,8,128]{3,2,1,0:T(8,128)S(1)} %get-tuple-element.29.refs_1_), channel_id=1, source_target_pairs={{0,64},{64,128},{128,192},{192,0},{1,65},{65,129},{129,193},{193,1... | collective-permute-start | bytes 49160 | tf_op jit(solution)/shard_map/ppermute | solution.py:176
  143.1 4.5 %collective-permute-start.18 = (f32[2,2,8,128]{3,2,1,0:T(8,128)S(1)}, f32[2,2,8,128]{3,2,1,0:T(8,128)S(1)}, u32[]{:S(2)}, u32[]{:S(2)}) collective-permute-start(f32[2,2,8,128]{3,2,1,0:T(8,128)S(1)} %get-tuple-element.29.refs_1_), channel_id=1, source_target_pairs={{0,128},{64,192},{128,0},{192,64},{1,129},{65,193},{129,1},{193,65... | collective-permute-start | bytes 49160 | tf_op jit(solution)/shard_map/ppermute | solution.py:176
  146.3 2.6 %collective-permute-start.19 = (f32[2,2,8,128]{3,2,1,0:T(8,128)S(1)}, f32[2,2,8,128]{3,2,1,0:T(8,128)S(1)}, u32[]{:S(2)}, u32[]{:S(2)}) collective-permute-start(f32[2,2,8,128]{3,2,1,0:T(8,128)S(1)} %get-tuple-element.29.refs_1_), channel_id=1, source_target_pairs={{0,192},{64,0},{128,64},{192,128},{1,193},{65,1},{129,65},{193,129... | collective-permute-start | bytes 49160 | tf_op jit(solution)/shard_map/ppermute | solution.py:176
  151.7 42.7 %all-to-all-start.1 = ((bf16[64,2,16,256]{3,2,1,0:T(8,128)(2,1)}), bf16[64,2,16,256]{3,2,1,0:T(8,128)(2,1)}, u32[]{:S(2)}, u32[]{:S(2)}) async-start(bf16[64,2,16,256]{3,2,1,0:T(8,128)(2,1)} %graft_scale.1.after), calls=%async_computation.1 | async-start | bytes 2097152 | tf_op jit(solution)/shard_map/all_to_all | solution.py:306
  169.6 4.3 %collective-permute-start.20 = (f32[2,2]{1,0:T(2,128)S(1)}, f32[2,2]{1,0:T(2,128)S(1)}, u32[]{:S(2)}, u32[]{:S(2)}) collective-permute-start(f32[2,2]{1,0:T(2,128)S(1)} %pad_maximum_fusion.2), channel_id=1, source_target_pairs={{0,64},{64,128},{128,192},{192,0},{1,65},{65,129},{129,193},{193,1... | collective-permute-start | bytes 56 | tf_op jit(solution)/shard_map/ppermute | solution.py:176
  169.7 4.4 %collective-permute-start.21 = (f32[2,2]{1,0:T(2,128)S(1)}, f32[2,2]{1,0:T(2,128)S(1)}, u32[]{:S(2)}, u32[]{:S(2)}) collective-permute-start(f32[2,2]{1,0:T(2,128)S(1)} %pad_maximum_fusion.2), channel_id=1, source_target_pairs={{0,128},{64,192},{128,0},{192,64},{1,129},{65,193},{129,1},{193,65... | collective-permute-start | bytes 56 | tf_op jit(solution)/shard_map/ppermute | solution.py:176
  172.1 2.8 %collective-permute-start.22 = (f32[2,2]{1,0:T(2,128)S(1)}, f32[2,2]{1,0:T(2,128)S(1)}, u32[]{:S(2)}, u32[]{:S(2)}) collective-permute-start(f32[2,2]{1,0:T(2,128)S(1)} %pad_maximum_fusion.2), channel_id=1, source_target_pairs={{0,192},{64,0},{128,64},{192,128},{1,193},{65,1},{129,65},{193,129... | collective-permute-start | bytes 56 | tf_op jit(solution)/shard_map/ppermute | solution.py:176
  195.6 7.6 %collective-permute-start.23 = (bf16[12,16,256]{2,1,0:T(8,128)(2,1)S(1)}, bf16[12,16,256]{2,1,0:T(8,128)(2,1)S(1)}, u32[]{:S(2)}, u32[]{:S(2)}) collective-permute-start(bf16[12,16,256]{2,1,0:T(8,128)(2,1)S(1)} %get-tuple-element.34), channel_id=1, source_target_pairs={{0,16},{1,17},{2,18},{3,19},{4,20},{5,21},{6,22},{7,23},{8,24},{9,... | collective-permute-start | bytes 294920 | tf_op jit(solution)/shard_map/ppermute | solution.py:180
  196.7 13.5 %collective-permute-start.24 = (bf16[12,16,256]{2,1,0:T(8,128)(2,1)S(1)}, bf16[12,16,256]{2,1,0:T(8,128)(2,1)S(1)}, u32[]{:S(2)}, u32[]{:S(2)}) collective-permute-start(bf16[12,16,256]{2,1,0:T(8,128)(2,1)S(1)} %get-tuple-element.35), channel_id=1, source_target_pairs={{0,32},{1,33},{2,34},{3,35},{4,36},{5,37},{6,38},{7,39},{8,40},{9,... | collective-permute-start | bytes 294920 | tf_op jit(solution)/shard_map/ppermute | solution.py:180
  200.8 11.3 %collective-permute-start.25 = (bf16[12,16,256]{2,1,0:T(8,128)(2,1)S(1)}, bf16[12,16,256]{2,1,0:T(8,128)(2,1)S(1)}, u32[]{:S(2)}, u32[]{:S(2)}) collective-permute-start(bf16[12,16,256]{2,1,0:T(8,128)(2,1)S(1)} %get-tuple-element.36), channel_id=1, source_target_pairs={{0,48},{1,49},{2,50},{3,51},{4,52},{5,53},{6,54},{7,55},{8,56},{9,... | collective-permute-start | bytes 294920 | tf_op jit(solution)/shard_map/ppermute | solution.py:180
  (8 other events, 17.4 us)

commit v4 on v3

v4 whole, which is shorter than its diff:
```python
import jax
import jax.numpy as jnp
from jax import lax
from jax.experimental import pallas as pl
from jax.experimental.pallas import tpu as pltpu
from jax.sharding import PartitionSpec as P

DECAY = 0.99
SHRINKAGE = 0.1
EPSILON = 1e-06
F32 = jnp.float32
BF16 = jnp.bfloat16
VMEM_LIMIT = 20 * 1024 * 1024
RELAY_COST = 10_000_000_000
SMEM_SPEC = pl.BlockSpec(memory_space=pltpu.SMEM)


def slot_tables(assignment, workers, slots):
    blocks = jnp.arange(assignment.shape[0], dtype=jnp.int32)
    same_worker = assignment[:, None] == assignment[None, :]
    earlier = blocks[None, :] < blocks[:, None]
    slot_rank = jnp.sum((same_worker & earlier).astype(jnp.int32), axis=1)
    slot_ids = assignment * slots + slot_rank
    wanted = jnp.arange(workers * slots, dtype=jnp.int32)
    slot_hits = (slot_ids[None, :] == wanted[:, None]).astype(jnp.int32)
    filled = jnp.sum(slot_hits, axis=1) > 0
    block_ids = jnp.sum(slot_hits * blocks[None, :], axis=1)
    return (slot_ids, filled, block_ids)


def dot(a, b, contract=(1, 0)):
    dims = (((contract[0],), (contract[1],)), ((), ()))
    return lax.dot_general(a, b, dims, preferred_element_type=F32)


def fold(values):
    rows = values.shape[0]
    part = values[:, :128]
    for first in range(128, values.shape[1], 128):
        part = part + values[:, first : first + 128]
    return jnp.sum(part.reshape(rows // 8, 8, 128), axis=0)


def relay_kernel(before, behind, up, down):
    count = up.shape[0]
    up[...] = before[:count]
    down[...] = behind[count:]


def product_kernel(meta, arrived, r0, r1, far0, far1, r3, grad, sums, *products):
    slots, groups = grad.shape[:2]
    per_row = arrived.shape[0] // groups
    for s in range(slots):
        filled = meta[1 + slots + s] > 0
        parts = []
        g_sum = jnp.zeros((8, 128), F32)
        for i in range(groups):
            part = arrived[i * per_row : (i + 1) * per_row, s].reshape(grad.shape[2:])
            part = jnp.where(filled, part, jnp.zeros_like(part))
            grad[s, i] = part
            wide = part.astype(F32)
            g_sum = g_sum + fold(wide * wide)
            parts.append(part)
        own = jnp.concatenate(parts, 1)
        rights = (r0.at[2 * s], r1.at[2 * s], (far0, far1)[s].at[0], r3.at[2 * s])
        for product, right in zip(products, rights):
            product[s] = dot(own, right[...]).astype(BF16)
        sums[s] = g_sum


def root_kernel(meta, diags, g_sums, y0, y1, y2, y3, l0, l1, far0, far1, l3, out, sums, prods):
    me = meta[0]
    slots, size, quarter = out.shape
    reps = size // quarter
    piece = quarter // (reps * reps)
    column = me * quarter + lax.broadcasted_iota(jnp.int32, (quarter, quarter), 1)
    for s in range(slots):
        keep = (column < meta[1 + s]).astype(F32)
        for d, rows in enumerate((y0, y1, y2, y3)):
            r = lax.rem(me + d, reps)
            for t in range(reps):
                q = lax.rem(me + reps - t, reps)
                for p in range(reps):
                    source = pl.multiple_of((q * reps + p) * piece, piece)
                    target = pl.multiple_of(((t * reps + p) * reps + r) * piece, piece)
                    prods[pl.ds(target, piece), :] = rows[s, pl.ds(source, piece), :]
        far = (far0, far1)[s]
        n2 = 2 * s + 1
        p_sum = jnp.zeros((8, 128), F32)
        for n in range(reps):
            rows = slice(n * quarter, (n + 1) * quarter)
            lefts = (l0.at[n2, rows], l1.at[n2, rows], far.at[1, rows], l3.at[n2, rows])
            wide = jnp.concatenate([left[...] for left in lefts], 1)
            value = dot(wide, prods[...]) * keep
            out[s, rows] = value
            p_sum = p_sum + fold(value * value)
        sums[s, 0] = p_sum
        sums[s, 1] = g_sums[s]
        sums[s, 2] = jnp.full((8, 128), diags[0, s])
        sums[s, 3] = jnp.full((8, 128), diags[1, s])


def spread_kernel(place, h0, h1, h2, h3, out, held):
    workers, slots = out.shape[:2]
    for n, ref in enumerate((h0, h1, h2, h3)):
        held[n * ref.shape[0] : (n + 1) * ref.shape[0]] = ref[...]
    for w in range(workers):
        for s in range(slots):
            out[w, s] = held[place[w * slots + s]]


def collect_kernel(wanted, arrived, *outs):
    for n, out in enumerate(outs):
        for j in range(out.shape[0]):
            out[j] = arrived[wanted[n * out.shape[0] + j]]


def scale_kernel(groups, per_row, meta, value, s0, s1, s2, s3, out, adds):
    slots, size, _ = value.shape
    piece = out.shape[2]
    total = s0[...] + s1[...] + s2[...] + s3[...]
    for s in range(slots):
        p_square = jnp.sum(total[s, 0], keepdims=True)
        g_square = jnp.sum(total[s, 1], keepdims=True)
        scale = jnp.sqrt(g_square / (p_square + EPSILON))
        for side, width in enumerate((jnp.int32(size), meta[1 + s])):
            trace = DECAY * total[s, 2 + side] + (1.0 - DECAY) * g_square
            adds[side, s] = SHRINKAGE * trace / jnp.full((8, 128), width).astype(F32)
        for p in range(per_row):
            for i in range(groups):
                first = (p * groups + i) * piece
                out[i * per_row + p, s] = (value[s, first : first + piece, :] * scale).astype(BF16)


def stat_kernel(meta, adds, g0, g1, g3, far0, far1, left, right, left_new, right_new, whole):
    me = meta[0]
    slots, quarter, size = left.shape
    reps = size // quarter
    piece = quarter // (reps * reps)
    keep = 1.0 - SHRINKAGE
    row = lax.broadcasted_iota(jnp.int32, (quarter, quarter), 0)
    col = lax.broadcasted_iota(jnp.int32, (quarter, quarter), 1)
    first = pl.multiple_of(me * quarter, quarter)
    for s in range(slots):
        far = (far0, far1)[s]
        for d, block in enumerate((g0.at[s], g3.at[s], far.at[0], g1.at[s])):
            r = lax.rem(me + d, reps)
            for p in range(reps * reps):
                target = pl.multiple_of((p * reps + r) * piece, piece)
                for i in range(reps):
                    whole[pl.ds(target, piece), i * quarter : (i + 1) * quarter] = block[
                        i, p * piece : (p + 1) * piece, :
                    ]
        mine = whole[pl.ds(first, quarter), :]
        for n in range(reps):
            cols = slice(n * quarter, (n + 1) * quarter)
            gram = dot(mine, whole[cols, :], (1, 1))
            total = keep * (DECAY * left[s, :, cols] + (1.0 - DECAY) * gram)
            on = col + n * quarter == row + first
            left_new[s, :, cols] = total + jnp.where(on, adds[0, s, :1, :1], 0.0)
        mine = whole[:, pl.ds(first, quarter)]
        for n in range(reps):
            cols = slice(n * quarter, (n + 1) * quarter)
            gram = dot(mine, whole[:, cols], (0, 0))
            total = keep * (DECAY * right[s, :, cols] + (1.0 - DECAY) * gram)
            on = (col + n * quarter == row + first) & (row + first < meta[1 + s])
            right_new[s, :, cols] = total + jnp.where(on, adds[1, s, :1, :1], 0.0)


def on_device(grad_parts, col_widths, assignment, left_stat, right_stat, left_root, right_root):
    workers = lax.axis_size("fsdp")
    reps = lax.axis_size("replica")
    me_rep = lax.axis_index("replica")
    me_work = lax.axis_index("fsdp")
    slots, quarter, block_size = left_stat.shape
    rows_dev = grad_parts.shape[1]
    ncols = grad_parts.shape[2]
    per_row = block_size // rows_dev
    groups = workers // per_row
    piece = rows_dev // groups
    me_group = me_work // per_row

    def turn_x(value, shift):
        pairs = [(a, (a + shift) % reps) for a in range(reps)]
        return lax.ppermute(value, "replica", pairs)

    def turn_group(value, shift):
        pairs = [(a, (a + shift * per_row) % workers) for a in range(workers)]
        return lax.ppermute(value, "fsdp", pairs)

    slot_ids, filled, block_ids = slot_tables(assignment, workers, slots)
    col_index = jnp.arange(block_size, dtype=jnp.int32)
    col_mask = (col_index[None, :] < col_widths[:, None]).astype(F32)
    terms = (grad_parts[0].astype(F32) * col_mask[None]).astype(BF16)
    terms = jnp.transpose(terms, (1, 0, 2))

    def rows_of(rep):
        return lax.dynamic_slice_in_dim(terms, rep * piece, piece, 1)

    def add(a, b):
        return (a.astype(F32) + b.astype(F32)).astype(BF16)

    half = ncols // 2
    up, down = rows_of((me_rep + 1) % reps), rows_of((me_rep + 3) % reps)
    far = rows_of((me_rep + 2) % reps)
    relay_up = turn_x(far[:half], 1)
    relay_down = turn_x(far[half:], 3)
    direct_up = turn_x(up[half:], 1)
    direct_down = turn_x(down[:half], 3)
    joint_up = turn_x(add(up[:half], relay_up), 1)
    joint_down = turn_x(add(down[half:], relay_down), 3)
    own = rows_of(me_rep).astype(F32)
    summed = jnp.concatenate(
        [
            own[:half] + joint_up.astype(F32) + direct_down.astype(F32),
            own[half:] + direct_up.astype(F32) + joint_down.astype(F32),
        ]
    ).astype(BF16)
    roots = jnp.concatenate([right_root[:1], left_root[:1], right_root[1:], left_root[1:]])
    summed, roots = lax.optimization_barrier((summed, roots))

    my_blocks = lax.dynamic_slice_in_dim(block_ids, me_work * slots, slots)
    my_filled = lax.dynamic_slice_in_dim(filled, me_work * slots, slots)
    my_col = my_blocks % ncols
    looked_up = jnp.sum(
        jnp.where(
            my_col[:, None] == jnp.arange(ncols, dtype=jnp.int32)[None, :], col_widths[None, :], 0
        ),
        axis=1,
    )
    my_width = jnp.where(my_filled, looked_up, block_size)
    meta = jnp.concatenate([me_rep[None], my_width, my_filled]).astype(jnp.int32)
    global_rows = me_rep * quarter + jnp.arange(quarter, dtype=jnp.int32)
    unit_rows = (col_index[None, :] == global_rows[:, None]).astype(F32)
    within_width = (global_rows[None, :] < my_width[:, None]).astype(F32)
    left_diag = jnp.sum(left_stat * unit_rows[None], axis=(1, 2))
    right_diag = jnp.sum(jnp.sum(right_stat * unit_rows[None], axis=2) * within_width, axis=1)
    diag_own = jnp.stack([left_diag, right_diag])

    params = pltpu.CompilerParams(vmem_limit_bytes=VMEM_LIMIT)
    vmem = pl.BlockSpec(memory_space=pltpu.VMEM)

    def relay(before, behind):
        shape = (before.shape[0] // 2,) + before.shape[1:]
        up, down = pl.pallas_call(
            relay_kernel,
            in_specs=[vmem] * 2,
            out_shape=[jax.ShapeDtypeStruct(shape, BF16)] * 2,
            compiler_params=params,
            cost_estimate=pl.CostEstimate(flops=RELAY_COST, bytes_accessed=0, transcendentals=0),
            name="relay",
        )(before, behind)
        return (turn_x(up, 1), turn_x(down, 3))

    roots_prev, roots_next = turn_x(roots, 1), turn_x(roots, 3)
    roots_far = relay(roots_prev, roots_next)

    def columns_of(group):
        return lax.dynamic_slice_in_dim(summed, group * quarter, quarter, 2)

    held = [columns_of(me_group)]
    for shift in range(1, groups):
        held.append(turn_group(columns_of((me_group + shift) % groups), shift))
    place = ((me_group - block_ids // ncols) % groups) * ncols + block_ids % ncols
    outgoing = pl.pallas_call(
        spread_kernel,
        in_specs=[SMEM_SPEC] + [vmem] * groups,
        out_shape=jax.ShapeDtypeStruct((workers, slots, piece, quarter), BF16),
        scratch_shapes=[pltpu.VMEM((groups * ncols, piece, quarter), BF16)],
        compiler_params=params,
        name="spread",
    )(place.astype(jnp.int32), *held)
    incoming = lax.all_to_all(outgoing, "fsdp", split_axis=0, concat_axis=0, tiled=True)

    quarters = jax.ShapeDtypeStruct((slots, quarter, quarter), BF16)
    g_mine, g_sums, *products = pl.pallas_call(
        product_kernel,
        in_specs=[SMEM_SPEC] + [vmem] * 6,
        out_shape=[
            jax.ShapeDtypeStruct((slots, groups, quarter, quarter), BF16),
            jax.ShapeDtypeStruct((slots, 8, 128), F32),
        ]
        + [quarters] * reps,
        compiler_params=params,
        name="right_products",
    )(meta, incoming, roots, roots_prev, *roots_far, roots_next)
    products = [products[0]] + [turn_x(products[n], reps - n) for n in range(1, reps)]
    precond, sums = pl.pallas_call(
        root_kernel,
        in_specs=[SMEM_SPEC] * 2 + [vmem] * 10,
        out_shape=[
            jax.ShapeDtypeStruct((slots, block_size, quarter), F32),
            jax.ShapeDtypeStruct((slots, 4, 8, 128), F32),
        ],
        scratch_shapes=[pltpu.VMEM((block_size, quarter), BF16)],
        compiler_params=params,
        name="left_products",
    )(meta, diag_own, g_sums, *products, roots, roots_prev, *roots_far, roots_next)
    all_sums = [sums] + [turn_x(sums, shift) for shift in (1, 2, 3)]
    all_sums = lax.optimization_barrier((*all_sums, g_mine))
    g_mine = all_sums[reps]
    returning, adds = pl.pallas_call(
        lambda *refs: scale_kernel(groups, per_row, *refs),
        in_specs=[SMEM_SPEC] + [vmem] * 5,
        out_shape=[
            jax.ShapeDtypeStruct((workers, slots, piece, quarter), BF16),
            jax.ShapeDtypeStruct((2, slots, 8, 128), F32),
        ],
        compiler_params=params,
        name="graft_scale",
    )(meta, precond, *all_sums[:reps])
    arrived = lax.all_to_all(returning, "fsdp", split_axis=0, concat_axis=0, tiled=True)
    arrived = arrived.reshape(workers * slots, piece, quarter)

    g_prev = turn_x(g_mine, 1)
    g_next = turn_x(g_mine, reps - 1)
    g_far = relay(g_prev, g_next)
    left_new, right_new = pl.pallas_call(
        stat_kernel,
        in_specs=[SMEM_SPEC] + [vmem] * 8,
        out_shape=[jax.ShapeDtypeStruct(left_stat.shape, F32)] * 2,
        scratch_shapes=[pltpu.VMEM((block_size, block_size), BF16)],
        compiler_params=params,
        cost_estimate=pl.CostEstimate(
            flops=8 * block_size * block_size * quarter,
            bytes_accessed=40 * block_size * quarter * 2,
            transcendentals=0,
        ),
        name="stat_update",
    )(meta, adds, g_mine, g_prev, g_next, *g_far, left_stat, right_stat)
    arrived, left_new, right_new = lax.optimization_barrier((arrived, left_new, right_new))

    block = jnp.arange(groups * ncols, dtype=jnp.int32)
    wanted = jnp.take(slot_ids, (block + me_group * ncols) % (groups * ncols), mode="clip")
    back = pl.pallas_call(
        collect_kernel,
        in_specs=[SMEM_SPEC, pl.BlockSpec(memory_space=pltpu.VMEM)],
        out_shape=[jax.ShapeDtypeStruct((ncols, piece, quarter), BF16)] * groups,
        compiler_params=params,
        name="collect",
    )(wanted, arrived)
    back = [back[0]] + [turn_group(back[shift], shift) for shift in range(1, groups)]
    back = jnp.stack(back)
    order = (me_group - jnp.arange(groups, dtype=jnp.int32)) % groups
    back = jnp.take(back, order, axis=0, mode="clip")
    update = jnp.transpose(back, (0, 2, 1, 3)).reshape(rows_dev, ncols, quarter)
    return (update, left_new, right_new)


def solution(mesh):
    in_specs = (
        P("replica", "fsdp", None, None),
        P(),
        P(),
        P("fsdp", "replica", None),
        P("fsdp", "replica", None),
        P("fsdp", None, "replica"),
        P("fsdp", None, "replica"),
    )
    out_specs = (P("fsdp", None, "replica"), P("fsdp", "replica", None), P("fsdp", "replica", None))
    return jax.shard_map(
        on_device, mesh=mesh, in_specs=in_specs, out_specs=out_specs, check_vma=False
    )
```

time: 214 us -> 192 us (0.90)
  waiting for transfers between devices: 107 us -> 78.5 us
  Pallas kernels: 15.6 us -> 26.3 us
  local copies, waits for them, and re-layouts: 11.4 us -> 4.03 us
  starting transfers between devices: 71 us -> 75.2 us
    ppermute x20, waiting for transfers between devices: 81.4 us -> 54.9 us  [turn_x(): return lax.ppermute(value, 'replica', pairs)]
    pallas_call x4 -> x7, Pallas kernels: 14.3 us -> 25.7 us  [the longest x1 7.1 us: on_device(): pl.pallas_call(stat_kernel, in_specs=[SMEM_SPEC] + [vmem] * 8, out_shape=...]
    all_to_all x1, waiting for transfers between devices: 11.4 us -> 4.49 us  [on_device(): lax.all_to_all(returning, 'fsdp', split_axis=0, concat_axis=0, tiled=True)]
    all_to_all x1, starting transfers between devices: 14.7 us -> 20.3 us  [on_device(): lax.all_to_all(returning, 'fsdp', split_axis=0, concat_axis=0, tiled=True)]
    all_to_all x1, waiting for transfers between devices: 0.01 us -> 4.66 us  [on_device(): lax.all_to_all(outgoing, 'fsdp', split_axis=0, concat_axis=0, tiled=True)]
    unnamed x24 -> x18, local copies, waits for them, and re-layouts: 6.24 us -> 1.63 us
    slice x4 -> x1, local copies, waits for them, and re-layouts: 2.76 us -> 0.14 us  [on_device(): right_root[:1]]
  transfers between devices with their start and end apart: 28 -> 28, of which waited for: 20 -> 21; matrix products, arithmetic and copies ran while one was open for 4% -> 2% of each run, Pallas kernels for 3% -> 9%
where the time goes in v4:
time: 192 us; the launch traced here: 191 us
  waiting for transfers between devices  78.5 us (41%)
  starting transfers between devices  75.2 us (39%)
  Pallas kernels  26.3 us (14%)
  other arithmetic  6.25 us (3%)
  local copies, waits for them, and re-layouts  4.03 us (2%)
    ppermute x20, waiting for transfers between devices, turn_x(): return lax.ppermute(value, 'replica', pairs)  54.9 us
    ppermute x20, starting transfers between devices, turn_x(): return lax.ppermute(value, 'replica', pairs)  25.2 us
    all_to_all x1, starting transfers between devices, on_device(): lax.all_to_all(returning, 'fsdp', split_axis=0, concat_axis=0, tiled=True)  20.3 us
    ppermute x6, starting transfers between devices, turn_group(): return lax.ppermute(value, 'fsdp', pairs)  16.2 us
    ppermute x6, waiting for transfers between devices, turn_group(): return lax.ppermute(value, 'fsdp', pairs)  14.4 us
    all_to_all x1, starting transfers between devices, on_device(): lax.all_to_all(outgoing, 'fsdp', split_axis=0, concat_axis=0, tiled=True)  13.4 us
    pallas_call x1, Pallas kernels, on_device(): pl.pallas_call(stat_kernel, in_specs=[SMEM_SPEC] + [vmem] * 8, out_shape=...  7.1 us
    pallas_call x2, Pallas kernels, relay(): pl.pallas_call(relay_kernel, in_specs=[vmem] * 2, out_shape=[jax.ShapeDty...  6.41 us
  transfers between devices with their start and end apart: 28, of which 21 were waited for; matrix products, arithmetic and copies ran while one was open for 2% of the time, Pallas kernels for 9%

profile of v4, /device:TPU:1, one launch (start us, length us, event | category | flops | bytes accessed | tf_op | source)
XLA Modules:
  0.0 191.1 jit_solution(8034016094483275104)
XLA Ops:
  1.4 1.8 fusion
  3.5 3.4 %collective-permute-start.4 = (bf16[6,16,1024]{2,1,0:T(8,128)(2,1)S(1)}, bf16[6,16,1024]{2,1,0:T(8,128)(2,1)S(1)}, u32[]{:S(2)}, u32[]{:S(2)}) collective-permute-start(bf16[6,16,1024]{2,1,0:T(8,128)(2,1)S(1)} %get-tuple-element.82), channel_id=1, source_target_pairs={{0,192},{64,0},{128,64},{192,128},{1,193},{65,1},{129,65},{193,129... | collective-permute-start | bytes 589832 | tf_op jit(solution)/shard_map/ppermute | solution.py:185
  6.9 2.8 %collective-permute-start.2 = (bf16[6,16,1024]{2,1,0:T(8,128)(2,1)S(1)}, bf16[6,16,1024]{2,1,0:T(8,128)(2,1)S(1)}, u32[]{:S(2)}, u32[]{:S(2)}) collective-permute-start(bf16[6,16,1024]{2,1,0:T(8,128)(2,1)S(1)} %slice.55), channel_id=1, source_target_pairs={{0,192},{64,0},{128,64},{192,128},{1,193},{65,1},{129,65},{193,129... | collective-permute-start | bytes 589832 | tf_op jit(solution)/shard_map/ppermute | solution.py:185
  10.5 3.5 %collective-permute-start.5 = (bf16[6,16,1024]{2,1,0:T(8,128)(2,1)S(1)}, bf16[6,16,1024]{2,1,0:T(8,128)(2,1)S(1)}, u32[]{:S(2)}, u32[]{:S(2)}) collective-permute-start(bf16[6,16,1024]{2,1,0:T(8,128)(2,1)S(1)} %add_convert_fusion), channel_id=1, source_target_pairs={{0,192},{64,0},{128,64},{192,128},{1,193},{65,1},{129,65},{193,129... | collective-permute-start | bytes 589832 | tf_op jit(solution)/shard_map/ppermute | solution.py:185
  14.7 3.3 %collective-permute-done.3 = bf16[6,16,1024]{2,1,0:T(8,128)(2,1)S(1)} collective-permute-done((bf16[6,16,1024]{2,1,0:T(8,128)(2,1)S(1)}, bf16[6,16,1024]{2,1,0:T(8,128)(2,1)S(1)}, u32[]{:S(2)}, u32[]{:S(2)}) %collective-permute-start.3) | collective-permute-done | bytes 196640 | tf_op jit(solution)/shard_map/ppermute | solution.py:185
  18.0 3.1 %collective-permute-done.1 = bf16[6,16,1024]{2,1,0:T(8,128)(2,1)S(1)} collective-permute-done((bf16[6,16,1024]{2,1,0:T(8,128)(2,1)S(1)}, bf16[6,16,1024]{2,1,0:T(8,128)(2,1)S(1)}, u32[]{:S(2)}, u32[]{:S(2)}) %collective-permute-start.1) | collective-permute-done | bytes 196640 | tf_op jit(solution)/shard_map/ppermute | solution.py:185
  23.2 3.1 %collective-permute-start.6 = (bf16[12,16,256]{2,1,0:T(8,128)(2,1)S(1)}, bf16[12,16,256]{2,1,0:T(8,128)(2,1)S(1)}, u32[]{:S(2)}, u32[]{:S(2)}) collective-permute-start(bf16[12,16,256]{2,1,0:T(8,128)(2,1)S(1)} %get-tuple-element.79), channel_id=1, source_target_pairs={{0,16},{1,17},{2,18},{3,19},{4,20},{5,21},{6,22},{7,23},{8,24},{9,... | collective-permute-start | bytes 294920 | tf_op jit(solution)/shard_map/ppermute | solution.py:189
  26.3 5.1 %collective-permute-start.7 = (bf16[12,16,256]{2,1,0:T(8,128)(2,1)S(1)}, bf16[12,16,256]{2,1,0:T(8,128)(2,1)S(1)}, u32[]{:S(2)}, u32[]{:S(2)}) collective-permute-start(bf16[12,16,256]{2,1,0:T(8,128)(2,1)S(1)} %get-tuple-element.78), channel_id=1, source_target_pairs={{0,32},{1,33},{2,34},{3,35},{4,36},{5,37},{6,38},{7,39},{8,40},{9,... | collective-permute-start | bytes 294920 | tf_op jit(solution)/shard_map/ppermute | solution.py:189
  31.4 2.4 %collective-permute-start.8 = (bf16[12,16,256]{2,1,0:T(8,128)(2,1)S(1)}, bf16[12,16,256]{2,1,0:T(8,128)(2,1)S(1)}, u32[]{:S(2)}, u32[]{:S(2)}) collective-permute-start(bf16[12,16,256]{2,1,0:T(8,128)(2,1)S(1)} %get-tuple-element.77), channel_id=1, source_target_pairs={{0,48},{1,49},{2,50},{3,51},{4,52},{5,53},{6,54},{7,55},{8,56},{9,... | collective-permute-start | bytes 294920 | tf_op jit(solution)/shard_map/ppermute | solution.py:189
  35.1 2.3 %collective-permute-done.8.h3 = bf16[12,16,256]{2,1,0:T(8,128)(2,1)S(1)} collective-permute-done((bf16[12,16,256]{2,1,0:T(8,128)(2,1)S(1)}, bf16[12,16,256]{2,1,0:T(8,128)(2,1)S(1)}, u32[]{:S(2)}, u32[]{:S(2)}) %collective-permute-start.8) | collective-permute-done | bytes 98336 | tf_op jit(solution)/shard_map/ppermute | solution.py:189
  39.1 13.4 %all-to-all-start = ((bf16[64,2,16,256]{3,2,1,0:T(8,128)(2,1)}), bf16[64,2,16,256]{3,2,1,0:T(8,128)(2,1)}, u32[]{:S(2)}, u32[]{:S(2)}) async-start(bf16[64,2,16,256]{3,2,1,0:T(8,128)(2,1)} %spread.1), calls=%async_computation | async-start | bytes 2097152 | tf_op jit(solution)/shard_map/all_to_all | solution.py:273
  52.5 13.1 %collective-permute-done.10.behind.r3.l3 = bf16[4,1024,256]{2,1,0:T(8,128)(2,1)} collective-permute-done((bf16[4,1024,256]{2,1,0:T(8,128)(2,1)S(1)}, bf16[4,1024,256]{2,1,0:T(8,128)(2,1)}, u32[]{:S(2)}, u32[]{:S(2)}) %collective-permute-start.10) | collective-permute-done | bytes 2097184 | tf_op jit(solution)/shard_map/ppermute | solution.py:185
  65.6 2.1 %collective-permute-done.9.before.r1.l1 = bf16[4,1024,256]{2,1,0:T(8,128)(2,1)} collective-permute-done((bf16[4,1024,256]{2,1,0:T(8,128)(2,1)S(1)}, bf16[4,1024,256]{2,1,0:T(8,128)(2,1)}, u32[]{:S(2)}, u32[]{:S(2)}) %collective-permute-start.9) | collective-permute-done | bytes 2097184 | tf_op jit(solution)/shard_map/ppermute | solution.py:185
  67.7 3.7 %relay.2 = (bf16[2,1024,256]{2,1,0:T(8,128)(2,1)}, bf16[2,1024,256]{2,1,0:T(8,128)(2,1)}) custom-call(bf16[4,1024,256]{2,1,0:T(8,128)(2,1)} %collective-permute-done.9.before.r1.l1, bf16[4,1024,256]{2,1,0:T(8,128)(2,1)} %collective-permute-done.10.behind.r3.l3), custom_call_target="tpu_custom_call" | custom-call | flops 10000000000 | tf_op jit(solution)/shard_map/relay/pallas_call | solution.py:245
  71.4 2.7 %collective-permute-start.12 = (bf16[2,1024,256]{2,1,0:T(8,128)(2,1)}, bf16[2,1024,256]{2,1,0:T(8,128)(2,1)}, u32[]{:S(2)}, u32[]{:S(2)}) collective-permute-start(bf16[2,1024,256]{2,1,0:T(8,128)(2,1)} %get-tuple-element.36), channel_id=1, source_target_pairs={{0,192},{64,0},{128,64},{192,128},{1,193},{65,1},{129,65},{193,129... | collective-permute-start | bytes 3145736 | tf_op jit(solution)/shard_map/ppermute | solution.py:185
  75.7 4.7 %all-to-all-done.arrived = bf16[64,2,16,256]{3,2,1,0:T(8,128)(2,1)} async-done(((bf16[64,2,16,256]{3,2,1,0:T(8,128)(2,1)}), bf16[64,2,16,256]{3,2,1,0:T(8,128)(2,1)}, u32[]{:S(2)}, u32[]{:S(2)}) %all-to-all-start) | async-done | bytes 1048608 | tf_op jit(solution)/shard_map/all_to_all | solution.py:273
  80.4 13.6 %collective-permute-done.11.far0 = bf16[2,1024,256]{2,1,0:T(8,128)(2,1)S(1)} collective-permute-done((bf16[2,1024,256]{2,1,0:T(8,128)(2,1)}, bf16[2,1024,256]{2,1,0:T(8,128)(2,1)S(1)}, u32[]{:S(2)}, u32[]{:S(2)}) %collective-permute-start.11) | collective-permute-done | bytes 1048608 | tf_op jit(solution)/shard_map/ppermute | solution.py:185
  94.0 4.9 %right_products.1 = (bf16[2,4,256,256]{3,2,1,0:T(8,128)(2,1)}, f32[2,8,128]{2,1,0:T(8,128)S(1)}, bf16[2,256,256]{2,1,0:T(8,128)(2,1)S(1)}, bf16[2,256,256]{2,1,0...) custom-call(s32[5]{0:T(128)S(1)} %pad_add_fusion.meta.refs_0_, ...), custom_call_target="tpu_custom_call" | custom-call | tf_op jit(solution)/shard_map/right_products/pallas_call | solution.py:276
  98.9 2.5 %collective-permute-start.13 = (bf16[2,256,256]{2,1,0:T(8,128)(2,1)S(1)}, bf16[2,256,256]{2,1,0:T(8,128)(2,1)S(1)}, u32[]{:S(2)}, u32[]{:S(2)}) collective-permute-start(bf16[2,256,256]{2,1,0:T(8,128)(2,1)S(1)} %get-tuple-element.39), channel_id=1, source_target_pairs={{0,192},{64,0},{128,64},{192,128},{1,193},{65,1},{129,65},{193,129... | collective-permute-start | bytes 786440 | tf_op jit(solution)/shard_map/ppermute | solution.py:185
  102.9 4.9 %collective-permute-done.13.y1 = bf16[2,256,256]{2,1,0:T(8,128)(2,1)S(1)} collective-permute-done((bf16[2,256,256]{2,1,0:T(8,128)(2,1)S(1)}, bf16[2,256,256]{2,1,0:T(8,128)(2,1)S(1)}, u32[]{:S(2)}, u32[]{:S(2)}) %collective-permute-start.13) | collective-permute-done | bytes 262176 | tf_op jit(solution)/shard_map/ppermute | solution.py:185
  108.2 2.8 %collective-permute-done.15.y3 = bf16[2,256,256]{2,1,0:T(8,128)(2,1)S(1)} collective-permute-done((bf16[2,256,256]{2,1,0:T(8,128)(2,1)S(1)}, bf16[2,256,256]{2,1,0:T(8,128)(2,1)S(1)}, u32[]{:S(2)}, u32[]{:S(2)}) %collective-permute-start.15) | collective-permute-done | bytes 262176 | tf_op jit(solution)/shard_map/ppermute | solution.py:185
  111.0 3.9 %left_products.1 = (f32[2,1024,256]{2,1,0:T(8,128)S(1)}, f32[2,4,8,128]{3,2,1,0:T(8,128)S(1)}) custom-call(s32[5]{0:T(128)S(1)} %pad_add_fusion.meta.refs_0_, f32[2,2]{1,0:T(2,128)S(1)} %pad_maximum_fusion.3.diags, f32[2,8,128]{2,1,0:T(8,128)S(1)} %get-tuple-element.37.g_sums, bf16[2,256,256]{2,1,0:T(8,128)(2,1)S(1)} %get-tuple-element.38.y0, ...), custom_call_target="tpu_custom_call" | custom-call | tf_op jit(solution)/shard_map/left_products/pallas_call | solution.py:288
  115.0 1.8 collective-permute-start.17
  124.4 20.3 %all-to-all-start.1 = ((bf16[64,2,16,256]{3,2,1,0:T(8,128)(2,1)}), bf16[64,2,16,256]{3,2,1,0:T(8,128)(2,1)S(1)}, u32[]{:S(2)}, u32[]{:S(2)}) async-start(bf16[64,2,16,256]{3,2,1,0:T(8,128)(2,1)} %get-tuple-element.49), calls=%async_computation.1 | async-start | bytes 2097152 | tf_op jit(solution)/shard_map/all_to_all | solution.py:312
  144.7 2.7 %relay.3 = (bf16[1,4,256,256]{3,2,1,0:T(8,128)(2,1)}, bf16[1,4,256,256]{3,2,1,0:T(8,128)(2,1)}) custom-call(bf16[2,4,256,256]{3,2,1,0:T(8,128)(2,1)} %collective-permute-done.19.before.g1, bf16[2,4,256,256]{3,2,1,0:T(8,128)(2,1)} %collective-permute-done.20.behind.g3), custom_call_target="tpu_custom_call" | custom-call | flops 10000000000 | tf_op jit(solution)/shard_map/relay/pallas_call | solution.py:245
  147.4 2.7 %collective-permute-start.22 = (bf16[1,4,256,256]{3,2,1,0:T(8,128)(2,1)}, bf16[1,4,256,256]{3,2,1,0:T(8,128)(2,1)}, u32[]{:S(2)}, u32[]{:S(2)}) collective-permute-start(bf16[1,4,256,256]{3,2,1,0:T(8,128)(2,1)} %get-tuple-element.53), channel_id=1, source_target_pairs={{0,192},{64,0},{128,64},{192,128},{1,193},{65,1},{129,65},{193,129... | collective-permute-start | bytes 1572872 | tf_op jit(solution)/shard_map/ppermute | solution.py:185
  150.9 8.6 %collective-permute-done.21.far0 = bf16[1,4,256,256]{3,2,1,0:T(8,128)(2,1)} collective-permute-done((bf16[1,4,256,256]{3,2,1,0:T(8,128)(2,1)}, bf16[1,4,256,256]{3,2,1,0:T(8,128)(2,1)}, u32[]{:S(2)}, u32[]{:S(2)}) %collective-permute-start.21) | collective-permute-done | bytes 524320 | tf_op jit(solution)/shard_map/ppermute | solution.py:185
  161.1 7.1 %stat_update.1 = (f32[2,256,1024]{2,1,0:T(8,128)}, f32[2,256,1024]{2,1,0:T(8,128)}) custom-call(s32[5]{0:T(128)S(1)} %pad_add_fusion.meta.refs_0_, f32[2,2,8,128]{3,2,1,0:T(8,128)S(1)} %get-tuple-element.50.adds, bf16[2,4,256,256]{3,2,1,0:T(8,128)(2,1)} %get-tuple-element.51.g0, bf16[2,4,256,256]{3,2,1,0:T(8,128)(2,1)} %collective-permute-done.19.before.g1, ...), custom_call_target="tpu_custom_call" | custom-call | flops 2147483648 | bytes 20971520 | tf_op jit(solution)/shard_map/stat_update/pallas_call | solution.py:318
  168.2 4.5 %all-to-all-done.1 = bf16[64,2,16,256]{3,2,1,0:T(8,128)(2,1)S(1)} async-done(((bf16[64,2,16,256]{3,2,1,0:T(8,128)(2,1)}), bf16[64,2,16,256]{3,2,1,0:T(8,128)(2,1)S(1)}, u32[]{:S(2)}, u32[]{:S(2)}) %all-to-all-start.1) | async-done | bytes 1048608 | tf_op jit(solution)/shard_map/all_to_all | solution.py:312
  174.4 4.1 %collective-permute-start.24 = (bf16[12,16,256]{2,1,0:T(8,128)(2,1)S(1)}, bf16[12,16,256]{2,1,0:T(8,128)(2,1)S(1)}, u32[]{:S(2)}, u32[]{:S(2)}) collective-permute-start(bf16[12,16,256]{2,1,0:T(8,128)(2,1)S(1)} %get-tuple-element.59), channel_id=1, source_target_pairs={{0,32},{1,33},{2,34},{3,35},{4,36},{5,37},{6,38},{7,39},{8,40},{9,... | collective-permute-start | bytes 294920 | tf_op jit(solution)/shard_map/ppermute | solution.py:189
  180.7 6.8 %collective-permute-done.24 = bf16[12,16,256]{2,1,0:T(8,128)(2,1)S(1)} collective-permute-done((bf16[12,16,256]{2,1,0:T(8,128)(2,1)S(1)}, bf16[12,16,256]{2,1,0:T(8,128)(2,1)S(1)}, u32[]{:S(2)}, u32[]{:S(2)}) %collective-permute-start.24) | collective-permute-done | bytes 98336 | tf_op jit(solution)/shard_map/ppermute | solution.py:189
  187.6 2.2 %collective-permute-done.25 = bf16[12,16,256]{2,1,0:T(8,128)(2,1)S(1)} collective-permute-done((bf16[12,16,256]{2,1,0:T(8,128)(2,1)S(1)}, bf16[12,16,256]{2,1,0:T(8,128)(2,1)S(1)}, u32[]{:S(2)}, u32[]{:S(2)}) %collective-permute-start.25) | collective-permute-done | bytes 98336 | tf_op jit(solution)/shard_map/ppermute | solution.py:189
  (86 shorter events, 26.5 us)
Async XLA Ops:
  3.5 7.0 %collective-permute-start.4 = (bf16[6,16,1024]{2,1,0:T(8,128)(2,1)S(1)}, bf16[6,16,1024]{2,1,0:T(8,128)(2,1)S(1)}, u32[]{:S(2)}, u32[]{:S(2)}) collective-permute-start(bf16[6,16,1024]{2,1,0:T(8,128)(2,1)S(1)} %get-tuple-element.82), channel_id=1, source_target_pairs={{0,192},{64,0},{128,64},{192,128},{1,193},{65,1},{129,65},{193,129... | collective-permute-start | bytes 589832 | tf_op jit(solution)/shard_map/ppermute | solution.py:185
  6.9 7.1 %collective-permute-start = (bf16[6,16,1024]{2,1,0:T(8,128)(2,1)S(1)}, bf16[6,16,1024]{2,1,0:T(8,128)(2,1)S(1)}, u32[]{:S(2)}, u32[]{:S(2)}) collective-permute-start(bf16[6,16,1024]{2,1,0:T(8,128)(2,1)S(1)} %get-tuple-element.81), channel_id=1, source_target_pairs={{0,64},{64,128},{128,192},{192,0},{1,65},{65,129},{129,193},{193,1... | collective-permute-start | bytes 589832 | tf_op jit(solution)/shard_map/ppermute | solution.py:185
  6.9 7.8 %collective-permute-start.2 = (bf16[6,16,1024]{2,1,0:T(8,128)(2,1)S(1)}, bf16[6,16,1024]{2,1,0:T(8,128)(2,1)S(1)}, u32[]{:S(2)}, u32[]{:S(2)}) collective-permute-start(bf16[6,16,1024]{2,1,0:T(8,128)(2,1)S(1)} %slice.55), channel_id=1, source_target_pairs={{0,192},{64,0},{128,64},{192,128},{1,193},{65,1},{129,65},{193,129... | collective-permute-start | bytes 589832 | tf_op jit(solution)/shard_map/ppermute | solution.py:185
  9.7 8.3 %collective-permute-start.3 = (bf16[6,16,1024]{2,1,0:T(8,128)(2,1)S(1)}, bf16[6,16,1024]{2,1,0:T(8,128)(2,1)S(1)}, u32[]{:S(2)}, u32[]{:S(2)}) collective-permute-start(bf16[6,16,1024]{2,1,0:T(8,128)(2,1)S(1)} %slice.57), channel_id=1, source_target_pairs={{0,64},{64,128},{128,192},{192,0},{1,65},{65,129},{129,193},{193,1... | collective-permute-start | bytes 589832 | tf_op jit(solution)/shard_map/ppermute | solution.py:185
  10.5 7.4 %collective-permute-start.5 = (bf16[6,16,1024]{2,1,0:T(8,128)(2,1)S(1)}, bf16[6,16,1024]{2,1,0:T(8,128)(2,1)S(1)}, u32[]{:S(2)}, u32[]{:S(2)}) collective-permute-start(bf16[6,16,1024]{2,1,0:T(8,128)(2,1)S(1)} %add_convert_fusion), channel_id=1, source_target_pairs={{0,192},{64,0},{128,64},{192,128},{1,193},{65,1},{129,65},{193,129... | collective-permute-start | bytes 589832 | tf_op jit(solution)/shard_map/ppermute | solution.py:185
  14.1 7.0 %collective-permute-start.1 = (bf16[6,16,1024]{2,1,0:T(8,128)(2,1)S(1)}, bf16[6,16,1024]{2,1,0:T(8,128)(2,1)S(1)}, u32[]{:S(2)}, u32[]{:S(2)}) collective-permute-start(bf16[6,16,1024]{2,1,0:T(8,128)(2,1)S(1)} %add_convert_fusion.1), channel_id=1, source_target_pairs={{0,64},{64,128},{128,192},{192,0},{1,65},{65,129},{129,193},{193,1... | collective-permute-start | bytes 589832 | tf_op jit(solution)/shard_map/ppermute | solution.py:185
  21.3 44.4 %collective-permute-start.10 = (bf16[4,1024,256]{2,1,0:T(8,128)(2,1)S(1)}, bf16[4,1024,256]{2,1,0:T(8,128)(2,1)}, u32[]{:S(2)}, u32[]{:S(2)}) collective-permute-start(bf16[4,1024,256]{2,1,0:T(8,128)(2,1)S(1)} %pad_maximum_fusion.r0.l0), channel_id=1, source_target_pairs={{0,192},{64,0},{128,64},{192,128},{1,193},{65,1},{129,65},{193,129... | collective-permute-start | bytes 6291464 | tf_op jit(solution)/shard_map/ppermute | solution.py:185
  21.9 45.9 %collective-permute-start.9 = (bf16[4,1024,256]{2,1,0:T(8,128)(2,1)S(1)}, bf16[4,1024,256]{2,1,0:T(8,128)(2,1)}, u32[]{:S(2)}, u32[]{:S(2)}) collective-permute-start(bf16[4,1024,256]{2,1,0:T(8,128)(2,1)S(1)} %pad_maximum_fusion.r0.l0), channel_id=1, source_target_pairs={{0,64},{64,128},{128,192},{192,0},{1,65},{65,129},{129,193},{193,1... | collective-permute-start | bytes 6291464 | tf_op jit(solution)/shard_map/ppermute | solution.py:185
  23.2 10.6 %collective-permute-start.6 = (bf16[12,16,256]{2,1,0:T(8,128)(2,1)S(1)}, bf16[12,16,256]{2,1,0:T(8,128)(2,1)S(1)}, u32[]{:S(2)}, u32[]{:S(2)}) collective-permute-start(bf16[12,16,256]{2,1,0:T(8,128)(2,1)S(1)} %get-tuple-element.79), channel_id=1, source_target_pairs={{0,16},{1,17},{2,18},{3,19},{4,20},{5,21},{6,22},{7,23},{8,24},{9,... | collective-permute-start | bytes 294920 | tf_op jit(solution)/shard_map/ppermute | solution.py:189
  26.3 8.9 %collective-permute-start.7 = (bf16[12,16,256]{2,1,0:T(8,128)(2,1)S(1)}, bf16[12,16,256]{2,1,0:T(8,128)(2,1)S(1)}, u32[]{:S(2)}, u32[]{:S(2)}) collective-permute-start(bf16[12,16,256]{2,1,0:T(8,128)(2,1)S(1)} %get-tuple-element.78), channel_id=1, source_target_pairs={{0,32},{1,33},{2,34},{3,35},{4,36},{5,37},{6,38},{7,39},{8,40},{9,... | collective-permute-start | bytes 294920 | tf_op jit(solution)/shard_map/ppermute | solution.py:189
  31.4 6.1 %collective-permute-start.8 = (bf16[12,16,256]{2,1,0:T(8,128)(2,1)S(1)}, bf16[12,16,256]{2,1,0:T(8,128)(2,1)S(1)}, u32[]{:S(2)}, u32[]{:S(2)}) collective-permute-start(bf16[12,16,256]{2,1,0:T(8,128)(2,1)S(1)} %get-tuple-element.77), channel_id=1, source_target_pairs={{0,48},{1,49},{2,50},{3,51},{4,52},{5,53},{6,54},{7,55},{8,56},{9,... | collective-permute-start | bytes 294920 | tf_op jit(solution)/shard_map/ppermute | solution.py:189
  39.1 41.3 %all-to-all-start = ((bf16[64,2,16,256]{3,2,1,0:T(8,128)(2,1)}), bf16[64,2,16,256]{3,2,1,0:T(8,128)(2,1)}, u32[]{:S(2)}, u32[]{:S(2)}) async-start(bf16[64,2,16,256]{3,2,1,0:T(8,128)(2,1)} %spread.1), calls=%async_computation | async-start | bytes 2097152 | tf_op jit(solution)/shard_map/all_to_all | solution.py:273
  52.5 21.8 %copy-start.7 = (s32[12]{0:T(128)S(1)}, s32[12]{0:T(128)}, u32[]{:S(2)}) copy-start(s32[12]{0:T(128)} %param.8) | copy-start | bytes 148
  71.4 22.6 %collective-permute-start.11 = (bf16[2,1024,256]{2,1,0:T(8,128)(2,1)}, bf16[2,1024,256]{2,1,0:T(8,128)(2,1)S(1)}, u32[]{:S(2)}, u32[]{:S(2)}) collective-permute-start(bf16[2,1024,256]{2,1,0:T(8,128)(2,1)} %get-tuple-element.35), channel_id=1, source_target_pairs={{0,64},{64,128},{128,192},{192,0},{1,65},{65,129},{129,193},{193,1... | collective-permute-start | bytes 3145736 | tf_op jit(solution)/shard_map/ppermute | solution.py:185
  71.4 22.6 %collective-permute-start.12 = (bf16[2,1024,256]{2,1,0:T(8,128)(2,1)}, bf16[2,1024,256]{2,1,0:T(8,128)(2,1)}, u32[]{:S(2)}, u32[]{:S(2)}) collective-permute-start(bf16[2,1024,256]{2,1,0:T(8,128)(2,1)} %get-tuple-element.36), channel_id=1, source_target_pairs={{0,192},{64,0},{128,64},{192,128},{1,193},{65,1},{129,65},{193,129... | collective-permute-start | bytes 3145736 | tf_op jit(solution)/shard_map/ppermute | solution.py:185
  80.4 21.6 %copy-start = (f32[2,256,1024]{2,1,0:T(8,128)S(1)}, f32[2,256,1024]{2,1,0:T(8,128)}, u32[]{:S(2)}) copy-start(f32[2,256,1024]{2,1,0:T(8,128)} %left.1) | copy-start | bytes 6291460
  80.4 21.6 %copy-start.2 = (f32[2,256,1024]{2,1,0:T(8,128)S(1)}, f32[2,256,1024]{2,1,0:T(8,128)}, u32[]{:S(2)}) copy-start(f32[2,256,1024]{2,1,0:T(8,128)} %right.1) | copy-start | bytes 6291460
  80.4 21.6 %copy-start.4 = (f32[256,1024]{1,0:T(8,128)S(1)}, f32[256,1024]{1,0:T(8,128)}, u32[]{:S(2)}) copy-start(f32[256,1024]{1,0:T(8,128)} %fusion.1) | copy-start | bytes 3145732
  98.9 8.9 %collective-permute-start.13 = (bf16[2,256,256]{2,1,0:T(8,128)(2,1)S(1)}, bf16[2,256,256]{2,1,0:T(8,128)(2,1)S(1)}, u32[]{:S(2)}, u32[]{:S(2)}) collective-permute-start(bf16[2,256,256]{2,1,0:T(8,128)(2,1)S(1)} %get-tuple-element.39), channel_id=1, source_target_pairs={{0,192},{64,0},{128,64},{192,128},{1,193},{65,1},{129,65},{193,129... | collective-permute-start | bytes 786440 | tf_op jit(solution)/shard_map/ppermute | solution.py:185
  101.4 6.8 %collective-permute-start.14 = (bf16[2,256,256]{2,1,0:T(8,128)(2,1)S(1)}, bf16[2,256,256]{2,1,0:T(8,128)(2,1)S(1)}, u32[]{:S(2)}, u32[]{:S(2)}) collective-permute-start(bf16[2,256,256]{2,1,0:T(8,128)(2,1)S(1)} %get-tuple-element.40), channel_id=1, source_target_pairs={{0,128},{64,192},{128,0},{192,64},{1,129},{65,193},{129,1},{193,65... | collective-permute-start | bytes 786440 | tf_op jit(solution)/shard_map/ppermute | solution.py:185
  101.4 9.6 %collective-permute-start.15 = (bf16[2,256,256]{2,1,0:T(8,128)(2,1)S(1)}, bf16[2,256,256]{2,1,0:T(8,128)(2,1)S(1)}, u32[]{:S(2)}, u32[]{:S(2)}) collective-permute-start(bf16[2,256,256]{2,1,0:T(8,128)(2,1)S(1)} %get-tuple-element.41), channel_id=1, source_target_pairs={{0,64},{64,128},{128,192},{192,0},{1,65},{65,129},{129,193},{193,1... | collective-permute-start | bytes 786440 | tf_op jit(solution)/shard_map/ppermute | solution.py:185
  114.9 4.1 %collective-permute-start.16 = (f32[2,4,8,128]{3,2,1,0:T(8,128)S(1)}, f32[2,4,8,128]{3,2,1,0:T(8,128)S(1)}, u32[]{:S(2)}, u32[]{:S(2)}) collective-permute-start(f32[2,4,8,128]{3,2,1,0:T(8,128)S(1)} %get-tuple-element.45.refs_2_), channel_id=1, source_target_pairs={{0,64},{64,128},{128,192},{192,0},{1,65},{65,129},{129,193},{193,1... | collective-permute-start | bytes 98312 | tf_op jit(solution)/shard_map/ppermute | solution.py:185
  115.0 4.4 %collective-permute-start.17 = (f32[2,4,8,128]{3,2,1,0:T(8,128)S(1)}, f32[2,4,8,128]{3,2,1,0:T(8,128)S(1)}, u32[]{:S(2)}, u32[]{:S(2)}) collective-permute-start(f32[2,4,8,128]{3,2,1,0:T(8,128)S(1)} %get-tuple-element.45.refs_2_), channel_id=1, source_target_pairs={{0,128},{64,192},{128,0},{192,64},{1,129},{65,193},{129,1},{193,65... | collective-permute-start | bytes 98312 | tf_op jit(solution)/shard_map/ppermute | solution.py:185
  116.9 3.1 %collective-permute-start.18 = (f32[2,4,8,128]{3,2,1,0:T(8,128)S(1)}, f32[2,4,8,128]{3,2,1,0:T(8,128)S(1)}, u32[]{:S(2)}, u32[]{:S(2)}) collective-permute-start(f32[2,4,8,128]{3,2,1,0:T(8,128)S(1)} %get-tuple-element.45.refs_2_), channel_id=1, source_target_pairs={{0,192},{64,0},{128,64},{192,128},{1,193},{65,1},{129,65},{193,129... | collective-permute-start | bytes 98312 | tf_op jit(solution)/shard_map/ppermute | solution.py:185
  119.9 24.8 %collective-permute-start.19 = (bf16[2,4,256,256]{3,2,1,0:T(8,128)(2,1)}, bf16[2,4,256,256]{3,2,1,0:T(8,128)(2,1)}, u32[]{:S(2)}, u32[]{:S(2)}) collective-permute-start(bf16[2,4,256,256]{3,2,1,0:T(8,128)(2,1)} %get-tuple-element.51.g0), channel_id=1, source_target_pairs={{0,64},{64,128},{128,192},{192,0},{1,65},{65,129},{129,193},{193,1... | collective-permute-start | bytes 3145736 | tf_op jit(solution)/shard_map/ppermute | solution.py:185
  121.0 23.7 %collective-permute-start.20 = (bf16[2,4,256,256]{3,2,1,0:T(8,128)(2,1)}, bf16[2,4,256,256]{3,2,1,0:T(8,128)(2,1)}, u32[]{:S(2)}, u32[]{:S(2)}) collective-permute-start(bf16[2,4,256,256]{3,2,1,0:T(8,128)(2,1)} %get-tuple-element.51.g0), channel_id=1, source_target_pairs={{0,192},{64,0},{128,64},{192,128},{1,193},{65,1},{129,65},{193,129... | collective-permute-start | bytes 3145736 | tf_op jit(solution)/shard_map/ppermute | solution.py:185
  124.4 48.3 %all-to-all-start.1 = ((bf16[64,2,16,256]{3,2,1,0:T(8,128)(2,1)}), bf16[64,2,16,256]{3,2,1,0:T(8,128)(2,1)S(1)}, u32[]{:S(2)}, u32[]{:S(2)}) async-start(bf16[64,2,16,256]{3,2,1,0:T(8,128)(2,1)} %get-tuple-element.49), calls=%async_computation.1 | async-start | bytes 2097152 | tf_op jit(solution)/shard_map/all_to_all | solution.py:312
  147.4 12.1 %collective-permute-start.21 = (bf16[1,4,256,256]{3,2,1,0:T(8,128)(2,1)}, bf16[1,4,256,256]{3,2,1,0:T(8,128)(2,1)}, u32[]{:S(2)}, u32[]{:S(2)}) collective-permute-start(bf16[1,4,256,256]{3,2,1,0:T(8,128)(2,1)} %get-tuple-element.52), channel_id=1, source_target_pairs={{0,64},{64,128},{128,192},{192,0},{1,65},{65,129},{129,193},{193,1... | collective-permute-start | bytes 1572872 | tf_op jit(solution)/shard_map/ppermute | solution.py:185
  147.4 12.1 %collective-permute-start.22 = (bf16[1,4,256,256]{3,2,1,0:T(8,128)(2,1)}, bf16[1,4,256,256]{3,2,1,0:T(8,128)(2,1)}, u32[]{:S(2)}, u32[]{:S(2)}) collective-permute-start(bf16[1,4,256,256]{3,2,1,0:T(8,128)(2,1)} %get-tuple-element.53), channel_id=1, source_target_pairs={{0,192},{64,0},{128,64},{192,128},{1,193},{65,1},{129,65},{193,129... | collective-permute-start | bytes 1572872 | tf_op jit(solution)/shard_map/ppermute | solution.py:185
  173.3 7.5 %collective-permute-start.23 = (bf16[12,16,256]{2,1,0:T(8,128)(2,1)S(1)}, bf16[12,16,256]{2,1,0:T(8,128)(2,1)S(1)}, u32[]{:S(2)}, u32[]{:S(2)}) collective-permute-start(bf16[12,16,256]{2,1,0:T(8,128)(2,1)S(1)} %get-tuple-element.58), channel_id=1, source_target_pairs={{0,16},{1,17},{2,18},{3,19},{4,20},{5,21},{6,22},{7,23},{8,24},{9,... | collective-permute-start | bytes 294920 | tf_op jit(solution)/shard_map/ppermute | solution.py:189
  174.4 13.2 %collective-permute-start.24 = (bf16[12,16,256]{2,1,0:T(8,128)(2,1)S(1)}, bf16[12,16,256]{2,1,0:T(8,128)(2,1)S(1)}, u32[]{:S(2)}, u32[]{:S(2)}) collective-permute-start(bf16[12,16,256]{2,1,0:T(8,128)(2,1)S(1)} %get-tuple-element.59), channel_id=1, source_target_pairs={{0,32},{1,33},{2,34},{3,35},{4,36},{5,37},{6,38},{7,39},{8,40},{9,... | collective-permute-start | bytes 294920 | tf_op jit(solution)/shard_map/ppermute | solution.py:189
  178.5 11.2 %collective-permute-start.25 = (bf16[12,16,256]{2,1,0:T(8,128)(2,1)S(1)}, bf16[12,16,256]{2,1,0:T(8,128)(2,1)S(1)}, u32[]{:S(2)}, u32[]{:S(2)}) collective-permute-start(bf16[12,16,256]{2,1,0:T(8,128)(2,1)S(1)} %get-tuple-element.60), channel_id=1, source_target_pairs={{0,48},{1,49},{2,50},{3,51},{4,52},{5,53},{6,54},{7,55},{8,56},{9,... | collective-permute-start | bytes 294920 | tf_op jit(solution)/shard_map/ppermute | solution.py:189
  (5 other events, 46.0 us)

commit v5 on v4

--- a/solution.py
+++ b/solution.py
@@ -12,6 +12,7 @@
 BF16 = jnp.bfloat16
 VMEM_LIMIT = 20 * 1024 * 1024
 RELAY_COST = 10_000_000_000
+COSTS = (10_000_000_000, 10_000_000_000, 5_000_000_000)
 SMEM_SPEC = pl.BlockSpec(memory_space=pltpu.SMEM)
 
 
@@ -41,13 +42,29 @@
     return jnp.sum(part.reshape(rows // 8, 8, 128), axis=0)
 
 
+def join_kernel(up, relay_up, down, relay_down, joint_up, joint_down):
+    joint_up[...] = (up[...].astype(F32) + relay_up[...].astype(F32)).astype(BF16)
+    joint_down[...] = (down[...].astype(F32) + relay_down[...].astype(F32)).astype(BF16)
+
+
+def sum_kernel(group, own, top0, top1, bottom0, bottom1, *outs):
+    half = top0.shape[0]
+    quarter = outs[0].shape[2]
+    for t, out in enumerate(outs):
+        g = lax.rem(group[0] + t, len(outs))
+        cols = pl.ds(pl.multiple_of(g * quarter, quarter), quarter)
+        for rows, a, b in ((slice(0, half), top0, top1), (slice(half, None), bottom0, bottom1)):
+            total = own[rows, :, cols].astype(F32) + a[:, :, cols].astype(F32)
+            out[rows] = (total + b[:, :, cols].astype(F32)).astype(BF16)
+
+
 def relay_kernel(before, behind, up, down):
     count = up.shape[0]
     up[...] = before[:count]
     down[...] = behind[count:]
 
 
-def product_kernel(meta, arrived, r0, r1, far0, far1, r3, grad, sums, *products):
+def product_kernel(meta, arrived, r0, r1, r2, r3, grad, sums, *products):
     slots, groups = grad.shape[:2]
     per_row = arrived.shape[0] // groups
     for s in range(slots):
@@ -62,13 +79,12 @@
             g_sum = g_sum + fold(wide * wide)
             parts.append(part)
         own = jnp.concatenate(parts, 1)
-        rights = (r0.at[2 * s], r1.at[2 * s], (far0, far1)[s].at[0], r3.at[2 * s])
-        for product, right in zip(products, rights):
-            product[s] = dot(own, right[...]).astype(BF16)
+        for product, right in zip(products, (r0, r1, r2, r3)):
+            product[s] = dot(own, right[s]).astype(BF16)
         sums[s] = g_sum
 
 
-def root_kernel(meta, diags, g_sums, y0, y1, y2, y3, l0, l1, far0, far1, l3, out, sums, prods):
+def root_kernel(meta, diags, g_sums, y0, y1, y2, y3, l0, l1, l2, l3, out, sums, prods):
     me = meta[0]
     slots, size, quarter = out.shape
     reps = size // quarter
@@ -84,13 +100,10 @@
                     source = pl.multiple_of((q * reps + p) * piece, piece)
                     target = pl.multiple_of(((t * reps + p) * reps + r) * piece, piece)
                     prods[pl.ds(target, piece), :] = rows[s, pl.ds(source, piece), :]
-        far = (far0, far1)[s]
-        n2 = 2 * s + 1
         p_sum = jnp.zeros((8, 128), F32)
         for n in range(reps):
             rows = slice(n * quarter, (n + 1) * quarter)
-            lefts = (l0.at[n2, rows], l1.at[n2, rows], far.at[1, rows], l3.at[n2, rows])
-            wide = jnp.concatenate([left[...] for left in lefts], 1)
+            wide = jnp.concatenate([l0[s, rows], l1[s, rows], l2[s, rows], l3[s, rows]], 1)
             value = dot(wide, prods[...]) * keep
             out[s, rows] = value
             p_sum = p_sum + fold(value * value)
@@ -197,9 +210,8 @@
     def rows_of(rep):
         return lax.dynamic_slice_in_dim(terms, rep * piece, piece, 1)
 
-    def add(a, b):
-        return (a.astype(F32) + b.astype(F32)).astype(BF16)
-
+    params = pltpu.CompilerParams(vmem_limit_bytes=VMEM_LIMIT)
+    vmem = pl.BlockSpec(memory_space=pltpu.VMEM)
     half = ncols // 2
     up, down = rows_of((me_rep + 1) % reps), rows_of((me_rep + 3) % reps)
     far = rows_of((me_rep + 2) % reps)
@@ -207,17 +219,23 @@
     relay_down = turn_x(far[half:], 3)
     direct_up = turn_x(up[half:], 1)
     direct_down = turn_x(down[:half], 3)
-    joint_up = turn_x(add(up[:half], relay_up), 1)
-    joint_down = turn_x(add(down[half:], relay_down), 3)
-    own = rows_of(me_rep).astype(F32)
-    summed = jnp.concatenate(
-        [
-            own[:half] + joint_up.astype(F32) + direct_down.astype(F32),
-            own[half:] + direct_up.astype(F32) + joint_down.astype(F32),
-        ]
-    ).astype(BF16)
-    roots = jnp.concatenate([right_root[:1], left_root[:1], right_root[1:], left_root[1:]])
-    summed, roots = lax.optimization_barrier((summed, roots))
+    joint_up, joint_down = pl.pallas_call(
+        join_kernel,
+        in_specs=[vmem] * 4,
+        out_shape=[jax.ShapeDtypeStruct((half, piece, block_size), BF16)] * 2,
+        compiler_params=params,
+        cost_estimate=pl.CostEstimate(flops=RELAY_COST, bytes_accessed=0, transcendentals=0),
+        name="join",
+    )(up[:half], relay_up, down[half:], relay_down)
+    joint_up, joint_down = turn_x(joint_up, 1), turn_x(joint_down, 3)
+    held = pl.pallas_call(
+        sum_kernel,
+        in_specs=[SMEM_SPEC] + [vmem] * 5,
+        out_shape=[jax.ShapeDtypeStruct((ncols, piece, quarter), BF16)] * groups,
+        compiler_params=params,
+        name="sum",
+    )(me_group[None], rows_of(me_rep), joint_up, direct_down, direct_up, joint_down)
+    first, left_root, right_root = lax.optimization_barrier((held[0], left_root, right_root))
 
     my_blocks = lax.dynamic_slice_in_dim(block_ids, me_work * slots, slots)
     my_filled = lax.dynamic_slice_in_dim(filled, me_work * slots, slots)
@@ -230,15 +248,18 @@
     )
     my_width = jnp.where(my_filled, looked_up, block_size)
     meta = jnp.concatenate([me_rep[None], my_width, my_filled]).astype(jnp.int32)
-    global_rows = me_rep * quarter + jnp.arange(quarter, dtype=jnp.int32)
-    unit_rows = (col_index[None, :] == global_rows[:, None]).astype(F32)
-    within_width = (global_rows[None, :] < my_width[:, None]).astype(F32)
-    left_diag = jnp.sum(left_stat * unit_rows[None], axis=(1, 2))
-    right_diag = jnp.sum(jnp.sum(right_stat * unit_rows[None], axis=2) * within_width, axis=1)
+    local = jnp.arange(quarter, dtype=jnp.int32)
+    unit = (local[:, None] == local[None, :]).astype(F32)
+    within_width = (me_rep * quarter + local[None, :] < my_width[:, None]).astype(F32)
+
+    def diagonal_of(stat):
+        block = lax.dynamic_slice_in_dim(stat, me_rep * quarter, quarter, 2)
+        return jnp.sum(block * unit[None], axis=2)
+
+    left_diag = jnp.sum(diagonal_of(left_stat), axis=1)
+    right_diag = jnp.sum(diagonal_of(right_stat) * within_width, axis=1)
     diag_own = jnp.stack([left_diag, right_diag])
 
-    params = pltpu.CompilerParams(vmem_limit_bytes=VMEM_LIMIT)
-    vmem = pl.BlockSpec(memory_space=pltpu.VMEM)
 
     def relay(before, behind):
         shape = (before.shape[0] // 2,) + before.shape[1:]
@@ -252,15 +273,24 @@
         )(before, behind)
         return (turn_x(up, 1), turn_x(down, 3))
 
-    roots_prev, roots_next = turn_x(roots, 1), turn_x(roots, 3)
-    roots_far = relay(roots_prev, roots_next)
-
-    def columns_of(group):
-        return lax.dynamic_slice_in_dim(summed, group * quarter, quarter, 2)
-
-    held = [columns_of(me_group)]
-    for shift in range(1, groups):
-        held.append(turn_group(columns_of((me_group + shift) % groups), shift))
+    def hold(value, cost):
+        anywhere = pl.BlockSpec(memory_space=pl.ANY)
+        return pl.pallas_call(
+            lambda before, after: None,
+            in_specs=[anywhere],
+            out_specs=anywhere,
+            out_shape=jax.ShapeDtypeStruct(value.shape, value.dtype),
+            input_output_aliases={0: 0},
+            cost_estimate=pl.CostEstimate(flops=cost, bytes_accessed=0, transcendentals=0),
+            name="hold",
+        )(value)
+
+    r_prev, r_next = hold(turn_x(right_root, 1), COSTS[2]), hold(turn_x(right_root, 3), COSTS[2])
+    r_prev, r_next = lax.optimization_barrier((r_prev, r_next))
+    l_prev, l_next = hold(turn_x(left_root, 1), COSTS[0]), hold(turn_x(left_root, 3), COSTS[1])
+    r_far, l_far = turn_x(r_prev, 1), turn_x(l_next, 3)
+
+    held = [first] + [turn_group(held[shift], shift) for shift in range(1, groups)]
     place = ((me_group - block_ids // ncols) % groups) * ncols + block_ids % ncols
     outgoing = pl.pallas_call(
         spread_kernel,
@@ -272,10 +302,11 @@
     )(place.astype(jnp.int32), *held)
     incoming = lax.all_to_all(outgoing, "fsdp", split_axis=0, concat_axis=0, tiled=True)
 
+    incoming, l_prev, l_next = lax.optimization_barrier((incoming, l_prev, l_next))
     quarters = jax.ShapeDtypeStruct((slots, quarter, quarter), BF16)
     g_mine, g_sums, *products = pl.pallas_call(
         product_kernel,
-        in_specs=[SMEM_SPEC] + [vmem] * 6,
+        in_specs=[SMEM_SPEC] + [vmem] * 5,
         out_shape=[
             jax.ShapeDtypeStruct((slots, groups, quarter, quarter), BF16),
             jax.ShapeDtypeStruct((slots, 8, 128), F32),
@@ -283,11 +314,11 @@
         + [quarters] * reps,
         compiler_params=params,
         name="right_products",
-    )(meta, incoming, roots, roots_prev, *roots_far, roots_next)
+    )(meta, incoming, right_root, r_prev, r_far, r_next)
     products = [products[0]] + [turn_x(products[n], reps - n) for n in range(1, reps)]
     precond, sums = pl.pallas_call(
         root_kernel,
-        in_specs=[SMEM_SPEC] * 2 + [vmem] * 10,
+        in_specs=[SMEM_SPEC] * 2 + [vmem] * 9,
         out_shape=[
             jax.ShapeDtypeStruct((slots, block_size, quarter), F32),
             jax.ShapeDtypeStruct((slots, 4, 8, 128), F32),
@@ -295,10 +326,9 @@
         scratch_shapes=[pltpu.VMEM((block_size, quarter), BF16)],
         compiler_params=params,
         name="left_products",
-    )(meta, diag_own, g_sums, *products, roots, roots_prev, *roots_far, roots_next)
+    )(meta, diag_own, g_sums, *products, left_root, l_prev, l_far, l_next)
     all_sums = [sums] + [turn_x(sums, shift) for shift in (1, 2, 3)]
-    all_sums = lax.optimization_barrier((*all_sums, g_mine))
-    g_mine = all_sums[reps]
+    *all_sums, g_mine = lax.optimization_barrier((*all_sums, g_mine))
     returning, adds = pl.pallas_call(
         lambda *refs: scale_kernel(groups, per_row, *refs),
         in_specs=[SMEM_SPEC] + [vmem] * 5,
@@ -308,7 +338,7 @@
         ],
         compiler_params=params,
         name="graft_scale",
-    )(meta, precond, *all_sums[:reps])
+    )(meta, precond, *all_sums)
     arrived = lax.all_to_all(returning, "fsdp", split_axis=0, concat_axis=0, tiled=True)
     arrived = arrived.reshape(workers * slots, piece, quarter)
 
@@ -328,7 +358,6 @@
         ),
         name="stat_update",
     )(meta, adds, g_mine, g_prev, g_next, *g_far, left_stat, right_stat)
-    arrived, left_new, right_new = lax.optimization_barrier((arrived, left_new, right_new))
 
     block = jnp.arange(groups * ncols, dtype=jnp.int32)
     wanted = jnp.take(slot_ids, (block + me_group * ncols) % (groups * ncols), mode="clip")

time: 192 us -> 181 us (0.943)
  waiting for transfers between devices: 78.5 us -> 68.8 us
  Pallas kernels: 26.3 us -> 20.5 us
  local copies, waits for them, and re-layouts: 4.03 us -> 7.96 us
    ppermute x20 -> x22, waiting for transfers between devices: 54.9 us -> 29.7 us  [turn_x(): return lax.ppermute(value, 'replica', pairs)]
    all_to_all x1, waiting for transfers between devices: 4.49 us -> 21.9 us  [on_device(): lax.all_to_all(returning, 'fsdp', split_axis=0, concat_axis=0, tiled=True)]
    ppermute x6, waiting for transfers between devices: 14.4 us -> 2.9 us  [turn_group(): return lax.ppermute(value, 'fsdp', pairs)]
    all_to_all x1, waiting for transfers between devices: 4.66 us -> 14.2 us  [on_device(): lax.all_to_all(outgoing, 'fsdp', split_axis=0, concat_axis=0, tiled=True)]
    pallas_call x2 -> x1, Pallas kernels: 6.41 us -> 2.56 us  [relay(): pl.pallas_call(relay_kernel, in_specs=[vmem] * 2, out_shape=[jax.ShapeDty...]
    unnamed x18 -> x14, local copies, waits for them, and re-layouts: 1.63 us -> 4.17 us
    pallas_call x2 -> x8, Pallas kernels: 8.78 us -> 7.92 us  [the longest x1 4.15 us: on_device(): pl.pallas_call(product_kernel, in_specs=[SMEM_SPEC] + [vmem] * 5, out_sha...]
    ppermute x20 -> x22, starting transfers between devices: 25.2 us -> 25.6 us  [turn_x(): return lax.ppermute(value, 'replica', pairs)]
  transfers between devices with their start and end apart: 28 -> 30, of which waited for: 21 -> 13; matrix products, arithmetic and copies ran while one was open for 2% -> 3% of each run, Pallas kernels for 9% -> 9%
where the time goes in v5:
time: 181 us; the launch traced here: 179 us
  starting transfers between devices  75.4 us (42%)
  waiting for transfers between devices  68.8 us (38%)
  Pallas kernels  20.5 us (11%)
  local copies, waits for them, and re-layouts  7.96 us (4%)
  other arithmetic  5.73 us (3%)
    ppermute x22, waiting for transfers between devices, turn_x(): return lax.ppermute(value, 'replica', pairs)  29.7 us
    ppermute x22, starting transfers between devices, turn_x(): return lax.ppermute(value, 'replica', pairs)  25.6 us
    all_to_all x1, waiting for transfers between devices, on_device(): lax.all_to_all(returning, 'fsdp', split_axis=0, concat_axis=0, tiled=True)  21.9 us
    all_to_all x1, starting transfers between devices, on_device(): lax.all_to_all(returning, 'fsdp', split_axis=0, concat_axis=0, tiled=True)  20.3 us
    ppermute x6, starting transfers between devices, turn_group(): return lax.ppermute(value, 'fsdp', pairs)  15.7 us
    all_to_all x1, waiting for transfers between devices, on_device(): lax.all_to_all(outgoing, 'fsdp', split_axis=0, concat_axis=0, tiled=True)  14.2 us
    all_to_all x1, starting transfers between devices, on_device(): lax.all_to_all(outgoing, 'fsdp', split_axis=0, concat_axis=0, tiled=True)  13.8 us
    pallas_call x1, Pallas kernels, on_device(): pl.pallas_call(stat_kernel, in_specs=[SMEM_SPEC] + [vmem] * 8, out_shape=...  7.08 us
  transfers between devices with their start and end apart: 30, of which 13 were waited for; matrix products, arithmetic and copies ran while one was open for 3% of the time, Pallas kernels for 9%

profile of v5, /device:TPU:1, one launch (start us, length us, event | category | flops | bytes accessed | tf_op | source)
XLA Modules:
  0.0 179.3 jit_solution(16824985045541378219)
XLA Ops:
  1.4 1.8 %fusion = bf16[64,12,1024]{2,0,1:T(8,128)(2,1)S(1)} fusion(bf16[1,64,12,1024]{3,1,2,0:T(8,128)(2,1)} %param.7, f32[12,1024]{1,0:T(8,128)S(1)} %fusion.2), kind=kLoop, calls=%fused_computation.3 | loop fusion | flops 2359296 | bytes 3194880 | tf_op jit(solution)/shard_map/convert_element_type | solution.py:207
  3.5 2.1 %collective-permute-start = (bf16[6,16,1024]{2,1,0:T(8,128)(2,1)S(1)}, bf16[6,16,1024]{2,1,0:T(8,128)(2,1)S(1)}, u32[]{:S(2)}, u32[]{:S(2)}) collective-permute-start(bf16[6,16,1024]{2,1,0:T(8,128)(2,1)S(1)} %get-tuple-element.90), channel_id=1, source_target_pairs={{0,64},{64,128},{128,192},{192,0},{1,65},{65,129},{129,193},{193,1... | collective-permute-start | bytes 589832 | tf_op jit(solution)/shard_map/ppermute | solution.py:198
  7.7 1.4 collective-permute-start.3
  12.5 1.6 collective-permute-start.2
  16.0 4.0 %collective-permute-done.2.top0 = bf16[6,16,1024]{2,1,0:T(8,128)(2,1)S(1)} collective-permute-done((bf16[6,16,1024]{2,1,0:T(8,128)(2,1)S(1)}, bf16[6,16,1024]{2,1,0:T(8,128)(2,1)S(1)}, u32[]{:S(2)}, u32[]{:S(2)}) %collective-permute-start.2) | collective-permute-done | bytes 196640 | tf_op jit(solution)/shard_map/ppermute | solution.py:198
  21.5 1.8 collective-permute-start.12
  24.7 2.9 %collective-permute-start.6 = (bf16[12,16,256]{2,1,0:T(8,128)(2,1)S(1)}, bf16[12,16,256]{2,1,0:T(8,128)(2,1)S(1)}, u32[]{:S(2)}, u32[]{:S(2)}) collective-permute-start(bf16[12,16,256]{2,1,0:T(8,128)(2,1)S(1)} %get-tuple-element.44), channel_id=1, source_target_pairs={{0,16},{1,17},{2,18},{3,19},{4,20},{5,21},{6,22},{7,23},{8,24},{9,... | collective-permute-start | bytes 294920 | tf_op jit(solution)/shard_map/ppermute | solution.py:202
  27.7 5.1 %collective-permute-start.7 = (bf16[12,16,256]{2,1,0:T(8,128)(2,1)S(1)}, bf16[12,16,256]{2,1,0:T(8,128)(2,1)S(1)}, u32[]{:S(2)}, u32[]{:S(2)}) collective-permute-start(bf16[12,16,256]{2,1,0:T(8,128)(2,1)S(1)} %get-tuple-element.45), channel_id=1, source_target_pairs={{0,32},{1,33},{2,34},{3,35},{4,36},{5,37},{6,38},{7,39},{8,40},{9,... | collective-permute-start | bytes 294920 | tf_op jit(solution)/shard_map/ppermute | solution.py:202
  32.8 2.4 %collective-permute-start.8 = (bf16[12,16,256]{2,1,0:T(8,128)(2,1)S(1)}, bf16[12,16,256]{2,1,0:T(8,128)(2,1)S(1)}, u32[]{:S(2)}, u32[]{:S(2)}) collective-permute-start(bf16[12,16,256]{2,1,0:T(8,128)(2,1)S(1)} %get-tuple-element.46), channel_id=1, source_target_pairs={{0,48},{1,49},{2,50},{3,51},{4,52},{5,53},{6,54},{7,55},{8,56},{9,... | collective-permute-start | bytes 294920 | tf_op jit(solution)/shard_map/ppermute | solution.py:202
  36.8 2.1 %collective-permute-done.8.h3 = bf16[12,16,256]{2,1,0:T(8,128)(2,1)S(1)} collective-permute-done((bf16[12,16,256]{2,1,0:T(8,128)(2,1)S(1)}, bf16[12,16,256]{2,1,0:T(8,128)(2,1)S(1)}, u32[]{:S(2)}, u32[]{:S(2)}) %collective-permute-start.8) | collective-permute-done | bytes 98336 | tf_op jit(solution)/shard_map/ppermute | solution.py:202
  38.9 1.6 spread.1
  40.5 13.8 %all-to-all-start = ((bf16[64,2,16,256]{3,2,1,0:T(8,128)(2,1)}), bf16[64,2,16,256]{3,2,1,0:T(8,128)(2,1)S(1)}, u32[]{:S(2)}, u32[]{:S(2)}) async-start(bf16[64,2,16,256]{3,2,1,0:T(8,128)(2,1)} %spread.1), calls=%async_computation | async-start | bytes 2097152 | tf_op jit(solution)/shard_map/all_to_all | solution.py:303
  54.4 10.3 %collective-permute-done.10.before = bf16[2,1024,256]{2,1,0:T(8,128)(2,1)} collective-permute-done((bf16[2,1024,256]{2,1,0:T(8,128)(2,1)}, bf16[2,1024,256]{2,1,0:T(8,128)(2,1)}, u32[]{:S(2)}, u32[]{:S(2)}) %collective-permute-start.10) | collective-permute-done | bytes 1048608 | tf_op jit(solution)/shard_map/ppermute | solution.py:198
  64.8 3.3 %collective-permute-start.17 = (bf16[2,1024,256]{2,1,0:T(8,128)(2,1)}, bf16[2,1024,256]{2,1,0:T(8,128)(2,1)}, u32[]{:S(2)}, u32[]{:S(2)}) collective-permute-start(bf16[2,1024,256]{2,1,0:T(8,128)(2,1)} %hold.5.l3), channel_id=1, source_target_pairs={{0,192},{64,0},{128,64},{192,128},{1,193},{65,1},{129,65},{193,129... | collective-permute-start | bytes 3145736 | tf_op jit(solution)/shard_map/ppermute | solution.py:198
  68.0 14.2 %all-to-all-done.arrived = bf16[64,2,16,256]{3,2,1,0:T(8,128)(2,1)S(1)} async-done(((bf16[64,2,16,256]{3,2,1,0:T(8,128)(2,1)}), bf16[64,2,16,256]{3,2,1,0:T(8,128)(2,1)S(1)}, u32[]{:S(2)}, u32[]{:S(2)}) %all-to-all-start) | async-done | bytes 1048608 | tf_op jit(solution)/shard_map/all_to_all | solution.py:303
  82.3 5.5 %collective-permute-done.13.r2 = bf16[2,1024,256]{2,1,0:T(8,128)(2,1)} collective-permute-done((bf16[2,1024,256]{2,1,0:T(8,128)(2,1)}, bf16[2,1024,256]{2,1,0:T(8,128)(2,1)}, u32[]{:S(2)}, u32[]{:S(2)}) %collective-permute-start.13) | collective-permute-done | bytes 1048608 | tf_op jit(solution)/shard_map/ppermute | solution.py:198
  87.8 4.1 %right_products.1 = (bf16[2,4,256,256]{3,2,1,0:T(8,128)(2,1)}, f32[2,8,128]{2,1,0:T(8,128)S(1)}, bf16[2,256,256]{2,1,0:T(8,128)(2,1)S(1)}, bf16[2,256,256]{2,1,0...) custom-call(s32[5]{0:T(128)S(1)} %pad_add_fusion.meta.refs_0_, ...), custom_call_target="tpu_custom_call" | custom-call | tf_op jit(solution)/shard_map/right_products/pallas_call | solution.py:307
  92.0 1.5 collective-permute-start.15
  93.7 3.5 %collective-permute-done.14.y1 = bf16[2,256,256]{2,1,0:T(8,128)(2,1)S(1)} collective-permute-done((bf16[2,256,256]{2,1,0:T(8,128)(2,1)S(1)}, bf16[2,256,256]{2,1,0:T(8,128)(2,1)S(1)}, u32[]{:S(2)}, u32[]{:S(2)}) %collective-permute-start.14) | collective-permute-done | bytes 262176 | tf_op jit(solution)/shard_map/ppermute | solution.py:198
  97.2 1.6 collective-permute-done.15.y2
  98.8 2.7 %collective-permute-done.16.y3 = bf16[2,256,256]{2,1,0:T(8,128)(2,1)S(1)} collective-permute-done((bf16[2,256,256]{2,1,0:T(8,128)(2,1)S(1)}, bf16[2,256,256]{2,1,0:T(8,128)(2,1)S(1)}, u32[]{:S(2)}, u32[]{:S(2)}) %collective-permute-start.16) | collective-permute-done | bytes 262176 | tf_op jit(solution)/shard_map/ppermute | solution.py:198
  101.5 3.5 %left_products.1 = (f32[2,1024,256]{2,1,0:T(8,128)S(1)}, f32[2,4,8,128]{3,2,1,0:T(8,128)S(1)}) custom-call(s32[5]{0:T(128)S(1)} %pad_add_fusion.meta.refs_0_, f32[2,2]{1,0:T(2,128)S(1)} %pad_maximum_fusion.1.diags, f32[2,8,128]{2,1,0:T(8,128)S(1)} %get-tuple-element.52.g_sums, bf16[2,256,256]{2,1,0:T(8,128)(2,1)S(1)} %get-tuple-element.53.y0, ...), custom_call_target="tpu_custom_call" | custom-call | tf_op jit(solution)/shard_map/left_products/pallas_call | solution.py:319
  105.7 2.1 %collective-permute-start.19 = (f32[2,4,8,128]{3,2,1,0:T(8,128)S(1)}, f32[2,4,8,128]{3,2,1,0:T(8,128)S(1)}, u32[]{:S(2)}, u32[]{:S(2)}) collective-permute-start(f32[2,4,8,128]{3,2,1,0:T(8,128)S(1)} %get-tuple-element.62.refs_2_), channel_id=1, source_target_pairs={{0,128},{64,192},{128,0},{192,64},{1,129},{65,193},{129,1},{193,65... | collective-permute-start | bytes 98312 | tf_op jit(solution)/shard_map/ppermute | solution.py:198
  107.8 1.4 collective-permute-start.20
  111.4 1.8 %collective-permute-start.25 = (bf16[2,4,256,256]{3,2,1,0:T(8,128)(2,1)}, bf16[2,4,256,256]{3,2,1,0:T(8,128)(2,1)}, u32[]{:S(2)}, u32[]{:S(2)}) collective-permute-start(bf16[2,4,256,256]{3,2,1,0:T(8,128)(2,1)} %get-tuple-element.72.g0), channel_id=1, source_target_pairs={{0,192},{64,0},{128,64},{192,128},{1,193},{65,1},{129,65},{193,129... | collective-permute-start | bytes 3145736 | tf_op jit(solution)/shard_map/ppermute | solution.py:198
  115.0 20.3 %all-to-all-start.1 = ((bf16[64,2,16,256]{3,2,1,0:T(8,128)(2,1)}), bf16[64,2,16,256]{3,2,1,0:T(8,128)(2,1)S(1)}, u32[]{:S(2)}, u32[]{:S(2)}) async-start(bf16[64,2,16,256]{3,2,1,0:T(8,128)(2,1)} %copy-done.2), calls=%async_computation.1 | async-start | bytes 2097152 | tf_op jit(solution)/shard_map/all_to_all | solution.py:342
  135.3 2.6 %relay.1 = (bf16[1,4,256,256]{3,2,1,0:T(8,128)(2,1)}, bf16[1,4,256,256]{3,2,1,0:T(8,128)(2,1)}) custom-call(bf16[2,4,256,256]{3,2,1,0:T(8,128)(2,1)} %collective-permute-done.24.before.g1, bf16[2,4,256,256]{3,2,1,0:T(8,128)(2,1)} %collective-permute-done.25.behind.g3), custom_call_target="tpu_custom_call" | custom-call | flops 10000000000 | tf_op jit(solution)/shard_map/relay/pallas_call | solution.py:266
  137.9 2.7 %collective-permute-start.27 = (bf16[1,4,256,256]{3,2,1,0:T(8,128)(2,1)}, bf16[1,4,256,256]{3,2,1,0:T(8,128)(2,1)}, u32[]{:S(2)}, u32[]{:S(2)}) collective-permute-start(bf16[1,4,256,256]{3,2,1,0:T(8,128)(2,1)} %get-tuple-element.74), channel_id=1, source_target_pairs={{0,192},{64,0},{128,64},{192,128},{1,193},{65,1},{129,65},{193,129... | collective-permute-start | bytes 1572872 | tf_op jit(solution)/shard_map/ppermute | solution.py:198
  141.4 21.9 %all-to-all-done.1 = bf16[64,2,16,256]{3,2,1,0:T(8,128)(2,1)S(1)} async-done(((bf16[64,2,16,256]{3,2,1,0:T(8,128)(2,1)}), bf16[64,2,16,256]{3,2,1,0:T(8,128)(2,1)S(1)}, u32[]{:S(2)}, u32[]{:S(2)}) %all-to-all-start.1) | async-done | bytes 1048608 | tf_op jit(solution)/shard_map/all_to_all | solution.py:342
  163.9 3.1 %collective-permute-start.23 = (bf16[12,16,256]{2,1,0:T(8,128)(2,1)S(1)}, bf16[12,16,256]{2,1,0:T(8,128)(2,1)S(1)}, u32[]{:S(2)}, u32[]{:S(2)}) collective-permute-start(bf16[12,16,256]{2,1,0:T(8,128)(2,1)S(1)} %get-tuple-element.70), channel_id=1, source_target_pairs={{0,48},{1,49},{2,50},{3,51},{4,52},{5,53},{6,54},{7,55},{8,56},{9,... | collective-permute-start | bytes 294920 | tf_op jit(solution)/shard_map/ppermute | solution.py:202
  169.2 1.6 copy-done.1
  170.8 7.1 %stat_update.1 = (f32[2,256,1024]{2,1,0:T(8,128)}, f32[2,256,1024]{2,1,0:T(8,128)}) custom-call(s32[5]{0:T(128)S(1)} %pad_add_fusion.meta.refs_0_, f32[2,2,8,128]{3,2,1,0:T(8,128)S(1)} %get-tuple-element.71.adds, bf16[2,4,256,256]{3,2,1,0:T(8,128)(2,1)} %get-tuple-element.72.g0, bf16[2,4,256,256]{3,2,1,0:T(8,128)(2,1)} %collective-permute-done.24.before.g1, ...), custom_call_target="tpu_custom_call" | custom-call | flops 2147483648 | bytes 20971520 | tf_op jit(solution)/shard_map/stat_update/pallas_call | solution.py:348
  (84 shorter events, 22.7 us)
Async XLA Ops:
  3.5 6.7 %collective-permute-start = (bf16[6,16,1024]{2,1,0:T(8,128)(2,1)S(1)}, bf16[6,16,1024]{2,1,0:T(8,128)(2,1)S(1)}, u32[]{:S(2)}, u32[]{:S(2)}) collective-permute-start(bf16[6,16,1024]{2,1,0:T(8,128)(2,1)S(1)} %get-tuple-element.90), channel_id=1, source_target_pairs={{0,64},{64,128},{128,192},{192,0},{1,65},{65,129},{129,193},{193,1... | collective-permute-start | bytes 589832 | tf_op jit(solution)/shard_map/ppermute | solution.py:198
  5.7 5.1 %collective-permute-start.1 = (bf16[6,16,1024]{2,1,0:T(8,128)(2,1)S(1)}, bf16[6,16,1024]{2,1,0:T(8,128)(2,1)S(1)}, u32[]{:S(2)}, u32[]{:S(2)}) collective-permute-start(bf16[6,16,1024]{2,1,0:T(8,128)(2,1)S(1)} %get-tuple-element.89), channel_id=1, source_target_pairs={{0,192},{64,0},{128,64},{192,128},{1,193},{65,1},{129,65},{193,129... | collective-permute-start | bytes 589832 | tf_op jit(solution)/shard_map/ppermute | solution.py:198
  7.7 8.3 %collective-permute-start.3 = (bf16[6,16,1024]{2,1,0:T(8,128)(2,1)}, bf16[6,16,1024]{2,1,0:T(8,128)(2,1)S(1)}, u32[]{:S(2)}, u32[]{:S(2)}) collective-permute-start(bf16[6,16,1024]{2,1,0:T(8,128)(2,1)} %get-tuple-element.87), channel_id=1, source_target_pairs={{0,192},{64,0},{128,64},{192,128},{1,193},{65,1},{129,65},{193,129... | collective-permute-start | bytes 589832 | tf_op jit(solution)/shard_map/ppermute | solution.py:198
  9.8 6.2 %collective-permute-start.4 = (bf16[6,16,1024]{2,1,0:T(8,128)(2,1)}, bf16[6,16,1024]{2,1,0:T(8,128)(2,1)S(1)}, u32[]{:S(2)}, u32[]{:S(2)}) collective-permute-start(bf16[6,16,1024]{2,1,0:T(8,128)(2,1)} %get-tuple-element.85), channel_id=1, source_target_pairs={{0,64},{64,128},{128,192},{192,0},{1,65},{65,129},{129,193},{193,1... | collective-permute-start | bytes 589832 | tf_op jit(solution)/shard_map/ppermute | solution.py:198
  12.4 8.9 %copy-start.5 = (s32[12]{0:T(128)S(1)}, s32[12]{0:T(128)}, u32[]{:S(2)}) copy-start(s32[12]{0:T(128)} %param.8) | copy-start | bytes 148
  12.4 10.9 %copy-start = (f32[2,256,1024]{2,1,0:T(8,128)S(1)}, f32[2,256,1024]{2,1,0:T(8,128)}, u32[]{:S(2)}) copy-start(f32[2,256,1024]{2,1,0:T(8,128)} %left.1) | copy-start | bytes 6291460
  12.5 7.6 %collective-permute-start.2 = (bf16[6,16,1024]{2,1,0:T(8,128)(2,1)S(1)}, bf16[6,16,1024]{2,1,0:T(8,128)(2,1)S(1)}, u32[]{:S(2)}, u32[]{:S(2)}) collective-permute-start(bf16[6,16,1024]{2,1,0:T(8,128)(2,1)S(1)} %get-tuple-element.40), channel_id=1, source_target_pairs={{0,64},{64,128},{128,192},{192,0},{1,65},{65,129},{129,193},{193,1... | collective-permute-start | bytes 589832 | tf_op jit(solution)/shard_map/ppermute | solution.py:198
  14.1 6.0 %collective-permute-start.5 = (bf16[6,16,1024]{2,1,0:T(8,128)(2,1)S(1)}, bf16[6,16,1024]{2,1,0:T(8,128)(2,1)S(1)}, u32[]{:S(2)}, u32[]{:S(2)}) collective-permute-start(bf16[6,16,1024]{2,1,0:T(8,128)(2,1)S(1)} %get-tuple-element.41), channel_id=1, source_target_pairs={{0,192},{64,0},{128,64},{192,128},{1,193},{65,1},{129,65},{193,129... | collective-permute-start | bytes 589832 | tf_op jit(solution)/shard_map/ppermute | solution.py:198
  20.2 34.1 %collective-permute-start.11 = (bf16[2,1024,256]{2,1,0:T(8,128)(2,1)}, bf16[2,1024,256]{2,1,0:T(8,128)(2,1)}, u32[]{:S(2)}, u32[]{:S(2)}) collective-permute-start(bf16[2,1024,256]{2,1,0:T(8,128)(2,1)} %r0), channel_id=1, source_target_pairs={{0,64},{64,128},{128,192},{192,0},{1,65},{65,129},{129,193},{193,1... | collective-permute-start | bytes 3145736 | tf_op jit(solution)/shard_map/ppermute | solution.py:198
  21.5 32.8 %collective-permute-start.12 = (bf16[2,1024,256]{2,1,0:T(8,128)(2,1)}, bf16[2,1024,256]{2,1,0:T(8,128)(2,1)}, u32[]{:S(2)}, u32[]{:S(2)}) collective-permute-start(bf16[2,1024,256]{2,1,0:T(8,128)(2,1)} %r0), channel_id=1, source_target_pairs={{0,192},{64,0},{128,64},{192,128},{1,193},{65,1},{129,65},{193,129... | collective-permute-start | bytes 3145736 | tf_op jit(solution)/shard_map/ppermute | solution.py:198
  24.7 10.5 %collective-permute-start.6 = (bf16[12,16,256]{2,1,0:T(8,128)(2,1)S(1)}, bf16[12,16,256]{2,1,0:T(8,128)(2,1)S(1)}, u32[]{:S(2)}, u32[]{:S(2)}) collective-permute-start(bf16[12,16,256]{2,1,0:T(8,128)(2,1)S(1)} %get-tuple-element.44), channel_id=1, source_target_pairs={{0,16},{1,17},{2,18},{3,19},{4,20},{5,21},{6,22},{7,23},{8,24},{9,... | collective-permute-start | bytes 294920 | tf_op jit(solution)/shard_map/ppermute | solution.py:202
  27.7 8.8 %collective-permute-start.7 = (bf16[12,16,256]{2,1,0:T(8,128)(2,1)S(1)}, bf16[12,16,256]{2,1,0:T(8,128)(2,1)S(1)}, u32[]{:S(2)}, u32[]{:S(2)}) collective-permute-start(bf16[12,16,256]{2,1,0:T(8,128)(2,1)S(1)} %get-tuple-element.45), channel_id=1, source_target_pairs={{0,32},{1,33},{2,34},{3,35},{4,36},{5,37},{6,38},{7,39},{8,40},{9,... | collective-permute-start | bytes 294920 | tf_op jit(solution)/shard_map/ppermute | solution.py:202
  32.8 6.1 %collective-permute-start.8 = (bf16[12,16,256]{2,1,0:T(8,128)(2,1)S(1)}, bf16[12,16,256]{2,1,0:T(8,128)(2,1)S(1)}, u32[]{:S(2)}, u32[]{:S(2)}) collective-permute-start(bf16[12,16,256]{2,1,0:T(8,128)(2,1)S(1)} %get-tuple-element.46), channel_id=1, source_target_pairs={{0,48},{1,49},{2,50},{3,51},{4,52},{5,53},{6,54},{7,55},{8,56},{9,... | collective-permute-start | bytes 294920 | tf_op jit(solution)/shard_map/ppermute | solution.py:202
  35.2 29.6 %collective-permute-start.10 = (bf16[2,1024,256]{2,1,0:T(8,128)(2,1)}, bf16[2,1024,256]{2,1,0:T(8,128)(2,1)}, u32[]{:S(2)}, u32[]{:S(2)}) collective-permute-start(bf16[2,1024,256]{2,1,0:T(8,128)(2,1)} %l0), channel_id=1, source_target_pairs={{0,192},{64,0},{128,64},{192,128},{1,193},{65,1},{129,65},{193,129... | collective-permute-start | bytes 3145736 | tf_op jit(solution)/shard_map/ppermute | solution.py:198
  36.5 31.6 %collective-permute-start.9 = (bf16[2,1024,256]{2,1,0:T(8,128)(2,1)}, bf16[2,1024,256]{2,1,0:T(8,128)(2,1)}, u32[]{:S(2)}, u32[]{:S(2)}) collective-permute-start(bf16[2,1024,256]{2,1,0:T(8,128)(2,1)} %l0), channel_id=1, source_target_pairs={{0,64},{64,128},{128,192},{192,0},{1,65},{65,129},{129,193},{193,1... | collective-permute-start | bytes 3145736 | tf_op jit(solution)/shard_map/ppermute | solution.py:198
  40.5 41.8 %all-to-all-start = ((bf16[64,2,16,256]{3,2,1,0:T(8,128)(2,1)}), bf16[64,2,16,256]{3,2,1,0:T(8,128)(2,1)S(1)}, u32[]{:S(2)}, u32[]{:S(2)}) async-start(bf16[64,2,16,256]{3,2,1,0:T(8,128)(2,1)} %spread.1), calls=%async_computation | async-start | bytes 2097152 | tf_op jit(solution)/shard_map/all_to_all | solution.py:303
  54.3 33.5 %collective-permute-start.13 = (bf16[2,1024,256]{2,1,0:T(8,128)(2,1)}, bf16[2,1024,256]{2,1,0:T(8,128)(2,1)}, u32[]{:S(2)}, u32[]{:S(2)}) collective-permute-start(bf16[2,1024,256]{2,1,0:T(8,128)(2,1)} %hold.6.r1), channel_id=1, source_target_pairs={{0,64},{64,128},{128,192},{192,0},{1,65},{65,129},{129,193},{193,1... | collective-permute-start | bytes 3145736 | tf_op jit(solution)/shard_map/ppermute | solution.py:198
  64.8 28.9 %collective-permute-start.17 = (bf16[2,1024,256]{2,1,0:T(8,128)(2,1)}, bf16[2,1024,256]{2,1,0:T(8,128)(2,1)}, u32[]{:S(2)}, u32[]{:S(2)}) collective-permute-start(bf16[2,1024,256]{2,1,0:T(8,128)(2,1)} %hold.5.l3), channel_id=1, source_target_pairs={{0,192},{64,0},{128,64},{192,128},{1,193},{65,1},{129,65},{193,129... | collective-permute-start | bytes 3145736 | tf_op jit(solution)/shard_map/ppermute | solution.py:198
  92.0 5.2 %collective-permute-start.14 = (bf16[2,256,256]{2,1,0:T(8,128)(2,1)S(1)}, bf16[2,256,256]{2,1,0:T(8,128)(2,1)S(1)}, u32[]{:S(2)}, u32[]{:S(2)}) collective-permute-start(bf16[2,256,256]{2,1,0:T(8,128)(2,1)S(1)} %get-tuple-element.54), channel_id=1, source_target_pairs={{0,192},{64,0},{128,64},{192,128},{1,193},{65,1},{129,65},{193,129... | collective-permute-start | bytes 786440 | tf_op jit(solution)/shard_map/ppermute | solution.py:198
  92.0 6.8 %collective-permute-start.15 = (bf16[2,256,256]{2,1,0:T(8,128)(2,1)S(1)}, bf16[2,256,256]{2,1,0:T(8,128)(2,1)S(1)}, u32[]{:S(2)}, u32[]{:S(2)}) collective-permute-start(bf16[2,256,256]{2,1,0:T(8,128)(2,1)S(1)} %get-tuple-element.55), channel_id=1, source_target_pairs={{0,128},{64,192},{128,0},{192,64},{1,129},{65,193},{129,1},{193,65... | collective-permute-start | bytes 786440 | tf_op jit(solution)/shard_map/ppermute | solution.py:198
  93.4 8.1 %collective-permute-start.16 = (bf16[2,256,256]{2,1,0:T(8,128)(2,1)S(1)}, bf16[2,256,256]{2,1,0:T(8,128)(2,1)S(1)}, u32[]{:S(2)}, u32[]{:S(2)}) collective-permute-start(bf16[2,256,256]{2,1,0:T(8,128)(2,1)S(1)} %get-tuple-element.56), channel_id=1, source_target_pairs={{0,64},{64,128},{128,192},{192,0},{1,65},{65,129},{129,193},{193,1... | collective-permute-start | bytes 786440 | tf_op jit(solution)/shard_map/ppermute | solution.py:198
  105.0 4.1 %collective-permute-start.18 = (f32[2,4,8,128]{3,2,1,0:T(8,128)S(1)}, f32[2,4,8,128]{3,2,1,0:T(8,128)S(1)}, u32[]{:S(2)}, u32[]{:S(2)}) collective-permute-start(f32[2,4,8,128]{3,2,1,0:T(8,128)S(1)} %get-tuple-element.62.refs_2_), channel_id=1, source_target_pairs={{0,64},{64,128},{128,192},{192,0},{1,65},{65,129},{129,193},{193,1... | collective-permute-start | bytes 98312 | tf_op jit(solution)/shard_map/ppermute | solution.py:198
  105.7 4.3 %collective-permute-start.19 = (f32[2,4,8,128]{3,2,1,0:T(8,128)S(1)}, f32[2,4,8,128]{3,2,1,0:T(8,128)S(1)}, u32[]{:S(2)}, u32[]{:S(2)}) collective-permute-start(f32[2,4,8,128]{3,2,1,0:T(8,128)S(1)} %get-tuple-element.62.refs_2_), channel_id=1, source_target_pairs={{0,128},{64,192},{128,0},{192,64},{1,129},{65,193},{129,1},{193,65... | collective-permute-start | bytes 98312 | tf_op jit(solution)/shard_map/ppermute | solution.py:198
  107.8 2.8 %collective-permute-start.20 = (f32[2,4,8,128]{3,2,1,0:T(8,128)S(1)}, f32[2,4,8,128]{3,2,1,0:T(8,128)S(1)}, u32[]{:S(2)}, u32[]{:S(2)}) collective-permute-start(f32[2,4,8,128]{3,2,1,0:T(8,128)S(1)} %get-tuple-element.62.refs_2_), channel_id=1, source_target_pairs={{0,192},{64,0},{128,64},{192,128},{1,193},{65,1},{129,65},{193,129... | collective-permute-start | bytes 98312 | tf_op jit(solution)/shard_map/ppermute | solution.py:198
  110.5 24.8 %collective-permute-start.24 = (bf16[2,4,256,256]{3,2,1,0:T(8,128)(2,1)}, bf16[2,4,256,256]{3,2,1,0:T(8,128)(2,1)}, u32[]{:S(2)}, u32[]{:S(2)}) collective-permute-start(bf16[2,4,256,256]{3,2,1,0:T(8,128)(2,1)} %get-tuple-element.72.g0), channel_id=1, source_target_pairs={{0,64},{64,128},{128,192},{192,0},{1,65},{65,129},{129,193},{193,1... | collective-permute-start | bytes 3145736 | tf_op jit(solution)/shard_map/ppermute | solution.py:198
  111.4 23.9 %collective-permute-start.25 = (bf16[2,4,256,256]{3,2,1,0:T(8,128)(2,1)}, bf16[2,4,256,256]{3,2,1,0:T(8,128)(2,1)}, u32[]{:S(2)}, u32[]{:S(2)}) collective-permute-start(bf16[2,4,256,256]{3,2,1,0:T(8,128)(2,1)} %get-tuple-element.72.g0), channel_id=1, source_target_pairs={{0,192},{64,0},{128,64},{192,128},{1,193},{65,1},{129,65},{193,129... | collective-permute-start | bytes 3145736 | tf_op jit(solution)/shard_map/ppermute | solution.py:198
  115.0 48.3 %all-to-all-start.1 = ((bf16[64,2,16,256]{3,2,1,0:T(8,128)(2,1)}), bf16[64,2,16,256]{3,2,1,0:T(8,128)(2,1)S(1)}, u32[]{:S(2)}, u32[]{:S(2)}) async-start(bf16[64,2,16,256]{3,2,1,0:T(8,128)(2,1)} %copy-done.2), calls=%async_computation.1 | async-start | bytes 2097152 | tf_op jit(solution)/shard_map/all_to_all | solution.py:342
  137.9 31.3 %collective-permute-start.26 = (bf16[1,4,256,256]{3,2,1,0:T(8,128)(2,1)}, bf16[1,4,256,256]{3,2,1,0:T(8,128)(2,1)}, u32[]{:S(2)}, u32[]{:S(2)}) collective-permute-start(bf16[1,4,256,256]{3,2,1,0:T(8,128)(2,1)} %get-tuple-element.73), channel_id=1, source_target_pairs={{0,64},{64,128},{128,192},{192,0},{1,65},{65,129},{129,193},{193,1... | collective-permute-start | bytes 1572872 | tf_op jit(solution)/shard_map/ppermute | solution.py:198
  137.9 31.3 %collective-permute-start.27 = (bf16[1,4,256,256]{3,2,1,0:T(8,128)(2,1)}, bf16[1,4,256,256]{3,2,1,0:T(8,128)(2,1)}, u32[]{:S(2)}, u32[]{:S(2)}) collective-permute-start(bf16[1,4,256,256]{3,2,1,0:T(8,128)(2,1)} %get-tuple-element.74), channel_id=1, source_target_pairs={{0,192},{64,0},{128,64},{192,128},{1,193},{65,1},{129,65},{193,129... | collective-permute-start | bytes 1572872 | tf_op jit(solution)/shard_map/ppermute | solution.py:198
  163.9 14.0 %collective-permute-start.23 = (bf16[12,16,256]{2,1,0:T(8,128)(2,1)S(1)}, bf16[12,16,256]{2,1,0:T(8,128)(2,1)S(1)}, u32[]{:S(2)}, u32[]{:S(2)}) collective-permute-start(bf16[12,16,256]{2,1,0:T(8,128)(2,1)S(1)} %get-tuple-element.70), channel_id=1, source_target_pairs={{0,48},{1,49},{2,50},{3,51},{4,52},{5,53},{6,54},{7,55},{8,56},{9,... | collective-permute-start | bytes 294920 | tf_op jit(solution)/shard_map/ppermute | solution.py:202
  167.0 10.9 %collective-permute-start.22 = (bf16[12,16,256]{2,1,0:T(8,128)(2,1)S(1)}, bf16[12,16,256]{2,1,0:T(8,128)(2,1)S(1)}, u32[]{:S(2)}, u32[]{:S(2)}) collective-permute-start(bf16[12,16,256]{2,1,0:T(8,128)(2,1)S(1)} %get-tuple-element.69), channel_id=1, source_target_pairs={{0,32},{1,33},{2,34},{3,35},{4,36},{5,37},{6,38},{7,39},{8,40},{9,... | collective-permute-start | bytes 294920 | tf_op jit(solution)/shard_map/ppermute | solution.py:202
  168.3 9.6 %collective-permute-start.21 = (bf16[12,16,256]{2,1,0:T(8,128)(2,1)S(1)}, bf16[12,16,256]{2,1,0:T(8,128)(2,1)S(1)}, u32[]{:S(2)}, u32[]{:S(2)}) collective-permute-start(bf16[12,16,256]{2,1,0:T(8,128)(2,1)S(1)} %get-tuple-element.68), channel_id=1, source_target_pairs={{0,16},{1,17},{2,18},{3,19},{4,20},{5,21},{6,22},{7,23},{8,24},{9,... | collective-permute-start | bytes 294920 | tf_op jit(solution)/shard_map/ppermute | solution.py:202
  (5 other events, 10.8 us)

commit v6 on v5

--- a/solution.py
+++ b/solution.py
@@ -10,9 +10,9 @@
 EPSILON = 1e-06
 F32 = jnp.float32
 BF16 = jnp.bfloat16
-VMEM_LIMIT = 20 * 1024 * 1024
-RELAY_COST = 10_000_000_000
-COSTS = (10_000_000_000, 10_000_000_000, 5_000_000_000)
+VMEM_LIMIT = 24 * 1024 * 1024
+JOIN_COST = 10_000_000_000
+COSTS = (10_000_000_000, 10_000_000_000, 5_000_000_000, 10_000_000_000, 8_000_000_000)
 SMEM_SPEC = pl.BlockSpec(memory_space=pltpu.SMEM)
 
 
@@ -58,15 +58,28 @@
             out[rows] = (total + b[:, :, cols].astype(F32)).astype(BF16)
 
 
+def split_kernel(whole, first, second):
+    first[...] = whole[:1]
+    second[...] = whole[1:]
+
+
 def relay_kernel(before, behind, up, down):
     count = up.shape[0]
     up[...] = before[:count]
     down[...] = behind[count:]
 
 
-def product_kernel(meta, arrived, r0, r1, r2, r3, grad, sums, *products):
+def product_kernel(meta, arrived, r0, r1, r2, r3, grad, sums, *rest):
+    products, buffers, done = rest[:4], rest[4], rest[5]
     slots, groups = grad.shape[:2]
     per_row = arrived.shape[0] // groups
+    rights = (r0, r1, r3, r2)
+    copies = [
+        pltpu.make_async_copy(right, buffers.at[n], done.at[n]) for n, right in enumerate(rights)
+    ]
+    for copy in copies:
+        copy.start()
+    owns = []
     for s in range(slots):
         filled = meta[1 + slots + s] > 0
         parts = []
@@ -78,17 +91,32 @@
             wide = part.astype(F32)
             g_sum = g_sum + fold(wide * wide)
             parts.append(part)
-        own = jnp.concatenate(parts, 1)
-        for product, right in zip(products, (r0, r1, r2, r3)):
-            product[s] = dot(own, right[s]).astype(BF16)
+        owns.append(jnp.concatenate(parts, 1))
         sums[s] = g_sum
-
-
-def root_kernel(meta, diags, g_sums, y0, y1, y2, y3, l0, l1, l2, l3, out, sums, prods):
+    for n, product in enumerate((products[0], products[1], products[3], products[2])):
+        copies[n].wait()
+        for s in range(slots):
+            product[s] = dot(owns[s], buffers[n, s]).astype(BF16)
+
+
+def root_kernel(meta, diags, g_sums, y0, y1, y2, y3, *refs):
+    l0, l10, l11, l2, l3, out, sums, prods, buffers, done = refs
     me = meta[0]
-    slots, size, quarter = out.shape
+    slots, size, quarter = l0.shape
     reps = size // quarter
-    piece = quarter // (reps * reps)
+    piece = out.shape[2]
+    per_row = size // (reps * piece)
+    copies = []
+    for s in range(slots):
+        lefts = (l0.at[s], (l10, l11)[s].at[0], l2.at[s], l3.at[s])
+        copies.append(
+            [
+                pltpu.make_async_copy(left, buffers.at[s, t], done.at[s, t])
+                for t, left in enumerate(lefts)
+            ]
+        )
+        for copy in copies[s]:
+            copy.start()
     column = me * quarter + lax.broadcasted_iota(jnp.int32, (quarter, quarter), 1)
     for s in range(slots):
         keep = (column < meta[1 + s]).astype(F32)
@@ -100,12 +128,18 @@
                     source = pl.multiple_of((q * reps + p) * piece, piece)
                     target = pl.multiple_of(((t * reps + p) * reps + r) * piece, piece)
                     prods[pl.ds(target, piece), :] = rows[s, pl.ds(source, piece), :]
+        for copy in copies[s]:
+            copy.wait()
         p_sum = jnp.zeros((8, 128), F32)
         for n in range(reps):
             rows = slice(n * quarter, (n + 1) * quarter)
-            wide = jnp.concatenate([l0[s, rows], l1[s, rows], l2[s, rows], l3[s, rows]], 1)
+            wide = jnp.concatenate([buffers[s, t, rows] for t in range(reps)], 1)
             value = dot(wide, prods[...]) * keep
-            out[s, rows] = value
+            for p in range(per_row // reps):
+                for i in range(reps):
+                    first = (p * reps + i) * piece
+                    target = i * per_row + n * (per_row // reps) + p
+                    out[target, s] = value[first : first + piece].astype(BF16)
             p_sum = p_sum + fold(value * value)
         sums[s, 0] = p_sum
         sums[s, 1] = g_sums[s]
@@ -122,32 +156,64 @@
             out[w, s] = held[place[w * slots + s]]
 
 
-def collect_kernel(wanted, arrived, *outs):
+def collect_kernel(wanted, arrived, table, *outs):
+    high = table[...].astype(BF16).astype(F32)
+    middle = (table[...] - high).astype(BF16).astype(F32)
+    low = table[...] - high - middle
+    left = jnp.concatenate([high, middle], 0)
+    split = jnp.concatenate([left, jnp.concatenate([low, jnp.zeros_like(low)], 0)], 1)
     for n, out in enumerate(outs):
-        for j in range(out.shape[0]):
-            out[j] = arrived[wanted[n * out.shape[0] + j]]
-
-
-def scale_kernel(groups, per_row, meta, value, s0, s1, s2, s3, out, adds):
-    slots, size, _ = value.shape
-    piece = out.shape[2]
+        count = out.shape[0] - 1
+        for j in range(count):
+            out[j] = arrived[wanted[n * count + j]]
+        out[count] = split.astype(BF16)
+
+
+def scale_kernel(meta, s0, s1, s2, s3, table, adds):
+    slots = adds.shape[1]
+    size = 4 * 256
+    lane = lax.broadcasted_iota(jnp.int32, table.shape, 1)
     total = s0[...] + s1[...] + s2[...] + s3[...]
+    row = jnp.zeros(table.shape, F32)
     for s in range(slots):
         p_square = jnp.sum(total[s, 0], keepdims=True)
         g_square = jnp.sum(total[s, 1], keepdims=True)
         scale = jnp.sqrt(g_square / (p_square + EPSILON))
+        row = row + jnp.where(lane == meta[1 + 2 * slots] * slots + s, scale, 0.0)
         for side, width in enumerate((jnp.int32(size), meta[1 + s])):
             trace = DECAY * total[s, 2 + side] + (1.0 - DECAY) * g_square
             adds[side, s] = SHRINKAGE * trace / jnp.full((8, 128), width).astype(F32)
-        for p in range(per_row):
-            for i in range(groups):
-                first = (p * groups + i) * piece
-                out[i * per_row + p, s] = (value[s, first : first + piece, :] * scale).astype(BF16)
-
-
-def stat_kernel(meta, adds, g0, g1, g3, far0, far1, left, right, left_new, right_new, whole):
+    table[...] = row
+
+
+def final_kernel(mine, group, b0, b1, b2, b3, out):
+    groups, count = out.shape[:2]
+    total = jnp.zeros((8, 128), F32)
+    for block in (b0, b1, b2, b3):
+        split = block[count].astype(F32)
+        total = total + split[:8, :128] + split[8:, :128] + split[:8, 128:]
+    lane = lax.broadcasted_iota(jnp.int32, (1, 128), 1)
+    for j in range(count):
+        scale = jnp.sum(jnp.where(lane == mine[j], total[:1], 0.0), axis=1, keepdims=True)
+        for t, block in enumerate((b0, b1, b2, b3)):
+            g = lax.rem(group[0] + groups - t, groups)
+            out[g, j] = (block[j].astype(F32) * scale).astype(BF16)
+
+
+def stat_kernel(meta, adds, in0, in1, in3, in_far0, in_far1, left_stat, right_stat, *refs):
+    left_new, right_new, whole, g0, g1, g3, far0, far1, left, right, done = refs
     me = meta[0]
     slots, quarter, size = left.shape
+    sources = (in0, in1, in3, in_far0, in_far1, left_stat, right_stat)
+    targets = (g0, g1, g3, far0, far1, left, right)
+    copies = [
+        pltpu.make_async_copy(source, target, done.at[n])
+        for n, (source, target) in enumerate(zip(sources, targets))
+    ]
+    for copy in copies:
+        copy.start()
+    for copy in copies[:5]:
+        copy.wait()
     reps = size // quarter
     piece = quarter // (reps * reps)
     keep = 1.0 - SHRINKAGE
@@ -165,6 +231,9 @@
                         i, p * piece : (p + 1) * piece, :
                     ]
         mine = whole[pl.ds(first, quarter), :]
+        if s == 0:
+            for copy in copies[5:]:
+                copy.wait()
         for n in range(reps):
             cols = slice(n * quarter, (n + 1) * quarter)
             gram = dot(mine, whole[cols, :], (1, 1))
@@ -224,10 +293,13 @@
         in_specs=[vmem] * 4,
         out_shape=[jax.ShapeDtypeStruct((half, piece, block_size), BF16)] * 2,
         compiler_params=params,
-        cost_estimate=pl.CostEstimate(flops=RELAY_COST, bytes_accessed=0, transcendentals=0),
+        cost_estimate=pl.CostEstimate(flops=JOIN_COST, bytes_accessed=0, transcendentals=0),
         name="join",
     )(up[:half], relay_up, down[half:], relay_down)
     joint_up, joint_down = turn_x(joint_up, 1), turn_x(joint_down, 3)
+    joint_up, joint_down, left_root, right_root = lax.optimization_barrier(
+        (joint_up, joint_down, left_root, right_root)
+    )
     held = pl.pallas_call(
         sum_kernel,
         in_specs=[SMEM_SPEC] + [vmem] * 5,
@@ -235,7 +307,6 @@
         compiler_params=params,
         name="sum",
     )(me_group[None], rows_of(me_rep), joint_up, direct_down, direct_up, joint_down)
-    first, left_root, right_root = lax.optimization_barrier((held[0], left_root, right_root))
 
     my_blocks = lax.dynamic_slice_in_dim(block_ids, me_work * slots, slots)
     my_filled = lax.dynamic_slice_in_dim(filled, me_work * slots, slots)
@@ -247,7 +318,7 @@
         axis=1,
     )
     my_width = jnp.where(my_filled, looked_up, block_size)
-    meta = jnp.concatenate([me_rep[None], my_width, my_filled]).astype(jnp.int32)
+    meta = jnp.concatenate([me_rep[None], my_width, my_filled, me_work[None]]).astype(jnp.int32)
     local = jnp.arange(quarter, dtype=jnp.int32)
     unit = (local[:, None] == local[None, :]).astype(F32)
     within_width = (me_rep * quarter + local[None, :] < my_width[:, None]).astype(F32)
@@ -268,13 +339,14 @@
             in_specs=[vmem] * 2,
             out_shape=[jax.ShapeDtypeStruct(shape, BF16)] * 2,
             compiler_params=params,
-            cost_estimate=pl.CostEstimate(flops=RELAY_COST, bytes_accessed=0, transcendentals=0),
+            cost_estimate=pl.CostEstimate(flops=COSTS[3], bytes_accessed=0, transcendentals=0),
             name="relay",
         )(before, behind)
         return (turn_x(up, 1), turn_x(down, 3))
 
+    anywhere = pl.BlockSpec(memory_space=pl.ANY)
+
     def hold(value, cost):
-        anywhere = pl.BlockSpec(memory_space=pl.ANY)
         return pl.pallas_call(
             lambda before, after: None,
             in_specs=[anywhere],
@@ -287,10 +359,19 @@
 
     r_prev, r_next = hold(turn_x(right_root, 1), COSTS[2]), hold(turn_x(right_root, 3), COSTS[2])
     r_prev, r_next = lax.optimization_barrier((r_prev, r_next))
-    l_prev, l_next = hold(turn_x(left_root, 1), COSTS[0]), hold(turn_x(left_root, 3), COSTS[1])
+    left0, left1 = pl.pallas_call(
+        split_kernel,
+        in_specs=[vmem],
+        out_shape=[jax.ShapeDtypeStruct((1, block_size, quarter), BF16)] * slots,
+        compiler_params=params,
+        name="split",
+    )(left_root)
+    l_prev0, l_next = hold(turn_x(left0, 1), COSTS[0]), hold(turn_x(left_root, 3), COSTS[1])
+    l_prev0, left1 = lax.optimization_barrier((l_prev0, left1))
+    l_prev1 = turn_x(left1, 1)
     r_far, l_far = turn_x(r_prev, 1), turn_x(l_next, 3)
 
-    held = [first] + [turn_group(held[shift], shift) for shift in range(1, groups)]
+    held = [held[0]] + [turn_group(held[shift], shift) for shift in range(1, groups)]
     place = ((me_group - block_ids // ncols) % groups) * ncols + block_ids % ncols
     outgoing = pl.pallas_call(
         spread_kernel,
@@ -302,11 +383,15 @@
     )(place.astype(jnp.int32), *held)
     incoming = lax.all_to_all(outgoing, "fsdp", split_axis=0, concat_axis=0, tiled=True)
 
-    incoming, l_prev, l_next = lax.optimization_barrier((incoming, l_prev, l_next))
+    incoming, l_prev0, l_next = lax.optimization_barrier((incoming, l_prev0, l_next))
     quarters = jax.ShapeDtypeStruct((slots, quarter, quarter), BF16)
     g_mine, g_sums, *products = pl.pallas_call(
         product_kernel,
-        in_specs=[SMEM_SPEC] + [vmem] * 5,
+        in_specs=[SMEM_SPEC, vmem] + [anywhere] * 4,
+        scratch_shapes=[
+            pltpu.VMEM((reps, slots, block_size, quarter), BF16),
+            pltpu.SemaphoreType.DMA((reps,)),
+        ],
         out_shape=[
             jax.ShapeDtypeStruct((slots, groups, quarter, quarter), BF16),
             jax.ShapeDtypeStruct((slots, 8, 128), F32),
@@ -316,41 +401,59 @@
         name="right_products",
     )(meta, incoming, right_root, r_prev, r_far, r_next)
     products = [products[0]] + [turn_x(products[n], reps - n) for n in range(1, reps)]
-    precond, sums = pl.pallas_call(
+    returning, sums = pl.pallas_call(
         root_kernel,
-        in_specs=[SMEM_SPEC] * 2 + [vmem] * 9,
+        in_specs=[SMEM_SPEC] * 2 + [vmem] * 5 + [anywhere] * 5,
         out_shape=[
-            jax.ShapeDtypeStruct((slots, block_size, quarter), F32),
+            jax.ShapeDtypeStruct((workers, slots, piece, quarter), BF16),
             jax.ShapeDtypeStruct((slots, 4, 8, 128), F32),
         ],
-        scratch_shapes=[pltpu.VMEM((block_size, quarter), BF16)],
+        scratch_shapes=[
+            pltpu.VMEM((block_size, quarter), BF16),
+            pltpu.VMEM((slots, reps, block_size, quarter), BF16),
+            pltpu.SemaphoreType.DMA((slots, reps)),
+        ],
         compiler_params=params,
         name="left_products",
-    )(meta, diag_own, g_sums, *products, left_root, l_prev, l_far, l_next)
+    )(meta, diag_own, g_sums, *products, left_root, l_prev0, l_prev1, l_far, l_next)
+    returning, sums, g_mine = lax.optimization_barrier((returning, sums, g_mine))
+    arrived = lax.all_to_all(returning, "fsdp", split_axis=0, concat_axis=0, tiled=True)
+    arrived = arrived.reshape(workers * slots, piece, quarter)
     all_sums = [sums] + [turn_x(sums, shift) for shift in (1, 2, 3)]
-    *all_sums, g_mine = lax.optimization_barrier((*all_sums, g_mine))
-    returning, adds = pl.pallas_call(
-        lambda *refs: scale_kernel(groups, per_row, *refs),
-        in_specs=[SMEM_SPEC] + [vmem] * 5,
+    table, adds = pl.pallas_call(
+        scale_kernel,
+        in_specs=[SMEM_SPEC] + [vmem] * 4,
         out_shape=[
-            jax.ShapeDtypeStruct((workers, slots, piece, quarter), BF16),
+            jax.ShapeDtypeStruct((8, workers * slots), F32),
             jax.ShapeDtypeStruct((2, slots, 8, 128), F32),
         ],
         compiler_params=params,
+        cost_estimate=pl.CostEstimate(flops=COSTS[4], bytes_accessed=0, transcendentals=0),
         name="graft_scale",
-    )(meta, precond, *all_sums)
-    arrived = lax.all_to_all(returning, "fsdp", split_axis=0, concat_axis=0, tiled=True)
-    arrived = arrived.reshape(workers * slots, piece, quarter)
-
+    )(meta, *all_sums)
     g_prev = turn_x(g_mine, 1)
     g_next = turn_x(g_mine, reps - 1)
+    g_prev, g_next, table = lax.optimization_barrier((g_prev, g_next, table))
+    distance = 1
+    while distance < per_row:
+        pairs = [(a, a ^ distance) for a in range(workers)]
+        table = table + lax.ppermute(table, "fsdp", pairs)
+        distance *= 2
+
     g_far = relay(g_prev, g_next)
     left_new, right_new = pl.pallas_call(
         stat_kernel,
-        in_specs=[SMEM_SPEC] + [vmem] * 8,
+        in_specs=[SMEM_SPEC, vmem] + [anywhere] * 7,
         out_shape=[jax.ShapeDtypeStruct(left_stat.shape, F32)] * 2,
-        scratch_shapes=[pltpu.VMEM((block_size, block_size), BF16)],
-        compiler_params=params,
+        scratch_shapes=[
+            pltpu.VMEM((block_size, block_size), BF16),
+            *[pltpu.VMEM(g_mine.shape, BF16)] * 3,
+            *[pltpu.VMEM(g_far[0].shape, BF16)] * 2,
+            pltpu.VMEM(left_stat.shape, F32),
+            pltpu.VMEM(right_stat.shape, F32),
+            pltpu.SemaphoreType.DMA((7,)),
+        ],
+        compiler_params=pltpu.CompilerParams(vmem_limit_bytes=56 * 1024 * 1024),
         cost_estimate=pl.CostEstimate(
             flops=8 * block_size * block_size * quarter,
             bytes_accessed=40 * block_size * quarter * 2,
@@ -363,16 +466,20 @@
     wanted = jnp.take(slot_ids, (block + me_group * ncols) % (groups * ncols), mode="clip")
     back = pl.pallas_call(
         collect_kernel,
-        in_specs=[SMEM_SPEC, pl.BlockSpec(memory_space=pltpu.VMEM)],
-        out_shape=[jax.ShapeDtypeStruct((ncols, piece, quarter), BF16)] * groups,
+        in_specs=[SMEM_SPEC, vmem, vmem],
+        out_shape=[jax.ShapeDtypeStruct((ncols + 1, piece, quarter), BF16)] * groups,
         compiler_params=params,
         name="collect",
-    )(wanted, arrived)
+    )(wanted, arrived, table)
     back = [back[0]] + [turn_group(back[shift], shift) for shift in range(1, groups)]
-    back = jnp.stack(back)
-    order = (me_group - jnp.arange(groups, dtype=jnp.int32)) % groups
-    back = jnp.take(back, order, axis=0, mode="clip")
-    update = jnp.transpose(back, (0, 2, 1, 3)).reshape(rows_dev, ncols, quarter)
+    update = pl.pallas_call(
+        final_kernel,
+        in_specs=[SMEM_SPEC] * 2 + [vmem] * groups,
+        out_shape=jax.ShapeDtypeStruct((groups, ncols, piece, quarter), BF16),
+        compiler_params=params,
+        name="final",
+    )(wanted[:ncols], me_group[None], *back)
+    update = jnp.transpose(update, (0, 2, 1, 3)).reshape(rows_dev, ncols, quarter)
     return (update, left_new, right_new)
 
 

time: 181 us -> 176 us (0.972)
  waiting for transfers between devices: 68.8 us -> 59 us
  Pallas kernels: 20.5 us -> 23.3 us
    all_to_all x1, waiting for transfers between devices: 21.9 us -> 0.01 us  [on_device(): lax.all_to_all(returning, 'fsdp', split_axis=0, concat_axis=0, tiled=True)]
    ppermute x22 -> x23, waiting for transfers between devices: 29.7 us -> 42.8 us  [turn_x(): return lax.ppermute(value, 'replica', pairs)]
    all_to_all x1, starting transfers between devices: 20.3 us -> 12.4 us  [on_device(): lax.all_to_all(returning, 'fsdp', split_axis=0, concat_axis=0, tiled=True)]
    ppermute x0 -> x4, starting transfers between devices: none -> 6.64 us  [on_device(): table = table + lax.ppermute(table, 'fsdp', pairs)]
    ppermute x0 -> x4, waiting for transfers between devices: none -> 6.17 us  [on_device(): table = table + lax.ppermute(table, 'fsdp', pairs)]
    all_to_all x1, waiting for transfers between devices: 14.2 us -> 9.57 us  [on_device(): lax.all_to_all(outgoing, 'fsdp', split_axis=0, concat_axis=0, tiled=True)]
    pallas_call x5 -> x7, Pallas kernels: 16.1 us -> 18.8 us  [the longest x1 8.93 us: on_device(): pl.pallas_call(stat_kernel, in_specs=[SMEM_SPEC, vmem] + [anywhere] * 7,...]
    ppermute x22 -> x23, starting transfers between devices: 25.6 us -> 28.1 us  [turn_x(): return lax.ppermute(value, 'replica', pairs)]
  transfers between devices with their start and end apart: 30 -> 35, of which waited for: 13 -> 15; matrix products, arithmetic and copies ran while one was open for 3% -> 2% of each run, Pallas kernels for 9% -> 11%
where the time goes in v6:
time: 176 us; the launch traced here: 173 us
  starting transfers between devices  77.1 us (44%)
  waiting for transfers between devices  59 us (34%)
  Pallas kernels  23.3 us (13%)
  local copies, waits for them, and re-layouts  7.38 us (4%)
  other arithmetic  5.06 us (3%)
    ppermute x23, waiting for transfers between devices, turn_x(): return lax.ppermute(value, 'replica', pairs)  42.8 us
    ppermute x23, starting transfers between devices, turn_x(): return lax.ppermute(value, 'replica', pairs)  28.1 us
    ppermute x6, starting transfers between devices, turn_group(): return lax.ppermute(value, 'fsdp', pairs)  16 us
    all_to_all x1, starting transfers between devices, on_device(): lax.all_to_all(outgoing, 'fsdp', split_axis=0, concat_axis=0, tiled=True)  14 us
    all_to_all x1, starting transfers between devices, on_device(): lax.all_to_all(returning, 'fsdp', split_axis=0, concat_axis=0, tiled=True)  12.4 us
    all_to_all x1, waiting for transfers between devices, on_device(): lax.all_to_all(outgoing, 'fsdp', split_axis=0, concat_axis=0, tiled=True)  9.57 us
    pallas_call x1, Pallas kernels, on_device(): pl.pallas_call(stat_kernel, in_specs=[SMEM_SPEC, vmem] + [anywhere] * 7,...  8.93 us
    ppermute x4, starting transfers between devices, on_device(): table = table + lax.ppermute(table, 'fsdp', pairs)  6.64 us
  transfers between devices with their start and end apart: 35, of which 15 were waited for; matrix products, arithmetic and copies ran while one was open for 2% of the time, Pallas kernels for 11%

profile of v6, /device:TPU:1, one launch (start us, length us, event | category | flops | bytes accessed | tf_op | source)
XLA Modules:
  0.0 172.8 jit_solution(9698177901249558782)
XLA Ops:
  1.4 1.8 %fusion = bf16[64,12,1024]{2,0,1:T(8,128)(2,1)S(1)} fusion(bf16[1,64,12,1024]{3,1,2,0:T(8,128)(2,1)} %param.7, f32[12,1024]{1,0:T(8,128)S(1)} %fusion.2), kind=kLoop, calls=%fused_computation.2 | loop fusion | flops 2359296 | bytes 3194880 | tf_op jit(solution)/shard_map/convert_element_type | solution.py:276
  3.5 2.1 %collective-permute-start = (bf16[6,16,1024]{2,1,0:T(8,128)(2,1)S(1)}, bf16[6,16,1024]{2,1,0:T(8,128)(2,1)S(1)}, u32[]{:S(2)}, u32[]{:S(2)}) collective-permute-start(bf16[6,16,1024]{2,1,0:T(8,128)(2,1)S(1)} %get-tuple-element.102), channel_id=1, source_target_pairs={{0,64},{64,128},{128,192},{192,0},{1,65},{65,129},{129,193},{193,1... | collective-permute-start | bytes 589832 | tf_op jit(solution)/shard_map/ppermute | solution.py:267
  10.8 1.6 collective-permute-start.2
  13.7 6.2 %collective-permute-done.2.top0 = bf16[6,16,1024]{2,1,0:T(8,128)(2,1)S(1)} collective-permute-done((bf16[6,16,1024]{2,1,0:T(8,128)(2,1)S(1)}, bf16[6,16,1024]{2,1,0:T(8,128)(2,1)S(1)}, u32[]{:S(2)}, u32[]{:S(2)}) %collective-permute-start.2) | collective-permute-done | bytes 196640 | tf_op jit(solution)/shard_map/ppermute | solution.py:267
  20.1 2.6 %collective-permute-start.12 = (bf16[2,1024,256]{2,1,0:T(8,128)(2,1)}, bf16[2,1024,256]{2,1,0:T(8,128)(2,1)}, u32[]{:S(2)}, u32[]{:S(2)}) collective-permute-start(bf16[2,1024,256]{2,1,0:T(8,128)(2,1)} %r0), channel_id=1, source_target_pairs={{0,192},{64,0},{128,64},{192,128},{1,193},{65,1},{129,65},{193,129... | collective-permute-start | bytes 3145736 | tf_op jit(solution)/shard_map/ppermute | solution.py:267
  23.2 1.8 %collective-permute-start.6 = (bf16[12,16,256]{2,1,0:T(8,128)(2,1)S(1)}, bf16[12,16,256]{2,1,0:T(8,128)(2,1)S(1)}, u32[]{:S(2)}, u32[]{:S(2)}) collective-permute-start(bf16[12,16,256]{2,1,0:T(8,128)(2,1)S(1)} %get-tuple-element.51), channel_id=1, source_target_pairs={{0,16},{1,17},{2,18},{3,19},{4,20},{5,21},{6,22},{7,23},{8,24},{9,... | collective-permute-start | bytes 294920 | tf_op jit(solution)/shard_map/ppermute | solution.py:271
  25.0 5.2 %collective-permute-start.7 = (bf16[12,16,256]{2,1,0:T(8,128)(2,1)S(1)}, bf16[12,16,256]{2,1,0:T(8,128)(2,1)S(1)}, u32[]{:S(2)}, u32[]{:S(2)}) collective-permute-start(bf16[12,16,256]{2,1,0:T(8,128)(2,1)S(1)} %get-tuple-element.52), channel_id=1, source_target_pairs={{0,32},{1,33},{2,34},{3,35},{4,36},{5,37},{6,38},{7,39},{8,40},{9,... | collective-permute-start | bytes 294920 | tf_op jit(solution)/shard_map/ppermute | solution.py:271
  30.2 2.4 %collective-permute-start.8 = (bf16[12,16,256]{2,1,0:T(8,128)(2,1)S(1)}, bf16[12,16,256]{2,1,0:T(8,128)(2,1)S(1)}, u32[]{:S(2)}, u32[]{:S(2)}) collective-permute-start(bf16[12,16,256]{2,1,0:T(8,128)(2,1)S(1)} %get-tuple-element.53), channel_id=1, source_target_pairs={{0,48},{1,49},{2,50},{3,51},{4,52},{5,53},{6,54},{7,55},{8,56},{9,... | collective-permute-start | bytes 294920 | tf_op jit(solution)/shard_map/ppermute | solution.py:271
  32.6 1.5 collective-permute-start.10
  36.3 1.6 spread.1
  37.9 14.0 %all-to-all-start = ((bf16[64,2,16,256]{3,2,1,0:T(8,128)(2,1)}), bf16[64,2,16,256]{3,2,1,0:T(8,128)(2,1)S(1)}, u32[]{:S(2)}, u32[]{:S(2)}) async-start(bf16[64,2,16,256]{3,2,1,0:T(8,128)(2,1)} %spread.1), calls=%async_computation | async-start | bytes 2097152 | tf_op jit(solution)/shard_map/all_to_all | solution.py:384
  53.0 12.3 %collective-permute-done.10.before = bf16[2,1024,256]{2,1,0:T(8,128)(2,1)} collective-permute-done((bf16[2,1024,256]{2,1,0:T(8,128)(2,1)S(1)}, bf16[2,1024,256]{2,1,0:T(8,128)(2,1)}, u32[]{:S(2)}, u32[]{:S(2)}) %collective-permute-start.10) | collective-permute-done | bytes 1048608 | tf_op jit(solution)/shard_map/ppermute | solution.py:267
  65.3 3.5 %collective-permute-start.18 = (bf16[2,1024,256]{2,1,0:T(8,128)(2,1)}, bf16[2,1024,256]{2,1,0:T(8,128)(2,1)}, u32[]{:S(2)}, u32[]{:S(2)}) collective-permute-start(bf16[2,1024,256]{2,1,0:T(8,128)(2,1)} %hold.5.refs_4_), channel_id=1, source_target_pairs={{0,192},{64,0},{128,64},{192,128},{1,193},{65,1},{129,65},{193,129... | collective-permute-start | bytes 3145736 | tf_op jit(solution)/shard_map/ppermute | solution.py:267
  70.3 9.6 %all-to-all-done.arrived = bf16[64,2,16,256]{3,2,1,0:T(8,128)(2,1)S(1)} async-done(((bf16[64,2,16,256]{3,2,1,0:T(8,128)(2,1)}), bf16[64,2,16,256]{3,2,1,0:T(8,128)(2,1)S(1)}, u32[]{:S(2)}, u32[]{:S(2)}) %all-to-all-start) | async-done | bytes 1048608 | tf_op jit(solution)/shard_map/all_to_all | solution.py:384
  82.1 3.6 %right_products.1 = (bf16[2,4,256,256]{3,2,1,0:T(8,128)(2,1)S(1)}, f32[2,8,128]{2,1,0:T(8,128)S(1)}, bf16[2,256,256]{2,1,0:T(8,128)(2,1)S(1)}, bf16[2,256,256]{2...) custom-call(s32[6]{0:T(128)S(1)} %pad_add_fusion.meta, ...), custom_call_target="tpu_custom_call" | custom-call | tf_op jit(solution)/shard_map/right_products/pallas_call | solution.py:388
  85.7 2.8 %collective-permute-start.14 = (bf16[2,256,256]{2,1,0:T(8,128)(2,1)S(1)}, bf16[2,256,256]{2,1,0:T(8,128)(2,1)S(1)}, u32[]{:S(2)}, u32[]{:S(2)}) collective-permute-start(bf16[2,256,256]{2,1,0:T(8,128)(2,1)S(1)} %get-tuple-element.64), channel_id=1, source_target_pairs={{0,192},{64,0},{128,64},{192,128},{1,193},{65,1},{129,65},{193,129... | collective-permute-start | bytes 786440 | tf_op jit(solution)/shard_map/ppermute | solution.py:267
  90.2 5.4 %collective-permute-done.14.y1 = bf16[2,256,256]{2,1,0:T(8,128)(2,1)S(1)} collective-permute-done((bf16[2,256,256]{2,1,0:T(8,128)(2,1)S(1)}, bf16[2,256,256]{2,1,0:T(8,128)(2,1)S(1)}, u32[]{:S(2)}, u32[]{:S(2)}) %collective-permute-start.14) | collective-permute-done | bytes 262176 | tf_op jit(solution)/shard_map/ppermute | solution.py:267
  96.2 7.0 %collective-permute-done.16.y3 = bf16[2,256,256]{2,1,0:T(8,128)(2,1)S(1)} collective-permute-done((bf16[2,256,256]{2,1,0:T(8,128)(2,1)S(1)}, bf16[2,256,256]{2,1,0:T(8,128)(2,1)S(1)}, u32[]{:S(2)}, u32[]{:S(2)}) %collective-permute-start.16) | collective-permute-done | bytes 262176 | tf_op jit(solution)/shard_map/ppermute | solution.py:267
  103.1 3.5 %left_products.1 = (bf16[64,2,16,256]{3,2,1,0:T(8,128)(2,1)S(1)}, f32[2,4,8,128]{3,2,1,0:T(8,128)S(1)}) custom-call(s32[6]{0:T(128)S(1)} %pad_add_fusion.meta, f32[2,2]{1,0:T(2,128)S(1)} %pad_maximum_fusion.diags, f32[2,8,128]{2,1,0:T(8,128)S(1)} %get-tuple-element.62.g_sums, bf16[2,256,256]{2,1,0:T(8,128)(2,1)S(1)} %get-tuple-element.63.y0, ...), custom_call_target="tpu_custom_call" | custom-call | tf_op jit(solution)/shard_map/left_products/pallas_call | solution.py:404
  107.6 2.7 %collective-permute-start.20 = (bf16[2,4,256,256]{3,2,1,0:T(8,128)(2,1)S(1)}, bf16[2,4,256,256]{3,2,1,0:T(8,128)(2,1)}, u32[]{:S(2)}, u32[]{:S(2)}) collective-permute-start(bf16[2,4,256,256]{3,2,1,0:T(8,128)(2,1)S(1)} %get-tuple-element.74.in0), channel_id=1, source_target_pairs={{0,192},{64,0},{128,64},{192,128},{1,193},{65,1},{129,65},{193,129... | collective-permute-start | bytes 3145736 | tf_op jit(solution)/shard_map/ppermute | solution.py:267
  111.4 1.5 collective-permute-start.23
  112.9 12.4 %all-to-all-start.1 = ((bf16[64,2,16,256]{3,2,1,0:T(8,128)(2,1)}), bf16[64,2,16,256]{3,2,1,0:T(8,128)(2,1)S(1)}, u32[]{:S(2)}, u32[]{:S(2)}) async-start(bf16[64,2,16,256]{3,2,1,0:T(8,128)(2,1)} %copy-done.3), calls=%async_computation.1 | async-start | bytes 2097152 | tf_op jit(solution)/shard_map/all_to_all | solution.py:420
  125.3 8.6 %collective-permute-done.21.s1 = f32[2,4,8,128]{3,2,1,0:T(8,128)S(1)} collective-permute-done((f32[2,4,8,128]{3,2,1,0:T(8,128)S(1)}, f32[2,4,8,128]{3,2,1,0:T(8,128)S(1)}, u32[]{:S(2)}, u32[]{:S(2)}) %collective-permute-start.21) | collective-permute-done | bytes 32800 | tf_op jit(solution)/shard_map/ppermute | solution.py:267
  135.2 2.6 %relay.1 = (bf16[1,4,256,256]{3,2,1,0:T(8,128)(2,1)}, bf16[1,4,256,256]{3,2,1,0:T(8,128)(2,1)}) custom-call(bf16[2,4,256,256]{3,2,1,0:T(8,128)(2,1)S(1)} %collective-permute-done.19.before.in1, bf16[2,4,256,256]{3,2,1,0:T(8,128)(2,1)} %collective-permute-done.20.behind.in3), custom_call_target="tpu_custom_call" | custom-call | flops 10000000000 | tf_op jit(solution)/shard_map/relay/pallas_call | solution.py:337
  137.8 2.7 %collective-permute-start.32 = (bf16[1,4,256,256]{3,2,1,0:T(8,128)(2,1)}, bf16[1,4,256,256]{3,2,1,0:T(8,128)(2,1)S(1)}, u32[]{:S(2)}, u32[]{:S(2)}) collective-permute-start(bf16[1,4,256,256]{3,2,1,0:T(8,128)(2,1)} %get-tuple-element.86), channel_id=1, source_target_pairs={{0,192},{64,0},{128,64},{192,128},{1,193},{65,1},{129,65},{193,129... | collective-permute-start | bytes 1572872 | tf_op jit(solution)/shard_map/ppermute | solution.py:267
  140.5 2.4 %collective-permute-start.24 = (f32[8,128]{1,0:T(8,128)S(1)}, f32[8,128]{1,0:T(8,128)S(1)}, u32[]{:S(2)}, u32[]{:S(2)}) collective-permute-start(f32[8,128]{1,0:T(8,128)S(1)} %get-tuple-element.77), channel_id=1, source_target_pairs={{0,1},{1,0},{2,3},{3,2},{4,5},{5,4},{6,7},{7,6},{8,9},{9,8},{10,11... | collective-permute-start | bytes 12296 | tf_op jit(solution)/shard_map/ppermute | solution.py:440
  144.6 1.9 %collective-permute-done.25 = f32[8,128]{1,0:T(8,128)S(1)} collective-permute-done((f32[8,128]{1,0:T(8,128)S(1)}, f32[8,128]{1,0:T(8,128)S(1)}, u32[]{:S(2)}, u32[]{:S(2)}) %collective-permute-start.25) | collective-permute-done | bytes 4128 | tf_op jit(solution)/shard_map/ppermute | solution.py:440
  146.5 2.3 %collective-permute-start.26 = (f32[8,128]{1,0:T(8,128)S(1)}, f32[8,128]{1,0:T(8,128)S(1)}, u32[]{:S(2)}, u32[]{:S(2)}) collective-permute-start(f32[8,128]{1,0:T(8,128)S(1)} %add.135), channel_id=1, source_target_pairs={{0,4},{1,5},{2,6},{3,7},{4,0},{5,1},{6,2},{7,3},{8,12},{9,13},{10,... | collective-permute-start | bytes 12296 | tf_op jit(solution)/shard_map/ppermute | solution.py:440
  148.9 2.5 %collective-permute-done.26 = f32[8,128]{1,0:T(8,128)S(1)} collective-permute-done((f32[8,128]{1,0:T(8,128)S(1)}, f32[8,128]{1,0:T(8,128)S(1)}, u32[]{:S(2)}, u32[]{:S(2)}) %collective-permute-start.26) | collective-permute-done | bytes 4128 | tf_op jit(solution)/shard_map/ppermute | solution.py:440
  155.4 3.7 %collective-permute-start.29 = (bf16[13,16,256]{2,1,0:T(8,128)(2,1)S(1)}, bf16[13,16,256]{2,1,0:T(8,128)(2,1)S(1)}, u32[]{:S(2)}, u32[]{:S(2)}) collective-permute-start(bf16[13,16,256]{2,1,0:T(8,128)(2,1)S(1)} %get-tuple-element.80), channel_id=1, source_target_pairs={{0,32},{1,33},{2,34},{3,35},{4,36},{5,37},{6,38},{7,39},{8,40},{9,... | collective-permute-start | bytes 319496 | tf_op jit(solution)/shard_map/ppermute | solution.py:271
  159.1 2.3 %collective-permute-start.30 = (bf16[13,16,256]{2,1,0:T(8,128)(2,1)S(1)}, bf16[13,16,256]{2,1,0:T(8,128)(2,1)S(1)}, u32[]{:S(2)}, u32[]{:S(2)}) collective-permute-start(bf16[13,16,256]{2,1,0:T(8,128)(2,1)S(1)} %get-tuple-element.81), channel_id=1, source_target_pairs={{0,48},{1,49},{2,50},{3,51},{4,52},{5,53},{6,54},{7,55},{8,56},{9,... | collective-permute-start | bytes 319496 | tf_op jit(solution)/shard_map/ppermute | solution.py:271
  162.4 8.9 %stat_update.1 = (f32[2,256,1024]{2,1,0:T(8,128)}, f32[2,256,1024]{2,1,0:T(8,128)}) custom-call(s32[6]{0:T(128)} %copy-done.7, f32[2,2,8,128]{3,2,1,0:T(8,128)} %copy-done.6, bf16[2,4,256,256]{3,2,1,0:T(8,128)(2,1)} %copy-done.1, bf16[2,4,256,256]{3,2,1,0:T(8,128)(2,1)} %copy-done.2, bf16[2,4,256,256]{3,2,1,0:T(8,128)(2,1)} %collective-permute-done.20.behind.in3, ...), custom_call_target="tpu_custom_call" | custom-call | flops 2147483648 | bytes 20971520 | tf_op jit(solution)/shard_map/stat_update/pallas_call | solution.py:444
  (108 shorter events, 29.1 us)
Async XLA Ops:
  3.5 6.4 %collective-permute-start = (bf16[6,16,1024]{2,1,0:T(8,128)(2,1)S(1)}, bf16[6,16,1024]{2,1,0:T(8,128)(2,1)S(1)}, u32[]{:S(2)}, u32[]{:S(2)}) collective-permute-start(bf16[6,16,1024]{2,1,0:T(8,128)(2,1)S(1)} %get-tuple-element.102), channel_id=1, source_target_pairs={{0,64},{64,128},{128,192},{192,0},{1,65},{65,129},{129,193},{193,1... | collective-permute-start | bytes 589832 | tf_op jit(solution)/shard_map/ppermute | solution.py:267
  5.6 5.1 %collective-permute-start.1 = (bf16[6,16,1024]{2,1,0:T(8,128)(2,1)S(1)}, bf16[6,16,1024]{2,1,0:T(8,128)(2,1)S(1)}, u32[]{:S(2)}, u32[]{:S(2)}) collective-permute-start(bf16[6,16,1024]{2,1,0:T(8,128)(2,1)S(1)} %get-tuple-element.101), channel_id=1, source_target_pairs={{0,192},{64,0},{128,64},{192,128},{1,193},{65,1},{129,65},{193,129... | collective-permute-start | bytes 589832 | tf_op jit(solution)/shard_map/ppermute | solution.py:267
  7.0 16.0 %collective-permute-start.4 = (bf16[6,16,1024]{2,1,0:T(8,128)(2,1)S(1)}, bf16[6,16,1024]{2,1,0:T(8,128)(2,1)S(1)}, u32[]{:S(2)}, u32[]{:S(2)}) collective-permute-start(bf16[6,16,1024]{2,1,0:T(8,128)(2,1)S(1)} %get-tuple-element.99), channel_id=1, source_target_pairs={{0,192},{64,0},{128,64},{192,128},{1,193},{65,1},{129,65},{193,129... | collective-permute-start | bytes 589832 | tf_op jit(solution)/shard_map/ppermute | solution.py:267
  8.5 14.5 %collective-permute-start.5 = (bf16[6,16,1024]{2,1,0:T(8,128)(2,1)S(1)}, bf16[6,16,1024]{2,1,0:T(8,128)(2,1)S(1)}, u32[]{:S(2)}, u32[]{:S(2)}) collective-permute-start(bf16[6,16,1024]{2,1,0:T(8,128)(2,1)S(1)} %get-tuple-element.97), channel_id=1, source_target_pairs={{0,64},{64,128},{128,192},{192,0},{1,65},{65,129},{129,193},{193,1... | collective-permute-start | bytes 589832 | tf_op jit(solution)/shard_map/ppermute | solution.py:267
  10.8 9.1 %collective-permute-start.2 = (bf16[6,16,1024]{2,1,0:T(8,128)(2,1)S(1)}, bf16[6,16,1024]{2,1,0:T(8,128)(2,1)S(1)}, u32[]{:S(2)}, u32[]{:S(2)}) collective-permute-start(bf16[6,16,1024]{2,1,0:T(8,128)(2,1)S(1)} %get-tuple-element.46), channel_id=1, source_target_pairs={{0,64},{64,128},{128,192},{192,0},{1,65},{65,129},{129,193},{193,1... | collective-permute-start | bytes 589832 | tf_op jit(solution)/shard_map/ppermute | solution.py:267
  12.5 7.4 %collective-permute-start.3 = (bf16[6,16,1024]{2,1,0:T(8,128)(2,1)S(1)}, bf16[6,16,1024]{2,1,0:T(8,128)(2,1)S(1)}, u32[]{:S(2)}, u32[]{:S(2)}) collective-permute-start(bf16[6,16,1024]{2,1,0:T(8,128)(2,1)S(1)} %get-tuple-element.47), channel_id=1, source_target_pairs={{0,192},{64,0},{128,64},{192,128},{1,193},{65,1},{129,65},{193,129... | collective-permute-start | bytes 589832 | tf_op jit(solution)/shard_map/ppermute | solution.py:267
  19.9 32.0 %collective-permute-start.11 = (bf16[2,1024,256]{2,1,0:T(8,128)(2,1)}, bf16[2,1024,256]{2,1,0:T(8,128)(2,1)}, u32[]{:S(2)}, u32[]{:S(2)}) collective-permute-start(bf16[2,1024,256]{2,1,0:T(8,128)(2,1)} %r0), channel_id=1, source_target_pairs={{0,64},{64,128},{128,192},{192,0},{1,65},{65,129},{129,193},{193,1... | collective-permute-start | bytes 3145736 | tf_op jit(solution)/shard_map/ppermute | solution.py:267
  20.1 31.8 %collective-permute-start.12 = (bf16[2,1024,256]{2,1,0:T(8,128)(2,1)}, bf16[2,1024,256]{2,1,0:T(8,128)(2,1)}, u32[]{:S(2)}, u32[]{:S(2)}) collective-permute-start(bf16[2,1024,256]{2,1,0:T(8,128)(2,1)} %r0), channel_id=1, source_target_pairs={{0,192},{64,0},{128,64},{192,128},{1,193},{65,1},{129,65},{193,129... | collective-permute-start | bytes 3145736 | tf_op jit(solution)/shard_map/ppermute | solution.py:267
  23.2 9.4 %collective-permute-start.6 = (bf16[12,16,256]{2,1,0:T(8,128)(2,1)S(1)}, bf16[12,16,256]{2,1,0:T(8,128)(2,1)S(1)}, u32[]{:S(2)}, u32[]{:S(2)}) collective-permute-start(bf16[12,16,256]{2,1,0:T(8,128)(2,1)S(1)} %get-tuple-element.51), channel_id=1, source_target_pairs={{0,16},{1,17},{2,18},{3,19},{4,20},{5,21},{6,22},{7,23},{8,24},{9,... | collective-permute-start | bytes 294920 | tf_op jit(solution)/shard_map/ppermute | solution.py:271
  25.0 10.8 %collective-permute-start.7 = (bf16[12,16,256]{2,1,0:T(8,128)(2,1)S(1)}, bf16[12,16,256]{2,1,0:T(8,128)(2,1)S(1)}, u32[]{:S(2)}, u32[]{:S(2)}) collective-permute-start(bf16[12,16,256]{2,1,0:T(8,128)(2,1)S(1)} %get-tuple-element.52), channel_id=1, source_target_pairs={{0,32},{1,33},{2,34},{3,35},{4,36},{5,37},{6,38},{7,39},{8,40},{9,... | collective-permute-start | bytes 294920 | tf_op jit(solution)/shard_map/ppermute | solution.py:271
  30.2 6.1 %collective-permute-start.8 = (bf16[12,16,256]{2,1,0:T(8,128)(2,1)S(1)}, bf16[12,16,256]{2,1,0:T(8,128)(2,1)S(1)}, u32[]{:S(2)}, u32[]{:S(2)}) collective-permute-start(bf16[12,16,256]{2,1,0:T(8,128)(2,1)S(1)} %get-tuple-element.53), channel_id=1, source_target_pairs={{0,48},{1,49},{2,50},{3,51},{4,52},{5,53},{6,54},{7,55},{8,56},{9,... | collective-permute-start | bytes 294920 | tf_op jit(solution)/shard_map/ppermute | solution.py:271
  32.6 32.7 %collective-permute-start.10 = (bf16[2,1024,256]{2,1,0:T(8,128)(2,1)S(1)}, bf16[2,1024,256]{2,1,0:T(8,128)(2,1)}, u32[]{:S(2)}, u32[]{:S(2)}) collective-permute-start(bf16[2,1024,256]{2,1,0:T(8,128)(2,1)S(1)} %copy-done), channel_id=1, source_target_pairs={{0,192},{64,0},{128,64},{192,128},{1,193},{65,1},{129,65},{193,129... | collective-permute-start | bytes 3145736 | tf_op jit(solution)/shard_map/ppermute | solution.py:267
  35.8 33.0 %collective-permute-start.9 = (bf16[1,1024,256]{2,1,0:T(8,128)(2,1)}, bf16[1,1024,256]{2,1,0:T(8,128)(2,1)}, u32[]{:S(2)}, u32[]{:S(2)}) collective-permute-start(bf16[1,1024,256]{2,1,0:T(8,128)(2,1)} %get-tuple-element.55), channel_id=1, source_target_pairs={{0,64},{64,128},{128,192},{192,0},{1,65},{65,129},{129,193},{193,1... | collective-permute-start | bytes 1572872 | tf_op jit(solution)/shard_map/ppermute | solution.py:267
  37.9 42.0 %all-to-all-start = ((bf16[64,2,16,256]{3,2,1,0:T(8,128)(2,1)}), bf16[64,2,16,256]{3,2,1,0:T(8,128)(2,1)S(1)}, u32[]{:S(2)}, u32[]{:S(2)}) async-start(bf16[64,2,16,256]{3,2,1,0:T(8,128)(2,1)} %spread.1), calls=%async_computation | async-start | bytes 2097152 | tf_op jit(solution)/shard_map/all_to_all | solution.py:384
  51.9 27.9 %collective-permute-start.13 = (bf16[2,1024,256]{2,1,0:T(8,128)(2,1)}, bf16[2,1024,256]{2,1,0:T(8,128)(2,1)S(1)}, u32[]{:S(2)}, u32[]{:S(2)}) collective-permute-start(bf16[2,1024,256]{2,1,0:T(8,128)(2,1)} %hold.6.r1), channel_id=1, source_target_pairs={{0,64},{64,128},{128,192},{192,0},{1,65},{65,129},{129,193},{193,1... | collective-permute-start | bytes 3145736 | tf_op jit(solution)/shard_map/ppermute | solution.py:267
  65.3 24.9 %collective-permute-start.18 = (bf16[2,1024,256]{2,1,0:T(8,128)(2,1)}, bf16[2,1024,256]{2,1,0:T(8,128)(2,1)}, u32[]{:S(2)}, u32[]{:S(2)}) collective-permute-start(bf16[2,1024,256]{2,1,0:T(8,128)(2,1)} %hold.5.refs_4_), channel_id=1, source_target_pairs={{0,192},{64,0},{128,64},{192,128},{1,193},{65,1},{129,65},{193,129... | collective-permute-start | bytes 3145736 | tf_op jit(solution)/shard_map/ppermute | solution.py:267
  68.8 21.4 %collective-permute-start.17 = (bf16[1,1024,256]{2,1,0:T(8,128)(2,1)}, bf16[1,1024,256]{2,1,0:T(8,128)(2,1)}, u32[]{:S(2)}, u32[]{:S(2)}) collective-permute-start(bf16[1,1024,256]{2,1,0:T(8,128)(2,1)} %copy-done.8), channel_id=1, source_target_pairs={{0,64},{64,128},{128,192},{192,0},{1,65},{65,129},{129,193},{193,1... | collective-permute-start | bytes 1572872 | tf_op jit(solution)/shard_map/ppermute | solution.py:267
  85.7 9.9 %collective-permute-start.14 = (bf16[2,256,256]{2,1,0:T(8,128)(2,1)S(1)}, bf16[2,256,256]{2,1,0:T(8,128)(2,1)S(1)}, u32[]{:S(2)}, u32[]{:S(2)}) collective-permute-start(bf16[2,256,256]{2,1,0:T(8,128)(2,1)S(1)} %get-tuple-element.64), channel_id=1, source_target_pairs={{0,192},{64,0},{128,64},{192,128},{1,193},{65,1},{129,65},{193,129... | collective-permute-start | bytes 786440 | tf_op jit(solution)/shard_map/ppermute | solution.py:267
  88.4 7.8 %collective-permute-start.15 = (bf16[2,256,256]{2,1,0:T(8,128)(2,1)S(1)}, bf16[2,256,256]{2,1,0:T(8,128)(2,1)S(1)}, u32[]{:S(2)}, u32[]{:S(2)}) collective-permute-start(bf16[2,256,256]{2,1,0:T(8,128)(2,1)S(1)} %get-tuple-element.65), channel_id=1, source_target_pairs={{0,128},{64,192},{128,0},{192,64},{1,129},{65,193},{129,1},{193,65... | collective-permute-start | bytes 786440 | tf_op jit(solution)/shard_map/ppermute | solution.py:267
  88.4 14.7 %collective-permute-start.16 = (bf16[2,256,256]{2,1,0:T(8,128)(2,1)S(1)}, bf16[2,256,256]{2,1,0:T(8,128)(2,1)S(1)}, u32[]{:S(2)}, u32[]{:S(2)}) collective-permute-start(bf16[2,256,256]{2,1,0:T(8,128)(2,1)S(1)} %get-tuple-element.66), channel_id=1, source_target_pairs={{0,64},{64,128},{128,192},{192,0},{1,65},{65,129},{129,193},{193,1... | collective-permute-start | bytes 786440 | tf_op jit(solution)/shard_map/ppermute | solution.py:267
  107.6 27.6 %collective-permute-start.19 = (bf16[2,4,256,256]{3,2,1,0:T(8,128)(2,1)S(1)}, bf16[2,4,256,256]{3,2,1,0:T(8,128)(2,1)S(1)}, u32[]{:S(2)}, u32[]{:S(2)}) collective-permute-start(bf16[2,4,256,256]{3,2,1,0:T(8,128)(2,1)S(1)} %get-tuple-element.74.in0), channel_id=1, source_target_pairs={{0,64},{64,128},{128,192},{192,0},{1,65},{65,129},{129,193},{193,1... | collective-permute-start | bytes 3145736 | tf_op jit(solution)/shard_map/ppermute | solution.py:267
  107.6 27.6 %collective-permute-start.20 = (bf16[2,4,256,256]{3,2,1,0:T(8,128)(2,1)S(1)}, bf16[2,4,256,256]{3,2,1,0:T(8,128)(2,1)}, u32[]{:S(2)}, u32[]{:S(2)}) collective-permute-start(bf16[2,4,256,256]{3,2,1,0:T(8,128)(2,1)S(1)} %get-tuple-element.74.in0), channel_id=1, source_target_pairs={{0,192},{64,0},{128,64},{192,128},{1,193},{65,1},{129,65},{193,129... | collective-permute-start | bytes 3145736 | tf_op jit(solution)/shard_map/ppermute | solution.py:267
  110.2 23.6 %collective-permute-start.21 = (f32[2,4,8,128]{3,2,1,0:T(8,128)S(1)}, f32[2,4,8,128]{3,2,1,0:T(8,128)S(1)}, u32[]{:S(2)}, u32[]{:S(2)}) collective-permute-start(f32[2,4,8,128]{3,2,1,0:T(8,128)S(1)} %get-tuple-element.75.s0), channel_id=1, source_target_pairs={{0,64},{64,128},{128,192},{192,0},{1,65},{65,129},{129,193},{193,1... | collective-permute-start | bytes 98312 | tf_op jit(solution)/shard_map/ppermute | solution.py:267
  110.2 23.6 %collective-permute-start.22 = (f32[2,4,8,128]{3,2,1,0:T(8,128)S(1)}, f32[2,4,8,128]{3,2,1,0:T(8,128)S(1)}, u32[]{:S(2)}, u32[]{:S(2)}) collective-permute-start(f32[2,4,8,128]{3,2,1,0:T(8,128)S(1)} %get-tuple-element.75.s0), channel_id=1, source_target_pairs={{0,128},{64,192},{128,0},{192,64},{1,129},{65,193},{129,1},{193,65... | collective-permute-start | bytes 98312 | tf_op jit(solution)/shard_map/ppermute | solution.py:267
  111.4 22.5 %collective-permute-start.23 = (f32[2,4,8,128]{3,2,1,0:T(8,128)S(1)}, f32[2,4,8,128]{3,2,1,0:T(8,128)S(1)}, u32[]{:S(2)}, u32[]{:S(2)}) collective-permute-start(f32[2,4,8,128]{3,2,1,0:T(8,128)S(1)} %get-tuple-element.75.s0), channel_id=1, source_target_pairs={{0,192},{64,0},{128,64},{192,128},{1,193},{65,1},{129,65},{193,129... | collective-permute-start | bytes 98312 | tf_op jit(solution)/shard_map/ppermute | solution.py:267
  112.9 41.2 %all-to-all-start.1 = ((bf16[64,2,16,256]{3,2,1,0:T(8,128)(2,1)}), bf16[64,2,16,256]{3,2,1,0:T(8,128)(2,1)S(1)}, u32[]{:S(2)}, u32[]{:S(2)}) async-start(bf16[64,2,16,256]{3,2,1,0:T(8,128)(2,1)} %copy-done.3), calls=%async_computation.1 | async-start | bytes 2097152 | tf_op jit(solution)/shard_map/all_to_all | solution.py:420
  137.8 23.6 %collective-permute-start.31 = (bf16[1,4,256,256]{3,2,1,0:T(8,128)(2,1)}, bf16[1,4,256,256]{3,2,1,0:T(8,128)(2,1)S(1)}, u32[]{:S(2)}, u32[]{:S(2)}) collective-permute-start(bf16[1,4,256,256]{3,2,1,0:T(8,128)(2,1)} %get-tuple-element.85), channel_id=1, source_target_pairs={{0,64},{64,128},{128,192},{192,0},{1,65},{65,129},{129,193},{193,1... | collective-permute-start | bytes 1572872 | tf_op jit(solution)/shard_map/ppermute | solution.py:267
  137.8 23.6 %collective-permute-start.32 = (bf16[1,4,256,256]{3,2,1,0:T(8,128)(2,1)}, bf16[1,4,256,256]{3,2,1,0:T(8,128)(2,1)S(1)}, u32[]{:S(2)}, u32[]{:S(2)}) collective-permute-start(bf16[1,4,256,256]{3,2,1,0:T(8,128)(2,1)} %get-tuple-element.86), channel_id=1, source_target_pairs={{0,192},{64,0},{128,64},{192,128},{1,193},{65,1},{129,65},{193,129... | collective-permute-start | bytes 1572872 | tf_op jit(solution)/shard_map/ppermute | solution.py:267
  146.5 4.8 %collective-permute-start.26 = (f32[8,128]{1,0:T(8,128)S(1)}, f32[8,128]{1,0:T(8,128)S(1)}, u32[]{:S(2)}, u32[]{:S(2)}) collective-permute-start(f32[8,128]{1,0:T(8,128)S(1)} %add.135), channel_id=1, source_target_pairs={{0,4},{1,5},{2,6},{3,7},{4,0},{5,1},{6,2},{7,3},{8,12},{9,13},{10,... | collective-permute-start | bytes 12296 | tf_op jit(solution)/shard_map/ppermute | solution.py:440
  154.7 16.6 %collective-permute-start.28 = (bf16[13,16,256]{2,1,0:T(8,128)(2,1)S(1)}, bf16[13,16,256]{2,1,0:T(8,128)(2,1)S(1)}, u32[]{:S(2)}, u32[]{:S(2)}) collective-permute-start(bf16[13,16,256]{2,1,0:T(8,128)(2,1)S(1)} %get-tuple-element.79), channel_id=1, source_target_pairs={{0,16},{1,17},{2,18},{3,19},{4,20},{5,21},{6,22},{7,23},{8,24},{9,... | collective-permute-start | bytes 319496 | tf_op jit(solution)/shard_map/ppermute | solution.py:271
  155.4 16.0 %collective-permute-start.29 = (bf16[13,16,256]{2,1,0:T(8,128)(2,1)S(1)}, bf16[13,16,256]{2,1,0:T(8,128)(2,1)S(1)}, u32[]{:S(2)}, u32[]{:S(2)}) collective-permute-start(bf16[13,16,256]{2,1,0:T(8,128)(2,1)S(1)} %get-tuple-element.80), channel_id=1, source_target_pairs={{0,32},{1,33},{2,34},{3,35},{4,36},{5,37},{6,38},{7,39},{8,40},{9,... | collective-permute-start | bytes 319496 | tf_op jit(solution)/shard_map/ppermute | solution.py:271
  159.1 12.2 %collective-permute-start.30 = (bf16[13,16,256]{2,1,0:T(8,128)(2,1)S(1)}, bf16[13,16,256]{2,1,0:T(8,128)(2,1)S(1)}, u32[]{:S(2)}, u32[]{:S(2)}) collective-permute-start(bf16[13,16,256]{2,1,0:T(8,128)(2,1)S(1)} %get-tuple-element.81), channel_id=1, source_target_pairs={{0,48},{1,49},{2,50},{3,51},{4,52},{5,53},{6,54},{7,55},{8,56},{9,... | collective-permute-start | bytes 319496 | tf_op jit(solution)/shard_map/ppermute | solution.py:271
  (16 other events, 143.9 us)

commit v7 on v6

--- a/solution.py
+++ b/solution.py
@@ -12,7 +12,7 @@
 BF16 = jnp.bfloat16
 VMEM_LIMIT = 24 * 1024 * 1024
 JOIN_COST = 10_000_000_000
-COSTS = (10_000_000_000, 10_000_000_000, 5_000_000_000, 10_000_000_000, 8_000_000_000)
+COSTS = (10_000_000_000, 10_000_000_000, 5_000_000_000, 4_000_000_000, 0)
 SMEM_SPEC = pl.BlockSpec(memory_space=pltpu.SMEM)
 
 
@@ -61,12 +61,6 @@
 def split_kernel(whole, first, second):
     first[...] = whole[:1]
     second[...] = whole[1:]
-
-
-def relay_kernel(before, behind, up, down):
-    count = up.shape[0]
-    up[...] = before[:count]
-    down[...] = behind[count:]
 
 
 def product_kernel(meta, arrived, r0, r1, r2, r3, grad, sums, *rest):
@@ -200,29 +194,36 @@
             out[g, j] = (block[j].astype(F32) * scale).astype(BF16)
 
 
-def stat_kernel(meta, adds, in0, in1, in3, in_far0, in_far1, left_stat, right_stat, *refs):
-    left_new, right_new, whole, g0, g1, g3, far0, far1, left, right, done = refs
+def stat_kernel(meta, adds, in0, in1, in3, in_far, left_stat, right_stat, *refs):
+    left_new, right_new, whole, g0, g1, g3, far, left, right, left_out, right_out, done = refs
     me = meta[0]
     slots, quarter, size = left.shape
-    sources = (in0, in1, in3, in_far0, in_far1, left_stat, right_stat)
-    targets = (g0, g1, g3, far0, far1, left, right)
-    copies = [
-        pltpu.make_async_copy(source, target, done.at[n])
-        for n, (source, target) in enumerate(zip(sources, targets))
-    ]
-    for copy in copies:
-        copy.start()
-    for copy in copies[:5]:
-        copy.wait()
     reps = size // quarter
     piece = quarter // (reps * reps)
+    loads = []
+    for s in range(slots):
+        sources = (in0.at[s], in1.at[s], in3.at[s], in_far.at[s])
+        targets = (g0.at[s], g1.at[s], g3.at[s], far.at[s])
+        sources += (left_stat.at[s], right_stat.at[s])
+        targets += (left.at[s], right.at[s])
+        loads.append(
+            [
+                pltpu.make_async_copy(source, target, done.at[s, n])
+                for n, (source, target) in enumerate(zip(sources, targets))
+            ]
+        )
+    for copies in loads:
+        for copy in copies:
+            copy.start()
     keep = 1.0 - SHRINKAGE
     row = lax.broadcasted_iota(jnp.int32, (quarter, quarter), 0)
     col = lax.broadcasted_iota(jnp.int32, (quarter, quarter), 1)
     first = pl.multiple_of(me * quarter, quarter)
-    for s in range(slots):
-        far = (far0, far1)[s]
-        for d, block in enumerate((g0.at[s], g3.at[s], far.at[0], g1.at[s])):
+    stores = []
+    for s in range(slots):
+        for copy in loads[s][:4]:
+            copy.wait()
+        for d, block in enumerate((g0.at[s], g3.at[s], far.at[s], g1.at[s])):
             r = lax.rem(me + d, reps)
             for p in range(reps * reps):
                 target = pl.multiple_of((p * reps + r) * piece, piece)
@@ -230,23 +231,28 @@
                     whole[pl.ds(target, piece), i * quarter : (i + 1) * quarter] = block[
                         i, p * piece : (p + 1) * piece, :
                     ]
+        for copy in loads[s][4:]:
+            copy.wait()
         mine = whole[pl.ds(first, quarter), :]
-        if s == 0:
-            for copy in copies[5:]:
-                copy.wait()
         for n in range(reps):
             cols = slice(n * quarter, (n + 1) * quarter)
             gram = dot(mine, whole[cols, :], (1, 1))
-            total = keep * (DECAY * left[s, :, cols] + (1.0 - DECAY) * gram)
+            total = keep * DECAY * left[s, :, cols] + keep * (1.0 - DECAY) * gram
             on = col + n * quarter == row + first
-            left_new[s, :, cols] = total + jnp.where(on, adds[0, s, :1, :1], 0.0)
-        mine = whole[:, pl.ds(first, quarter)]
+            left_out[s, :, cols] = total + jnp.where(on, adds[0, s, :1, :1], 0.0)
+        stores.append(pltpu.make_async_copy(left_out.at[s], left_new.at[s], done.at[s, 6]))
+        stores[-1].start()
+        mine = whole[:, pl.ds(first, quarter)].T
         for n in range(reps):
             cols = slice(n * quarter, (n + 1) * quarter)
-            gram = dot(mine, whole[:, cols], (0, 0))
-            total = keep * (DECAY * right[s, :, cols] + (1.0 - DECAY) * gram)
+            gram = dot(mine, whole[:, cols])
+            total = keep * DECAY * right[s, :, cols] + keep * (1.0 - DECAY) * gram
             on = (col + n * quarter == row + first) & (row + first < meta[1 + s])
-            right_new[s, :, cols] = total + jnp.where(on, adds[1, s, :1, :1], 0.0)
+            right_out[s, :, cols] = total + jnp.where(on, adds[1, s, :1, :1], 0.0)
+        stores.append(pltpu.make_async_copy(right_out.at[s], right_new.at[s], done.at[s, 7]))
+        stores[-1].start()
+    for copy in stores:
+        copy.wait()
 
 
 def on_device(grad_parts, col_widths, assignment, left_stat, right_stat, left_root, right_root):
@@ -331,18 +337,6 @@
     right_diag = jnp.sum(diagonal_of(right_stat) * within_width, axis=1)
     diag_own = jnp.stack([left_diag, right_diag])
 
-
-    def relay(before, behind):
-        shape = (before.shape[0] // 2,) + before.shape[1:]
-        up, down = pl.pallas_call(
-            relay_kernel,
-            in_specs=[vmem] * 2,
-            out_shape=[jax.ShapeDtypeStruct(shape, BF16)] * 2,
-            compiler_params=params,
-            cost_estimate=pl.CostEstimate(flops=COSTS[3], bytes_accessed=0, transcendentals=0),
-            name="relay",
-        )(before, behind)
-        return (turn_x(up, 1), turn_x(down, 3))
 
     anywhere = pl.BlockSpec(memory_space=pl.ANY)
 
@@ -433,6 +427,7 @@
     )(meta, *all_sums)
     g_prev = turn_x(g_mine, 1)
     g_next = turn_x(g_mine, reps - 1)
+    g_prev, g_next = hold(g_prev, COSTS[3]), hold(g_next, COSTS[3])
     g_prev, g_next, table = lax.optimization_barrier((g_prev, g_next, table))
     distance = 1
     while distance < per_row:
@@ -440,18 +435,17 @@
         table = table + lax.ppermute(table, "fsdp", pairs)
         distance *= 2
 
-    g_far = relay(g_prev, g_next)
+    g_far = turn_x(g_prev, 1)
     left_new, right_new = pl.pallas_call(
         stat_kernel,
-        in_specs=[SMEM_SPEC, vmem] + [anywhere] * 7,
+        in_specs=[SMEM_SPEC, vmem] + [anywhere] * 6,
+        out_specs=[anywhere] * 2,
         out_shape=[jax.ShapeDtypeStruct(left_stat.shape, F32)] * 2,
         scratch_shapes=[
             pltpu.VMEM((block_size, block_size), BF16),
-            *[pltpu.VMEM(g_mine.shape, BF16)] * 3,
-            *[pltpu.VMEM(g_far[0].shape, BF16)] * 2,
-            pltpu.VMEM(left_stat.shape, F32),
-            pltpu.VMEM(right_stat.shape, F32),
-            pltpu.SemaphoreType.DMA((7,)),
+            *[pltpu.VMEM(g_mine.shape, BF16)] * 4,
+            *[pltpu.VMEM(left_stat.shape, F32)] * 4,
+            pltpu.SemaphoreType.DMA((slots, 8)),
         ],
         compiler_params=pltpu.CompilerParams(vmem_limit_bytes=56 * 1024 * 1024),
         cost_estimate=pl.CostEstimate(
@@ -460,7 +454,7 @@
             transcendentals=0,
         ),
         name="stat_update",
-    )(meta, adds, g_mine, g_prev, g_next, *g_far, left_stat, right_stat)
+    )(meta, adds, g_mine, g_prev, g_next, g_far, left_stat, right_stat)
 
     block = jnp.arange(groups * ncols, dtype=jnp.int32)
     wanted = jnp.take(slot_ids, (block + me_group * ncols) % (groups * ncols), mode="clip")

time: 176 us -> 174 us (0.989); the launches traced: 173 us -> 173 us
  waiting for transfers between devices: 59 us -> 63.8 us
  starting transfers between devices: 77.1 us -> 73.4 us
  Pallas kernels: 23.3 us -> 20.2 us
  local copies, waits for them, and re-layouts: 7.38 us -> 10 us
    ppermute x23 -> x22, starting transfers between devices: 28.1 us -> 23.1 us  [turn_x(): return lax.ppermute(value, 'replica', pairs)]
    pallas_call x2 -> x1, Pallas kernels: 11.5 us -> 7.26 us  [on_device(): pl.pallas_call(stat_kernel, in_specs=[SMEM_SPEC, vmem] + [anywhere] * 6,...]
    ppermute x23 -> x22, waiting for transfers between devices: 42.8 us -> 45.3 us  [turn_x(): return lax.ppermute(value, 'replica', pairs)]
    all_to_all x1, waiting for transfers between devices: 9.57 us -> 12.1 us  [on_device(): lax.all_to_all(outgoing, 'fsdp', split_axis=0, concat_axis=0, tiled=True)]
    ppermute x6, starting transfers between devices: 16 us -> 17.9 us  [turn_group(): return lax.ppermute(value, 'fsdp', pairs)]
  transfers between devices with their start and end apart: 35 -> 34, of which waited for: 15 -> 16; matrix products, arithmetic and copies ran while one was open for 2% -> 3% of each run, Pallas kernels for 11% -> 9%
where the time goes in v7:
time: 174 us; the launch traced here: 173 us
  starting transfers between devices  73.4 us (42%)
  waiting for transfers between devices  63.8 us (37%)
  Pallas kernels  20.2 us (12%)
  local copies, waits for them, and re-layouts  10 us (6%)
  other arithmetic  5.06 us (3%)
    ppermute x22, waiting for transfers between devices, turn_x(): return lax.ppermute(value, 'replica', pairs)  45.3 us
    ppermute x22, starting transfers between devices, turn_x(): return lax.ppermute(value, 'replica', pairs)  23.1 us
    ppermute x6, starting transfers between devices, turn_group(): return lax.ppermute(value, 'fsdp', pairs)  17.9 us
    all_to_all x1, starting transfers between devices, on_device(): lax.all_to_all(outgoing, 'fsdp', split_axis=0, concat_axis=0, tiled=True)  14.3 us
    all_to_all x1, waiting for transfers between devices, on_device(): lax.all_to_all(outgoing, 'fsdp', split_axis=0, concat_axis=0, tiled=True)  12.1 us
    all_to_all x1, starting transfers between devices, on_device(): lax.all_to_all(returning, 'fsdp', split_axis=0, concat_axis=0, tiled=True)  11.7 us
    pallas_call x1, Pallas kernels, on_device(): pl.pallas_call(stat_kernel, in_specs=[SMEM_SPEC, vmem] + [anywhere] * 6,...  7.26 us
    unnamed x26, local copies, waits for them, and re-layouts  6.81 us
  transfers between devices with their start and end apart: 34, of which 16 were waited for; matrix products, arithmetic and copies ran while one was open for 3% of the time, Pallas kernels for 9%

profile of v7, /device:TPU:1, one launch (start us, length us, event | category | flops | bytes accessed | tf_op | source)
XLA Modules:
  0.0 173.5 jit_solution(2289477262711900648)
XLA Ops:
  1.4 1.8 %fusion = bf16[64,12,1024]{2,0,1:T(8,128)(2,1)S(1)} fusion(bf16[1,64,12,1024]{3,1,2,0:T(8,128)(2,1)} %param.7, f32[12,1024]{1,0:T(8,128)S(1)} %fusion.2), kind=kLoop, calls=%fused_computation.2 | loop fusion | flops 2359296 | bytes 3194880 | tf_op jit(solution)/shard_map/convert_element_type | solution.py:282
  3.5 2.1 %collective-permute-start = (bf16[6,16,1024]{2,1,0:T(8,128)(2,1)S(1)}, bf16[6,16,1024]{2,1,0:T(8,128)(2,1)S(1)}, u32[]{:S(2)}, u32[]{:S(2)}) collective-permute-start(bf16[6,16,1024]{2,1,0:T(8,128)(2,1)S(1)} %get-tuple-element.98), channel_id=1, source_target_pairs={{0,64},{64,128},{128,192},{192,0},{1,65},{65,129},{129,193},{193,1... | collective-permute-start | bytes 589832 | tf_op jit(solution)/shard_map/ppermute | solution.py:273
  11.5 1.6 collective-permute-start.2
  14.3 5.9 %collective-permute-done.2.top0 = bf16[6,16,1024]{2,1,0:T(8,128)(2,1)S(1)} collective-permute-done((bf16[6,16,1024]{2,1,0:T(8,128)(2,1)}, bf16[6,16,1024]{2,1,0:T(8,128)(2,1)S(1)}, u32[]{:S(2)}, u32[]{:S(2)}) %collective-permute-start.2) | collective-permute-done | bytes 196640 | tf_op jit(solution)/shard_map/ppermute | solution.py:273
  20.2 2.7 %collective-permute-start.12 = (bf16[2,1024,256]{2,1,0:T(8,128)(2,1)S(1)}, bf16[2,1024,256]{2,1,0:T(8,128)(2,1)}, u32[]{:S(2)}, u32[]{:S(2)}) collective-permute-start(bf16[2,1024,256]{2,1,0:T(8,128)(2,1)S(1)} %copy-done.2), channel_id=1, source_target_pairs={{0,192},{64,0},{128,64},{192,128},{1,193},{65,1},{129,65},{193,129... | collective-permute-start | bytes 3145736 | tf_op jit(solution)/shard_map/ppermute | solution.py:273
  23.4 3.4 %collective-permute-start.6 = (bf16[12,16,256]{2,1,0:T(8,128)(2,1)S(1)}, bf16[12,16,256]{2,1,0:T(8,128)(2,1)S(1)}, u32[]{:S(2)}, u32[]{:S(2)}) collective-permute-start(bf16[12,16,256]{2,1,0:T(8,128)(2,1)S(1)} %get-tuple-element.49), channel_id=1, source_target_pairs={{0,16},{1,17},{2,18},{3,19},{4,20},{5,21},{6,22},{7,23},{8,24},{9,... | collective-permute-start | bytes 294920 | tf_op jit(solution)/shard_map/ppermute | solution.py:277
  26.9 5.2 %collective-permute-start.7 = (bf16[12,16,256]{2,1,0:T(8,128)(2,1)S(1)}, bf16[12,16,256]{2,1,0:T(8,128)(2,1)S(1)}, u32[]{:S(2)}, u32[]{:S(2)}) collective-permute-start(bf16[12,16,256]{2,1,0:T(8,128)(2,1)S(1)} %get-tuple-element.50), channel_id=1, source_target_pairs={{0,32},{1,33},{2,34},{3,35},{4,36},{5,37},{6,38},{7,39},{8,40},{9,... | collective-permute-start | bytes 294920 | tf_op jit(solution)/shard_map/ppermute | solution.py:277
  32.1 2.4 %collective-permute-start.8 = (bf16[12,16,256]{2,1,0:T(8,128)(2,1)S(1)}, bf16[12,16,256]{2,1,0:T(8,128)(2,1)S(1)}, u32[]{:S(2)}, u32[]{:S(2)}) collective-permute-start(bf16[12,16,256]{2,1,0:T(8,128)(2,1)S(1)} %get-tuple-element.51), channel_id=1, source_target_pairs={{0,48},{1,49},{2,50},{3,51},{4,52},{5,53},{6,54},{7,55},{8,56},{9,... | collective-permute-start | bytes 294920 | tf_op jit(solution)/shard_map/ppermute | solution.py:277
  36.2 1.4 collective-permute-start.9
  38.2 1.6 spread.1
  39.8 14.3 %all-to-all-start = ((bf16[64,2,16,256]{3,2,1,0:T(8,128)(2,1)}), bf16[64,2,16,256]{3,2,1,0:T(8,128)(2,1)S(1)}, u32[]{:S(2)}, u32[]{:S(2)}) async-start(bf16[64,2,16,256]{3,2,1,0:T(8,128)(2,1)} %spread.1), calls=%async_computation | async-start | bytes 2097152 | tf_op jit(solution)/shard_map/all_to_all | solution.py:378
  54.3 10.7 %collective-permute-done.10.before = bf16[2,1024,256]{2,1,0:T(8,128)(2,1)} collective-permute-done((bf16[2,1024,256]{2,1,0:T(8,128)(2,1)S(1)}, bf16[2,1024,256]{2,1,0:T(8,128)(2,1)}, u32[]{:S(2)}, u32[]{:S(2)}) %collective-permute-start.10) | collective-permute-done | bytes 1048608 | tf_op jit(solution)/shard_map/ppermute | solution.py:273
  64.9 3.5 %collective-permute-start.18 = (bf16[2,1024,256]{2,1,0:T(8,128)(2,1)}, bf16[2,1024,256]{2,1,0:T(8,128)(2,1)}, u32[]{:S(2)}, u32[]{:S(2)}) collective-permute-start(bf16[2,1024,256]{2,1,0:T(8,128)(2,1)} %hold.7.refs_4_), channel_id=1, source_target_pairs={{0,192},{64,0},{128,64},{192,128},{1,193},{65,1},{129,65},{193,129... | collective-permute-start | bytes 3145736 | tf_op jit(solution)/shard_map/ppermute | solution.py:273
  68.5 1.4 multiply_reduce_fusion.1
  70.0 12.1 %all-to-all-done.arrived = bf16[64,2,16,256]{3,2,1,0:T(8,128)(2,1)S(1)} async-done(((bf16[64,2,16,256]{3,2,1,0:T(8,128)(2,1)}), bf16[64,2,16,256]{3,2,1,0:T(8,128)(2,1)S(1)}, u32[]{:S(2)}, u32[]{:S(2)}) %all-to-all-start) | async-done | bytes 1048608 | tf_op jit(solution)/shard_map/all_to_all | solution.py:378
  85.5 3.2 %right_products.1 = (bf16[2,4,256,256]{3,2,1,0:T(8,128)(2,1)S(1)}, f32[2,8,128]{2,1,0:T(8,128)S(1)}, bf16[2,256,256]{2,1,0:T(8,128)(2,1)S(1)}, bf16[2,256,256]{2...) custom-call(s32[6]{0:T(128)S(1)} %pad_add_fusion.meta, ...), custom_call_target="tpu_custom_call" | custom-call | tf_op jit(solution)/shard_map/right_products/pallas_call | solution.py:382
  91.1 6.0 %collective-permute-done.14.y1 = bf16[2,256,256]{2,1,0:T(8,128)(2,1)S(1)} collective-permute-done((bf16[2,256,256]{2,1,0:T(8,128)(2,1)S(1)}, bf16[2,256,256]{2,1,0:T(8,128)(2,1)S(1)}, u32[]{:S(2)}, u32[]{:S(2)}) %collective-permute-start.14) | collective-permute-done | bytes 262176 | tf_op jit(solution)/shard_map/ppermute | solution.py:273
  97.5 7.6 %collective-permute-done.16.y3 = bf16[2,256,256]{2,1,0:T(8,128)(2,1)S(1)} collective-permute-done((bf16[2,256,256]{2,1,0:T(8,128)(2,1)S(1)}, bf16[2,256,256]{2,1,0:T(8,128)(2,1)S(1)}, u32[]{:S(2)}, u32[]{:S(2)}) %collective-permute-start.16) | collective-permute-done | bytes 262176 | tf_op jit(solution)/shard_map/ppermute | solution.py:273
  105.1 4.4 %left_products.1 = (bf16[64,2,16,256]{3,2,1,0:T(8,128)(2,1)}, f32[2,4,8,128]{3,2,1,0:T(8,128)S(1)}) custom-call(s32[6]{0:T(128)S(1)} %pad_add_fusion.meta, f32[2,2]{1,0:T(2,128)S(1)} %pad_maximum_fusion.diags, f32[2,8,128]{2,1,0:T(8,128)S(1)} %get-tuple-element.60.g_sums, bf16[2,256,256]{2,1,0:T(8,128)(2,1)S(1)} %get-tuple-element.61.y0, ...), custom_call_target="tpu_custom_call" | custom-call | tf_op jit(solution)/shard_map/left_products/pallas_call | solution.py:398
  109.6 2.7 %collective-permute-start.20 = (bf16[2,4,256,256]{3,2,1,0:T(8,128)(2,1)S(1)}, bf16[2,4,256,256]{3,2,1,0:T(8,128)(2,1)S(1)}, u32[]{:S(2)}, u32[]{:S(2)}) collective-permute-start(bf16[2,4,256,256]{3,2,1,0:T(8,128)(2,1)S(1)} %get-tuple-element.72.in0), channel_id=1, source_target_pairs={{0,192},{64,0},{128,64},{192,128},{1,193},{65,1},{129,65},{193,129... | collective-permute-start | bytes 3145736 | tf_op jit(solution)/shard_map/ppermute | solution.py:273
  112.3 11.7 %all-to-all-start.1 = ((bf16[64,2,16,256]{3,2,1,0:T(8,128)(2,1)}), bf16[64,2,16,256]{3,2,1,0:T(8,128)(2,1)S(1)}, u32[]{:S(2)}, u32[]{:S(2)}) async-start(bf16[64,2,16,256]{3,2,1,0:T(8,128)(2,1)} %get-tuple-element.71), calls=%async_computation.1 | async-start | bytes 2097152 | tf_op jit(solution)/shard_map/all_to_all | solution.py:414
  124.1 2.8 %collective-permute-start.22 = (f32[2,4,8,128]{3,2,1,0:T(8,128)S(1)}, f32[2,4,8,128]{3,2,1,0:T(8,128)S(1)}, u32[]{:S(2)}, u32[]{:S(2)}) collective-permute-start(f32[2,4,8,128]{3,2,1,0:T(8,128)S(1)} %get-tuple-element.73.s0), channel_id=1, source_target_pairs={{0,128},{64,192},{128,0},{192,64},{1,129},{65,193},{129,1},{193,65... | collective-permute-start | bytes 98312 | tf_op jit(solution)/shard_map/ppermute | solution.py:273
  127.2 9.3 %collective-permute-done.21.s1 = f32[2,4,8,128]{3,2,1,0:T(8,128)S(1)} collective-permute-done((f32[2,4,8,128]{3,2,1,0:T(8,128)S(1)}, f32[2,4,8,128]{3,2,1,0:T(8,128)S(1)}, u32[]{:S(2)}, u32[]{:S(2)}) %collective-permute-start.21) | collective-permute-done | bytes 32800 | tf_op jit(solution)/shard_map/ppermute | solution.py:273
  138.9 1.7 %collective-permute-start.24 = (f32[8,128]{1,0:T(8,128)S(1)}, f32[8,128]{1,0:T(8,128)S(1)}, u32[]{:S(2)}, u32[]{:S(2)}) collective-permute-start(f32[8,128]{1,0:T(8,128)S(1)} %get-tuple-element.75), channel_id=1, source_target_pairs={{0,1},{1,0},{2,3},{3,2},{4,5},{5,4},{6,7},{7,6},{8,9},{9,8},{10,11... | collective-permute-start | bytes 12296 | tf_op jit(solution)/shard_map/ppermute | solution.py:435
  142.3 1.9 %collective-permute-done.25 = f32[8,128]{1,0:T(8,128)S(1)} collective-permute-done((f32[8,128]{1,0:T(8,128)S(1)}, f32[8,128]{1,0:T(8,128)S(1)}, u32[]{:S(2)}, u32[]{:S(2)}) %collective-permute-start.25) | collective-permute-done | bytes 4128 | tf_op jit(solution)/shard_map/ppermute | solution.py:435
  144.2 2.3 %collective-permute-start.26 = (f32[8,128]{1,0:T(8,128)S(1)}, f32[8,128]{1,0:T(8,128)S(1)}, u32[]{:S(2)}, u32[]{:S(2)}) collective-permute-start(f32[8,128]{1,0:T(8,128)S(1)} %add.135), channel_id=1, source_target_pairs={{0,4},{1,5},{2,6},{3,7},{4,0},{5,1},{6,2},{7,3},{8,12},{9,13},{10,... | collective-permute-start | bytes 12296 | tf_op jit(solution)/shard_map/ppermute | solution.py:435
  146.6 1.9 %collective-permute-done.26 = f32[8,128]{1,0:T(8,128)S(1)} collective-permute-done((f32[8,128]{1,0:T(8,128)S(1)}, f32[8,128]{1,0:T(8,128)S(1)}, u32[]{:S(2)}, u32[]{:S(2)}) %collective-permute-start.26) | collective-permute-done | bytes 4128 | tf_op jit(solution)/shard_map/ppermute | solution.py:435
  148.5 1.4 collective-permute-start.27
  153.7 4.1 %collective-permute-start.29 = (bf16[13,16,256]{2,1,0:T(8,128)(2,1)S(1)}, bf16[13,16,256]{2,1,0:T(8,128)(2,1)S(1)}, u32[]{:S(2)}, u32[]{:S(2)}) collective-permute-start(bf16[13,16,256]{2,1,0:T(8,128)(2,1)S(1)} %get-tuple-element.78), channel_id=1, source_target_pairs={{0,32},{1,33},{2,34},{3,35},{4,36},{5,37},{6,38},{7,39},{8,40},{9,... | collective-permute-start | bytes 319496 | tf_op jit(solution)/shard_map/ppermute | solution.py:277
  157.8 1.7 collective-permute-start.30
  159.4 4.3 %collective-permute-done.31.in_far = bf16[2,4,256,256]{3,2,1,0:T(8,128)(2,1)S(1)} collective-permute-done((bf16[2,4,256,256]{3,2,1,0:T(8,128)(2,1)}, bf16[2,4,256,256]{3,2,1,0:T(8,128)(2,1)S(1)}, u32[]{:S(2)}, u32[]{:S(2)}) %collective-permute-start.31) | collective-permute-done | bytes 1048608 | tf_op jit(solution)/shard_map/ppermute | solution.py:273
  164.7 7.3 %stat_update.1 = (f32[2,256,1024]{2,1,0:T(8,128)}, f32[2,256,1024]{2,1,0:T(8,128)}) custom-call(s32[6]{0:T(128)} %copy-done.7, f32[2,2,8,128]{3,2,1,0:T(8,128)} %copy-done.6, bf16[2,4,256,256]{3,2,1,0:T(8,128)(2,1)} %copy-done.1, bf16[2,4,256,256]{3,2,1,0:T(8,128)(2,1)} %hold.10.in1, bf16[2,4,256,256]{3,2,1,0:T(8,128)(2,1)} %hold.11.in3, ...), custom_call_target="tpu_custom_call" | custom-call | flops 2147483648 | bytes 20971520 | tf_op jit(solution)/shard_map/stat_update/pallas_call | solution.py:439
  (107 shorter events, 27.8 us)
Async XLA Ops:
  3.5 6.5 %collective-permute-start = (bf16[6,16,1024]{2,1,0:T(8,128)(2,1)S(1)}, bf16[6,16,1024]{2,1,0:T(8,128)(2,1)S(1)}, u32[]{:S(2)}, u32[]{:S(2)}) collective-permute-start(bf16[6,16,1024]{2,1,0:T(8,128)(2,1)S(1)} %get-tuple-element.98), channel_id=1, source_target_pairs={{0,64},{64,128},{128,192},{192,0},{1,65},{65,129},{129,193},{193,1... | collective-permute-start | bytes 589832 | tf_op jit(solution)/shard_map/ppermute | solution.py:273
  5.7 5.1 %collective-permute-start.1 = (bf16[6,16,1024]{2,1,0:T(8,128)(2,1)S(1)}, bf16[6,16,1024]{2,1,0:T(8,128)(2,1)S(1)}, u32[]{:S(2)}, u32[]{:S(2)}) collective-permute-start(bf16[6,16,1024]{2,1,0:T(8,128)(2,1)S(1)} %get-tuple-element.97), channel_id=1, source_target_pairs={{0,192},{64,0},{128,64},{192,128},{1,193},{65,1},{129,65},{193,129... | collective-permute-start | bytes 589832 | tf_op jit(solution)/shard_map/ppermute | solution.py:273
  7.7 15.6 %collective-permute-start.4 = (bf16[6,16,1024]{2,1,0:T(8,128)(2,1)}, bf16[6,16,1024]{2,1,0:T(8,128)(2,1)S(1)}, u32[]{:S(2)}, u32[]{:S(2)}) collective-permute-start(bf16[6,16,1024]{2,1,0:T(8,128)(2,1)} %get-tuple-element.95), channel_id=1, source_target_pairs={{0,192},{64,0},{128,64},{192,128},{1,193},{65,1},{129,65},{193,129... | collective-permute-start | bytes 589832 | tf_op jit(solution)/shard_map/ppermute | solution.py:273
  9.8 13.5 %collective-permute-start.5 = (bf16[6,16,1024]{2,1,0:T(8,128)(2,1)}, bf16[6,16,1024]{2,1,0:T(8,128)(2,1)S(1)}, u32[]{:S(2)}, u32[]{:S(2)}) collective-permute-start(bf16[6,16,1024]{2,1,0:T(8,128)(2,1)} %get-tuple-element.93), channel_id=1, source_target_pairs={{0,64},{64,128},{128,192},{192,0},{1,65},{65,129},{129,193},{193,1... | collective-permute-start | bytes 589832 | tf_op jit(solution)/shard_map/ppermute | solution.py:273
  11.5 8.7 %collective-permute-start.2 = (bf16[6,16,1024]{2,1,0:T(8,128)(2,1)}, bf16[6,16,1024]{2,1,0:T(8,128)(2,1)S(1)}, u32[]{:S(2)}, u32[]{:S(2)}) collective-permute-start(bf16[6,16,1024]{2,1,0:T(8,128)(2,1)} %get-tuple-element.44), channel_id=1, source_target_pairs={{0,64},{64,128},{128,192},{192,0},{1,65},{65,129},{129,193},{193,1... | collective-permute-start | bytes 589832 | tf_op jit(solution)/shard_map/ppermute | solution.py:273
  13.0 7.1 %collective-permute-start.3 = (bf16[6,16,1024]{2,1,0:T(8,128)(2,1)S(1)}, bf16[6,16,1024]{2,1,0:T(8,128)(2,1)S(1)}, u32[]{:S(2)}, u32[]{:S(2)}) collective-permute-start(bf16[6,16,1024]{2,1,0:T(8,128)(2,1)S(1)} %get-tuple-element.45), channel_id=1, source_target_pairs={{0,192},{64,0},{128,64},{192,128},{1,193},{65,1},{129,65},{193,129... | collective-permute-start | bytes 589832 | tf_op jit(solution)/shard_map/ppermute | solution.py:273
  20.1 34.0 %collective-permute-start.11 = (bf16[2,1024,256]{2,1,0:T(8,128)(2,1)S(1)}, bf16[2,1024,256]{2,1,0:T(8,128)(2,1)}, u32[]{:S(2)}, u32[]{:S(2)}) collective-permute-start(bf16[2,1024,256]{2,1,0:T(8,128)(2,1)S(1)} %copy-done.2), channel_id=1, source_target_pairs={{0,64},{64,128},{128,192},{192,0},{1,65},{65,129},{129,193},{193,1... | collective-permute-start | bytes 3145736 | tf_op jit(solution)/shard_map/ppermute | solution.py:273
  20.2 34.0 %collective-permute-start.12 = (bf16[2,1024,256]{2,1,0:T(8,128)(2,1)S(1)}, bf16[2,1024,256]{2,1,0:T(8,128)(2,1)}, u32[]{:S(2)}, u32[]{:S(2)}) collective-permute-start(bf16[2,1024,256]{2,1,0:T(8,128)(2,1)S(1)} %copy-done.2), channel_id=1, source_target_pairs={{0,192},{64,0},{128,64},{192,128},{1,193},{65,1},{129,65},{193,129... | collective-permute-start | bytes 3145736 | tf_op jit(solution)/shard_map/ppermute | solution.py:273
  23.4 11.0 %collective-permute-start.6 = (bf16[12,16,256]{2,1,0:T(8,128)(2,1)S(1)}, bf16[12,16,256]{2,1,0:T(8,128)(2,1)S(1)}, u32[]{:S(2)}, u32[]{:S(2)}) collective-permute-start(bf16[12,16,256]{2,1,0:T(8,128)(2,1)S(1)} %get-tuple-element.49), channel_id=1, source_target_pairs={{0,16},{1,17},{2,18},{3,19},{4,20},{5,21},{6,22},{7,23},{8,24},{9,... | collective-permute-start | bytes 294920 | tf_op jit(solution)/shard_map/ppermute | solution.py:277
  26.9 9.3 %collective-permute-start.7 = (bf16[12,16,256]{2,1,0:T(8,128)(2,1)S(1)}, bf16[12,16,256]{2,1,0:T(8,128)(2,1)S(1)}, u32[]{:S(2)}, u32[]{:S(2)}) collective-permute-start(bf16[12,16,256]{2,1,0:T(8,128)(2,1)S(1)} %get-tuple-element.50), channel_id=1, source_target_pairs={{0,32},{1,33},{2,34},{3,35},{4,36},{5,37},{6,38},{7,39},{8,40},{9,... | collective-permute-start | bytes 294920 | tf_op jit(solution)/shard_map/ppermute | solution.py:277
  32.1 6.1 %collective-permute-start.8 = (bf16[12,16,256]{2,1,0:T(8,128)(2,1)S(1)}, bf16[12,16,256]{2,1,0:T(8,128)(2,1)S(1)}, u32[]{:S(2)}, u32[]{:S(2)}) collective-permute-start(bf16[12,16,256]{2,1,0:T(8,128)(2,1)S(1)} %get-tuple-element.51), channel_id=1, source_target_pairs={{0,48},{1,49},{2,50},{3,51},{4,52},{5,53},{6,54},{7,55},{8,56},{9,... | collective-permute-start | bytes 294920 | tf_op jit(solution)/shard_map/ppermute | solution.py:277
  34.5 30.5 %collective-permute-start.10 = (bf16[2,1024,256]{2,1,0:T(8,128)(2,1)S(1)}, bf16[2,1024,256]{2,1,0:T(8,128)(2,1)}, u32[]{:S(2)}, u32[]{:S(2)}) collective-permute-start(bf16[2,1024,256]{2,1,0:T(8,128)(2,1)S(1)} %copy-done), channel_id=1, source_target_pairs={{0,192},{64,0},{128,64},{192,128},{1,193},{65,1},{129,65},{193,129... | collective-permute-start | bytes 3145736 | tf_op jit(solution)/shard_map/ppermute | solution.py:273
  36.2 32.2 %collective-permute-start.9 = (bf16[1,1024,256]{2,1,0:T(8,128)(2,1)}, bf16[1,1024,256]{2,1,0:T(8,128)(2,1)}, u32[]{:S(2)}, u32[]{:S(2)}) collective-permute-start(bf16[1,1024,256]{2,1,0:T(8,128)(2,1)} %get-tuple-element.53), channel_id=1, source_target_pairs={{0,64},{64,128},{128,192},{192,0},{1,65},{65,129},{129,193},{193,1... | collective-permute-start | bytes 1572872 | tf_op jit(solution)/shard_map/ppermute | solution.py:273
  39.8 42.3 %all-to-all-start = ((bf16[64,2,16,256]{3,2,1,0:T(8,128)(2,1)}), bf16[64,2,16,256]{3,2,1,0:T(8,128)(2,1)S(1)}, u32[]{:S(2)}, u32[]{:S(2)}) async-start(bf16[64,2,16,256]{3,2,1,0:T(8,128)(2,1)} %spread.1), calls=%async_computation | async-start | bytes 2097152 | tf_op jit(solution)/shard_map/all_to_all | solution.py:378
  54.2 27.9 %collective-permute-start.13 = (bf16[2,1024,256]{2,1,0:T(8,128)(2,1)}, bf16[2,1024,256]{2,1,0:T(8,128)(2,1)S(1)}, u32[]{:S(2)}, u32[]{:S(2)}) collective-permute-start(bf16[2,1024,256]{2,1,0:T(8,128)(2,1)} %hold.8.r1), channel_id=1, source_target_pairs={{0,64},{64,128},{128,192},{192,0},{1,65},{65,129},{129,193},{193,1... | collective-permute-start | bytes 3145736 | tf_op jit(solution)/shard_map/ppermute | solution.py:273
  64.9 26.1 %collective-permute-start.18 = (bf16[2,1024,256]{2,1,0:T(8,128)(2,1)}, bf16[2,1024,256]{2,1,0:T(8,128)(2,1)}, u32[]{:S(2)}, u32[]{:S(2)}) collective-permute-start(bf16[2,1024,256]{2,1,0:T(8,128)(2,1)} %hold.7.refs_4_), channel_id=1, source_target_pairs={{0,192},{64,0},{128,64},{192,128},{1,193},{65,1},{129,65},{193,129... | collective-permute-start | bytes 3145736 | tf_op jit(solution)/shard_map/ppermute | solution.py:273
  68.5 22.6 %collective-permute-start.17 = (bf16[1,1024,256]{2,1,0:T(8,128)(2,1)}, bf16[1,1024,256]{2,1,0:T(8,128)(2,1)}, u32[]{:S(2)}, u32[]{:S(2)}) collective-permute-start(bf16[1,1024,256]{2,1,0:T(8,128)(2,1)} %copy-done.8), channel_id=1, source_target_pairs={{0,64},{64,128},{128,192},{192,0},{1,65},{65,129},{129,193},{193,1... | collective-permute-start | bytes 1572872 | tf_op jit(solution)/shard_map/ppermute | solution.py:273
  88.7 8.4 %collective-permute-start.14 = (bf16[2,256,256]{2,1,0:T(8,128)(2,1)S(1)}, bf16[2,256,256]{2,1,0:T(8,128)(2,1)S(1)}, u32[]{:S(2)}, u32[]{:S(2)}) collective-permute-start(bf16[2,256,256]{2,1,0:T(8,128)(2,1)S(1)} %get-tuple-element.62), channel_id=1, source_target_pairs={{0,192},{64,0},{128,64},{192,128},{1,193},{65,1},{129,65},{193,129... | collective-permute-start | bytes 786440 | tf_op jit(solution)/shard_map/ppermute | solution.py:273
  89.7 7.7 %collective-permute-start.15 = (bf16[2,256,256]{2,1,0:T(8,128)(2,1)S(1)}, bf16[2,256,256]{2,1,0:T(8,128)(2,1)S(1)}, u32[]{:S(2)}, u32[]{:S(2)}) collective-permute-start(bf16[2,256,256]{2,1,0:T(8,128)(2,1)S(1)} %get-tuple-element.63), channel_id=1, source_target_pairs={{0,128},{64,192},{128,0},{192,64},{1,129},{65,193},{129,1},{193,65... | collective-permute-start | bytes 786440 | tf_op jit(solution)/shard_map/ppermute | solution.py:273
  90.3 14.8 %collective-permute-start.16 = (bf16[2,256,256]{2,1,0:T(8,128)(2,1)S(1)}, bf16[2,256,256]{2,1,0:T(8,128)(2,1)S(1)}, u32[]{:S(2)}, u32[]{:S(2)}) collective-permute-start(bf16[2,256,256]{2,1,0:T(8,128)(2,1)S(1)} %get-tuple-element.64), channel_id=1, source_target_pairs={{0,64},{64,128},{128,192},{192,0},{1,65},{65,129},{129,193},{193,1... | collective-permute-start | bytes 786440 | tf_op jit(solution)/shard_map/ppermute | solution.py:273
  109.5 28.3 %collective-permute-start.19 = (bf16[2,4,256,256]{3,2,1,0:T(8,128)(2,1)S(1)}, bf16[2,4,256,256]{3,2,1,0:T(8,128)(2,1)}, u32[]{:S(2)}, u32[]{:S(2)}) collective-permute-start(bf16[2,4,256,256]{3,2,1,0:T(8,128)(2,1)S(1)} %get-tuple-element.72.in0), channel_id=1, source_target_pairs={{0,64},{64,128},{128,192},{192,0},{1,65},{65,129},{129,193},{193,1... | collective-permute-start | bytes 3145736 | tf_op jit(solution)/shard_map/ppermute | solution.py:273
  109.6 28.2 %collective-permute-start.20 = (bf16[2,4,256,256]{3,2,1,0:T(8,128)(2,1)S(1)}, bf16[2,4,256,256]{3,2,1,0:T(8,128)(2,1)S(1)}, u32[]{:S(2)}, u32[]{:S(2)}) collective-permute-start(bf16[2,4,256,256]{3,2,1,0:T(8,128)(2,1)S(1)} %get-tuple-element.72.in0), channel_id=1, source_target_pairs={{0,192},{64,0},{128,64},{192,128},{1,193},{65,1},{129,65},{193,129... | collective-permute-start | bytes 3145736 | tf_op jit(solution)/shard_map/ppermute | solution.py:273
  112.3 39.7 %all-to-all-start.1 = ((bf16[64,2,16,256]{3,2,1,0:T(8,128)(2,1)}), bf16[64,2,16,256]{3,2,1,0:T(8,128)(2,1)S(1)}, u32[]{:S(2)}, u32[]{:S(2)}) async-start(bf16[64,2,16,256]{3,2,1,0:T(8,128)(2,1)} %get-tuple-element.71), calls=%async_computation.1 | async-start | bytes 2097152 | tf_op jit(solution)/shard_map/all_to_all | solution.py:414
  124.0 12.6 %collective-permute-start.21 = (f32[2,4,8,128]{3,2,1,0:T(8,128)S(1)}, f32[2,4,8,128]{3,2,1,0:T(8,128)S(1)}, u32[]{:S(2)}, u32[]{:S(2)}) collective-permute-start(f32[2,4,8,128]{3,2,1,0:T(8,128)S(1)} %get-tuple-element.73.s0), channel_id=1, source_target_pairs={{0,64},{64,128},{128,192},{192,0},{1,65},{65,129},{129,193},{193,1... | collective-permute-start | bytes 98312 | tf_op jit(solution)/shard_map/ppermute | solution.py:273
  124.1 12.5 %collective-permute-start.22 = (f32[2,4,8,128]{3,2,1,0:T(8,128)S(1)}, f32[2,4,8,128]{3,2,1,0:T(8,128)S(1)}, u32[]{:S(2)}, u32[]{:S(2)}) collective-permute-start(f32[2,4,8,128]{3,2,1,0:T(8,128)S(1)} %get-tuple-element.73.s0), channel_id=1, source_target_pairs={{0,128},{64,192},{128,0},{192,64},{1,129},{65,193},{129,1},{193,65... | collective-permute-start | bytes 98312 | tf_op jit(solution)/shard_map/ppermute | solution.py:273
  126.9 9.7 %collective-permute-start.23 = (f32[2,4,8,128]{3,2,1,0:T(8,128)S(1)}, f32[2,4,8,128]{3,2,1,0:T(8,128)S(1)}, u32[]{:S(2)}, u32[]{:S(2)}) collective-permute-start(f32[2,4,8,128]{3,2,1,0:T(8,128)S(1)} %get-tuple-element.73.s0), channel_id=1, source_target_pairs={{0,192},{64,0},{128,64},{192,128},{1,193},{65,1},{129,65},{193,129... | collective-permute-start | bytes 98312 | tf_op jit(solution)/shard_map/ppermute | solution.py:273
  138.9 24.8 %collective-permute-start.31 = (bf16[2,4,256,256]{3,2,1,0:T(8,128)(2,1)}, bf16[2,4,256,256]{3,2,1,0:T(8,128)(2,1)S(1)}, u32[]{:S(2)}, u32[]{:S(2)}) collective-permute-start(bf16[2,4,256,256]{3,2,1,0:T(8,128)(2,1)} %hold.10.in1), channel_id=1, source_target_pairs={{0,64},{64,128},{128,192},{192,0},{1,65},{65,129},{129,193},{193,1... | collective-permute-start | bytes 3145736 | tf_op jit(solution)/shard_map/ppermute | solution.py:273
  141.4 2.8 %collective-permute-start.25 = (f32[8,128]{1,0:T(8,128)S(1)}, f32[8,128]{1,0:T(8,128)S(1)}, u32[]{:S(2)}, u32[]{:S(2)}) collective-permute-start(f32[8,128]{1,0:T(8,128)S(1)} %add.134), channel_id=1, source_target_pairs={{0,2},{1,3},{2,0},{3,1},{4,6},{5,7},{6,4},{7,5},{8,10},{9,11},{10,... | collective-permute-start | bytes 12296 | tf_op jit(solution)/shard_map/ppermute | solution.py:435
  144.2 4.2 %collective-permute-start.26 = (f32[8,128]{1,0:T(8,128)S(1)}, f32[8,128]{1,0:T(8,128)S(1)}, u32[]{:S(2)}, u32[]{:S(2)}) collective-permute-start(f32[8,128]{1,0:T(8,128)S(1)} %add.135), channel_id=1, source_target_pairs={{0,4},{1,5},{2,6},{3,7},{4,0},{5,1},{6,2},{7,3},{8,12},{9,13},{10,... | collective-permute-start | bytes 12296 | tf_op jit(solution)/shard_map/ppermute | solution.py:435
  152.6 19.4 %collective-permute-start.28 = (bf16[13,16,256]{2,1,0:T(8,128)(2,1)S(1)}, bf16[13,16,256]{2,1,0:T(8,128)(2,1)S(1)}, u32[]{:S(2)}, u32[]{:S(2)}) collective-permute-start(bf16[13,16,256]{2,1,0:T(8,128)(2,1)S(1)} %get-tuple-element.77), channel_id=1, source_target_pairs={{0,16},{1,17},{2,18},{3,19},{4,20},{5,21},{6,22},{7,23},{8,24},{9,... | collective-permute-start | bytes 319496 | tf_op jit(solution)/shard_map/ppermute | solution.py:277
  153.7 18.3 %collective-permute-start.29 = (bf16[13,16,256]{2,1,0:T(8,128)(2,1)S(1)}, bf16[13,16,256]{2,1,0:T(8,128)(2,1)S(1)}, u32[]{:S(2)}, u32[]{:S(2)}) collective-permute-start(bf16[13,16,256]{2,1,0:T(8,128)(2,1)S(1)} %get-tuple-element.78), channel_id=1, source_target_pairs={{0,32},{1,33},{2,34},{3,35},{4,36},{5,37},{6,38},{7,39},{8,40},{9,... | collective-permute-start | bytes 319496 | tf_op jit(solution)/shard_map/ppermute | solution.py:277
  157.8 14.2 %collective-permute-start.30 = (bf16[13,16,256]{2,1,0:T(8,128)(2,1)S(1)}, bf16[13,16,256]{2,1,0:T(8,128)(2,1)S(1)}, u32[]{:S(2)}, u32[]{:S(2)}) collective-permute-start(bf16[13,16,256]{2,1,0:T(8,128)(2,1)S(1)} %get-tuple-element.79), channel_id=1, source_target_pairs={{0,48},{1,49},{2,50},{3,51},{4,52},{5,53},{6,54},{7,55},{8,56},{9,... | collective-permute-start | bytes 319496 | tf_op jit(solution)/shard_map/ppermute | solution.py:277
  (15 other events, 153.0 us)

commit v8 on v7

--- a/solution.py
+++ b/solution.py
@@ -12,7 +12,7 @@
 BF16 = jnp.bfloat16
 VMEM_LIMIT = 24 * 1024 * 1024
 JOIN_COST = 10_000_000_000
-COSTS = (10_000_000_000, 10_000_000_000, 5_000_000_000, 4_000_000_000, 0)
+COSTS = (10_000_000_000, 10_000_000_000, 5_000_000_000, 4_000_000_000, 8_000_000_000)
 SMEM_SPEC = pl.BlockSpec(memory_space=pltpu.SMEM)
 
 
@@ -428,7 +428,6 @@
     g_prev = turn_x(g_mine, 1)
     g_next = turn_x(g_mine, reps - 1)
     g_prev, g_next = hold(g_prev, COSTS[3]), hold(g_next, COSTS[3])
-    g_prev, g_next, table = lax.optimization_barrier((g_prev, g_next, table))
     distance = 1
     while distance < per_row:
         pairs = [(a, a ^ distance) for a in range(workers)]

time: 174 us -> 172 us (0.989)
  waiting for transfers between devices: 63.8 us -> 59.5 us
  starting transfers between devices: 73.4 us -> 75.7 us
    ppermute x22, waiting for transfers between devices: 45.3 us -> 41.5 us  [turn_x(): return lax.ppermute(value, 'replica', pairs)]
    ppermute x6, starting transfers between devices: 17.9 us -> 20.2 us  [turn_group(): return lax.ppermute(value, 'fsdp', pairs)]
where the time goes in v8:
time: 172 us; the launch traced here: 171 us
  starting transfers between devices  75.7 us (44%)
  waiting for transfers between devices  59.5 us (35%)
  Pallas kernels  20.2 us (12%)
  local copies, waits for them, and re-layouts  9.45 us (5%)
  other arithmetic  5.06 us (3%)
    ppermute x22, waiting for transfers between devices, turn_x(): return lax.ppermute(value, 'replica', pairs)  41.5 us
    ppermute x22, starting transfers between devices, turn_x(): return lax.ppermute(value, 'replica', pairs)  22.7 us
    ppermute x6, starting transfers between devices, turn_group(): return lax.ppermute(value, 'fsdp', pairs)  20.2 us
    all_to_all x1, starting transfers between devices, on_device(): lax.all_to_all(outgoing, 'fsdp', split_axis=0, concat_axis=0, tiled=True)  14.3 us
    all_to_all x1, starting transfers between devices, on_device(): lax.all_to_all(returning, 'fsdp', split_axis=0, concat_axis=0, tiled=True)  12.2 us
    all_to_all x1, waiting for transfers between devices, on_device(): lax.all_to_all(outgoing, 'fsdp', split_axis=0, concat_axis=0, tiled=True)  12.1 us
    pallas_call x1, Pallas kernels, on_device(): pl.pallas_call(stat_kernel, in_specs=[SMEM_SPEC, vmem] + [anywhere] * 6,...  7.26 us
    ppermute x4, starting transfers between devices, on_device(): table = table + lax.ppermute(table, 'fsdp', pairs)  6.46 us
  transfers between devices with their start and end apart: 34, of which 16 were waited for; matrix products, arithmetic and copies ran while one was open for 3% of the time, Pallas kernels for 9%

profile of v8, /device:TPU:1, one launch (start us, length us, event | category | flops | bytes accessed | tf_op | source)
XLA Modules:
  0.0 170.9 jit_solution(439970300301588051)
XLA Ops:
  1.4 1.8 %fusion = bf16[64,12,1024]{2,0,1:T(8,128)(2,1)S(1)} fusion(bf16[1,64,12,1024]{3,1,2,0:T(8,128)(2,1)} %param.7, f32[12,1024]{1,0:T(8,128)S(1)} %fusion.2), kind=kLoop, calls=%fused_computation.2 | loop fusion | flops 2359296 | bytes 3194880 | tf_op jit(solution)/shard_map/convert_element_type | solution.py:282
  3.5 2.1 %collective-permute-start = (bf16[6,16,1024]{2,1,0:T(8,128)(2,1)S(1)}, bf16[6,16,1024]{2,1,0:T(8,128)(2,1)S(1)}, u32[]{:S(2)}, u32[]{:S(2)}) collective-permute-start(bf16[6,16,1024]{2,1,0:T(8,128)(2,1)S(1)} %get-tuple-element.92), channel_id=1, source_target_pairs={{0,64},{64,128},{128,192},{192,0},{1,65},{65,129},{129,193},{193,1... | collective-permute-start | bytes 589832 | tf_op jit(solution)/shard_map/ppermute | solution.py:273
  11.5 1.6 collective-permute-start.2
  14.3 5.9 %collective-permute-done.2.top0 = bf16[6,16,1024]{2,1,0:T(8,128)(2,1)S(1)} collective-permute-done((bf16[6,16,1024]{2,1,0:T(8,128)(2,1)}, bf16[6,16,1024]{2,1,0:T(8,128)(2,1)S(1)}, u32[]{:S(2)}, u32[]{:S(2)}) %collective-permute-start.2) | collective-permute-done | bytes 196640 | tf_op jit(solution)/shard_map/ppermute | solution.py:273
  20.2 2.7 %collective-permute-start.12 = (bf16[2,1024,256]{2,1,0:T(8,128)(2,1)S(1)}, bf16[2,1024,256]{2,1,0:T(8,128)(2,1)}, u32[]{:S(2)}, u32[]{:S(2)}) collective-permute-start(bf16[2,1024,256]{2,1,0:T(8,128)(2,1)S(1)} %copy-done.2), channel_id=1, source_target_pairs={{0,192},{64,0},{128,64},{192,128},{1,193},{65,1},{129,65},{193,129... | collective-permute-start | bytes 3145736 | tf_op jit(solution)/shard_map/ppermute | solution.py:273
  23.4 3.4 %collective-permute-start.6 = (bf16[12,16,256]{2,1,0:T(8,128)(2,1)S(1)}, bf16[12,16,256]{2,1,0:T(8,128)(2,1)S(1)}, u32[]{:S(2)}, u32[]{:S(2)}) collective-permute-start(bf16[12,16,256]{2,1,0:T(8,128)(2,1)S(1)} %get-tuple-element.46), channel_id=1, source_target_pairs={{0,16},{1,17},{2,18},{3,19},{4,20},{5,21},{6,22},{7,23},{8,24},{9,... | collective-permute-start | bytes 294920 | tf_op jit(solution)/shard_map/ppermute | solution.py:277
  26.9 5.2 %collective-permute-start.7 = (bf16[12,16,256]{2,1,0:T(8,128)(2,1)S(1)}, bf16[12,16,256]{2,1,0:T(8,128)(2,1)S(1)}, u32[]{:S(2)}, u32[]{:S(2)}) collective-permute-start(bf16[12,16,256]{2,1,0:T(8,128)(2,1)S(1)} %get-tuple-element.47), channel_id=1, source_target_pairs={{0,32},{1,33},{2,34},{3,35},{4,36},{5,37},{6,38},{7,39},{8,40},{9,... | collective-permute-start | bytes 294920 | tf_op jit(solution)/shard_map/ppermute | solution.py:277
  32.1 2.4 %collective-permute-start.8 = (bf16[12,16,256]{2,1,0:T(8,128)(2,1)S(1)}, bf16[12,16,256]{2,1,0:T(8,128)(2,1)S(1)}, u32[]{:S(2)}, u32[]{:S(2)}) collective-permute-start(bf16[12,16,256]{2,1,0:T(8,128)(2,1)S(1)} %get-tuple-element.48), channel_id=1, source_target_pairs={{0,48},{1,49},{2,50},{3,51},{4,52},{5,53},{6,54},{7,55},{8,56},{9,... | collective-permute-start | bytes 294920 | tf_op jit(solution)/shard_map/ppermute | solution.py:277
  36.2 1.4 collective-permute-start.9
  38.2 1.6 spread.1
  39.8 14.3 %all-to-all-start = ((bf16[64,2,16,256]{3,2,1,0:T(8,128)(2,1)}), bf16[64,2,16,256]{3,2,1,0:T(8,128)(2,1)S(1)}, u32[]{:S(2)}, u32[]{:S(2)}) async-start(bf16[64,2,16,256]{3,2,1,0:T(8,128)(2,1)} %spread.1), calls=%async_computation | async-start | bytes 2097152 | tf_op jit(solution)/shard_map/all_to_all | solution.py:378
  54.2 10.7 %collective-permute-done.10.before = bf16[2,1024,256]{2,1,0:T(8,128)(2,1)} collective-permute-done((bf16[2,1024,256]{2,1,0:T(8,128)(2,1)S(1)}, bf16[2,1024,256]{2,1,0:T(8,128)(2,1)}, u32[]{:S(2)}, u32[]{:S(2)}) %collective-permute-start.10) | collective-permute-done | bytes 1048608 | tf_op jit(solution)/shard_map/ppermute | solution.py:273
  64.9 3.5 %collective-permute-start.18 = (bf16[2,1024,256]{2,1,0:T(8,128)(2,1)}, bf16[2,1024,256]{2,1,0:T(8,128)(2,1)}, u32[]{:S(2)}, u32[]{:S(2)}) collective-permute-start(bf16[2,1024,256]{2,1,0:T(8,128)(2,1)} %hold.7.refs_4_), channel_id=1, source_target_pairs={{0,192},{64,0},{128,64},{192,128},{1,193},{65,1},{129,65},{193,129... | collective-permute-start | bytes 3145736 | tf_op jit(solution)/shard_map/ppermute | solution.py:273
  68.5 1.4 multiply_reduce_fusion.1
  70.0 12.1 %all-to-all-done.arrived = bf16[64,2,16,256]{3,2,1,0:T(8,128)(2,1)S(1)} async-done(((bf16[64,2,16,256]{3,2,1,0:T(8,128)(2,1)}), bf16[64,2,16,256]{3,2,1,0:T(8,128)(2,1)S(1)}, u32[]{:S(2)}, u32[]{:S(2)}) %all-to-all-start) | async-done | bytes 1048608 | tf_op jit(solution)/shard_map/all_to_all | solution.py:378
  85.5 3.2 %right_products.1 = (bf16[2,4,256,256]{3,2,1,0:T(8,128)(2,1)S(1)}, f32[2,8,128]{2,1,0:T(8,128)S(1)}, bf16[2,256,256]{2,1,0:T(8,128)(2,1)S(1)}, bf16[2,256,256]{2...) custom-call(s32[6]{0:T(128)S(1)} %pad_add_fusion.meta, ...), custom_call_target="tpu_custom_call" | custom-call | tf_op jit(solution)/shard_map/right_products/pallas_call | solution.py:382
  91.1 6.1 %collective-permute-done.14.y1 = bf16[2,256,256]{2,1,0:T(8,128)(2,1)S(1)} collective-permute-done((bf16[2,256,256]{2,1,0:T(8,128)(2,1)S(1)}, bf16[2,256,256]{2,1,0:T(8,128)(2,1)S(1)}, u32[]{:S(2)}, u32[]{:S(2)}) %collective-permute-start.14) | collective-permute-done | bytes 262176 | tf_op jit(solution)/shard_map/ppermute | solution.py:273
  97.5 7.6 %collective-permute-done.16.y3 = bf16[2,256,256]{2,1,0:T(8,128)(2,1)S(1)} collective-permute-done((bf16[2,256,256]{2,1,0:T(8,128)(2,1)S(1)}, bf16[2,256,256]{2,1,0:T(8,128)(2,1)S(1)}, u32[]{:S(2)}, u32[]{:S(2)}) %collective-permute-start.16) | collective-permute-done | bytes 262176 | tf_op jit(solution)/shard_map/ppermute | solution.py:273
  105.1 4.4 %left_products.1 = (bf16[64,2,16,256]{3,2,1,0:T(8,128)(2,1)}, f32[2,4,8,128]{3,2,1,0:T(8,128)S(1)}) custom-call(s32[6]{0:T(128)S(1)} %pad_add_fusion.meta, f32[2,2]{1,0:T(2,128)S(1)} %pad_maximum_fusion.diags, f32[2,8,128]{2,1,0:T(8,128)S(1)} %get-tuple-element.57.g_sums, bf16[2,256,256]{2,1,0:T(8,128)(2,1)S(1)} %get-tuple-element.58.y0, ...), custom_call_target="tpu_custom_call" | custom-call | tf_op jit(solution)/shard_map/left_products/pallas_call | solution.py:398
  109.6 12.2 %all-to-all-start.1 = ((bf16[64,2,16,256]{3,2,1,0:T(8,128)(2,1)}), bf16[64,2,16,256]{3,2,1,0:T(8,128)(2,1)S(1)}, u32[]{:S(2)}, u32[]{:S(2)}) async-start(bf16[64,2,16,256]{3,2,1,0:T(8,128)(2,1)} %get-tuple-element.68), calls=%async_computation.1 | async-start | bytes 2097152 | tf_op jit(solution)/shard_map/all_to_all | solution.py:414
  121.9 3.4 %collective-permute-start.20 = (f32[2,4,8,128]{3,2,1,0:T(8,128)S(1)}, f32[2,4,8,128]{3,2,1,0:T(8,128)S(1)}, u32[]{:S(2)}, u32[]{:S(2)}) collective-permute-start(f32[2,4,8,128]{3,2,1,0:T(8,128)S(1)} %get-tuple-element.69.s0), channel_id=1, source_target_pairs={{0,128},{64,192},{128,0},{192,64},{1,129},{65,193},{129,1},{193,65... | collective-permute-start | bytes 98312 | tf_op jit(solution)/shard_map/ppermute | solution.py:273
  125.3 2.0 %collective-permute-start.21 = (f32[2,4,8,128]{3,2,1,0:T(8,128)S(1)}, f32[2,4,8,128]{3,2,1,0:T(8,128)S(1)}, u32[]{:S(2)}, u32[]{:S(2)}) collective-permute-start(f32[2,4,8,128]{3,2,1,0:T(8,128)S(1)} %get-tuple-element.69.s0), channel_id=1, source_target_pairs={{0,192},{64,0},{128,64},{192,128},{1,193},{65,1},{129,65},{193,129... | collective-permute-start | bytes 98312 | tf_op jit(solution)/shard_map/ppermute | solution.py:273
  127.3 8.5 %collective-permute-done.29.before = bf16[2,4,256,256]{3,2,1,0:T(8,128)(2,1)S(1)} collective-permute-done((bf16[2,4,256,256]{3,2,1,0:T(8,128)(2,1)S(1)}, bf16[2,4,256,256]{3,2,1,0:T(8,128)(2,1)S(1)}, u32[]{:S(2)}, u32[]{:S(2)}) %collective-permute-start.29) | collective-permute-done | bytes 1048608 | tf_op jit(solution)/shard_map/ppermute | solution.py:273
  137.5 1.8 %collective-permute-start.22 = (f32[8,128]{1,0:T(8,128)S(1)}, f32[8,128]{1,0:T(8,128)S(1)}, u32[]{:S(2)}, u32[]{:S(2)}) collective-permute-start(f32[8,128]{1,0:T(8,128)S(1)} %get-tuple-element.70), channel_id=1, source_target_pairs={{0,1},{1,0},{2,3},{3,2},{4,5},{5,4},{6,7},{7,6},{8,9},{9,8},{10,11... | collective-permute-start | bytes 12296 | tf_op jit(solution)/shard_map/ppermute | solution.py:434
  141.0 2.0 %collective-permute-done.23 = f32[8,128]{1,0:T(8,128)S(1)} collective-permute-done((f32[8,128]{1,0:T(8,128)S(1)}, f32[8,128]{1,0:T(8,128)S(1)}, u32[]{:S(2)}, u32[]{:S(2)}) %collective-permute-start.23) | collective-permute-done | bytes 4128 | tf_op jit(solution)/shard_map/ppermute | solution.py:434
  143.0 2.3 %collective-permute-start.24 = (f32[8,128]{1,0:T(8,128)S(1)}, f32[8,128]{1,0:T(8,128)S(1)}, u32[]{:S(2)}, u32[]{:S(2)}) collective-permute-start(f32[8,128]{1,0:T(8,128)S(1)} %add.135), channel_id=1, source_target_pairs={{0,4},{1,5},{2,6},{3,7},{4,0},{5,1},{6,2},{7,3},{8,12},{9,13},{10,... | collective-permute-start | bytes 12296 | tf_op jit(solution)/shard_map/ppermute | solution.py:434
  145.3 1.9 %collective-permute-done.24 = f32[8,128]{1,0:T(8,128)S(1)} collective-permute-done((f32[8,128]{1,0:T(8,128)S(1)}, f32[8,128]{1,0:T(8,128)S(1)}, u32[]{:S(2)}, u32[]{:S(2)}) %collective-permute-start.24) | collective-permute-done | bytes 4128 | tf_op jit(solution)/shard_map/ppermute | solution.py:434
  147.2 1.5 collective-permute-start.25
  151.3 2.5 %collective-permute-start.26 = (bf16[13,16,256]{2,1,0:T(8,128)(2,1)S(1)}, bf16[13,16,256]{2,1,0:T(8,128)(2,1)S(1)}, u32[]{:S(2)}, u32[]{:S(2)}) collective-permute-start(bf16[13,16,256]{2,1,0:T(8,128)(2,1)S(1)} %get-tuple-element.72), channel_id=1, source_target_pairs={{0,16},{1,17},{2,18},{3,19},{4,20},{5,21},{6,22},{7,23},{8,24},{9,... | collective-permute-start | bytes 319496 | tf_op jit(solution)/shard_map/ppermute | solution.py:277
  153.8 3.5 %collective-permute-start.27 = (bf16[13,16,256]{2,1,0:T(8,128)(2,1)S(1)}, bf16[13,16,256]{2,1,0:T(8,128)(2,1)S(1)}, u32[]{:S(2)}, u32[]{:S(2)}) collective-permute-start(bf16[13,16,256]{2,1,0:T(8,128)(2,1)S(1)} %get-tuple-element.73), channel_id=1, source_target_pairs={{0,32},{1,33},{2,34},{3,35},{4,36},{5,37},{6,38},{7,39},{8,40},{9,... | collective-permute-start | bytes 319496 | tf_op jit(solution)/shard_map/ppermute | solution.py:277
  157.2 3.2 %collective-permute-start.28 = (bf16[13,16,256]{2,1,0:T(8,128)(2,1)S(1)}, bf16[13,16,256]{2,1,0:T(8,128)(2,1)S(1)}, u32[]{:S(2)}, u32[]{:S(2)}) collective-permute-start(bf16[13,16,256]{2,1,0:T(8,128)(2,1)S(1)} %get-tuple-element.74), channel_id=1, source_target_pairs={{0,48},{1,49},{2,50},{3,51},{4,52},{5,53},{6,54},{7,55},{8,56},{9,... | collective-permute-start | bytes 319496 | tf_op jit(solution)/shard_map/ppermute | solution.py:277
  162.1 7.3 %stat_update.1 = (f32[2,256,1024]{2,1,0:T(8,128)}, f32[2,256,1024]{2,1,0:T(8,128)}) custom-call(s32[6]{0:T(128)} %copy-done.7, f32[2,2,8,128]{3,2,1,0:T(8,128)} %copy-done.6, bf16[2,4,256,256]{3,2,1,0:T(8,128)(2,1)} %copy-done.1, bf16[2,4,256,256]{3,2,1,0:T(8,128)(2,1)} %hold.10.in1, bf16[2,4,256,256]{3,2,1,0:T(8,128)(2,1)} %hold.11.in3, ...), custom_call_target="tpu_custom_call" | custom-call | flops 2147483648 | bytes 20971520 | tf_op jit(solution)/shard_map/stat_update/pallas_call | solution.py:438
  (107 shorter events, 26.5 us)
Async XLA Ops:
  3.5 6.5 %collective-permute-start = (bf16[6,16,1024]{2,1,0:T(8,128)(2,1)S(1)}, bf16[6,16,1024]{2,1,0:T(8,128)(2,1)S(1)}, u32[]{:S(2)}, u32[]{:S(2)}) collective-permute-start(bf16[6,16,1024]{2,1,0:T(8,128)(2,1)S(1)} %get-tuple-element.92), channel_id=1, source_target_pairs={{0,64},{64,128},{128,192},{192,0},{1,65},{65,129},{129,193},{193,1... | collective-permute-start | bytes 589832 | tf_op jit(solution)/shard_map/ppermute | solution.py:273
  5.7 5.1 %collective-permute-start.1 = (bf16[6,16,1024]{2,1,0:T(8,128)(2,1)S(1)}, bf16[6,16,1024]{2,1,0:T(8,128)(2,1)S(1)}, u32[]{:S(2)}, u32[]{:S(2)}) collective-permute-start(bf16[6,16,1024]{2,1,0:T(8,128)(2,1)S(1)} %get-tuple-element.91), channel_id=1, source_target_pairs={{0,192},{64,0},{128,64},{192,128},{1,193},{65,1},{129,65},{193,129... | collective-permute-start | bytes 589832 | tf_op jit(solution)/shard_map/ppermute | solution.py:273
  7.7 15.5 %collective-permute-start.4 = (bf16[6,16,1024]{2,1,0:T(8,128)(2,1)}, bf16[6,16,1024]{2,1,0:T(8,128)(2,1)S(1)}, u32[]{:S(2)}, u32[]{:S(2)}) collective-permute-start(bf16[6,16,1024]{2,1,0:T(8,128)(2,1)} %get-tuple-element.89), channel_id=1, source_target_pairs={{0,192},{64,0},{128,64},{192,128},{1,193},{65,1},{129,65},{193,129... | collective-permute-start | bytes 589832 | tf_op jit(solution)/shard_map/ppermute | solution.py:273
  9.8 13.5 %collective-permute-start.5 = (bf16[6,16,1024]{2,1,0:T(8,128)(2,1)}, bf16[6,16,1024]{2,1,0:T(8,128)(2,1)S(1)}, u32[]{:S(2)}, u32[]{:S(2)}) collective-permute-start(bf16[6,16,1024]{2,1,0:T(8,128)(2,1)} %get-tuple-element.87), channel_id=1, source_target_pairs={{0,64},{64,128},{128,192},{192,0},{1,65},{65,129},{129,193},{193,1... | collective-permute-start | bytes 589832 | tf_op jit(solution)/shard_map/ppermute | solution.py:273
  11.5 8.6 %collective-permute-start.2 = (bf16[6,16,1024]{2,1,0:T(8,128)(2,1)}, bf16[6,16,1024]{2,1,0:T(8,128)(2,1)S(1)}, u32[]{:S(2)}, u32[]{:S(2)}) collective-permute-start(bf16[6,16,1024]{2,1,0:T(8,128)(2,1)} %get-tuple-element.41), channel_id=1, source_target_pairs={{0,64},{64,128},{128,192},{192,0},{1,65},{65,129},{129,193},{193,1... | collective-permute-start | bytes 589832 | tf_op jit(solution)/shard_map/ppermute | solution.py:273
  13.0 7.1 %collective-permute-start.3 = (bf16[6,16,1024]{2,1,0:T(8,128)(2,1)S(1)}, bf16[6,16,1024]{2,1,0:T(8,128)(2,1)S(1)}, u32[]{:S(2)}, u32[]{:S(2)}) collective-permute-start(bf16[6,16,1024]{2,1,0:T(8,128)(2,1)S(1)} %get-tuple-element.42), channel_id=1, source_target_pairs={{0,192},{64,0},{128,64},{192,128},{1,193},{65,1},{129,65},{193,129... | collective-permute-start | bytes 589832 | tf_op jit(solution)/shard_map/ppermute | solution.py:273
  20.1 34.0 %collective-permute-start.11 = (bf16[2,1024,256]{2,1,0:T(8,128)(2,1)S(1)}, bf16[2,1024,256]{2,1,0:T(8,128)(2,1)}, u32[]{:S(2)}, u32[]{:S(2)}) collective-permute-start(bf16[2,1024,256]{2,1,0:T(8,128)(2,1)S(1)} %copy-done.2), channel_id=1, source_target_pairs={{0,64},{64,128},{128,192},{192,0},{1,65},{65,129},{129,193},{193,1... | collective-permute-start | bytes 3145736 | tf_op jit(solution)/shard_map/ppermute | solution.py:273
  20.2 33.9 %collective-permute-start.12 = (bf16[2,1024,256]{2,1,0:T(8,128)(2,1)S(1)}, bf16[2,1024,256]{2,1,0:T(8,128)(2,1)}, u32[]{:S(2)}, u32[]{:S(2)}) collective-permute-start(bf16[2,1024,256]{2,1,0:T(8,128)(2,1)S(1)} %copy-done.2), channel_id=1, source_target_pairs={{0,192},{64,0},{128,64},{192,128},{1,193},{65,1},{129,65},{193,129... | collective-permute-start | bytes 3145736 | tf_op jit(solution)/shard_map/ppermute | solution.py:273
  23.4 11.1 %collective-permute-start.6 = (bf16[12,16,256]{2,1,0:T(8,128)(2,1)S(1)}, bf16[12,16,256]{2,1,0:T(8,128)(2,1)S(1)}, u32[]{:S(2)}, u32[]{:S(2)}) collective-permute-start(bf16[12,16,256]{2,1,0:T(8,128)(2,1)S(1)} %get-tuple-element.46), channel_id=1, source_target_pairs={{0,16},{1,17},{2,18},{3,19},{4,20},{5,21},{6,22},{7,23},{8,24},{9,... | collective-permute-start | bytes 294920 | tf_op jit(solution)/shard_map/ppermute | solution.py:277
  26.9 9.3 %collective-permute-start.7 = (bf16[12,16,256]{2,1,0:T(8,128)(2,1)S(1)}, bf16[12,16,256]{2,1,0:T(8,128)(2,1)S(1)}, u32[]{:S(2)}, u32[]{:S(2)}) collective-permute-start(bf16[12,16,256]{2,1,0:T(8,128)(2,1)S(1)} %get-tuple-element.47), channel_id=1, source_target_pairs={{0,32},{1,33},{2,34},{3,35},{4,36},{5,37},{6,38},{7,39},{8,40},{9,... | collective-permute-start | bytes 294920 | tf_op jit(solution)/shard_map/ppermute | solution.py:277
  32.1 6.1 %collective-permute-start.8 = (bf16[12,16,256]{2,1,0:T(8,128)(2,1)S(1)}, bf16[12,16,256]{2,1,0:T(8,128)(2,1)S(1)}, u32[]{:S(2)}, u32[]{:S(2)}) collective-permute-start(bf16[12,16,256]{2,1,0:T(8,128)(2,1)S(1)} %get-tuple-element.48), channel_id=1, source_target_pairs={{0,48},{1,49},{2,50},{3,51},{4,52},{5,53},{6,54},{7,55},{8,56},{9,... | collective-permute-start | bytes 294920 | tf_op jit(solution)/shard_map/ppermute | solution.py:277
  34.5 30.4 %collective-permute-start.10 = (bf16[2,1024,256]{2,1,0:T(8,128)(2,1)S(1)}, bf16[2,1024,256]{2,1,0:T(8,128)(2,1)}, u32[]{:S(2)}, u32[]{:S(2)}) collective-permute-start(bf16[2,1024,256]{2,1,0:T(8,128)(2,1)S(1)} %copy-done), channel_id=1, source_target_pairs={{0,192},{64,0},{128,64},{192,128},{1,193},{65,1},{129,65},{193,129... | collective-permute-start | bytes 3145736 | tf_op jit(solution)/shard_map/ppermute | solution.py:273
  36.2 32.2 %collective-permute-start.9 = (bf16[1,1024,256]{2,1,0:T(8,128)(2,1)}, bf16[1,1024,256]{2,1,0:T(8,128)(2,1)}, u32[]{:S(2)}, u32[]{:S(2)}) collective-permute-start(bf16[1,1024,256]{2,1,0:T(8,128)(2,1)} %get-tuple-element.50), channel_id=1, source_target_pairs={{0,64},{64,128},{128,192},{192,0},{1,65},{65,129},{129,193},{193,1... | collective-permute-start | bytes 1572872 | tf_op jit(solution)/shard_map/ppermute | solution.py:273
  39.8 42.3 %all-to-all-start = ((bf16[64,2,16,256]{3,2,1,0:T(8,128)(2,1)}), bf16[64,2,16,256]{3,2,1,0:T(8,128)(2,1)S(1)}, u32[]{:S(2)}, u32[]{:S(2)}) async-start(bf16[64,2,16,256]{3,2,1,0:T(8,128)(2,1)} %spread.1), calls=%async_computation | async-start | bytes 2097152 | tf_op jit(solution)/shard_map/all_to_all | solution.py:378
  54.1 27.9 %collective-permute-start.13 = (bf16[2,1024,256]{2,1,0:T(8,128)(2,1)}, bf16[2,1024,256]{2,1,0:T(8,128)(2,1)S(1)}, u32[]{:S(2)}, u32[]{:S(2)}) collective-permute-start(bf16[2,1024,256]{2,1,0:T(8,128)(2,1)} %hold.8.r1), channel_id=1, source_target_pairs={{0,64},{64,128},{128,192},{192,0},{1,65},{65,129},{129,193},{193,1... | collective-permute-start | bytes 3145736 | tf_op jit(solution)/shard_map/ppermute | solution.py:273
  64.9 26.1 %collective-permute-start.18 = (bf16[2,1024,256]{2,1,0:T(8,128)(2,1)}, bf16[2,1024,256]{2,1,0:T(8,128)(2,1)}, u32[]{:S(2)}, u32[]{:S(2)}) collective-permute-start(bf16[2,1024,256]{2,1,0:T(8,128)(2,1)} %hold.7.refs_4_), channel_id=1, source_target_pairs={{0,192},{64,0},{128,64},{192,128},{1,193},{65,1},{129,65},{193,129... | collective-permute-start | bytes 3145736 | tf_op jit(solution)/shard_map/ppermute | solution.py:273
  68.5 22.6 %collective-permute-start.17 = (bf16[1,1024,256]{2,1,0:T(8,128)(2,1)}, bf16[1,1024,256]{2,1,0:T(8,128)(2,1)}, u32[]{:S(2)}, u32[]{:S(2)}) collective-permute-start(bf16[1,1024,256]{2,1,0:T(8,128)(2,1)} %copy-done.8), channel_id=1, source_target_pairs={{0,64},{64,128},{128,192},{192,0},{1,65},{65,129},{129,193},{193,1... | collective-permute-start | bytes 1572872 | tf_op jit(solution)/shard_map/ppermute | solution.py:273
  88.7 8.4 %collective-permute-start.14 = (bf16[2,256,256]{2,1,0:T(8,128)(2,1)S(1)}, bf16[2,256,256]{2,1,0:T(8,128)(2,1)S(1)}, u32[]{:S(2)}, u32[]{:S(2)}) collective-permute-start(bf16[2,256,256]{2,1,0:T(8,128)(2,1)S(1)} %get-tuple-element.59), channel_id=1, source_target_pairs={{0,192},{64,0},{128,64},{192,128},{1,193},{65,1},{129,65},{193,129... | collective-permute-start | bytes 786440 | tf_op jit(solution)/shard_map/ppermute | solution.py:273
  89.7 7.7 %collective-permute-start.15 = (bf16[2,256,256]{2,1,0:T(8,128)(2,1)S(1)}, bf16[2,256,256]{2,1,0:T(8,128)(2,1)S(1)}, u32[]{:S(2)}, u32[]{:S(2)}) collective-permute-start(bf16[2,256,256]{2,1,0:T(8,128)(2,1)S(1)} %get-tuple-element.60), channel_id=1, source_target_pairs={{0,128},{64,192},{128,0},{192,64},{1,129},{65,193},{129,1},{193,65... | collective-permute-start | bytes 786440 | tf_op jit(solution)/shard_map/ppermute | solution.py:273
  90.3 14.8 %collective-permute-start.16 = (bf16[2,256,256]{2,1,0:T(8,128)(2,1)S(1)}, bf16[2,256,256]{2,1,0:T(8,128)(2,1)S(1)}, u32[]{:S(2)}, u32[]{:S(2)}) collective-permute-start(bf16[2,256,256]{2,1,0:T(8,128)(2,1)S(1)} %get-tuple-element.61), channel_id=1, source_target_pairs={{0,64},{64,128},{128,192},{192,0},{1,65},{65,129},{129,193},{193,1... | collective-permute-start | bytes 786440 | tf_op jit(solution)/shard_map/ppermute | solution.py:273
  109.5 26.2 %collective-permute-start.29 = (bf16[2,4,256,256]{3,2,1,0:T(8,128)(2,1)S(1)}, bf16[2,4,256,256]{3,2,1,0:T(8,128)(2,1)S(1)}, u32[]{:S(2)}, u32[]{:S(2)}) collective-permute-start(bf16[2,4,256,256]{3,2,1,0:T(8,128)(2,1)S(1)} %get-tuple-element.76.in0), channel_id=1, source_target_pairs={{0,64},{64,128},{128,192},{192,0},{1,65},{65,129},{129,193},{193,1... | collective-permute-start | bytes 3145736 | tf_op jit(solution)/shard_map/ppermute | solution.py:273
  109.6 41.1 %all-to-all-start.1 = ((bf16[64,2,16,256]{3,2,1,0:T(8,128)(2,1)}), bf16[64,2,16,256]{3,2,1,0:T(8,128)(2,1)S(1)}, u32[]{:S(2)}, u32[]{:S(2)}) async-start(bf16[64,2,16,256]{3,2,1,0:T(8,128)(2,1)} %get-tuple-element.68), calls=%async_computation.1 | async-start | bytes 2097152 | tf_op jit(solution)/shard_map/all_to_all | solution.py:414
  121.8 15.0 %collective-permute-start.19 = (f32[2,4,8,128]{3,2,1,0:T(8,128)S(1)}, f32[2,4,8,128]{3,2,1,0:T(8,128)S(1)}, u32[]{:S(2)}, u32[]{:S(2)}) collective-permute-start(f32[2,4,8,128]{3,2,1,0:T(8,128)S(1)} %get-tuple-element.69.s0), channel_id=1, source_target_pairs={{0,64},{64,128},{128,192},{192,0},{1,65},{65,129},{129,193},{193,1... | collective-permute-start | bytes 98312 | tf_op jit(solution)/shard_map/ppermute | solution.py:273
  121.9 14.9 %collective-permute-start.20 = (f32[2,4,8,128]{3,2,1,0:T(8,128)S(1)}, f32[2,4,8,128]{3,2,1,0:T(8,128)S(1)}, u32[]{:S(2)}, u32[]{:S(2)}) collective-permute-start(f32[2,4,8,128]{3,2,1,0:T(8,128)S(1)} %get-tuple-element.69.s0), channel_id=1, source_target_pairs={{0,128},{64,192},{128,0},{192,64},{1,129},{65,193},{129,1},{193,65... | collective-permute-start | bytes 98312 | tf_op jit(solution)/shard_map/ppermute | solution.py:273
  125.3 11.5 %collective-permute-start.21 = (f32[2,4,8,128]{3,2,1,0:T(8,128)S(1)}, f32[2,4,8,128]{3,2,1,0:T(8,128)S(1)}, u32[]{:S(2)}, u32[]{:S(2)}) collective-permute-start(f32[2,4,8,128]{3,2,1,0:T(8,128)S(1)} %get-tuple-element.69.s0), channel_id=1, source_target_pairs={{0,192},{64,0},{128,64},{192,128},{1,193},{65,1},{129,65},{193,129... | collective-permute-start | bytes 98312 | tf_op jit(solution)/shard_map/ppermute | solution.py:273
  127.2 23.5 %collective-permute-start.30 = (bf16[2,4,256,256]{3,2,1,0:T(8,128)(2,1)S(1)}, bf16[2,4,256,256]{3,2,1,0:T(8,128)(2,1)}, u32[]{:S(2)}, u32[]{:S(2)}) collective-permute-start(bf16[2,4,256,256]{3,2,1,0:T(8,128)(2,1)S(1)} %get-tuple-element.76.in0), channel_id=1, source_target_pairs={{0,192},{64,0},{128,64},{192,128},{1,193},{65,1},{129,65},{193,129... | collective-permute-start | bytes 3145736 | tf_op jit(solution)/shard_map/ppermute | solution.py:273
  136.8 24.4 %collective-permute-start.31 = (bf16[2,4,256,256]{3,2,1,0:T(8,128)(2,1)}, bf16[2,4,256,256]{3,2,1,0:T(8,128)(2,1)S(1)}, u32[]{:S(2)}, u32[]{:S(2)}) collective-permute-start(bf16[2,4,256,256]{3,2,1,0:T(8,128)(2,1)} %hold.10.in1), channel_id=1, source_target_pairs={{0,64},{64,128},{128,192},{192,0},{1,65},{65,129},{129,193},{193,1... | collective-permute-start | bytes 3145736 | tf_op jit(solution)/shard_map/ppermute | solution.py:273
  140.1 2.9 %collective-permute-start.23 = (f32[8,128]{1,0:T(8,128)S(1)}, f32[8,128]{1,0:T(8,128)S(1)}, u32[]{:S(2)}, u32[]{:S(2)}) collective-permute-start(f32[8,128]{1,0:T(8,128)S(1)} %add.134), channel_id=1, source_target_pairs={{0,2},{1,3},{2,0},{3,1},{4,6},{5,7},{6,4},{7,5},{8,10},{9,11},{10,... | collective-permute-start | bytes 12296 | tf_op jit(solution)/shard_map/ppermute | solution.py:434
  143.0 4.3 %collective-permute-start.24 = (f32[8,128]{1,0:T(8,128)S(1)}, f32[8,128]{1,0:T(8,128)S(1)}, u32[]{:S(2)}, u32[]{:S(2)}) collective-permute-start(f32[8,128]{1,0:T(8,128)S(1)} %add.135), channel_id=1, source_target_pairs={{0,4},{1,5},{2,6},{3,7},{4,0},{5,1},{6,2},{7,3},{8,12},{9,13},{10,... | collective-permute-start | bytes 12296 | tf_op jit(solution)/shard_map/ppermute | solution.py:434
  151.3 18.1 %collective-permute-start.26 = (bf16[13,16,256]{2,1,0:T(8,128)(2,1)S(1)}, bf16[13,16,256]{2,1,0:T(8,128)(2,1)S(1)}, u32[]{:S(2)}, u32[]{:S(2)}) collective-permute-start(bf16[13,16,256]{2,1,0:T(8,128)(2,1)S(1)} %get-tuple-element.72), channel_id=1, source_target_pairs={{0,16},{1,17},{2,18},{3,19},{4,20},{5,21},{6,22},{7,23},{8,24},{9,... | collective-permute-start | bytes 319496 | tf_op jit(solution)/shard_map/ppermute | solution.py:277
  153.8 15.7 %collective-permute-start.27 = (bf16[13,16,256]{2,1,0:T(8,128)(2,1)S(1)}, bf16[13,16,256]{2,1,0:T(8,128)(2,1)S(1)}, u32[]{:S(2)}, u32[]{:S(2)}) collective-permute-start(bf16[13,16,256]{2,1,0:T(8,128)(2,1)S(1)} %get-tuple-element.73), channel_id=1, source_target_pairs={{0,32},{1,33},{2,34},{3,35},{4,36},{5,37},{6,38},{7,39},{8,40},{9,... | collective-permute-start | bytes 319496 | tf_op jit(solution)/shard_map/ppermute | solution.py:277
  157.2 12.2 %collective-permute-start.28 = (bf16[13,16,256]{2,1,0:T(8,128)(2,1)S(1)}, bf16[13,16,256]{2,1,0:T(8,128)(2,1)S(1)}, u32[]{:S(2)}, u32[]{:S(2)}) collective-permute-start(bf16[13,16,256]{2,1,0:T(8,128)(2,1)S(1)} %get-tuple-element.74), channel_id=1, source_target_pairs={{0,48},{1,49},{2,50},{3,51},{4,52},{5,53},{6,54},{7,55},{8,56},{9,... | collective-permute-start | bytes 319496 | tf_op jit(solution)/shard_map/ppermute | solution.py:277
  (15 other events, 183.7 us)
